TPU v7x, 128 devices: a whole 4x4x4 slice. The times are simulated.
128 devices in a mesh: row: 8 (over y, x_hi), col: 16 (over x_lo, z, core).
Axes of the slice: x: 4 (x_hi: 2, x_lo: 2; x = x_hi * 2 + x_lo), y: 4, z: 4, core: 2. Of those that a mesh axis runs over, the one named last changes fastest.
Arguments:
- view_a: float32 [2048, 16384], P('col', 'row'), may hold values from -200 to 200
- view_b: float32 [2048, 16384], P('row', 'col'), may hold values from -200 to 200
Outputs:
- loss_value: float32 [], replicated
- grad_a: float32 [2048, 16384], P('col', 'row')
- grad_b: float32 [2048, 16384], P('row', 'col')
All inputs are finite; a program needn't handle non-finite values.
Results may differ from a plain program's by a relative error of at most 0.0038.
Values may be sent and summed in bfloat16 or wider, within the bound.
No kernel may reach another device: no remote copies, remote signals or barrier semaphores. Data moves between devices by JAX's collectives and lax.ppermute only.
A program may use at most 192 MiB of HBM per device.

v0:
```python
import jax
import jax.numpy as jnp
from jax import lax
from jax.sharding import PartitionSpec as P

FEAT = 16384


off_weight = 0.0051
eps_value = 1e-05


def finish_stats(sums, squares, count, view):
    mean = sums / count
    inv = lax.rsqrt(squares / count - mean * mean + eps_value)
    return ((view - mean) * inv, inv)


def apply_back(upper, norm, inv, first, second, count):
    return inv * (upper - first / count - norm * (second / count))


def tile_terms(corr, height, breadth):
    row_ids = lax.axis_index("row") * height + jnp.arange(height)
    col_ids = lax.axis_index("col") * breadth + jnp.arange(breadth)
    diag = row_ids[:, None] == col_ids[None, :]
    miss = 1.0 - corr
    local_loss = jnp.sum(jnp.where(diag, miss * miss, off_weight * corr * corr))
    slope = jnp.where(diag, -2.0 * miss, 2.0 * off_weight * corr)
    return (local_loss, slope)


def against_rows(partner, slope):
    return lax.dot_general(
        partner.astype(jnp.float32),
        slope,
        (((1,), (1,)), ((), ())),
        precision=lax.Precision.HIGHEST,
        preferred_element_type=jnp.float32,
    )


def along_rows(partner, slope):
    return jnp.dot(
        partner.astype(jnp.float32),
        slope,
        precision=lax.Precision.HIGHEST,
        preferred_element_type=jnp.float32,
    )


def local(view_a, view_b):
    count = view_a.shape[0] * lax.axis_size("col")
    sums_a, squares_a = lax.psum((jnp.sum(view_a, axis=0), jnp.sum(view_a * view_a, axis=0)), "col")
    sums_b, squares_b = lax.psum((jnp.sum(view_b, axis=0), jnp.sum(view_b * view_b, axis=0)), "row")
    norm_a, inv_a = finish_stats(sums_a, squares_a, count, view_a)
    norm_b, inv_b = finish_stats(sums_b, squares_b, count, view_b)
    half_a = norm_a.astype(jnp.bfloat16)
    half_b = norm_b.astype(jnp.bfloat16)
    all_b = lax.all_gather(half_b, "row", axis=0, tiled=True)
    height = view_a.shape[1]
    breadth = view_b.shape[1]
    contract_rows = (((0,), (0,)), ((), ()))
    all_a = lax.all_gather(half_a, "col", axis=0, tiled=True)
    corr = lax.dot_general(all_a, all_b, contract_rows, preferred_element_type=jnp.float32) / count
    local_loss, slope = tile_terms(corr, height, breadth)
    up_a = lax.psum_scatter(against_rows(all_b, slope), "col", scatter_dimension=0, tiled=True)
    up_b = lax.psum_scatter(along_rows(all_a, slope), "row", scatter_dimension=0, tiled=True)
    loss_value = lax.psum(local_loss, ("row", "col")) / FEAT
    first_a, second_a = lax.psum((jnp.sum(up_a, axis=0), jnp.sum(up_a * norm_a, axis=0)), "col")
    first_b, second_b = lax.psum((jnp.sum(up_b, axis=0), jnp.sum(up_b * norm_b, axis=0)), "row")
    grad_a = apply_back(up_a, norm_a, inv_a, first_a, second_a, count)
    grad_b = apply_back(up_b, norm_b, inv_b, first_b, second_b, count)
    return (loss_value, grad_a, grad_b)


def solution(mesh):
    return jax.shard_map(
        local,
        mesh=mesh,
        in_specs=(P("col", "row"), P("row", "col")),
        out_specs=(P(), P("col", "row"), P("row", "col")),
        check_vma=False,
    )
```

profile of v0, /device:TPU:9, one launch (start us, length us, event | category | flops | bytes accessed | tf_op | source)
XLA Modules:
  0.0 482.6 jit_solution(2687141168416578961)
XLA Ops:
  7.2 0.0 all-gather.5.cloned.1.call-start
  7.2 1.4 fusion.27
  8.6 18.8 %all-reduce.3 = (f32[1024]{0:T(1024)S(1)}, f32[1024]{0:T(1024)S(1)}) all-reduce(f32[1024]{0:T(1024)S(1)} %get-tuple-element.8, f32[1024]{0:T(1024)S(1)} %get-tuple-element.7), channel_id=1, replica_groups=mesh['row'=8,'col'=16] {'row'}, use_global_device_ids=true, to_apply=%region_7.0 | all-reduce | flops 2048 | bytes 16384 | tf_op jit(solution)/shard_map/psum | solution.py:55
  27.4 2.1 fusion.16
  29.5 0.0 all-gather.5.cloned.1.call-update
  29.6 0.0 all-gather.3.cloned.1.call-start
  29.6 1.4 fusion.28
  31.0 53.4 %all-reduce.1 = (f32[2048]{0:T(1024)S(1)}, f32[2048]{0:T(1024)S(1)}) all-reduce(f32[2048]{0:T(1024)S(1)} %get-tuple-element.10, f32[2048]{0:T(1024)S(1)} %get-tuple-element.9), channel_id=1, replica_groups=mesh['row'=8,'col'=16] {'col'}, use_global_device_ids=true, to_apply=%region_3.0 | all-reduce | flops 4096 | bytes 32768 | tf_op jit(solution)/shard_map/psum | solution.py:54
  84.4 2.1 fusion.15
  86.5 0.0 all-gather.3.cloned.1.call-update
  86.5 0.0 reduce-scatter.5.cloned.1.call-start
  86.6 16.2 %all-gather.5.cloned.1.call-done = bf16[2048,1024]{1,0:T(8,128)(2,1)} async-done(((bf16[256,1024]{1,0:T(8,128)(2,1)}), bf16[2048,1024]{1,0:T(8,128)(2,1)}) %all-gather.5.cloned.1.call-update) | async-done | bytes 4194320 | tf_op jit(solution)/shard_map/all_gather | solution.py:60
  102.8 54.3 %all-gather.3.cloned.1.call-done = bf16[2048,2048]{1,0:T(8,128)(2,1)} async-done(((bf16[128,2048]{1,0:T(8,128)(2,1)}), bf16[2048,2048]{1,0:T(8,128)(2,1)}) %all-gather.3.cloned.1.call-update) | async-done | bytes 8388624 | tf_op jit(solution)/shard_map/all_gather | solution.py:64
  157.1 0.0 copy-start.2
  157.1 15.7 %fusion = (f32[]{:T(128)}, f32[2048,1024]{1,0:T(8,128)S(1)}) fusion(s32[1024]{0:T(1024)S(1)} %iota_add_fusion.1, s32[2048]{0:T(1024)S(1)} %iota_add_fusion, bf16[2048,2048]{1,0:T(8,128)(2,1)} %all-gather.3.cloned.1.call-done, bf16[2048,1024]{1,0:T(8,128)(2,1)} %all-gather.5.cloned.1.call-done), kind=kOutput, calls=%fused_computation.2 | convolution fusion | flops 8606711808 | bytes 20983812 | tf_op jit(solution)/shard_map/dot_general | solution.py:65
  172.8 0.0 copy-start.3
  172.8 3.2 copy-done.3
  176.1 0.0 copy-done.2
  176.1 29.2 %fusion.1 = f32[2048,1024]{1,0:T(8,128)} fusion(bf16[2048,2048]{1,0:T(8,128)(2,1)S(1)} %copy-done.2, f32[2048,1024]{1,0:T(8,128)S(1)} %get-tuple-element.24, s32[1024]{0:T(1024)S(1)} %iota_add_fusion.1, s32[2048]{0:T(1024)S(1)} %iota_add_fusion), kind=kOutput, calls=%fused_computation.3 | convolution fusion | flops 51552190464 | bytes 25178112 | tf_op jit(solution)/shard_map/dot_general | solution.py:44
  205.3 0.0 reduce-scatter.5.cloned.1.call-update
  205.3 0.0 reduce-scatter.3.cloned.1.call-start
  205.4 33.4 %fusion.2 = f32[2048,2048]{1,0:T(8,128)} fusion(bf16[2048,1024]{1,0:T(8,128)(2,1)} %all-gather.5.cloned.1.call-done, f32[2048,1024]{1,0:T(8,128)} %copy-done.3, s32[1024]{0:T(1024)S(1)} %iota_add_fusion.1, s32[2048]{0:T(1024)S(1)} %iota_add_fusion), kind=kOutput, calls=%fused_computation.4 | convolution fusion | flops 51552190464 | bytes 29372416 | tf_op jit(solution)/shard_map/dot_general | solution.py:34
  238.8 0.0 copy-start
  238.8 0.0 copy-start.1
  238.8 0.0 reduce-scatter.3.cloned.1.call-update
  238.8 77.2 %psum.67 = f32[]{:T(128)} all-reduce(f32[]{:T(128)} %get-tuple-element.23), channel_id=1, replica_groups=mesh['row'=8,'col'=16] {'row','col'}, use_global_device_ids=true, to_apply=%region_9.10 | all-reduce | flops 1 | bytes 8 | tf_op jit(solution)/shard_map/psum | solution.py:69
  316.7 3.2 reduce-scatter.5.cloned.1.call-done
  319.9 0.0 copy-done
  319.9 1.5 fusion.25
  321.4 15.8 %all-reduce.2 = (f32[1024]{0:T(1024)S(1)}, f32[1024]{0:T(1024)S(1)}) all-reduce(f32[1024]{0:T(1024)S(1)} %get-tuple-element.4, f32[1024]{0:T(1024)S(1)} %get-tuple-element.3), channel_id=1, replica_groups=mesh['row'=8,'col'=16] {'row'}, use_global_device_ids=true, to_apply=%region_19.20 | all-reduce | flops 2048 | bytes 16384 | tf_op jit(solution)/shard_map/psum | solution.py:71
  337.2 2.5 subtract_multiply_fusion
  339.7 78.8 %reduce-scatter.3.cloned.1.call-done = f32[128,2048]{1,0:T(8,128)} async-done(((f32[2048,2048]{1,0:T(8,128)}), f32[128,2048]{1,0:T(8,128)}) %reduce-scatter.3.cloned.1.call-update) | async-done | bytes 1048592 | tf_op jit(solution)/shard_map/reduce_scatter | solution.py:67
  418.5 0.0 copy-done.1
  418.5 1.5 fusion.26
  420.0 52.5 %all-reduce = (f32[2048]{0:T(1024)S(1)}, f32[2048]{0:T(1024)S(1)}) all-reduce(f32[2048]{0:T(1024)S(1)} %get-tuple-element.6, f32[2048]{0:T(1024)S(1)} %get-tuple-element.5), channel_id=1, replica_groups=mesh['row'=8,'col'=16] {'col'}, use_global_device_ids=true, to_apply=%region_14.15 | all-reduce | flops 4096 | bytes 32768 | tf_op jit(solution)/shard_map/psum | solution.py:70
  472.5 2.5 subtract_multiply_fusion.1
  (6 shorter events, 0.0 us)
Async XLA Ops:
  7.2 95.6 %all-gather.5.cloned.1.call-start = ((), (), s32[]{:S(2)}) async-start(), calls=%async_computation.3 | async-start | bytes 4718592 | tf_op jit(solution)/shard_map/all_gather | solution.py:60
  29.6 127.6 %all-gather.3.cloned.1.call-start = ((), (), s32[]{:S(2)}) async-start(), calls=%async_computation.2 | async-start | bytes 8912896 | tf_op jit(solution)/shard_map/all_gather | solution.py:64
  86.5 233.4 %reduce-scatter.5.cloned.1.call-start = ((), (), s32[]{:S(2)}) async-start(), calls=%async_computation.5 | async-start | bytes 9437184 | tf_op jit(solution)/shard_map/reduce_scatter | solution.py:68
  157.1 18.9 %copy-start.2 = (bf16[2048,2048]{1,0:T(8,128)(2,1)S(1)}, bf16[2048,2048]{1,0:T(8,128)(2,1)}, u32[]{:S(2)}) copy-start(bf16[2048,2048]{1,0:T(8,128)(2,1)} %all-gather.3.cloned.1.call-done) | copy-start | bytes 25165828
  172.8 3.2 copy-start.3
  205.3 213.2 %reduce-scatter.3.cloned.1.call-start = ((), (), s32[]{:S(2)}) async-start(), calls=%async_computation.4 | async-start | bytes 17825792 | tf_op jit(solution)/shard_map/reduce_scatter | solution.py:67
  238.8 81.1 %copy-start = (f32[256,1024]{1,0:T(8,128)S(1)}, f32[256,1024]{1,0:T(8,128)}, u32[]{:S(2)}) copy-start(f32[256,1024]{1,0:T(8,128)} %param.3) | copy-start | bytes 3145732
  238.8 179.7 %copy-start.1 = (f32[128,2048]{1,0:T(8,128)S(1)}, f32[128,2048]{1,0:T(8,128)}, u32[]{:S(2)}) copy-start(f32[128,2048]{1,0:T(8,128)} %param.2) | copy-start | bytes 3145732
Sparse Core Ops, SparseCore 0:
  29.7 73.0 all-gather.4
  105.1 52.0 all-gather.2
  205.4 114.4 reduce-scatter.4
  322.3 96.1 reduce-scatter.2
where the time goes:
time: 487 us; the launch traced here: 483 us
  blocking collectives  218 us (45%)
  waiting for transfers between devices  153 us (31%)
  matrix products  78.4 us (16%)
  between operations  15.6 us (3%)
  other arithmetic  15 us (3%)
    reduce_scatter x1, waiting for transfers between devices, local(): lax.psum_scatter(against_rows(all_b, slope), 'col', scatter_dimension=0,...  78.8 us
    psum x1, blocking collectives, local(): loss_value = lax.psum(local_loss, ('row', 'col')) / FEAT  77.2 us
    all_gather x1, waiting for transfers between devices, local(): all_a = lax.all_gather(half_a, 'col', axis=0, tiled=True)  54.3 us
    psum x1, blocking collectives, local(): lax.psum((jnp.sum(view_a, axis=0), jnp.sum(view_a * view_a, axis=0)), 'col')  53.4 us
    psum x1, blocking collectives, local(): lax.psum((jnp.sum(up_a, axis=0), jnp.sum(up_a * norm_a, axis=0)), 'col')  52.5 us
    dot_general x1, matrix products, against_rows(): lax.dot_general(partner.astype(jnp.float32), slope, (((1,), (1,)), ((), (...  33.4 us
    dot_general x1, matrix products, along_rows(): jnp.dot(partner.astype(jnp.float32), slope, precision=lax.Precision.HIGHE...  29.2 us
    psum x1, blocking collectives, local(): lax.psum((jnp.sum(view_b, axis=0), jnp.sum(view_b * view_b, axis=0)), 'row')  18.8 us
  transfers between devices with their start and end apart: 4, of which 4 were waited for; matrix products, arithmetic and copies ran while one was open for 8% of the time, Pallas kernels for 0%

commit v1 on v0

v1 whole, which is shorter than its diff:
```python
import functools

import jax
import jax.numpy as jnp
from jax import lax
from jax.experimental import pallas as pl
from jax.experimental.pallas import tpu as pltpu
from jax.sharding import Mesh, PartitionSpec as P

FEAT = 16384
BATCH = 2048

off_weight = 0.0051
eps_value = 1e-05

f32 = jnp.float32
bf16 = jnp.bfloat16

NAMES = ("y1", "y0", "xh", "xl", "z1", "z0", "k")
ROW = ("y1", "y0", "xh")
COL = ("xl", "z1", "z0", "k")
SWAP = [(0, 1), (1, 0)]
AHEAD = [(i, (i + 1) % 4) for i in range(4)]
BACK = [(i, (i + 3) % 4) for i in range(4)]


TURN_A = (((0, 1, 0), (1, 0, 0), (1, 0, 1)), ((0, 1, 0, 1), (1, 1, 1, 0), (0, 1, 0, 1)))
TURN_B = ((((0, 0, 1), (0, 1, 0), (1, 0, 0)), ((0, 1, 1, 1), (1, 0, 1, 1), (1, 0, 1, 0))),) * 2


def spread(x, axes, n):
    return lax.all_to_all(jnp.broadcast_to(x[None], (n,) + x.shape), axes, 0, 0)


def bits(n):
    return [(n >> s) & 1 for s in range(6, -1, -1)]


def number(p):
    return sum(v << s for v, s in zip(p, range(6, -1, -1)))


def turned(first, second, rows):
    matrix, shift = rows
    out = []
    for m, v in zip(matrix, shift):
        out.append((sum(a * b for a, b in zip(m, first)) + sum(a * b for a, b in zip(v, second))) % 2)
    return out


def crossing_tables():
    pairs_a, wanted_a = [], [[0, 0, 0]] * 128
    pairs_b, wanted_b = [[], []], [[0] * 8 for _ in range(128)]
    for target in range(128):
        y1, y0, xh, xl, z1, z0, k = bits(target)
        g = turned((y1, y0, xh), (xl, z1, z0, k), TURN_A)
        source = number((xl, z1, z0, k, g[0], g[1], g[2]))
        pairs_a.append((source, target))
        wanted_a[source] = [y0, xh, y1]
        for step in range(2):
            g = turned((xl, z1, z0), (y1, y0, xh, k), TURN_B[step])
            source = number((g[0], g[1], g[2], y1, y0, xh, k ^ step))
            pairs_b[step].append((source, target))
            wanted_b[source][4 * step : 4 * step + 4] = [xl, z1, z0, k]
    return pairs_a, wanted_a, pairs_b, wanted_b


def finish_stats(sums, count, view):
    mean = sums[0] / count
    inv = lax.rsqrt(sums[1] / count - mean * mean + eps_value)
    return ((view - mean) * inv, mean, inv)


def stats(view):
    return jnp.stack([jnp.sum(view, axis=0), jnp.sum(view * view, axis=0)])


def dot(x, y, dims):
    return lax.dot_general(x, y, (dims, ((), ())), preferred_element_type=f32)


def pick(x, index):
    return lax.dynamic_index_in_dim(x, index, 0, keepdims=False)


def both(which, mine, other, axis):
    return jnp.concatenate([jnp.where(which == 0, mine, other), jnp.where(which == 0, other, mine)], axis=axis)


def tie(*xs):
    return lax.optimization_barrier(xs)


def ring_near(own, ring):
    return [lax.ppermute(own, ring, AHEAD), lax.ppermute(own, ring, BACK)]


def trade(blocks, axis):
    return [lax.ppermute(x, axis, SWAP) for x in blocks]


OFFSETS = (0, 3, 1, 2)


def places(ids):
    return [((ids[0] + offset) & 3, ids[1] ^ flip) for flip in range(2) for offset in OFFSETS]


def gram_kernel(first, ids, *refs):
    if first:
        result, send, held, sems, out, out_sems = refs[8:]
    else:
        mine, give, *sends, held, sems = refs[8:]
    copies = []
    for i, ref in enumerate(refs[:8]):
        slot = held.at[i // 4, pl.ds(256 * (i % 4), 256), :]
        copies.append(pltpu.make_async_copy(ref, slot, sems.at[i]))
        copies[-1].start()
    copies[0].wait()
    own = held[0, 0:256, :].T
    leaving = []
    for flip in range(2):
        for index in range(4 * flip, 4 * flip + 4):
            if index:
                copies[index].wait()
        prod = dot(held[flip], own, ((1,), (0,))).astype(bf16)
        for index in range(4 * flip, 4 * flip + 4):
            p, k = places(ids)[index]
            high, low = p >> 1, p & 1
            for s in range(2):
                at = 256 * (index % 4) + 128 * s
                part = prod[at : at + 128]
                if first:
                    rows = pl.ds(pl.multiple_of(128 * k, 128), 128)
                    for half in range(2):
                        out[2 * (2 * s + high) + low, half, rows, :] = part[:, 128 * half : 128 * (half + 1)]
                    wanted = (high == ids[2]) & (low == ids[3]) & (s == ids[4])

                    @pl.when(wanted)
                    def _():
                        send[k] = held[flip, at : at + 128, :]

                else:

                    @pl.when(ids[10] == s)
                    def _():
                        mine[2 * p + k] = part

                    @pl.when(ids[10] != s)
                    def _():
                        give[2 * p + k] = part

                    for step in range(2):
                        place = [ids[2 + 4 * step + j] for j in range(4)]
                        wanted = (high == place[0]) & (low == place[1]) & (k == place[2]) & (s == place[3])

                        @pl.when(wanted)
                        def _():
                            if step == 0:
                                sends[0][...] = held[flip, at : at + 64, :]
                                sends[1][...] = held[flip, at + 64 : at + 128, :]
                            else:
                                sends[2][...] = held[flip, at : at + 128, :]

        if first:
            rows = pl.ds(pl.multiple_of(128 * (ids[1] ^ flip), 128), 128)
            away = pltpu.make_async_copy(out.at[:, :, rows, :], result.at[:, :, rows, :], out_sems.at[flip])
            away.start()
            leaving.append(away)
    for away in leaving:
        away.wait()


def call(kernel, out_shape, extra, name, space=pltpu.VMEM, scratch=(), flops=2 * 256 * 2048 * 1024, far=()):
    vmem = pl.BlockSpec(memory_space=pltpu.VMEM)
    return pl.pallas_call(
        kernel,
        out_shape=out_shape,
        in_specs=[pl.BlockSpec(memory_space=pltpu.SMEM)] + [vmem] * extra + [pl.BlockSpec(memory_space=space)] * 8,
        out_specs=[pl.BlockSpec(memory_space=pltpu.HBM) if i in far else vmem for i in range(len(out_shape))],
        scratch_shapes=list(scratch),
        compiler_params=pltpu.CompilerParams(vmem_limit_bytes=14 * 1024 * 1024),
        cost_estimate=pl.CostEstimate(flops=flops, bytes_accessed=flops >> 8, transcendentals=0),
        name=name,
    )


def gram_part(first, ids, blocks):
    if first:
        shapes = [(8, 2, 256, 128), (2, 128, 1024)]
    else:
        shapes = [(8, 128, 256), (8, 128, 256), (64, 1024), (64, 1024), (128, 1024)]
    out = [jax.ShapeDtypeStruct(shape, bf16) for shape in shapes]
    scratch = [pltpu.VMEM((2, 1024, 1024), bf16), pltpu.SemaphoreType.DMA((8,))]
    if first:
        scratch += [pltpu.VMEM((8, 2, 256, 128), bf16), pltpu.SemaphoreType.DMA((2,))]
    flops = 2 * 256 * 2048 * 1024 if first else 1 << 20
    kernel = functools.partial(gram_kernel, first)
    return call(kernel, out, 0, "gram_part", pl.ANY, scratch, flops, (0,) if first else ())(ids, *blocks)


def blend_kernel(mine, traded, received, out):
    piece = received[0].astype(f32)
    for i in range(1, 16):
        piece = piece + received[i].astype(f32)
    piece = piece.astype(bf16)
    for i in range(8):
        out[i, 0:128] = (mine[i].astype(f32) + traded[i].astype(f32)).astype(bf16)
        out[i, 128:256, 0:128] = piece[0:128]
        out[i, 128:256, 128:256] = piece[128:256]


def blend(mine, traded, received):
    vmem = pl.BlockSpec(memory_space=pltpu.VMEM)
    return pl.pallas_call(
        blend_kernel,
        out_shape=jax.ShapeDtypeStruct((8, 256, 256), bf16),
        in_specs=[vmem] * 3,
        out_specs=vmem,
        compiler_params=pltpu.CompilerParams(vmem_limit_bytes=14 * 1024 * 1024),
        cost_estimate=pl.CostEstimate(flops=1 << 20, bytes_accessed=4 << 20, transcendentals=0),
        name="blend",
    )(mine, traded, received)


def apply(part, blocks, ids):
    out = None
    for ref, (p, k) in zip(blocks, places(ids)):
        left = jnp.concatenate([part(p >> 1, p & 1, k, s) for s in range(2)], axis=1)
        prod = dot(left, ref[...], ((1,), (0,)))
        out = prod if out is None else out + prod
    return out * (2.0 * off_weight / BATCH)


def image_sum(x):
    return jnp.sum(x, axis=0, keepdims=True)


def split(x):
    high = x.astype(bf16).astype(f32)
    return [high, x - high]


def send_all(part, result, start, rows, sems, first_sem):
    copies = []
    for i in range(16):
        copies.append(pltpu.make_async_copy(part, result.at[i, start : start + rows], sems.at[first_sem + i]))
        copies[-1].start()
    return copies


def second_kernel(ids, mixed, traded, partner, *refs):
    blocks, up, result, out, sems = refs[:8], refs[8], refs[9], refs[10], refs[11]

    def part(high, low, k, s):
        index = 4 * high + 2 * low + k
        rows = jnp.where(ids[10] == s, mixed[index, 128:256, :], traded[index])
        return jnp.concatenate([rows[:, 0:128], rows[:, 128:256]], axis=0)

    piece = mixed[0, 0:128].astype(f32)
    for i in range(1, 8):
        piece = piece + mixed[i, 0:128].astype(f32)
    out[0:128] = piece.astype(bf16)
    leaving = send_all(out.at[0:128], result, 0, 128, sems, 0)
    value = apply(part, blocks, ids)
    up[...] = value
    norm = blocks[0][...].astype(f32)
    sums = [image_sum(value), partner[0:1], image_sum(norm), jnp.zeros((1, 1024), f32)]
    sums += split(image_sum(value * norm)) + split(partner[1:2])
    row = lax.broadcasted_iota(jnp.int32, (8, 1024), 0)
    rows = jnp.zeros((8, 1024), f32)
    for i in range(8):
        rows = jnp.where(row == i, sums[i], rows)
    rows = jnp.concatenate([rows[:, 256 * i : 256 * (i + 1)] for i in range(4)], axis=0).astype(bf16)
    out[128:160] = rows
    leaving += send_all(out.at[128:160], result, 128, 32, sems, 16)
    for away in leaving:
        away.wait()


def second_view(ids, mixed, traded, partner, blocks):
    out = [jax.ShapeDtypeStruct((256, 1024), f32), jax.ShapeDtypeStruct((16, 160, 256), bf16)]
    scratch = [pltpu.VMEM((160, 256), bf16), pltpu.SemaphoreType.DMA((32,))]
    return call(second_kernel, out, 3, "second_view", scratch=scratch, far=(1,))(ids, mixed, traded, partner, *blocks)


def first_kernel(ids, last, *refs):
    blocks, keep, give, result, out, sems = refs[:8], refs[8], refs[9], refs[10], refs[11], refs[12]

    def part(high, low, k, s):
        at = pl.ds(pl.multiple_of(k * 128, 128), 128)
        index = 4 * (2 * s + high) + 2 * low
        return jnp.concatenate([last[index, 0:128, at], last[index + 1, 0:128, at]], axis=0)

    value = apply(part, blocks, ids)
    side = ids[5]
    keep[...] = jnp.where(side == 0, value[0:128], value[128:256])
    give[...] = jnp.where(side == 0, value[128:256], value[0:128]).astype(bf16)
    sums = [image_sum(value), image_sum(value * blocks[0][...].astype(f32))]
    terms = None
    for i in range(8):
        term = last[2 * i + side, 128:160].astype(f32)
        terms = term if terms is None else terms + term
    row = lax.broadcasted_iota(jnp.int32, (32, 256), 0) % 8
    loss = image_sum(jnp.where((row == 4) | (row == 5), terms, 0.0)) / (2.0 * BATCH)
    products = []
    for j in range(4):
        products.append(terms[8 * j + 6 : 8 * j + 7] + terms[8 * j + 7 : 8 * j + 8])
        corr = products[-1] / BATCH
        miss = 1.0 - corr
        loss = loss + miss * miss - off_weight * corr * corr
    sums.append(jnp.concatenate([loss, jnp.zeros((1, 768), f32)], axis=1))
    sums.append(jnp.concatenate([terms[8 * j + 2 : 8 * j + 3] for j in range(4)], axis=1))
    sums.append(jnp.concatenate(products, axis=1))
    for j in range(8):
        out[j : j + 1, :] = sums[j] if j < 5 else jnp.zeros((1, 1024), f32)
    for away in send_all(out, result, 0, 8, sems, 0):
        away.wait()


def first_view(ids, last, blocks):
    out = [
        jax.ShapeDtypeStruct((128, 1024), f32),
        jax.ShapeDtypeStruct((128, 1024), bf16),
        jax.ShapeDtypeStruct((16, 8, 1024), f32),
    ]
    scratch = [pltpu.VMEM((8, 1024), f32), pltpu.SemaphoreType.DMA((16,))]
    return call(first_kernel, out, 1, "first_view", scratch=scratch, far=(2,))(ids, last, *blocks)


def finish(up, up_norm, partner, partner_norm, count):
    corr = partner_norm / count
    diag = -2.0 * (1.0 - corr) - 2.0 * off_weight * corr
    return diag, (up + diag * partner) / count, (up_norm + diag * partner_norm) / count


def vmem_call(kernel, out_shape, args, name, flops):
    vmem = pl.BlockSpec(memory_space=pltpu.VMEM)
    smem = pl.BlockSpec(memory_space=pltpu.SMEM)
    return pl.pallas_call(
        kernel,
        out_shape=out_shape,
        in_specs=[smem] + [vmem] * (len(args) - 1),
        out_specs=vmem,
        compiler_params=pltpu.CompilerParams(vmem_limit_bytes=14 * 1024 * 1024),
        cost_estimate=pl.CostEstimate(flops=flops, bytes_accessed=1 << 20, transcendentals=0),
        name=name,
    )(*args)


def partner_kernel(ids, other, half, out):
    other = other[...].astype(f32)
    out[0:1, :] = image_sum(other)
    out[1:2, :] = image_sum(other * half[...].astype(f32))


def arrange_kernel(ids, early, mid, late, out):
    for half in range(2):
        columns = slice(1024 * half, 1024 * (half + 1))
        out[0:64, columns] = jnp.where(ids[1] == half, early[...], late[0:64])
        out[64:128, columns] = jnp.where(ids[1] == half, mid[...], late[64:128])


def finish_kernel(ids, sums, scales, view, keep, traded, block, grad, loss):
    xl, row = ids[0], ids[2]
    loss[0, 0] = jnp.sum(sums[:, 2, :]) / FEAT
    for half in range(2):
        columns = slice(1024 * half, 1024 * (half + 1))
        total = sums[8 * half]
        for i in range(1, 8):
            total = total + sums[8 * half + i]
        partner = sums[2 * row + half]
        diag, first, second = finish(total[0:1], total[1:2], partner[3:4], partner[4:5], BATCH)
        mean, inv = scales[0:1, columns], scales[1:2, columns]
        up = jnp.where(xl == half, keep[...], traded[...].astype(f32))
        norm = (view[:, columns] - mean) * inv
        grad[:, columns] = inv * (up + diag * block[:, columns].astype(f32) - first - norm * second)


def finish_first(ids, *args):
    vmem = pl.BlockSpec(memory_space=pltpu.VMEM)
    smem = pl.BlockSpec(memory_space=pltpu.SMEM)
    return pl.pallas_call(
        finish_kernel,
        out_shape=[jax.ShapeDtypeStruct((128, 2048), f32), jax.ShapeDtypeStruct((1, 1), f32)],
        in_specs=[smem] + [vmem] * len(args),
        out_specs=[vmem, smem],
        compiler_params=pltpu.CompilerParams(vmem_limit_bytes=14 * 1024 * 1024),
        cost_estimate=pl.CostEstimate(flops=1 << 22, bytes_accessed=4 << 20, transcendentals=0),
        name="finish_first",
    )(ids, *args)


def row_sum(x):
    x = x + sum(lax.ppermute(x, ("y1", "y0"), [(i, (i + step) % 4) for i in range(4)]) for step in (1, 2, 3))
    return x + lax.ppermute(x, "xh", SWAP)


def local(view_a, view_b):
    count = BATCH
    core = lax.axis_index("k")
    xl = lax.axis_index("xl")
    device = lax.axis_index(ROW + COL)
    pairs_a, wanted_a, pairs_b, wanted_b = crossing_tables()
    ids_a = jnp.concatenate([jnp.stack([lax.axis_index(("z1", "z0")), core]), jnp.array(wanted_a)[device], xl[None]])
    ids_b = jnp.concatenate([jnp.stack([lax.axis_index(("y1", "y0")), lax.axis_index("xh")]), jnp.array(wanted_b)[device], core[None]])

    stats_a, late_b = tie(stats(view_a), view_b)
    norm_a, mean_a, inv_a = finish_stats(jnp.sum(spread(stats_a, COL, 16), axis=0), count, view_a)
    norm_b, _, inv_b = finish_stats(row_sum(stats(late_b)), count, view_b)
    half_a = norm_a.astype(bf16)
    half_b = norm_b.astype(bf16)

    zs, ys = ("z1", "z0"), ("y1", "y0")
    parts_a = jnp.transpose(half_a.reshape(128, 2, 1024), (1, 0, 2))
    own_a = both(xl, pick(parts_a, xl), lax.ppermute(pick(parts_a, 1 - xl), "xl", SWAP), 0)
    near_b = ring_near(half_b, ys)
    own_a, late_half_b = tie(own_a, half_b)
    near_a = ring_near(own_a, zs)
    other_own_a = trade([own_a], "k")
    other_own_b = trade([late_half_b], "xh")
    *near_a, near_b[0], near_b[1], other_own_b[0] = tie(*near_a, *near_b, *other_own_b)
    far_pairs = [(2 * i + k, 2 * ((i + (3 if k else 1)) % 4) + k) for i in range(4) for k in range(2)]
    far_a = lax.ppermute(jnp.where(core == 0, near_a[0], near_a[1]), zs + ("k",), far_pairs)
    other_near_a = trade(near_a, "k")
    other_near_b = ring_near(other_own_b[0], ys)
    far_b = lax.ppermute(near_b[0], ys, AHEAD)
    other_far_a, *other_near_b = tie(*trade([far_a], "k"), *other_near_b)
    other_far_b = lax.ppermute(other_near_b[1], ys, BACK)
    blocks_a = [own_a, *near_a, far_a, *other_own_a, *other_near_a, other_far_a]

    part_a, send_a = gram_part(True, ids_a, blocks_a)
    part_a, far_b, other_far_b = tie(part_a, far_b, other_far_b)
    blocks_b = [half_b, *near_b, far_b, *other_own_b, *other_near_b, other_far_b]
    other_a = lax.ppermute(send_a.reshape(256, 1024), ROW + COL, pairs_a)
    piece_a = lax.all_to_all(part_a.reshape(16, 256, 128), ("y1", "y0", "xh", "xl"), 0, 0)
    mine_b, give_b, *send_b = gram_part(False, ids_b, blocks_b)
    mixed = blend(mine_b, lax.ppermute(give_b, "k", SWAP), piece_a)
    ids = jnp.stack([xl, core, lax.axis_index(ROW)])
    partner = vmem_call(partner_kernel, jax.ShapeDtypeStruct((2, 1024), f32), (ids, other_a, half_b), "partner", 1 << 34)
    mixed, partner = tie(mixed, partner)
    mixed = lax.all_to_all(mixed, ("xl", "z1", "z0"), 0, 0)

    mixed, early = tie(mixed, send_b[0])
    early = lax.ppermute(early, ROW + COL, pairs_b[0])
    traded = lax.ppermute(mixed[:, 128:], "k", SWAP)
    up_b, last = second_view(ids_b, mixed, traded, partner, blocks_b)
    last, early = tie(last, early)
    last = lax.all_to_all(last, ("y1", "y0", "xh", "xl"), 0, 0)
    last, *late = tie(last, *send_b[1:])
    late = [lax.ppermute(x, ROW + COL, pairs) for x, pairs in zip(late, pairs_b)]
    block = jax.ShapeDtypeStruct((128, 2048), bf16)
    block = vmem_call(arrange_kernel, block, (ids, early, *late), "arrange", 1 << 34)

    keep, give, sums_a = first_view(ids_a, last, blocks_a)
    sums_a, keep, give, up_b, last = tie(sums_a, keep, give, up_b, last)
    sums_a = lax.all_to_all(sums_a, COL, 0, 0)

    sums_b = pick(jnp.moveaxis(last[:, 128:].reshape(8, 2, 4, 8, 256), 1, 0), xl)
    sums_b = jnp.swapaxes(jnp.sum(sums_b.astype(f32), axis=0), 0, 1).reshape(8, 1024)
    partner_norm = sums_b[6] + sums_b[7]
    diag_b, first_b, second_b = finish(sums_b[0], sums_b[4] + sums_b[5], sums_b[1], partner_norm, count)
    grad_b = inv_b * (up_b + diag_b * other_a.astype(f32) - first_b - norm_b * second_b)

    traded = lax.ppermute(give, "xl", SWAP)
    grad_a, loss_value = finish_first(ids, sums_a, jnp.stack([mean_a, inv_a]), view_a, keep, traded, block)
    return (loss_value[0, 0], grad_a, grad_b)


def solution(mesh):
    fine = Mesh(mesh.devices.reshape((2,) * 7), NAMES)
    return jax.shard_map(
        local,
        mesh=fine,
        in_specs=(P(COL, ROW), P(ROW, COL)),
        out_specs=(P(), P(COL, ROW), P(ROW, COL)),
        check_vma=False,
    )
```

time: 487 us -> 218 us (0.45)
  blocking collectives: 218 us -> 17.3 us
  starting transfers between devices: 0.16 us -> 93.3 us
  waiting for transfers between devices: 153 us -> 60.6 us
  matrix products: 78.4 us -> 0 us
  Pallas kernels: 0 us -> 25 us
  between operations: 15.6 us -> 1.22 us
  local copies, waits for them, and re-layouts: 3.23 us -> 13.9 us
  other arithmetic: 15 us -> 5.41 us
    psum x5 -> x0, blocking collectives: 218 us -> none  [the longest x1 77.2 us: local(): loss_value = lax.psum(local_loss, ('row', 'col')) / FEAT]
    reduce_scatter x2 -> x0, waiting for transfers between devices: 82 us -> none  [the longest x1 78.8 us: local(): lax.psum_scatter(against_rows(all_b, slope), 'col', scatter_dimension=0,...]
    dot_general x3 -> x0, matrix products: 78.4 us -> none  [the longest x1 33.4 us: against_rows(): lax.dot_general(partner.astype(jnp.float32), slope, (((1,), (1,)), ((), (...]
    all_gather x2 -> x0, waiting for transfers between devices: 70.5 us -> none  [the longest x1 54.3 us: local(): all_a = lax.all_gather(half_a, 'col', axis=0, tiled=True)]
    ppermute x0 -> x26, starting transfers between devices: none -> 64.4 us  [the longest x1 18.8 us: local(): mixed = blend(mine_b, lax.ppermute(give_b, 'k', SWAP), piece_a)]
    ppermute x0 -> x26, waiting for transfers between devices: none -> 43.4 us  [the longest x2 13.6 us: local(): lax.ppermute(x, ROW + COL, pairs)]
    all_to_all x0 -> x4, starting transfers between devices: none -> 28.8 us  [the longest x1 8.47 us: local(): last = lax.all_to_all(last, ('y1', 'y0', 'xh', 'xl'), 0, 0)]
    pallas_call x0 -> x8, Pallas kernels: none -> 25 us  [the longest x2 10.6 us: gram_part(): call(kernel, out, 0, 'gram_part', pl.ANY, scratch, flops, (0,) if first e...]
  transfers between devices with their start and end apart: 4 -> 30, of which waited for: 4 -> 15; matrix products, arithmetic and copies ran while one was open for 8% -> 3% of each run, Pallas kernels for 0% -> 8%
where the time goes in v1:
time: 218 us; the launch traced here: 217 us
  starting transfers between devices  93.3 us (43%)
  waiting for transfers between devices  60.6 us (28%)
  Pallas kernels  25 us (11%)
  blocking collectives  17.3 us (8%)
  local copies, waits for them, and re-layouts  13.9 us (6%)
  other arithmetic  5.41 us (2%)
    ppermute x1, starting transfers between devices, local(): mixed = blend(mine_b, lax.ppermute(give_b, 'k', SWAP), piece_a)  18.8 us
    all_to_all x1, blocking collectives, local(): mixed = lax.all_to_all(mixed, ('xl', 'z1', 'z0'), 0, 0)  17.3 us
    all_to_all x1, waiting for transfers between devices, local(): last = lax.all_to_all(last, ('y1', 'y0', 'xh', 'xl'), 0, 0)  16.5 us
    ppermute x2, waiting for transfers between devices, local(): lax.ppermute(x, ROW + COL, pairs)  13.6 us
    pallas_call x2, Pallas kernels, gram_part(): call(kernel, out, 0, 'gram_part', pl.ANY, scratch, flops, (0,) if first e...  10.6 us
    unnamed x47, local copies, waits for them, and re-layouts  10.2 us
    ppermute x5, starting transfers between devices, trade(): return [lax.ppermute(x, axis, SWAP) for x in blocks]  9.03 us
    ppermute x2, starting transfers between devices, local(): lax.ppermute(x, ROW + COL, pairs)  8.59 us
  transfers between devices with their start and end apart: 30, of which 15 were waited for; matrix products, arithmetic and copies ran while one was open for 3% of the time, Pallas kernels for 8%

profile of v1, /device:TPU:9, one launch (start us, length us, event | category | flops | bytes accessed | tf_op | source)
XLA Modules:
  0.0 216.7 jit_solution(2774286703484949412)
XLA Ops:
  0.6 1.4 fusion.6
  2.4 2.5 %collective-permute-start.1 = (f32[2,1024]{1,0:T(2,128)S(1)}, f32[2,1024]{1,0:T(2,128)S(1)}, u32[]{:S(2)}, u32[]{:S(2)}) collective-permute-start(f32[2,1024]{1,0:T(2,128)S(1)} %pad_maximum_fusion.3), channel_id=1, source_target_pairs={{0,64},{32,96},{64,0},{96,32},{1,65},{33,97},{65,1},{97,33},{2,66}... | collective-permute-start | bytes 24584 | tf_op jit(solution)/shard_map/ppermute | solution.py:395
  4.9 1.6 collective-permute-start
  6.5 0.8 broadcast_in_dim.2
  7.3 7.8 %all-to-all-start = ((f32[16,2,2048]{2,1,0:T(2,128)}), f32[16,2,2048]{2,1,0:T(2,128)S(1)}, u32[]{:S(2)}, u32[]{:S(2)}) async-start(f32[16,2,2048]{2,1,0:T(2,128)} %broadcast_in_dim.2), calls=%async_computation | async-start | bytes 524288 | tf_op jit(solution)/shard_map/all_to_all | solution.py:32
  15.1 2.6 %collective-permute-start.3 = (f32[2,1024]{1,0:T(2,128)S(1)}, f32[2,1024]{1,0:T(2,128)S(1)}, u32[]{:S(2)}, u32[]{:S(2)}) collective-permute-start(f32[2,1024]{1,0:T(2,128)S(1)} %add_add_fusion), channel_id=1, source_target_pairs={{0,16},{16,0},{1,17},{17,1},{2,18},{18,2},{3,19},{19,3},{4,20},{20... | collective-permute-start | bytes 24584 | tf_op jit(solution)/shard_map/ppermute | solution.py:396
  17.7 3.9 %collective-permute-done.3 = f32[2,1024]{1,0:T(2,128)S(1)} collective-permute-done((f32[2,1024]{1,0:T(2,128)S(1)}, f32[2,1024]{1,0:T(2,128)S(1)}, u32[]{:S(2)}, u32[]{:S(2)}) %collective-permute-start.3) | collective-permute-done | bytes 8224 | tf_op jit(solution)/shard_map/ppermute | solution.py:396
  22.9 1.1 constant_dynamic-slice_fusion.1
  24.0 0.9 collective-permute-start.4
  25.1 1.5 collective-permute-start.7
  26.6 4.4 %collective-permute-done.4 = bf16[128,1024]{1,0:T(8,128)(2,1)S(1)} collective-permute-done((bf16[128,1024]{1,0:T(8,128)(2,1)S(1)}, bf16[128,1024]{1,0:T(8,128)(2,1)S(1)}, u32[]{:S(2)}, u32[]{:S(2)}) %collective-permute-start.4) | collective-permute-done | bytes 262176 | tf_op jit(solution)/shard_map/ppermute | solution.py:416
  31.1 2.5 %collective-permute-start.9 = (bf16[256,1024]{1,0:T(8,128)(2,1)S(1)}, bf16[256,1024]{1,0:T(8,128)(2,1)}, u32[]{:S(2)}, u32[]{:S(2)}) collective-permute-start(bf16[256,1024]{1,0:T(8,128)(2,1)S(1)} %fusion.refs_0_.half), channel_id=1, source_target_pairs={{0,16},{16,0},{1,17},{17,1},{2,18},{18,2},{3,19},{19,3},{4,20},{20... | collective-permute-start | bytes 1572872 | tf_op jit(solution)/shard_map/ppermute | solution.py:99
  33.6 2.6 %collective-permute-start.6 = (bf16[256,1024]{1,0:T(8,128)(2,1)S(1)}, bf16[256,1024]{1,0:T(8,128)(2,1)S(1)}, u32[]{:S(2)}, u32[]{:S(2)}) collective-permute-start(bf16[256,1024]{1,0:T(8,128)(2,1)S(1)} %pad_maximum_fusion.refs_0_), channel_id=1, source_target_pairs={{0,6},{2,0},{4,2},{6,4},{1,7},{3,1},{5,3},{7,5},{8,14},{10,8},{12,... | collective-permute-start | bytes 1572872 | tf_op jit(solution)/shard_map/ppermute | solution.py:95
  36.2 1.6 collective-permute-done.8.refs_2_
  38.2 6.1 %collective-permute-done.9.refs_4_ = bf16[256,1024]{1,0:T(8,128)(2,1)} collective-permute-done((bf16[256,1024]{1,0:T(8,128)(2,1)S(1)}, bf16[256,1024]{1,0:T(8,128)(2,1)}, u32[]{:S(2)}, u32[]{:S(2)}) %collective-permute-start.9) | collective-permute-done | bytes 524320 | tf_op jit(solution)/shard_map/ppermute | solution.py:99
  44.3 2.0 collective-permute-done.6.refs_2_
  46.3 3.1 %collective-permute-done.5.refs_1_ = bf16[256,1024]{1,0:T(8,128)(2,1)S(1)} collective-permute-done((bf16[256,1024]{1,0:T(8,128)(2,1)S(1)}, bf16[256,1024]{1,0:T(8,128)(2,1)S(1)}, u32[]{:S(2)}, u32[]{:S(2)}) %collective-permute-start.5) | collective-permute-done | bytes 524320 | tf_op jit(solution)/shard_map/ppermute | solution.py:95
  49.9 1.5 collective-permute-start.15
  51.3 6.7 %collective-permute-done.10.refs_3_ = bf16[256,1024]{1,0:T(8,128)(2,1)} collective-permute-done((bf16[256,1024]{1,0:T(8,128)(2,1)S(1)}, bf16[256,1024]{1,0:T(8,128)(2,1)}, u32[]{:S(2)}, u32[]{:S(2)}) %collective-permute-start.10) | collective-permute-done | bytes 524320 | tf_op jit(solution)/shard_map/ppermute | solution.py:424
  58.0 4.4 %collective-permute-start.14 = (bf16[256,1024]{1,0:T(8,128)(2,1)}, bf16[256,1024]{1,0:T(8,128)(2,1)}, u32[]{:S(2)}, u32[]{:S(2)}) collective-permute-start(bf16[256,1024]{1,0:T(8,128)(2,1)} %collective-permute-done.10.refs_3_), channel_id=1, source_target_pairs={{0,1},{1,0},{2,3},{3,2},{4,5},{5,4},{6,7},{7,6},{8,9},{9,8},{10,11... | collective-permute-start | bytes 1572872 | tf_op jit(solution)/shard_map/ppermute | solution.py:99
  62.9 1.6 collective-permute-start.13
  65.3 1.4 collective-permute-start.18
  66.8 5.4 %gram_part.2 = (bf16[8,2,256,128]{3,2,1,0:T(8,128)(2,1)S(1)}, bf16[2,128,1024]{2,1,0:T(8,128)(2,1)}) custom-call(s32[6]{0:T(128)S(1)} %pad_add_fusion.1.ids, bf16[256,1024]{1,0:T(8,128)(2,1)S(1)} %pad_maximum_fusion.refs_0_, bf16[256,1024]{1,0:T(8,128)(2,1)S(1)} %collective-permute-done.5.refs_1_, bf16[256,1024]{1,0:T(8,128)(2,1)S(1)} %collective-permute-done.6.refs_2_, ...), custom_call_target="tpu_custom_call" | custom-call | flops 1073741824 | bytes 4194304 | tf_op jit(solution)/shard_map/gram_part/pallas_call | solution.py:199
  72.2 1.0 copy-done.4
  73.2 6.1 %collective-permute-start.20 = (bf16[256,1024]{1,0:T(8,128)(2,1)}, bf16[256,1024]{1,0:T(8,128)(2,1)S(1)}, u32[]{:S(2)}, u32[]{:S(2)}) collective-permute-start(bf16[256,1024]{1,0:T(8,128)(2,1)} %bitcast.19), channel_id=1, source_target_pairs={{0,0},{13,1},{18,2},{31,3},{39,4},{42,5},{53,6},{56,7},{66,8},{79,... | collective-permute-start | bytes 1572872 | tf_op jit(solution)/shard_map/ppermute | solution.py:435
  80.2 4.5 %all-to-all-start.1 = ((bf16[16,256,128]{2,1,0:T(8,128)(2,1)}), bf16[16,256,128]{2,1,0:T(8,128)(2,1)}, u32[]{:S(2)}, u32[]{:S(2)}) async-start(bf16[16,256,128]{2,1,0:T(8,128)(2,1)} %bitcast.36), calls=%async_computation.1 | async-start | bytes 2097152 | tf_op jit(solution)/shard_map/all_to_all | solution.py:436
  84.7 5.2 %gram_part.3 = (bf16[8,128,256]{2,1,0:T(8,128)(2,1)S(1)}, bf16[8,128,256]{2,1,0:T(8,128)(2,1)S(1)}, bf16[64,1024]{1,0:T(8,128)(2,1)S(1)}, bf16[64,1024]{1,0:T(8,128)(2,1)S(1)}, bf16[128,1024]{1,0:T(8,128)(2,1)S(1)}) custom-call(s32[11]{0:T(128)S(1)} %pad_add_fusion.2.ids, bf16[256,1024]{1,0:T(8,128)(2,1)S(1)} %fusion.refs_0_.half, ...), custom_call_target="tpu_custom_call" | custom-call | flops 1048576 | bytes 4096 | tf_op jit(solution)/shard_map/gram_part/pallas_call | solution.py:199
  90.7 18.8 %collective-permute-start.19 = (bf16[8,128,256]{2,1,0:T(8,128)(2,1)S(1)}, bf16[8,128,256]{2,1,0:T(8,128)(2,1)S(1)}, u32[]{:S(2)}, u32[]{:S(2)}) collective-permute-start(bf16[8,128,256]{2,1,0:T(8,128)(2,1)S(1)} %get-tuple-element.62), channel_id=1, source_target_pairs={{0,1},{1,0},{2,3},{3,2},{4,5},{5,4},{6,7},{7,6},{8,9},{9,8},{10,11... | collective-permute-start | bytes 1572872 | tf_op jit(solution)/shard_map/ppermute | solution.py:438
  111.8 1.0 copy-done.12
  112.9 1.0 copy-done.14
  113.9 1.5 blend.1
  115.4 17.3 %all_to_all.25.mixed = bf16[8,256,256]{2,1,0:T(8,128)(2,1)S(1)} all-to-all(bf16[8,256,256]{2,1,0:T(8,128)(2,1)S(1)} %blend.1), channel_id=1, replica_groups=mesh['y1'=2,'y0'=2,'xh'=2,'xl'=2,'z1'=2,'z0'=2,'k'=2] {'xl','z1','z0'}, dimensions={0} | all-to-all | bytes 2097152 | tf_op jit(solution)/shard_map/all_to_all | solution.py:442
  132.7 3.8 %collective-permute-start.21 = (bf16[8,128,256]{2,1,0:T(8,128)(2,1)S(1)}, bf16[8,128,256]{2,1,0:T(8,128)(2,1)S(1)}, u32[]{:S(2)}, u32[]{:S(2)}) collective-permute-start(bf16[8,128,256]{2,1,0:T(8,128)(2,1)S(1)} %slice.46), channel_id=1, source_target_pairs={{0,1},{1,0},{2,3},{3,2},{4,5},{5,4},{6,7},{7,6},{8,9},{9,8},{10,11... | collective-permute-start | bytes 1572872 | tf_op jit(solution)/shard_map/ppermute | solution.py:446
  136.5 1.9 collective-permute-start.22
  138.5 5.5 %second_view.1 = (f32[256,1024]{1,0:T(8,128)S(1)}, bf16[16,160,256]{2,1,0:T(8,128)(2,1)S(1)}) custom-call(s32[11]{0:T(128)S(1)} %pad_add_fusion.2.ids, bf16[8,256,256]{2,1,0:T(8,128)(2,1)S(1)} %all_to_all.25.mixed, bf16[8,128,256]{2,1,0:T(8,128)(2,1)S(1)} %collective-permute-done.21.traded, f32[2,1024]{1,0:T(2,128)S(1)} %partner.1, ...), custom_call_target="tpu_custom_call" | custom-call | flops 1073741824 | bytes 4194304 | tf_op jit(solution)/shard_map/second_view/pallas_call | solution.py:284
  143.9 1.0 copy-done.5
  146.6 8.5 %all-to-all-start.3 = ((bf16[16,160,256]{2,1,0:T(8,128)(2,1)}), bf16[16,160,256]{2,1,0:T(8,128)(2,1)S(1)}, u32[]{:S(2)}, u32[]{:S(2)}) async-start(bf16[16,160,256]{2,1,0:T(8,128)(2,1)} %copy-done.3), calls=%async_computation.3 | async-start | bytes 2621440 | tf_op jit(solution)/shard_map/all_to_all | solution.py:449
  155.1 16.5 %all-to-all-done.3.last = bf16[16,160,256]{2,1,0:T(8,128)(2,1)S(1)} async-done(((bf16[16,160,256]{2,1,0:T(8,128)(2,1)}), bf16[16,160,256]{2,1,0:T(8,128)(2,1)S(1)}, u32[]{:S(2)}, u32[]{:S(2)}) %all-to-all-start.3) | async-done | bytes 1310752 | tf_op jit(solution)/shard_map/all_to_all | solution.py:449
  171.6 1.0 copy-done.2
  172.7 4.0 %first_view.1 = (f32[128,1024]{1,0:T(8,128)S(1)}, bf16[128,1024]{1,0:T(8,128)(2,1)S(1)}, f32[16,8,1024]{2,1,0:T(8,128)S(1)}) custom-call(s32[6]{0:T(128)S(1)} %pad_add_fusion.1.ids, bf16[16,160,256]{2,1,0:T(8,128)(2,1)S(1)} %all-to-all-done.3.last, bf16[256,1024]{1,0:T(8,128)(2,1)S(1)} %pad_maximum_fusion.refs_0_, bf16[256,1024]{1,0:T(8,128)(2,1)S(1)} %copy-done.2, ...), custom_call_target="tpu_custom_call" | custom-call | flops 1073741824 | bytes 4194304 | tf_op jit(solution)/shard_map/first_view/pallas_call | solution.py:328
  179.0 8.1 %all-to-all-start.4 = ((f32[16,8,1024]{2,1,0:T(8,128)}), f32[16,8,1024]{2,1,0:T(8,128)S(1)}, u32[]{:S(2)}, u32[]{:S(2)}) async-start(f32[16,8,1024]{2,1,0:T(8,128)} %copy-done.8), calls=%async_computation.4 | async-start | bytes 1048576 | tf_op jit(solution)/shard_map/all_to_all | solution.py:457
  187.1 4.1 %collective-permute-start.24 = (bf16[64,1024]{1,0:T(8,128)(2,1)}, bf16[64,1024]{1,0:T(8,128)(2,1)S(1)}, u32[]{:S(2)}, u32[]{:S(2)}) collective-permute-start(bf16[64,1024]{1,0:T(8,128)(2,1)} %copy-done.17), channel_id=1, source_target_pairs={{0,0},{97,1},{64,2},{33,3},{32,4},{65,5},{96,6},{1,7},{16,8},{113,... | collective-permute-start | bytes 393224 | tf_op jit(solution)/shard_map/ppermute | solution.py:451
  191.3 1.2 collective-permute-start.23
  192.6 4.4 %collective-permute-start.25 = (bf16[128,1024]{1,0:T(8,128)(2,1)}, bf16[128,1024]{1,0:T(8,128)(2,1)S(1)}, u32[]{:S(2)}, u32[]{:S(2)}) collective-permute-start(bf16[128,1024]{1,0:T(8,128)(2,1)} %copy-done.15), channel_id=1, source_target_pairs={{1,0},{96,1},{65,2},{32,3},{33,4},{64,5},{97,6},{0,7},{17,8},{112,... | collective-permute-start | bytes 786440 | tf_op jit(solution)/shard_map/ppermute | solution.py:451
  197.0 2.9 %subtract_multiply_fusion = f32[256,1024]{1,0:T(8,128)} fusion(f32[256,1024]{1,0:T(8,128)} %copy-done.5, bf16[256,1024]{1,0:T(8,128)(2,1)S(1)} %copy-done.10, f32[256,1024]{1,0:T(8,128)} %param.5, f32[1024]{0:T(1024)S(1)} %get-tuple-element.107, f32[1024]{0:T(1024)S(1)} %get-tuple-element.106, f32[1024]{0:T(1024)S(1)} %get-tuple-element.105, ...), kind=kLoop, calls=%fused_computation | loop fusion | flops 2359296 | bytes 3690496 | tf_op jit(solution)/shard_map/mul | solution.py:463
  199.9 1.7 collective-permute-done.24.mid
  201.7 11.9 %collective-permute-done.25.late = bf16[128,1024]{1,0:T(8,128)(2,1)S(1)} collective-permute-done((bf16[128,1024]{1,0:T(8,128)(2,1)}, bf16[128,1024]{1,0:T(8,128)(2,1)S(1)}, u32[]{:S(2)}, u32[]{:S(2)}) %collective-permute-start.25) | collective-permute-done | bytes 262176 | tf_op jit(solution)/shard_map/ppermute | solution.py:451
  214.2 2.3 %finish_first.1 = (f32[128,2048]{1,0:T(8,128)}, f32[1,1]{1,0:T(1,128)}) custom-call(s32[3]{0:T(128)S(1)} %pad_add_fusion.ids, f32[16,8,1024]{2,1,0:T(8,128)S(1)} %all-to-all-done.4.sums, f32[2,2048]{1,0:T(2,128)S(1)} %pad_maximum_fusion.2.scales, f32[128,2048]{1,0:T(8,128)S(1)} %copy-done, f32[128,1024]{1,0:T(8,128)S(1)} %copy-done.7, ...), custom_call_target="tpu_custom_call" | custom-call | flops 4194304 | bytes 4194304 | tf_op jit(solution)/shard_map/finish_first/pallas_call | solution.py:383
  (97 shorter events, 12.9 us)
Async XLA Ops:
  0.6 1.5 copy-start.22
  2.1 20.3 %copy-start = (f32[128,2048]{1,0:T(8,128)S(1)}, f32[128,2048]{1,0:T(8,128)}, u32[]{:S(2)}) copy-start(f32[128,2048]{1,0:T(8,128)} %view.1) | copy-start | bytes 3145732
  2.3 12.7 %collective-permute-start.2 = (f32[2,1024]{1,0:T(2,128)S(1)}, f32[2,1024]{1,0:T(2,128)S(1)}, u32[]{:S(2)}, u32[]{:S(2)}) collective-permute-start(f32[2,1024]{1,0:T(2,128)S(1)} %pad_maximum_fusion.3), channel_id=1, source_target_pairs={{0,96},{32,0},{64,32},{96,64},{1,97},{33,1},{65,33},{97,65},{2,98}... | collective-permute-start | bytes 24584 | tf_op jit(solution)/shard_map/ppermute | solution.py:395
  2.4 12.7 %collective-permute-start.1 = (f32[2,1024]{1,0:T(2,128)S(1)}, f32[2,1024]{1,0:T(2,128)S(1)}, u32[]{:S(2)}, u32[]{:S(2)}) collective-permute-start(f32[2,1024]{1,0:T(2,128)S(1)} %pad_maximum_fusion.3), channel_id=1, source_target_pairs={{0,64},{32,96},{64,0},{96,32},{1,65},{33,97},{65,1},{97,33},{2,66}... | collective-permute-start | bytes 24584 | tf_op jit(solution)/shard_map/ppermute | solution.py:395
  4.9 10.2 %collective-permute-start = (f32[2,1024]{1,0:T(2,128)S(1)}, f32[2,1024]{1,0:T(2,128)S(1)}, u32[]{:S(2)}, u32[]{:S(2)}) collective-permute-start(f32[2,1024]{1,0:T(2,128)S(1)} %pad_maximum_fusion.3), channel_id=1, source_target_pairs={{0,32},{32,64},{64,96},{96,0},{1,33},{33,65},{65,97},{97,1},{2,34}... | collective-permute-start | bytes 24584 | tf_op jit(solution)/shard_map/ppermute | solution.py:395
  7.3 14.9 %all-to-all-start = ((f32[16,2,2048]{2,1,0:T(2,128)}), f32[16,2,2048]{2,1,0:T(2,128)S(1)}, u32[]{:S(2)}, u32[]{:S(2)}) async-start(f32[16,2,2048]{2,1,0:T(2,128)} %broadcast_in_dim.2), calls=%async_computation | async-start | bytes 524288 | tf_op jit(solution)/shard_map/all_to_all | solution.py:32
  15.1 6.5 %collective-permute-start.3 = (f32[2,1024]{1,0:T(2,128)S(1)}, f32[2,1024]{1,0:T(2,128)S(1)}, u32[]{:S(2)}, u32[]{:S(2)}) collective-permute-start(f32[2,1024]{1,0:T(2,128)S(1)} %add_add_fusion), channel_id=1, source_target_pairs={{0,16},{16,0},{1,17},{17,1},{2,18},{18,2},{3,19},{19,3},{4,20},{20... | collective-permute-start | bytes 24584 | tf_op jit(solution)/shard_map/ppermute | solution.py:396
  24.0 6.9 %collective-permute-start.4 = (bf16[128,1024]{1,0:T(8,128)(2,1)S(1)}, bf16[128,1024]{1,0:T(8,128)(2,1)S(1)}, u32[]{:S(2)}, u32[]{:S(2)}) collective-permute-start(bf16[128,1024]{1,0:T(8,128)(2,1)S(1)} %bitcast.38), channel_id=1, source_target_pairs={{0,8},{8,0},{1,9},{9,1},{2,10},{10,2},{3,11},{11,3},{4,12},{12,4},... | collective-permute-start | bytes 786440 | tf_op jit(solution)/shard_map/ppermute | solution.py:416
  25.1 12.8 %collective-permute-start.8 = (bf16[256,1024]{1,0:T(8,128)(2,1)S(1)}, bf16[256,1024]{1,0:T(8,128)(2,1)}, u32[]{:S(2)}, u32[]{:S(2)}) collective-permute-start(bf16[256,1024]{1,0:T(8,128)(2,1)S(1)} %fusion.refs_0_.half), channel_id=1, source_target_pairs={{0,96},{32,0},{64,32},{96,64},{1,97},{33,1},{65,33},{97,65},{2,98}... | collective-permute-start | bytes 1572872 | tf_op jit(solution)/shard_map/ppermute | solution.py:95
  25.1 13.1 %collective-permute-start.7 = (bf16[256,1024]{1,0:T(8,128)(2,1)S(1)}, bf16[256,1024]{1,0:T(8,128)(2,1)}, u32[]{:S(2)}, u32[]{:S(2)}) collective-permute-start(bf16[256,1024]{1,0:T(8,128)(2,1)S(1)} %fusion.refs_0_.half), channel_id=1, source_target_pairs={{0,32},{32,64},{64,96},{96,0},{1,33},{33,65},{65,97},{97,1},{2,34}... | collective-permute-start | bytes 1572872 | tf_op jit(solution)/shard_map/ppermute | solution.py:95
  31.1 13.2 %collective-permute-start.9 = (bf16[256,1024]{1,0:T(8,128)(2,1)S(1)}, bf16[256,1024]{1,0:T(8,128)(2,1)}, u32[]{:S(2)}, u32[]{:S(2)}) collective-permute-start(bf16[256,1024]{1,0:T(8,128)(2,1)S(1)} %fusion.refs_0_.half), channel_id=1, source_target_pairs={{0,16},{16,0},{1,17},{17,1},{2,18},{18,2},{3,19},{19,3},{4,20},{20... | collective-permute-start | bytes 1572872 | tf_op jit(solution)/shard_map/ppermute | solution.py:99
  33.6 12.7 %collective-permute-start.6 = (bf16[256,1024]{1,0:T(8,128)(2,1)S(1)}, bf16[256,1024]{1,0:T(8,128)(2,1)S(1)}, u32[]{:S(2)}, u32[]{:S(2)}) collective-permute-start(bf16[256,1024]{1,0:T(8,128)(2,1)S(1)} %pad_maximum_fusion.refs_0_), channel_id=1, source_target_pairs={{0,6},{2,0},{4,2},{6,4},{1,7},{3,1},{5,3},{7,5},{8,14},{10,8},{12,... | collective-permute-start | bytes 1572872 | tf_op jit(solution)/shard_map/ppermute | solution.py:95
  36.2 13.2 %collective-permute-start.5 = (bf16[256,1024]{1,0:T(8,128)(2,1)S(1)}, bf16[256,1024]{1,0:T(8,128)(2,1)S(1)}, u32[]{:S(2)}, u32[]{:S(2)}) collective-permute-start(bf16[256,1024]{1,0:T(8,128)(2,1)S(1)} %pad_maximum_fusion.refs_0_), channel_id=1, source_target_pairs={{0,2},{2,4},{4,6},{6,0},{1,3},{3,5},{5,7},{7,1},{8,10},{10,12},{12... | collective-permute-start | bytes 1572872 | tf_op jit(solution)/shard_map/ppermute | solution.py:95
  49.5 22.7 %copy-start.1 = (bf16[256,1024]{1,0:T(8,128)(2,1)}, bf16[256,1024]{1,0:T(8,128)(2,1)S(1)}, u32[]{:S(2)}) copy-start(bf16[256,1024]{1,0:T(8,128)(2,1)S(1)} %collective-permute-done.5.refs_1_) | copy-start | bytes 1572868
  49.5 8.5 %collective-permute-start.10 = (bf16[256,1024]{1,0:T(8,128)(2,1)S(1)}, bf16[256,1024]{1,0:T(8,128)(2,1)}, u32[]{:S(2)}, u32[]{:S(2)}) collective-permute-start(bf16[256,1024]{1,0:T(8,128)(2,1)S(1)} %broadcast_select_fusion), channel_id=1, source_target_pairs={{0,2},{1,7},{2,4},{3,1},{4,6},{5,3},{6,0},{7,5},{8,10},{9,15},{10,... | collective-permute-start | bytes 1572872 | tf_op jit(solution)/shard_map/ppermute | solution.py:424
  49.9 13.1 %collective-permute-start.16 = (bf16[256,1024]{1,0:T(8,128)(2,1)}, bf16[256,1024]{1,0:T(8,128)(2,1)}, u32[]{:S(2)}, u32[]{:S(2)}) collective-permute-start(bf16[256,1024]{1,0:T(8,128)(2,1)} %collective-permute-done.9.refs_4_), channel_id=1, source_target_pairs={{0,96},{32,0},{64,32},{96,64},{1,97},{33,1},{65,33},{97,65},{2,98}... | collective-permute-start | bytes 1572872 | tf_op jit(solution)/shard_map/ppermute | solution.py:95
  49.9 15.4 %collective-permute-start.15 = (bf16[256,1024]{1,0:T(8,128)(2,1)}, bf16[256,1024]{1,0:T(8,128)(2,1)}, u32[]{:S(2)}, u32[]{:S(2)}) collective-permute-start(bf16[256,1024]{1,0:T(8,128)(2,1)} %collective-permute-done.9.refs_4_), channel_id=1, source_target_pairs={{0,32},{32,64},{64,96},{96,0},{1,33},{33,65},{65,97},{97,1},{2,34}... | collective-permute-start | bytes 1572872 | tf_op jit(solution)/shard_map/ppermute | solution.py:95
  58.0 7.3 %collective-permute-start.14 = (bf16[256,1024]{1,0:T(8,128)(2,1)}, bf16[256,1024]{1,0:T(8,128)(2,1)}, u32[]{:S(2)}, u32[]{:S(2)}) collective-permute-start(bf16[256,1024]{1,0:T(8,128)(2,1)} %collective-permute-done.10.refs_3_), channel_id=1, source_target_pairs={{0,1},{1,0},{2,3},{3,2},{4,5},{5,4},{6,7},{7,6},{8,9},{9,8},{10,11... | collective-permute-start | bytes 1572872 | tf_op jit(solution)/shard_map/ppermute | solution.py:99
  62.4 4.4 %collective-permute-start.11 = (bf16[256,1024]{1,0:T(8,128)(2,1)S(1)}, bf16[256,1024]{1,0:T(8,128)(2,1)}, u32[]{:S(2)}, u32[]{:S(2)}) collective-permute-start(bf16[256,1024]{1,0:T(8,128)(2,1)S(1)} %pad_maximum_fusion.refs_0_), channel_id=1, source_target_pairs={{0,1},{1,0},{2,3},{3,2},{4,5},{5,4},{6,7},{7,6},{8,9},{9,8},{10,11... | collective-permute-start | bytes 1572872 | tf_op jit(solution)/shard_map/ppermute | solution.py:99
  62.4 4.4 %collective-permute-start.12 = (bf16[256,1024]{1,0:T(8,128)(2,1)S(1)}, bf16[256,1024]{1,0:T(8,128)(2,1)}, u32[]{:S(2)}, u32[]{:S(2)}) collective-permute-start(bf16[256,1024]{1,0:T(8,128)(2,1)S(1)} %collective-permute-done.5.refs_1_), channel_id=1, source_target_pairs={{0,1},{1,0},{2,3},{3,2},{4,5},{5,4},{6,7},{7,6},{8,9},{9,8},{10,11... | collective-permute-start | bytes 1572872 | tf_op jit(solution)/shard_map/ppermute | solution.py:99
  62.9 3.9 %collective-permute-start.13 = (bf16[256,1024]{1,0:T(8,128)(2,1)S(1)}, bf16[256,1024]{1,0:T(8,128)(2,1)}, u32[]{:S(2)}, u32[]{:S(2)}) collective-permute-start(bf16[256,1024]{1,0:T(8,128)(2,1)S(1)} %collective-permute-done.6.refs_2_), channel_id=1, source_target_pairs={{0,1},{1,0},{2,3},{3,2},{4,5},{5,4},{6,7},{7,6},{8,9},{9,8},{10,11... | collective-permute-start | bytes 1572872 | tf_op jit(solution)/shard_map/ppermute | solution.py:99
  65.3 14.8 %collective-permute-start.17 = (bf16[256,1024]{1,0:T(8,128)(2,1)}, bf16[256,1024]{1,0:T(8,128)(2,1)}, u32[]{:S(2)}, u32[]{:S(2)}) collective-permute-start(bf16[256,1024]{1,0:T(8,128)(2,1)} %collective-permute-done.7.refs_1_), channel_id=1, source_target_pairs={{0,32},{32,64},{64,96},{96,0},{1,33},{33,65},{65,97},{97,1},{2,34}... | collective-permute-start | bytes 1572872 | tf_op jit(solution)/shard_map/ppermute | solution.py:427
  65.3 14.8 %collective-permute-start.18 = (bf16[256,1024]{1,0:T(8,128)(2,1)}, bf16[256,1024]{1,0:T(8,128)(2,1)}, u32[]{:S(2)}, u32[]{:S(2)}) collective-permute-start(bf16[256,1024]{1,0:T(8,128)(2,1)} %collective-permute-done.16.refs_6_), channel_id=1, source_target_pairs={{0,96},{32,0},{64,32},{96,64},{1,97},{33,1},{65,33},{97,65},{2,98}... | collective-permute-start | bytes 1572872 | tf_op jit(solution)/shard_map/ppermute | solution.py:429
  72.2 1.0 copy-start.4
  73.2 36.3 %collective-permute-start.20 = (bf16[256,1024]{1,0:T(8,128)(2,1)}, bf16[256,1024]{1,0:T(8,128)(2,1)S(1)}, u32[]{:S(2)}, u32[]{:S(2)}) collective-permute-start(bf16[256,1024]{1,0:T(8,128)(2,1)} %bitcast.19), channel_id=1, source_target_pairs={{0,0},{13,1},{18,2},{31,3},{39,4},{42,5},{53,6},{56,7},{66,8},{79,... | collective-permute-start | bytes 1572872 | tf_op jit(solution)/shard_map/ppermute | solution.py:435
  80.2 31.6 %all-to-all-start.1 = ((bf16[16,256,128]{2,1,0:T(8,128)(2,1)}), bf16[16,256,128]{2,1,0:T(8,128)(2,1)}, u32[]{:S(2)}, u32[]{:S(2)}) async-start(bf16[16,256,128]{2,1,0:T(8,128)(2,1)} %bitcast.36), calls=%async_computation.1 | async-start | bytes 2097152 | tf_op jit(solution)/shard_map/all_to_all | solution.py:436
  89.9 0.8 copy-start.11
  90.7 18.8 %copy-start.15 = (bf16[128,1024]{1,0:T(8,128)(2,1)}, bf16[128,1024]{1,0:T(8,128)(2,1)S(1)}, u32[]{:S(2)}) copy-start(bf16[128,1024]{1,0:T(8,128)(2,1)S(1)} %get-tuple-element.84) | copy-start | bytes 786436
  90.7 19.5 %copy-start.17 = (bf16[64,1024]{1,0:T(8,128)(2,1)}, bf16[64,1024]{1,0:T(8,128)(2,1)S(1)}, u32[]{:S(2)}) copy-start(bf16[64,1024]{1,0:T(8,128)(2,1)S(1)} %get-tuple-element.83) | copy-start | bytes 393220
  90.7 19.5 %copy-start.20 = (bf16[64,1024]{1,0:T(8,128)(2,1)}, bf16[64,1024]{1,0:T(8,128)(2,1)S(1)}, u32[]{:S(2)}) copy-start(bf16[64,1024]{1,0:T(8,128)(2,1)S(1)} %get-tuple-element.70) | copy-start | bytes 393220
  90.7 20.3 %collective-permute-start.19 = (bf16[8,128,256]{2,1,0:T(8,128)(2,1)S(1)}, bf16[8,128,256]{2,1,0:T(8,128)(2,1)S(1)}, u32[]{:S(2)}, u32[]{:S(2)}) collective-permute-start(bf16[8,128,256]{2,1,0:T(8,128)(2,1)S(1)} %get-tuple-element.62), channel_id=1, source_target_pairs={{0,1},{1,0},{2,3},{3,2},{4,5},{5,4},{6,7},{7,6},{8,9},{9,8},{10,11... | collective-permute-start | bytes 1572872 | tf_op jit(solution)/shard_map/ppermute | solution.py:438
  111.8 1.0 copy-start.12
  112.9 1.0 copy-start.14
  115.4 21.1 %copy-start.21 = (bf16[64,1024]{1,0:T(8,128)(2,1)S(1)}, bf16[64,1024]{1,0:T(8,128)(2,1)}, u32[]{:S(2)}) copy-start(bf16[64,1024]{1,0:T(8,128)(2,1)} %copy-done.20) | copy-start | bytes 393220
  132.7 5.7 %collective-permute-start.21 = (bf16[8,128,256]{2,1,0:T(8,128)(2,1)S(1)}, bf16[8,128,256]{2,1,0:T(8,128)(2,1)S(1)}, u32[]{:S(2)}, u32[]{:S(2)}) collective-permute-start(bf16[8,128,256]{2,1,0:T(8,128)(2,1)S(1)} %slice.46), channel_id=1, source_target_pairs={{0,1},{1,0},{2,3},{3,2},{4,5},{5,4},{6,7},{7,6},{8,9},{9,8},{10,11... | collective-permute-start | bytes 1572872 | tf_op jit(solution)/shard_map/ppermute | solution.py:446
  136.5 9.1 %collective-permute-start.22 = (bf16[64,1024]{1,0:T(8,128)(2,1)S(1)}, bf16[64,1024]{1,0:T(8,128)(2,1)S(1)}, u32[]{:S(2)}, u32[]{:S(2)}) collective-permute-start(bf16[64,1024]{1,0:T(8,128)(2,1)S(1)} %copy-done.21), channel_id=1, source_target_pairs={{0,0},{97,1},{64,2},{33,3},{32,4},{65,5},{96,6},{1,7},{16,8},{113,... | collective-permute-start | bytes 393224 | tf_op jit(solution)/shard_map/ppermute | solution.py:445
  143.9 1.0 copy-start.5
  144.9 1.1 copy-start.3
  146.6 25.0 %all-to-all-start.3 = ((bf16[16,160,256]{2,1,0:T(8,128)(2,1)}), bf16[16,160,256]{2,1,0:T(8,128)(2,1)S(1)}, u32[]{:S(2)}, u32[]{:S(2)}) async-start(bf16[16,160,256]{2,1,0:T(8,128)(2,1)} %copy-done.3), calls=%async_computation.3 | async-start | bytes 2621440 | tf_op jit(solution)/shard_map/all_to_all | solution.py:449
  171.6 1.0 copy-start.2
  176.6 0.8 copy-start.6
  178.2 18.9 %copy-start.10 = (bf16[256,1024]{1,0:T(8,128)(2,1)S(1)}, bf16[256,1024]{1,0:T(8,128)(2,1)}, u32[]{:S(2)}) copy-start(bf16[256,1024]{1,0:T(8,128)(2,1)} %copy-done.9) | copy-start | bytes 1572868
  179.0 35.2 %all-to-all-start.4 = ((f32[16,8,1024]{2,1,0:T(8,128)}), f32[16,8,1024]{2,1,0:T(8,128)S(1)}, u32[]{:S(2)}, u32[]{:S(2)}) async-start(f32[16,8,1024]{2,1,0:T(8,128)} %copy-done.8), calls=%async_computation.4 | async-start | bytes 1048576 | tf_op jit(solution)/shard_map/all_to_all | solution.py:457
  187.1 14.6 %collective-permute-start.24 = (bf16[64,1024]{1,0:T(8,128)(2,1)}, bf16[64,1024]{1,0:T(8,128)(2,1)S(1)}, u32[]{:S(2)}, u32[]{:S(2)}) collective-permute-start(bf16[64,1024]{1,0:T(8,128)(2,1)} %copy-done.17), channel_id=1, source_target_pairs={{0,0},{97,1},{64,2},{33,3},{32,4},{65,5},{96,6},{1,7},{16,8},{113,... | collective-permute-start | bytes 393224 | tf_op jit(solution)/shard_map/ppermute | solution.py:451
  191.3 22.9 %collective-permute-start.23 = (bf16[128,1024]{1,0:T(8,128)(2,1)}, bf16[128,1024]{1,0:T(8,128)(2,1)S(1)}, u32[]{:S(2)}, u32[]{:S(2)}) collective-permute-start(bf16[128,1024]{1,0:T(8,128)(2,1)} %copy-done.16), channel_id=1, source_target_pairs={{0,8},{8,0},{1,9},{9,1},{2,10},{10,2},{3,11},{11,3},{4,12},{12,4},... | collective-permute-start | bytes 786440 | tf_op jit(solution)/shard_map/ppermute | solution.py:465
  192.6 21.0 %collective-permute-start.25 = (bf16[128,1024]{1,0:T(8,128)(2,1)}, bf16[128,1024]{1,0:T(8,128)(2,1)S(1)}, u32[]{:S(2)}, u32[]{:S(2)}) collective-permute-start(bf16[128,1024]{1,0:T(8,128)(2,1)} %copy-done.15), channel_id=1, source_target_pairs={{1,0},{96,1},{65,2},{32,3},{33,4},{64,5},{97,6},{0,7},{17,8},{112,... | collective-permute-start | bytes 786440 | tf_op jit(solution)/shard_map/ppermute | solution.py:451
  197.0 16.6 %copy-start.19 = (bf16[64,1024]{1,0:T(8,128)(2,1)S(1)}, bf16[64,1024]{1,0:T(8,128)(2,1)}, u32[]{:S(2)}) copy-start(bf16[64,1024]{1,0:T(8,128)(2,1)} %copy-done.18) | copy-start | bytes 393220
  199.9 14.3 %copy-start.7 = (f32[128,1024]{1,0:T(8,128)S(1)}, f32[128,1024]{1,0:T(8,128)}, u32[]{:S(2)}) copy-start(f32[128,1024]{1,0:T(8,128)} %copy-done.6) | copy-start | bytes 1572868
  (5 other events, 3.7 us)

commit v2 on v1

--- a/solution.py
+++ b/solution.py
@@ -108,7 +108,7 @@
 
 def gram_kernel(first, ids, *refs):
     if first:
-        result, send, held, sems, out, out_sems = refs[8:]
+        out, send, held, sems = refs[8:]
     else:
         mine, give, *sends, held, sems = refs[8:]
     copies = []
@@ -118,7 +118,6 @@
         copies[-1].start()
     copies[0].wait()
     own = held[0, 0:256, :].T
-    leaving = []
     for flip in range(2):
         for index in range(4 * flip, 4 * flip + 4):
             if index:
@@ -162,22 +161,14 @@
                             else:
                                 sends[2][...] = held[flip, at : at + 128, :]
 
-        if first:
-            rows = pl.ds(pl.multiple_of(128 * (ids[1] ^ flip), 128), 128)
-            away = pltpu.make_async_copy(out.at[:, :, rows, :], result.at[:, :, rows, :], out_sems.at[flip])
-            away.start()
-            leaving.append(away)
-    for away in leaving:
-        away.wait()
-
-
-def call(kernel, out_shape, extra, name, space=pltpu.VMEM, scratch=(), flops=2 * 256 * 2048 * 1024, far=()):
+
+def call(kernel, out_shape, extra, name, space=pltpu.VMEM, scratch=(), flops=2 * 256 * 2048 * 1024):
     vmem = pl.BlockSpec(memory_space=pltpu.VMEM)
     return pl.pallas_call(
         kernel,
         out_shape=out_shape,
         in_specs=[pl.BlockSpec(memory_space=pltpu.SMEM)] + [vmem] * extra + [pl.BlockSpec(memory_space=space)] * 8,
-        out_specs=[pl.BlockSpec(memory_space=pltpu.HBM) if i in far else vmem for i in range(len(out_shape))],
+        out_specs=[vmem] * len(out_shape),
         scratch_shapes=list(scratch),
         compiler_params=pltpu.CompilerParams(vmem_limit_bytes=14 * 1024 * 1024),
         cost_estimate=pl.CostEstimate(flops=flops, bytes_accessed=flops >> 8, transcendentals=0),
@@ -192,11 +183,8 @@
         shapes = [(8, 128, 256), (8, 128, 256), (64, 1024), (64, 1024), (128, 1024)]
     out = [jax.ShapeDtypeStruct(shape, bf16) for shape in shapes]
     scratch = [pltpu.VMEM((2, 1024, 1024), bf16), pltpu.SemaphoreType.DMA((8,))]
-    if first:
-        scratch += [pltpu.VMEM((8, 2, 256, 128), bf16), pltpu.SemaphoreType.DMA((2,))]
     flops = 2 * 256 * 2048 * 1024 if first else 1 << 20
-    kernel = functools.partial(gram_kernel, first)
-    return call(kernel, out, 0, "gram_part", pl.ANY, scratch, flops, (0,) if first else ())(ids, *blocks)
+    return call(functools.partial(gram_kernel, first), out, 0, "gram_part", pl.ANY, scratch, flops)(ids, *blocks)
 
 
 def blend_kernel(mine, traded, received, out):
@@ -241,16 +229,8 @@
     return [high, x - high]
 
 
-def send_all(part, result, start, rows, sems, first_sem):
-    copies = []
-    for i in range(16):
-        copies.append(pltpu.make_async_copy(part, result.at[i, start : start + rows], sems.at[first_sem + i]))
-        copies[-1].start()
-    return copies
-
-
 def second_kernel(ids, mixed, traded, partner, *refs):
-    blocks, up, result, out, sems = refs[:8], refs[8], refs[9], refs[10], refs[11]
+    blocks, up, out = refs[:8], refs[8], refs[9]
 
     def part(high, low, k, s):
         index = 4 * high + 2 * low + k
@@ -260,8 +240,9 @@
     piece = mixed[0, 0:128].astype(f32)
     for i in range(1, 8):
         piece = piece + mixed[i, 0:128].astype(f32)
-    out[0:128] = piece.astype(bf16)
-    leaving = send_all(out.at[0:128], result, 0, 128, sems, 0)
+    piece = piece.astype(bf16)
+    for i in range(16):
+        out[i, 0:128] = piece
     value = apply(part, blocks, ids)
     up[...] = value
     norm = blocks[0][...].astype(f32)
@@ -272,20 +253,17 @@
     for i in range(8):
         rows = jnp.where(row == i, sums[i], rows)
     rows = jnp.concatenate([rows[:, 256 * i : 256 * (i + 1)] for i in range(4)], axis=0).astype(bf16)
-    out[128:160] = rows
-    leaving += send_all(out.at[128:160], result, 128, 32, sems, 16)
-    for away in leaving:
-        away.wait()
+    for i in range(16):
+        out[i, 128:160] = rows
 
 
 def second_view(ids, mixed, traded, partner, blocks):
     out = [jax.ShapeDtypeStruct((256, 1024), f32), jax.ShapeDtypeStruct((16, 160, 256), bf16)]
-    scratch = [pltpu.VMEM((160, 256), bf16), pltpu.SemaphoreType.DMA((32,))]
-    return call(second_kernel, out, 3, "second_view", scratch=scratch, far=(1,))(ids, mixed, traded, partner, *blocks)
+    return call(second_kernel, out, 3, "second_view")(ids, mixed, traded, partner, *blocks)
 
 
 def first_kernel(ids, last, *refs):
-    blocks, keep, give, result, out, sems = refs[:8], refs[8], refs[9], refs[10], refs[11], refs[12]
+    blocks, (keep, give, out, second_sums) = refs[:8], refs[8:]
 
     def part(high, low, k, s):
         at = pl.ds(pl.multiple_of(k * 128, 128), 128)
@@ -301,6 +279,7 @@
     for i in range(8):
         term = last[2 * i + side, 128:160].astype(f32)
         terms = term if terms is None else terms + term
+    second_sums[...] = terms
     row = lax.broadcasted_iota(jnp.int32, (32, 256), 0) % 8
     loss = image_sum(jnp.where((row == 4) | (row == 5), terms, 0.0)) / (2.0 * BATCH)
     products = []
@@ -312,20 +291,19 @@
     sums.append(jnp.concatenate([loss, jnp.zeros((1, 768), f32)], axis=1))
     sums.append(jnp.concatenate([terms[8 * j + 2 : 8 * j + 3] for j in range(4)], axis=1))
     sums.append(jnp.concatenate(products, axis=1))
-    for j in range(8):
-        out[j : j + 1, :] = sums[j] if j < 5 else jnp.zeros((1, 1024), f32)
-    for away in send_all(out, result, 0, 8, sems, 0):
-        away.wait()
+    for i in range(16):
+        for j in range(5):
+            out[i, j : j + 1, :] = sums[j]
 
 
 def first_view(ids, last, blocks):
     out = [
         jax.ShapeDtypeStruct((128, 1024), f32),
         jax.ShapeDtypeStruct((128, 1024), bf16),
-        jax.ShapeDtypeStruct((16, 8, 1024), f32),
+        jax.ShapeDtypeStruct((16, 5, 1024), f32),
+        jax.ShapeDtypeStruct((32, 256), f32),
     ]
-    scratch = [pltpu.VMEM((8, 1024), f32), pltpu.SemaphoreType.DMA((16,))]
-    return call(first_kernel, out, 1, "first_view", scratch=scratch, far=(2,))(ids, last, *blocks)
+    return call(first_kernel, out, 1, "first_view", flops=1 << 20)(ids, last, *blocks)
 
 
 def finish(up, up_norm, partner, partner_norm, count):
@@ -341,9 +319,9 @@
         kernel,
         out_shape=out_shape,
         in_specs=[smem] + [vmem] * (len(args) - 1),
-        out_specs=vmem,
+        out_specs=jax.tree.map(lambda _: vmem, out_shape),
         compiler_params=pltpu.CompilerParams(vmem_limit_bytes=14 * 1024 * 1024),
-        cost_estimate=pl.CostEstimate(flops=flops, bytes_accessed=1 << 20, transcendentals=0),
+        cost_estimate=pl.CostEstimate(flops=flops, bytes_accessed=1 << 16, transcendentals=0),
         name=name,
     )(*args)
 
@@ -354,15 +332,26 @@
     out[1:2, :] = image_sum(other * half[...].astype(f32))
 
 
-def arrange_kernel(ids, early, mid, late, out):
+def arrange_kernel(ids, early, mid, late, keep, traded, block, up):
     for half in range(2):
         columns = slice(1024 * half, 1024 * (half + 1))
-        out[0:64, columns] = jnp.where(ids[1] == half, early[...], late[0:64])
-        out[64:128, columns] = jnp.where(ids[1] == half, mid[...], late[64:128])
-
-
-def finish_kernel(ids, sums, scales, view, keep, traded, block, grad, loss):
-    xl, row = ids[0], ids[2]
+        block[0:64, columns] = jnp.where(ids[1] == half, early[...], late[0:64])
+        block[64:128, columns] = jnp.where(ids[1] == half, mid[...], late[64:128])
+        up[:, columns] = jnp.where(ids[0] == half, keep[...], traded[...].astype(f32))
+
+
+def finish_second_kernel(ids, terms, scales, view, up, partner, grad):
+    for part in range(4):
+        columns = slice(256 * part, 256 * (part + 1))
+        rows = [terms[8 * part + i : 8 * part + i + 1] for i in range(8)]
+        diag, first, second = finish(rows[0], rows[4] + rows[5], rows[1], rows[6] + rows[7], BATCH)
+        mean, inv = scales[0:1, columns], scales[1:2, columns]
+        norm = (view[:, columns] - mean) * inv
+        grad[:, columns] = inv * (up[:, columns] + diag * partner[:, columns].astype(f32) - first - norm * second)
+
+
+def finish_kernel(ids, sums, scales, view, up, block, grad, loss):
+    row = ids[2]
     loss[0, 0] = jnp.sum(sums[:, 2, :]) / FEAT
     for half in range(2):
         columns = slice(1024 * half, 1024 * (half + 1))
@@ -372,9 +361,8 @@
         partner = sums[2 * row + half]
         diag, first, second = finish(total[0:1], total[1:2], partner[3:4], partner[4:5], BATCH)
         mean, inv = scales[0:1, columns], scales[1:2, columns]
-        up = jnp.where(xl == half, keep[...], traded[...].astype(f32))
         norm = (view[:, columns] - mean) * inv
-        grad[:, columns] = inv * (up + diag * block[:, columns].astype(f32) - first - norm * second)
+        grad[:, columns] = inv * (up[:, columns] + diag * block[:, columns].astype(f32) - first - norm * second)
 
 
 def finish_first(ids, *args):
@@ -386,7 +374,7 @@
         in_specs=[smem] + [vmem] * len(args),
         out_specs=[vmem, smem],
         compiler_params=pltpu.CompilerParams(vmem_limit_bytes=14 * 1024 * 1024),
-        cost_estimate=pl.CostEstimate(flops=1 << 22, bytes_accessed=4 << 20, transcendentals=0),
+        cost_estimate=pl.CostEstimate(flops=1 << 20, bytes_accessed=1 << 16, transcendentals=0),
         name="finish_first",
     )(ids, *args)
 
@@ -407,7 +395,7 @@
 
     stats_a, late_b = tie(stats(view_a), view_b)
     norm_a, mean_a, inv_a = finish_stats(jnp.sum(spread(stats_a, COL, 16), axis=0), count, view_a)
-    norm_b, _, inv_b = finish_stats(row_sum(stats(late_b)), count, view_b)
+    norm_b, mean_b, inv_b = finish_stats(row_sum(stats(late_b)), count, view_b)
     half_a = norm_a.astype(bf16)
     half_b = norm_b.astype(bf16)
 
@@ -449,21 +437,17 @@
     last = lax.all_to_all(last, ("y1", "y0", "xh", "xl"), 0, 0)
     last, *late = tie(last, *send_b[1:])
     late = [lax.ppermute(x, ROW + COL, pairs) for x, pairs in zip(late, pairs_b)]
-    block = jax.ShapeDtypeStruct((128, 2048), bf16)
-    block = vmem_call(arrange_kernel, block, (ids, early, *late), "arrange", 1 << 34)
-
-    keep, give, sums_a = first_view(ids_a, last, blocks_a)
-    sums_a, keep, give, up_b, last = tie(sums_a, keep, give, up_b, last)
+
+    keep, give, sums_a, sums_b = first_view(ids_a, last, blocks_a)
+    traded = lax.ppermute(give, "xl", SWAP)
+    out = [jax.ShapeDtypeStruct((128, 2048), bf16), jax.ShapeDtypeStruct((128, 2048), f32)]
+    block, up_own = vmem_call(arrange_kernel, out, (ids, early, *late, keep, traded), "arrange", 1 << 34)
+    sums_a, sums_b = tie(sums_a, sums_b)
     sums_a = lax.all_to_all(sums_a, COL, 0, 0)
 
-    sums_b = pick(jnp.moveaxis(last[:, 128:].reshape(8, 2, 4, 8, 256), 1, 0), xl)
-    sums_b = jnp.swapaxes(jnp.sum(sums_b.astype(f32), axis=0), 0, 1).reshape(8, 1024)
-    partner_norm = sums_b[6] + sums_b[7]
-    diag_b, first_b, second_b = finish(sums_b[0], sums_b[4] + sums_b[5], sums_b[1], partner_norm, count)
-    grad_b = inv_b * (up_b + diag_b * other_a.astype(f32) - first_b - norm_b * second_b)
-
-    traded = lax.ppermute(give, "xl", SWAP)
-    grad_a, loss_value = finish_first(ids, sums_a, jnp.stack([mean_a, inv_a]), view_a, keep, traded, block)
+    args = (ids, sums_b, jnp.stack([mean_b, inv_b]), view_b, up_b, other_a)
+    grad_b = vmem_call(finish_second_kernel, jax.ShapeDtypeStruct((256, 1024), f32), args, "finish_second", 1 << 20)
+    grad_a, loss_value = finish_first(ids, sums_a, jnp.stack([mean_a, inv_a]), view_a, up_own, block)
     return (loss_value[0, 0], grad_a, grad_b)
 
 

time: 218 us -> 213 us (0.977)
  blocking collectives: 17.3 us -> 42.7 us
  waiting for transfers between devices: 60.6 us -> 41.1 us
  starting transfers between devices: 93.3 us -> 80.5 us
  Pallas kernels: 25 us -> 27.5 us
    all_to_all x0 -> x1, blocking collectives: none -> 25.3 us  [local(): last = lax.all_to_all(last, ('y1', 'y0', 'xh', 'xl'), 0, 0)]
    all_to_all x1 -> x0, waiting for transfers between devices: 16.5 us -> none  [local(): last = lax.all_to_all(last, ('y1', 'y0', 'xh', 'xl'), 0, 0)]
    all_to_all x1 -> x0, starting transfers between devices: 8.47 us -> none  [local(): last = lax.all_to_all(last, ('y1', 'y0', 'xh', 'xl'), 0, 0)]
    ppermute x2, waiting for transfers between devices: 13.6 us -> 6.61 us  [local(): lax.ppermute(x, ROW + COL, pairs)]
    pallas_call x2 -> x3, Pallas kernels: 1.23 us -> 4.81 us  [vmem_call(): pl.pallas_call(kernel, out_shape=out_shape, in_specs=[smem] + [vmem] * (l...]
    ppermute x1, waiting for transfers between devices: 0.73 us -> 3.66 us  [local(): early = lax.ppermute(early, ROW + COL, pairs_b[0])]
    mul x1 -> x0, other arithmetic: 2.91 us -> none  [local(): inv_b * (up_b + diag_b * other_a.astype(f32) - first_b - norm_b * second_b)]
    all_to_all x1, starting transfers between devices: 8.11 us -> 5.3 us  [local(): sums_a = lax.all_to_all(sums_a, COL, 0, 0)]
  transfers between devices with their start and end apart: 30 -> 29, of which waited for: 15 -> 13; matrix products, arithmetic and copies ran while one was open for 3% -> 1% of each run, Pallas kernels for 8% -> 9%
where the time goes in v2:
time: 213 us; the launch traced here: 210 us
  starting transfers between devices  80.5 us (38%)
  blocking collectives  42.7 us (20%)
  waiting for transfers between devices  41.1 us (19%)
  Pallas kernels  27.5 us (13%)
  local copies, waits for them, and re-layouts  13 us (6%)
  other arithmetic  3.5 us (2%)
    all_to_all x1, blocking collectives, local(): last = lax.all_to_all(last, ('y1', 'y0', 'xh', 'xl'), 0, 0)  25.3 us
    ppermute x1, starting transfers between devices, local(): mixed = blend(mine_b, lax.ppermute(give_b, 'k', SWAP), piece_a)  18.5 us
    all_to_all x1, blocking collectives, local(): mixed = lax.all_to_all(mixed, ('xl', 'z1', 'z0'), 0, 0)  17.5 us
    pallas_call x2, Pallas kernels, gram_part(): call(functools.partial(gram_kernel, first), out, 0, 'gram_part', pl.ANY,...  11.4 us
    unnamed x37, local copies, waits for them, and re-layouts  9.31 us
    ppermute x5, starting transfers between devices, trade(): return [lax.ppermute(x, axis, SWAP) for x in blocks]  9.03 us
    ppermute x2, starting transfers between devices, local(): lax.ppermute(x, ROW + COL, pairs)  8.32 us
    all_to_all x1, starting transfers between devices, spread(): return lax.all_to_all(jnp.broadcast_to(x[None], (n,) + x.shape), axes, 0, 0)  7.77 us
  transfers between devices with their start and end apart: 29, of which 13 were waited for; matrix products, arithmetic and copies ran while one was open for 1% of the time, Pallas kernels for 9%

profile of v2, /device:TPU:9, one launch (start us, length us, event | category | flops | bytes accessed | tf_op | source)
XLA Modules:
  0.0 209.6 jit_solution(11373426944706451174)
XLA Ops:
  0.6 1.4 fusion.5
  2.4 2.5 %collective-permute-start.1 = (f32[2,1024]{1,0:T(2,128)S(1)}, f32[2,1024]{1,0:T(2,128)S(1)}, u32[]{:S(2)}, u32[]{:S(2)}) collective-permute-start(f32[2,1024]{1,0:T(2,128)S(1)} %pad_maximum_fusion.3), channel_id=1, source_target_pairs={{0,64},{32,96},{64,0},{96,32},{1,65},{33,97},{65,1},{97,33},{2,66}... | collective-permute-start | bytes 24584 | tf_op jit(solution)/shard_map/ppermute | solution.py:383
  4.9 1.6 collective-permute-start
  7.3 7.8 %all-to-all-start = ((f32[16,2,2048]{2,1,0:T(2,128)}), f32[16,2,2048]{2,1,0:T(2,128)S(1)}, u32[]{:S(2)}, u32[]{:S(2)}) async-start(f32[16,2,2048]{2,1,0:T(2,128)} %broadcast_in_dim.2), calls=%async_computation | async-start | bytes 524288 | tf_op jit(solution)/shard_map/all_to_all | solution.py:32
  15.1 2.6 %collective-permute-start.3 = (f32[2,1024]{1,0:T(2,128)S(1)}, f32[2,1024]{1,0:T(2,128)S(1)}, u32[]{:S(2)}, u32[]{:S(2)}) collective-permute-start(f32[2,1024]{1,0:T(2,128)S(1)} %add_add_fusion), channel_id=1, source_target_pairs={{0,16},{16,0},{1,17},{17,1},{2,18},{18,2},{3,19},{19,3},{4,20},{20... | collective-permute-start | bytes 24584 | tf_op jit(solution)/shard_map/ppermute | solution.py:384
  17.7 3.9 %collective-permute-done.3 = f32[2,1024]{1,0:T(2,128)S(1)} collective-permute-done((f32[2,1024]{1,0:T(2,128)S(1)}, f32[2,1024]{1,0:T(2,128)S(1)}, u32[]{:S(2)}, u32[]{:S(2)}) %collective-permute-start.3) | collective-permute-done | bytes 8224 | tf_op jit(solution)/shard_map/ppermute | solution.py:384
  22.9 1.1 constant_dynamic-slice_fusion.1
  25.1 1.5 collective-permute-start.7
  26.6 4.4 %collective-permute-done.4 = bf16[128,1024]{1,0:T(8,128)(2,1)S(1)} collective-permute-done((bf16[128,1024]{1,0:T(8,128)(2,1)S(1)}, bf16[128,1024]{1,0:T(8,128)(2,1)S(1)}, u32[]{:S(2)}, u32[]{:S(2)}) %collective-permute-start.4) | collective-permute-done | bytes 262176 | tf_op jit(solution)/shard_map/ppermute | solution.py:404
  31.1 2.5 %collective-permute-start.9 = (bf16[256,1024]{1,0:T(8,128)(2,1)S(1)}, bf16[256,1024]{1,0:T(8,128)(2,1)}, u32[]{:S(2)}, u32[]{:S(2)}) collective-permute-start(bf16[256,1024]{1,0:T(8,128)(2,1)S(1)} %multiply_convert_fusion.1.refs_0_.half), channel_id=1, source_target_pairs={{0,16},{16,0},{1,17},{17,1},{2,18},{18,2},{3,19},{19,3},{4,20},{20... | collective-permute-start | bytes 1572872 | tf_op jit(solution)/shard_map/ppermute | solution.py:99
  33.6 2.6 %collective-permute-start.6 = (bf16[256,1024]{1,0:T(8,128)(2,1)S(1)}, bf16[256,1024]{1,0:T(8,128)(2,1)}, u32[]{:S(2)}, u32[]{:S(2)}) collective-permute-start(bf16[256,1024]{1,0:T(8,128)(2,1)S(1)} %pad_maximum_fusion.refs_0_), channel_id=1, source_target_pairs={{0,6},{2,0},{4,2},{6,4},{1,7},{3,1},{5,3},{7,5},{8,14},{10,8},{12,... | collective-permute-start | bytes 1572872 | tf_op jit(solution)/shard_map/ppermute | solution.py:95
  36.2 1.6 collective-permute-done.8.refs_2_
  38.2 6.1 %collective-permute-done.9.refs_4_ = bf16[256,1024]{1,0:T(8,128)(2,1)} collective-permute-done((bf16[256,1024]{1,0:T(8,128)(2,1)S(1)}, bf16[256,1024]{1,0:T(8,128)(2,1)}, u32[]{:S(2)}, u32[]{:S(2)}) %collective-permute-start.9) | collective-permute-done | bytes 524320 | tf_op jit(solution)/shard_map/ppermute | solution.py:99
  44.3 2.0 collective-permute-done.6.refs_2_
  46.3 3.2 %collective-permute-done.5.refs_1_ = bf16[256,1024]{1,0:T(8,128)(2,1)} collective-permute-done((bf16[256,1024]{1,0:T(8,128)(2,1)S(1)}, bf16[256,1024]{1,0:T(8,128)(2,1)}, u32[]{:S(2)}, u32[]{:S(2)}) %collective-permute-start.5) | collective-permute-done | bytes 524320 | tf_op jit(solution)/shard_map/ppermute | solution.py:95
  49.6 1.1 broadcast_select_fusion
  51.0 1.5 collective-permute-start.15
  52.5 6.7 %collective-permute-done.10.refs_3_ = bf16[256,1024]{1,0:T(8,128)(2,1)} collective-permute-done((bf16[256,1024]{1,0:T(8,128)(2,1)S(1)}, bf16[256,1024]{1,0:T(8,128)(2,1)}, u32[]{:S(2)}, u32[]{:S(2)}) %collective-permute-start.10) | collective-permute-done | bytes 524320 | tf_op jit(solution)/shard_map/ppermute | solution.py:412
  59.2 4.4 %collective-permute-start.14 = (bf16[256,1024]{1,0:T(8,128)(2,1)}, bf16[256,1024]{1,0:T(8,128)(2,1)}, u32[]{:S(2)}, u32[]{:S(2)}) collective-permute-start(bf16[256,1024]{1,0:T(8,128)(2,1)} %collective-permute-done.10.refs_3_), channel_id=1, source_target_pairs={{0,1},{1,0},{2,3},{3,2},{4,5},{5,4},{6,7},{7,6},{8,9},{9,8},{10,11... | collective-permute-start | bytes 1572872 | tf_op jit(solution)/shard_map/ppermute | solution.py:99
  64.1 1.6 collective-permute-start.13
  66.5 1.4 collective-permute-start.18
  67.9 5.5 %gram_part.2 = (bf16[8,2,256,128]{3,2,1,0:T(8,128)(2,1)S(1)}, bf16[2,128,1024]{2,1,0:T(8,128)(2,1)}) custom-call(s32[6]{0:T(128)S(1)} %pad_add_fusion.1.ids, bf16[256,1024]{1,0:T(8,128)(2,1)S(1)} %pad_maximum_fusion.refs_0_, bf16[256,1024]{1,0:T(8,128)(2,1)} %collective-permute-done.5.refs_1_, bf16[256,1024]{1,0:T(8,128)(2,1)} %collective-permute-done.6.refs_2_, ...), custom_call_target="tpu_custom_call" | custom-call | flops 1073741824 | bytes 4194304 | tf_op jit(solution)/shard_map/gram_part/pallas_call | solution.py:187
  73.5 1.0 copy-done.2
  74.5 6.0 %collective-permute-start.20 = (bf16[256,1024]{1,0:T(8,128)(2,1)}, bf16[256,1024]{1,0:T(8,128)(2,1)}, u32[]{:S(2)}, u32[]{:S(2)}) collective-permute-start(bf16[256,1024]{1,0:T(8,128)(2,1)} %bitcast.19), channel_id=1, source_target_pairs={{0,0},{13,1},{18,2},{31,3},{39,4},{42,5},{53,6},{56,7},{66,8},{79,... | collective-permute-start | bytes 1572872 | tf_op jit(solution)/shard_map/ppermute | solution.py:423
  81.3 4.5 %all-to-all-start.1 = ((bf16[16,256,128]{2,1,0:T(8,128)(2,1)}), bf16[16,256,128]{2,1,0:T(8,128)(2,1)}, u32[]{:S(2)}, u32[]{:S(2)}) async-start(bf16[16,256,128]{2,1,0:T(8,128)(2,1)} %bitcast.30), calls=%async_computation.1 | async-start | bytes 2097152 | tf_op jit(solution)/shard_map/all_to_all | solution.py:424
  85.8 5.9 %gram_part.3 = (bf16[8,128,256]{2,1,0:T(8,128)(2,1)S(1)}, bf16[8,128,256]{2,1,0:T(8,128)(2,1)S(1)}, bf16[64,1024]{1,0:T(8,128)(2,1)S(1)}, bf16[64,1024]{1,0:T(8,128)(2,1)}, bf16[128,1024]{1,0:T(8,128)(2,1)S(1)}) custom-call(s32[11]{0:T(128)S(1)} %pad_add_fusion.2.ids, bf16[256,1024]{1,0:T(8,128)(2,1)S(1)} %multiply_convert_fusion.1.refs_0_.half, ...), custom_call_target="tpu_custom_call" | custom-call | flops 1048576 | bytes 4096 | tf_op jit(solution)/shard_map/gram_part/pallas_call | solution.py:187
  91.7 18.5 %collective-permute-start.19 = (bf16[8,128,256]{2,1,0:T(8,128)(2,1)S(1)}, bf16[8,128,256]{2,1,0:T(8,128)(2,1)S(1)}, u32[]{:S(2)}, u32[]{:S(2)}) collective-permute-start(bf16[8,128,256]{2,1,0:T(8,128)(2,1)S(1)} %get-tuple-element.62), channel_id=1, source_target_pairs={{0,1},{1,0},{2,3},{3,2},{4,5},{5,4},{6,7},{7,6},{8,9},{9,8},{10,11... | collective-permute-start | bytes 1572872 | tf_op jit(solution)/shard_map/ppermute | solution.py:426
  110.2 1.2 partner.1
  112.6 1.0 copy-done.7
  113.6 1.0 copy-done.11
  114.7 1.5 blend.1
  116.2 17.5 %all_to_all.25.mixed = bf16[8,256,256]{2,1,0:T(8,128)(2,1)S(1)} all-to-all(bf16[8,256,256]{2,1,0:T(8,128)(2,1)S(1)} %blend.1), channel_id=1, replica_groups=mesh['y1'=2,'y0'=2,'xh'=2,'xl'=2,'z1'=2,'z0'=2,'k'=2] {'xl','z1','z0'}, dimensions={0} | all-to-all | bytes 2097152 | tf_op jit(solution)/shard_map/all_to_all | solution.py:430
  133.7 3.8 %collective-permute-start.21 = (bf16[8,128,256]{2,1,0:T(8,128)(2,1)S(1)}, bf16[8,128,256]{2,1,0:T(8,128)(2,1)S(1)}, u32[]{:S(2)}, u32[]{:S(2)}) collective-permute-start(bf16[8,128,256]{2,1,0:T(8,128)(2,1)S(1)} %slice.19), channel_id=1, source_target_pairs={{0,1},{1,0},{2,3},{3,2},{4,5},{5,4},{6,7},{7,6},{8,9},{9,8},{10,11... | collective-permute-start | bytes 1572872 | tf_op jit(solution)/shard_map/ppermute | solution.py:434
  137.5 1.9 collective-permute-start.22
  139.4 3.5 %second_view.1 = (f32[256,1024]{1,0:T(8,128)S(1)}, bf16[16,160,256]{2,1,0:T(8,128)(2,1)S(1)}) custom-call(s32[11]{0:T(128)S(1)} %pad_add_fusion.2.ids, bf16[8,256,256]{2,1,0:T(8,128)(2,1)S(1)} %all_to_all.25.mixed, bf16[8,128,256]{2,1,0:T(8,128)(2,1)S(1)} %collective-permute-done.21.traded, f32[2,1024]{1,0:T(2,128)S(1)} %partner.1, ...), custom_call_target="tpu_custom_call" | custom-call | flops 1073741824 | bytes 4194304 | tf_op jit(solution)/shard_map/second_view/pallas_call | solution.py:262
  142.9 3.7 %collective-permute-done.22.early = bf16[64,1024]{1,0:T(8,128)(2,1)S(1)} collective-permute-done((bf16[64,1024]{1,0:T(8,128)(2,1)S(1)}, bf16[64,1024]{1,0:T(8,128)(2,1)S(1)}, u32[]{:S(2)}, u32[]{:S(2)}) %collective-permute-start.22) | collective-permute-done | bytes 131104 | tf_op jit(solution)/shard_map/ppermute | solution.py:433
  147.2 25.3 %all_to_all.26.last = bf16[16,160,256]{2,1,0:T(8,128)(2,1)S(1)} all-to-all(bf16[16,160,256]{2,1,0:T(8,128)(2,1)S(1)} %get-tuple-element.71), channel_id=1, replica_groups=mesh['y1'=2,'y0'=2,'xh'=2,'xl'=2,'z1'=2,'z0'=2,'k'=2] {'y1','y0','xh','xl'}, dimensions={0} | all-to-all | bytes 2621440 | tf_op jit(solution)/shard_map/all_to_all | solution.py:437
  172.5 4.2 %first_view.1 = (f32[128,1024]{1,0:T(8,128)S(1)}, bf16[128,1024]{1,0:T(8,128)(2,1)}, f32[16,5,1024]{2,1,0:T(8,128)S(1)}, f32[32,256]{1,0:T(8,128)S(1)}) custom-call(s32[6]{0:T(128)S(1)} %pad_add_fusion.1.ids, bf16[16,160,256]{2,1,0:T(8,128)(2,1)S(1)} %all_to_all.26.last, bf16[256,1024]{1,0:T(8,128)(2,1)S(1)} %pad_maximum_fusion.refs_0_, ...), custom_call_target="tpu_custom_call" | custom-call | flops 1048576 | bytes 4096 | tf_op jit(solution)/shard_map/first_view/pallas_call | solution.py:306
  178.6 5.4 %collective-permute-start.24 = (bf16[128,1024]{1,0:T(8,128)(2,1)S(1)}, bf16[128,1024]{1,0:T(8,128)(2,1)}, u32[]{:S(2)}, u32[]{:S(2)}) collective-permute-start(bf16[128,1024]{1,0:T(8,128)(2,1)S(1)} %get-tuple-element.80), channel_id=1, source_target_pairs={{1,0},{96,1},{65,2},{32,3},{33,4},{64,5},{97,6},{0,7},{17,8},{112,... | collective-permute-start | bytes 786440 | tf_op jit(solution)/shard_map/ppermute | solution.py:439
  184.0 3.0 %collective-permute-start.23 = (bf16[64,1024]{1,0:T(8,128)(2,1)}, bf16[64,1024]{1,0:T(8,128)(2,1)}, u32[]{:S(2)}, u32[]{:S(2)}) collective-permute-start(bf16[64,1024]{1,0:T(8,128)(2,1)} %get-tuple-element.79), channel_id=1, source_target_pairs={{0,0},{97,1},{64,2},{33,3},{32,4},{65,5},{96,6},{1,7},{16,8},{113,... | collective-permute-start | bytes 393224 | tf_op jit(solution)/shard_map/ppermute | solution.py:439
  187.0 5.3 %all-to-all-start.4 = ((f32[16,5,1024]{2,1,0:T(8,128)}), f32[16,5,1024]{2,1,0:T(8,128)S(1)}, u32[]{:S(2)}, u32[]{:S(2)}) async-start(f32[16,5,1024]{2,1,0:T(8,128)} %copy-done.5), calls=%async_computation.4 | async-start | bytes 1048576 | tf_op jit(solution)/shard_map/all_to_all | solution.py:446
  192.3 1.2 copy-done.4
  193.5 2.4 %finish_second.1 = f32[256,1024]{1,0:T(8,128)} custom-call(s32[3]{0:T(128)S(1)} %pad_add_fusion.ids, f32[32,256]{1,0:T(8,128)S(1)} %get-tuple-element.87.terms, f32[2,1024]{1,0:T(2,128)S(1)} %pad_maximum_fusion.4.scales, f32[256,1024]{1,0:T(8,128)S(1)} %copy-done.1, f32[256,1024]{1,0:T(8,128)S(1)} %copy-done.4, ...), custom_call_target="tpu_custom_call" | custom-call | flops 1048576 | bytes 65536 | tf_op jit(solution)/shard_map/finish_second/pallas_call | solution.py:318
  195.9 6.6 %collective-permute-done.23.mid = bf16[64,1024]{1,0:T(8,128)(2,1)} collective-permute-done((bf16[64,1024]{1,0:T(8,128)(2,1)}, bf16[64,1024]{1,0:T(8,128)(2,1)}, u32[]{:S(2)}, u32[]{:S(2)}) %collective-permute-start.23) | collective-permute-done | bytes 131104 | tf_op jit(solution)/shard_map/ppermute | solution.py:439
  202.6 1.2 arrange.1
  204.6 1.5 all-to-all-done.4.sums
  206.1 1.0 copy-done.9
  207.2 2.2 %finish_first.1 = (f32[128,2048]{1,0:T(8,128)}, f32[1,1]{1,0:T(1,128)}) custom-call(s32[3]{0:T(128)S(1)} %pad_add_fusion.ids, f32[16,5,1024]{2,1,0:T(8,128)S(1)} %all-to-all-done.4.sums, f32[2,2048]{1,0:T(2,128)S(1)} %pad_maximum_fusion.2.scales, f32[128,2048]{1,0:T(8,128)S(1)} %copy-done, f32[128,2048]{1,0:T(8,128)S(1)} %get-tuple-element.83.up, ...), custom_call_target="tpu_custom_call" | custom-call | flops 1048576 | bytes 65536 | tf_op jit(solution)/shard_map/finish_first/pallas_call | solution.py:371
  (83 shorter events, 11.3 us)
Async XLA Ops:
  0.6 1.5 copy-start.1
  2.1 20.3 %copy-start = (f32[128,2048]{1,0:T(8,128)S(1)}, f32[128,2048]{1,0:T(8,128)}, u32[]{:S(2)}) copy-start(f32[128,2048]{1,0:T(8,128)} %view.2) | copy-start | bytes 3145732
  2.3 12.7 %collective-permute-start.2 = (f32[2,1024]{1,0:T(2,128)S(1)}, f32[2,1024]{1,0:T(2,128)S(1)}, u32[]{:S(2)}, u32[]{:S(2)}) collective-permute-start(f32[2,1024]{1,0:T(2,128)S(1)} %pad_maximum_fusion.3), channel_id=1, source_target_pairs={{0,96},{32,0},{64,32},{96,64},{1,97},{33,1},{65,33},{97,65},{2,98}... | collective-permute-start | bytes 24584 | tf_op jit(solution)/shard_map/ppermute | solution.py:383
  2.4 12.7 %collective-permute-start.1 = (f32[2,1024]{1,0:T(2,128)S(1)}, f32[2,1024]{1,0:T(2,128)S(1)}, u32[]{:S(2)}, u32[]{:S(2)}) collective-permute-start(f32[2,1024]{1,0:T(2,128)S(1)} %pad_maximum_fusion.3), channel_id=1, source_target_pairs={{0,64},{32,96},{64,0},{96,32},{1,65},{33,97},{65,1},{97,33},{2,66}... | collective-permute-start | bytes 24584 | tf_op jit(solution)/shard_map/ppermute | solution.py:383
  4.9 10.2 %collective-permute-start = (f32[2,1024]{1,0:T(2,128)S(1)}, f32[2,1024]{1,0:T(2,128)S(1)}, u32[]{:S(2)}, u32[]{:S(2)}) collective-permute-start(f32[2,1024]{1,0:T(2,128)S(1)} %pad_maximum_fusion.3), channel_id=1, source_target_pairs={{0,32},{32,64},{64,96},{96,0},{1,33},{33,65},{65,97},{97,1},{2,34}... | collective-permute-start | bytes 24584 | tf_op jit(solution)/shard_map/ppermute | solution.py:383
  7.3 14.9 %all-to-all-start = ((f32[16,2,2048]{2,1,0:T(2,128)}), f32[16,2,2048]{2,1,0:T(2,128)S(1)}, u32[]{:S(2)}, u32[]{:S(2)}) async-start(f32[16,2,2048]{2,1,0:T(2,128)} %broadcast_in_dim.2), calls=%async_computation | async-start | bytes 524288 | tf_op jit(solution)/shard_map/all_to_all | solution.py:32
  15.1 6.5 %collective-permute-start.3 = (f32[2,1024]{1,0:T(2,128)S(1)}, f32[2,1024]{1,0:T(2,128)S(1)}, u32[]{:S(2)}, u32[]{:S(2)}) collective-permute-start(f32[2,1024]{1,0:T(2,128)S(1)} %add_add_fusion), channel_id=1, source_target_pairs={{0,16},{16,0},{1,17},{17,1},{2,18},{18,2},{3,19},{19,3},{4,20},{20... | collective-permute-start | bytes 24584 | tf_op jit(solution)/shard_map/ppermute | solution.py:384
  24.0 6.9 %collective-permute-start.4 = (bf16[128,1024]{1,0:T(8,128)(2,1)S(1)}, bf16[128,1024]{1,0:T(8,128)(2,1)S(1)}, u32[]{:S(2)}, u32[]{:S(2)}) collective-permute-start(bf16[128,1024]{1,0:T(8,128)(2,1)S(1)} %bitcast.31), channel_id=1, source_target_pairs={{0,8},{8,0},{1,9},{9,1},{2,10},{10,2},{3,11},{11,3},{4,12},{12,4},... | collective-permute-start | bytes 786440 | tf_op jit(solution)/shard_map/ppermute | solution.py:404
  25.1 12.8 %collective-permute-start.8 = (bf16[256,1024]{1,0:T(8,128)(2,1)S(1)}, bf16[256,1024]{1,0:T(8,128)(2,1)}, u32[]{:S(2)}, u32[]{:S(2)}) collective-permute-start(bf16[256,1024]{1,0:T(8,128)(2,1)S(1)} %multiply_convert_fusion.1.refs_0_.half), channel_id=1, source_target_pairs={{0,96},{32,0},{64,32},{96,64},{1,97},{33,1},{65,33},{97,65},{2,98}... | collective-permute-start | bytes 1572872 | tf_op jit(solution)/shard_map/ppermute | solution.py:95
  25.1 13.1 %collective-permute-start.7 = (bf16[256,1024]{1,0:T(8,128)(2,1)S(1)}, bf16[256,1024]{1,0:T(8,128)(2,1)}, u32[]{:S(2)}, u32[]{:S(2)}) collective-permute-start(bf16[256,1024]{1,0:T(8,128)(2,1)S(1)} %multiply_convert_fusion.1.refs_0_.half), channel_id=1, source_target_pairs={{0,32},{32,64},{64,96},{96,0},{1,33},{33,65},{65,97},{97,1},{2,34}... | collective-permute-start | bytes 1572872 | tf_op jit(solution)/shard_map/ppermute | solution.py:95
  31.1 13.2 %collective-permute-start.9 = (bf16[256,1024]{1,0:T(8,128)(2,1)S(1)}, bf16[256,1024]{1,0:T(8,128)(2,1)}, u32[]{:S(2)}, u32[]{:S(2)}) collective-permute-start(bf16[256,1024]{1,0:T(8,128)(2,1)S(1)} %multiply_convert_fusion.1.refs_0_.half), channel_id=1, source_target_pairs={{0,16},{16,0},{1,17},{17,1},{2,18},{18,2},{3,19},{19,3},{4,20},{20... | collective-permute-start | bytes 1572872 | tf_op jit(solution)/shard_map/ppermute | solution.py:99
  33.6 12.7 %collective-permute-start.6 = (bf16[256,1024]{1,0:T(8,128)(2,1)S(1)}, bf16[256,1024]{1,0:T(8,128)(2,1)}, u32[]{:S(2)}, u32[]{:S(2)}) collective-permute-start(bf16[256,1024]{1,0:T(8,128)(2,1)S(1)} %pad_maximum_fusion.refs_0_), channel_id=1, source_target_pairs={{0,6},{2,0},{4,2},{6,4},{1,7},{3,1},{5,3},{7,5},{8,14},{10,8},{12,... | collective-permute-start | bytes 1572872 | tf_op jit(solution)/shard_map/ppermute | solution.py:95
  36.2 13.3 %collective-permute-start.5 = (bf16[256,1024]{1,0:T(8,128)(2,1)S(1)}, bf16[256,1024]{1,0:T(8,128)(2,1)}, u32[]{:S(2)}, u32[]{:S(2)}) collective-permute-start(bf16[256,1024]{1,0:T(8,128)(2,1)S(1)} %pad_maximum_fusion.refs_0_), channel_id=1, source_target_pairs={{0,2},{2,4},{4,6},{6,0},{1,3},{3,5},{5,7},{7,1},{8,10},{10,12},{12... | collective-permute-start | bytes 1572872 | tf_op jit(solution)/shard_map/ppermute | solution.py:95
  50.7 8.5 %collective-permute-start.10 = (bf16[256,1024]{1,0:T(8,128)(2,1)S(1)}, bf16[256,1024]{1,0:T(8,128)(2,1)}, u32[]{:S(2)}, u32[]{:S(2)}) collective-permute-start(bf16[256,1024]{1,0:T(8,128)(2,1)S(1)} %broadcast_select_fusion), channel_id=1, source_target_pairs={{0,2},{1,7},{2,4},{3,1},{4,6},{5,3},{6,0},{7,5},{8,10},{9,15},{10,... | collective-permute-start | bytes 1572872 | tf_op jit(solution)/shard_map/ppermute | solution.py:412
  51.0 13.1 %collective-permute-start.16 = (bf16[256,1024]{1,0:T(8,128)(2,1)}, bf16[256,1024]{1,0:T(8,128)(2,1)}, u32[]{:S(2)}, u32[]{:S(2)}) collective-permute-start(bf16[256,1024]{1,0:T(8,128)(2,1)} %collective-permute-done.9.refs_4_), channel_id=1, source_target_pairs={{0,96},{32,0},{64,32},{96,64},{1,97},{33,1},{65,33},{97,65},{2,98}... | collective-permute-start | bytes 1572872 | tf_op jit(solution)/shard_map/ppermute | solution.py:95
  51.0 15.4 %collective-permute-start.15 = (bf16[256,1024]{1,0:T(8,128)(2,1)}, bf16[256,1024]{1,0:T(8,128)(2,1)}, u32[]{:S(2)}, u32[]{:S(2)}) collective-permute-start(bf16[256,1024]{1,0:T(8,128)(2,1)} %collective-permute-done.9.refs_4_), channel_id=1, source_target_pairs={{0,32},{32,64},{64,96},{96,0},{1,33},{33,65},{65,97},{97,1},{2,34}... | collective-permute-start | bytes 1572872 | tf_op jit(solution)/shard_map/ppermute | solution.py:95
  59.2 7.3 %collective-permute-start.14 = (bf16[256,1024]{1,0:T(8,128)(2,1)}, bf16[256,1024]{1,0:T(8,128)(2,1)}, u32[]{:S(2)}, u32[]{:S(2)}) collective-permute-start(bf16[256,1024]{1,0:T(8,128)(2,1)} %collective-permute-done.10.refs_3_), channel_id=1, source_target_pairs={{0,1},{1,0},{2,3},{3,2},{4,5},{5,4},{6,7},{7,6},{8,9},{9,8},{10,11... | collective-permute-start | bytes 1572872 | tf_op jit(solution)/shard_map/ppermute | solution.py:99
  63.6 4.4 %collective-permute-start.11 = (bf16[256,1024]{1,0:T(8,128)(2,1)S(1)}, bf16[256,1024]{1,0:T(8,128)(2,1)}, u32[]{:S(2)}, u32[]{:S(2)}) collective-permute-start(bf16[256,1024]{1,0:T(8,128)(2,1)S(1)} %pad_maximum_fusion.refs_0_), channel_id=1, source_target_pairs={{0,1},{1,0},{2,3},{3,2},{4,5},{5,4},{6,7},{7,6},{8,9},{9,8},{10,11... | collective-permute-start | bytes 1572872 | tf_op jit(solution)/shard_map/ppermute | solution.py:99
  63.6 4.4 %collective-permute-start.12 = (bf16[256,1024]{1,0:T(8,128)(2,1)}, bf16[256,1024]{1,0:T(8,128)(2,1)}, u32[]{:S(2)}, u32[]{:S(2)}) collective-permute-start(bf16[256,1024]{1,0:T(8,128)(2,1)} %collective-permute-done.5.refs_1_), channel_id=1, source_target_pairs={{0,1},{1,0},{2,3},{3,2},{4,5},{5,4},{6,7},{7,6},{8,9},{9,8},{10,11... | collective-permute-start | bytes 1572872 | tf_op jit(solution)/shard_map/ppermute | solution.py:99
  64.1 3.9 %collective-permute-start.13 = (bf16[256,1024]{1,0:T(8,128)(2,1)}, bf16[256,1024]{1,0:T(8,128)(2,1)}, u32[]{:S(2)}, u32[]{:S(2)}) collective-permute-start(bf16[256,1024]{1,0:T(8,128)(2,1)} %collective-permute-done.6.refs_2_), channel_id=1, source_target_pairs={{0,1},{1,0},{2,3},{3,2},{4,5},{5,4},{6,7},{7,6},{8,9},{9,8},{10,11... | collective-permute-start | bytes 1572872 | tf_op jit(solution)/shard_map/ppermute | solution.py:99
  66.4 14.8 %collective-permute-start.17 = (bf16[256,1024]{1,0:T(8,128)(2,1)}, bf16[256,1024]{1,0:T(8,128)(2,1)}, u32[]{:S(2)}, u32[]{:S(2)}) collective-permute-start(bf16[256,1024]{1,0:T(8,128)(2,1)} %collective-permute-done.7.refs_1_), channel_id=1, source_target_pairs={{0,32},{32,64},{64,96},{96,0},{1,33},{33,65},{65,97},{97,1},{2,34}... | collective-permute-start | bytes 1572872 | tf_op jit(solution)/shard_map/ppermute | solution.py:415
  66.5 14.8 %collective-permute-start.18 = (bf16[256,1024]{1,0:T(8,128)(2,1)}, bf16[256,1024]{1,0:T(8,128)(2,1)}, u32[]{:S(2)}, u32[]{:S(2)}) collective-permute-start(bf16[256,1024]{1,0:T(8,128)(2,1)} %collective-permute-done.16.refs_6_), channel_id=1, source_target_pairs={{0,96},{32,0},{64,32},{96,64},{1,97},{33,1},{65,33},{97,65},{2,98}... | collective-permute-start | bytes 1572872 | tf_op jit(solution)/shard_map/ppermute | solution.py:417
  73.5 1.0 copy-start.2
  74.5 35.8 %collective-permute-start.20 = (bf16[256,1024]{1,0:T(8,128)(2,1)}, bf16[256,1024]{1,0:T(8,128)(2,1)}, u32[]{:S(2)}, u32[]{:S(2)}) collective-permute-start(bf16[256,1024]{1,0:T(8,128)(2,1)} %bitcast.19), channel_id=1, source_target_pairs={{0,0},{13,1},{18,2},{31,3},{39,4},{42,5},{53,6},{56,7},{66,8},{79,... | collective-permute-start | bytes 1572872 | tf_op jit(solution)/shard_map/ppermute | solution.py:423
  81.3 31.3 %all-to-all-start.1 = ((bf16[16,256,128]{2,1,0:T(8,128)(2,1)}), bf16[16,256,128]{2,1,0:T(8,128)(2,1)}, u32[]{:S(2)}, u32[]{:S(2)}) async-start(bf16[16,256,128]{2,1,0:T(8,128)(2,1)} %bitcast.30), calls=%async_computation.1 | async-start | bytes 2097152 | tf_op jit(solution)/shard_map/all_to_all | solution.py:424
  91.7 19.7 %copy-start.6 = (bf16[8,128,256]{2,1,0:T(8,128)(2,1)}, bf16[8,128,256]{2,1,0:T(8,128)(2,1)S(1)}, u32[]{:S(2)}) copy-start(bf16[8,128,256]{2,1,0:T(8,128)(2,1)S(1)} %get-tuple-element.61.mine) | copy-start | bytes 1572868
  91.7 19.7 %copy-start.16 = (bf16[64,1024]{1,0:T(8,128)(2,1)}, bf16[64,1024]{1,0:T(8,128)(2,1)S(1)}, u32[]{:S(2)}) copy-start(bf16[64,1024]{1,0:T(8,128)(2,1)S(1)} %get-tuple-element.70) | copy-start | bytes 393220
  91.7 20.0 %collective-permute-start.19 = (bf16[8,128,256]{2,1,0:T(8,128)(2,1)S(1)}, bf16[8,128,256]{2,1,0:T(8,128)(2,1)S(1)}, u32[]{:S(2)}, u32[]{:S(2)}) collective-permute-start(bf16[8,128,256]{2,1,0:T(8,128)(2,1)S(1)} %get-tuple-element.62), channel_id=1, source_target_pairs={{0,1},{1,0},{2,3},{3,2},{4,5},{5,4},{6,7},{7,6},{8,9},{9,8},{10,11... | collective-permute-start | bytes 1572872 | tf_op jit(solution)/shard_map/ppermute | solution.py:426
  111.8 0.8 copy-start.10
  112.6 1.0 copy-start.7
  113.6 1.0 copy-start.11
  116.1 21.3 %copy-start.17 = (bf16[64,1024]{1,0:T(8,128)(2,1)S(1)}, bf16[64,1024]{1,0:T(8,128)(2,1)}, u32[]{:S(2)}) copy-start(bf16[64,1024]{1,0:T(8,128)(2,1)} %copy-done.16) | copy-start | bytes 393220
  133.7 5.7 %collective-permute-start.21 = (bf16[8,128,256]{2,1,0:T(8,128)(2,1)S(1)}, bf16[8,128,256]{2,1,0:T(8,128)(2,1)S(1)}, u32[]{:S(2)}, u32[]{:S(2)}) collective-permute-start(bf16[8,128,256]{2,1,0:T(8,128)(2,1)S(1)} %slice.19), channel_id=1, source_target_pairs={{0,1},{1,0},{2,3},{3,2},{4,5},{5,4},{6,7},{7,6},{8,9},{9,8},{10,11... | collective-permute-start | bytes 1572872 | tf_op jit(solution)/shard_map/ppermute | solution.py:434
  137.5 9.1 %collective-permute-start.22 = (bf16[64,1024]{1,0:T(8,128)(2,1)S(1)}, bf16[64,1024]{1,0:T(8,128)(2,1)S(1)}, u32[]{:S(2)}, u32[]{:S(2)}) collective-permute-start(bf16[64,1024]{1,0:T(8,128)(2,1)S(1)} %copy-done.17), channel_id=1, source_target_pairs={{0,0},{97,1},{64,2},{33,3},{32,4},{65,5},{96,6},{1,7},{16,8},{113,... | collective-permute-start | bytes 393224 | tf_op jit(solution)/shard_map/ppermute | solution.py:433
  142.9 29.6 %copy-start.3 = (f32[256,1024]{1,0:T(8,128)}, f32[256,1024]{1,0:T(8,128)S(1)}, u32[]{:S(2)}) copy-start(f32[256,1024]{1,0:T(8,128)S(1)} %get-tuple-element.88.up) | copy-start | bytes 3145732
  146.6 0.7 copy-start.14
  176.7 0.8 copy-start.5
  177.5 0.8 copy-start.12
  178.3 24.3 %collective-permute-start.25 = (bf16[128,1024]{1,0:T(8,128)(2,1)}, bf16[128,1024]{1,0:T(8,128)(2,1)}, u32[]{:S(2)}, u32[]{:S(2)}) collective-permute-start(bf16[128,1024]{1,0:T(8,128)(2,1)} %get-tuple-element.82), channel_id=1, source_target_pairs={{0,8},{8,0},{1,9},{9,1},{2,10},{10,2},{3,11},{11,3},{4,12},{12,4},... | collective-permute-start | bytes 786440 | tf_op jit(solution)/shard_map/ppermute | solution.py:442
  178.6 23.9 %collective-permute-start.24 = (bf16[128,1024]{1,0:T(8,128)(2,1)S(1)}, bf16[128,1024]{1,0:T(8,128)(2,1)}, u32[]{:S(2)}, u32[]{:S(2)}) collective-permute-start(bf16[128,1024]{1,0:T(8,128)(2,1)S(1)} %get-tuple-element.80), channel_id=1, source_target_pairs={{1,0},{96,1},{65,2},{32,3},{33,4},{64,5},{97,6},{0,7},{17,8},{112,... | collective-permute-start | bytes 786440 | tf_op jit(solution)/shard_map/ppermute | solution.py:439
  184.0 18.5 %collective-permute-start.23 = (bf16[64,1024]{1,0:T(8,128)(2,1)}, bf16[64,1024]{1,0:T(8,128)(2,1)}, u32[]{:S(2)}, u32[]{:S(2)}) collective-permute-start(bf16[64,1024]{1,0:T(8,128)(2,1)} %get-tuple-element.79), channel_id=1, source_target_pairs={{0,0},{97,1},{64,2},{33,3},{32,4},{65,5},{96,6},{1,7},{16,8},{113,... | collective-permute-start | bytes 393224 | tf_op jit(solution)/shard_map/ppermute | solution.py:439
  187.0 19.1 %all-to-all-start.4 = ((f32[16,5,1024]{2,1,0:T(8,128)}), f32[16,5,1024]{2,1,0:T(8,128)S(1)}, u32[]{:S(2)}, u32[]{:S(2)}) async-start(f32[16,5,1024]{2,1,0:T(8,128)} %copy-done.5), calls=%async_computation.4 | async-start | bytes 1048576 | tf_op jit(solution)/shard_map/all_to_all | solution.py:446
  192.3 1.2 copy-start.4
  193.5 9.0 %copy-start.13 = (f32[128,1024]{1,0:T(8,128)S(1)}, f32[128,1024]{1,0:T(8,128)}, u32[]{:S(2)}) copy-start(f32[128,1024]{1,0:T(8,128)} %copy-done.12) | copy-start | bytes 1572868
  193.5 9.0 %copy-start.15 = (bf16[64,1024]{1,0:T(8,128)(2,1)S(1)}, bf16[64,1024]{1,0:T(8,128)(2,1)}, u32[]{:S(2)}) copy-start(bf16[64,1024]{1,0:T(8,128)(2,1)} %copy-done.14) | copy-start | bytes 393220
  203.8 0.8 copy-start.8
  206.1 1.0 copy-start.9

commit v3 on v2

--- a/solution.py
+++ b/solution.py
@@ -187,24 +187,31 @@
     return call(functools.partial(gram_kernel, first), out, 0, "gram_part", pl.ANY, scratch, flops)(ids, *blocks)
 
 
-def blend_kernel(mine, traded, received, out):
-    piece = received[0].astype(f32)
+def blend_kernel(mine, traded, received, out, held_mine, held_traded, held, sems):
+    pairs = ((received, held), (mine, held_mine), (traded, held_traded))
+    copies = [pltpu.make_async_copy(ref, slot, sems.at[i]) for i, (ref, slot) in enumerate(pairs)]
+    for copy in copies:
+        copy.start()
+    copies[0].wait()
+    piece = held[0].astype(f32)
     for i in range(1, 16):
-        piece = piece + received[i].astype(f32)
+        piece = piece + held[i].astype(f32)
     piece = piece.astype(bf16)
+    for copy in copies[1:]:
+        copy.wait()
     for i in range(8):
-        out[i, 0:128] = (mine[i].astype(f32) + traded[i].astype(f32)).astype(bf16)
+        out[i, 0:128] = (held_mine[i].astype(f32) + held_traded[i].astype(f32)).astype(bf16)
         out[i, 128:256, 0:128] = piece[0:128]
         out[i, 128:256, 128:256] = piece[128:256]
 
 
 def blend(mine, traded, received):
-    vmem = pl.BlockSpec(memory_space=pltpu.VMEM)
     return pl.pallas_call(
         blend_kernel,
         out_shape=jax.ShapeDtypeStruct((8, 256, 256), bf16),
-        in_specs=[vmem] * 3,
-        out_specs=vmem,
+        in_specs=[pl.BlockSpec(memory_space=pl.ANY)] * 3,
+        out_specs=pl.BlockSpec(memory_space=pltpu.VMEM),
+        scratch_shapes=[pltpu.VMEM(x.shape, bf16) for x in (mine, traded, received)] + [pltpu.SemaphoreType.DMA((3,))],
         compiler_params=pltpu.CompilerParams(vmem_limit_bytes=14 * 1024 * 1024),
         cost_estimate=pl.CostEstimate(flops=1 << 20, bytes_accessed=4 << 20, transcendentals=0),
         name="blend",
@@ -418,7 +425,7 @@
     blocks_a = [own_a, *near_a, far_a, *other_own_a, *other_near_a, other_far_a]
 
     part_a, send_a = gram_part(True, ids_a, blocks_a)
-    part_a, far_b, other_far_b = tie(part_a, far_b, other_far_b)
+    send_a, far_b, other_far_b = tie(send_a, far_b, other_far_b)
     blocks_b = [half_b, *near_b, far_b, *other_own_b, *other_near_b, other_far_b]
     other_a = lax.ppermute(send_a.reshape(256, 1024), ROW + COL, pairs_a)
     piece_a = lax.all_to_all(part_a.reshape(16, 256, 128), ("y1", "y0", "xh", "xl"), 0, 0)
@@ -427,21 +434,22 @@
     ids = jnp.stack([xl, core, lax.axis_index(ROW)])
     partner = vmem_call(partner_kernel, jax.ShapeDtypeStruct((2, 1024), f32), (ids, other_a, half_b), "partner", 1 << 34)
     mixed, partner = tie(mixed, partner)
+    early = lax.ppermute(send_b[0], ROW + COL, pairs_b[0])
     mixed = lax.all_to_all(mixed, ("xl", "z1", "z0"), 0, 0)
 
-    mixed, early = tie(mixed, send_b[0])
-    early = lax.ppermute(early, ROW + COL, pairs_b[0])
+    mixed, early, mid = tie(mixed, early, send_b[1])
+    mid = lax.ppermute(mid, ROW + COL, pairs_b[0])
     traded = lax.ppermute(mixed[:, 128:], "k", SWAP)
     up_b, last = second_view(ids_b, mixed, traded, partner, blocks_b)
-    last, early = tie(last, early)
+    last, mid = tie(last, mid)
     last = lax.all_to_all(last, ("y1", "y0", "xh", "xl"), 0, 0)
-    last, *late = tie(last, *send_b[1:])
-    late = [lax.ppermute(x, ROW + COL, pairs) for x, pairs in zip(late, pairs_b)]
+    last, late = tie(last, send_b[2])
+    late = lax.ppermute(late, ROW + COL, pairs_b[1])
 
     keep, give, sums_a, sums_b = first_view(ids_a, last, blocks_a)
     traded = lax.ppermute(give, "xl", SWAP)
     out = [jax.ShapeDtypeStruct((128, 2048), bf16), jax.ShapeDtypeStruct((128, 2048), f32)]
-    block, up_own = vmem_call(arrange_kernel, out, (ids, early, *late, keep, traded), "arrange", 1 << 34)
+    block, up_own = vmem_call(arrange_kernel, out, (ids, early, mid, late, keep, traded), "arrange", 1 << 34)
     sums_a, sums_b = tie(sums_a, sums_b)
     sums_a = lax.all_to_all(sums_a, COL, 0, 0)
 

time: 213 us -> 205 us (0.962)
  waiting for transfers between devices: 41.1 us -> 65.9 us
  starting transfers between devices: 80.5 us -> 62 us
  blocking collectives: 42.7 us -> 27.7 us
  local copies, waits for them, and re-layouts: 13 us -> 15.2 us
    ppermute x1, starting transfers between devices: 18.5 us -> 0.3 us  [local(): mixed = blend(mine_b, lax.ppermute(give_b, 'k', SWAP), piece_a)]
    all_to_all x1 -> x0, blocking collectives: 17.5 us -> none  [local(): mixed = lax.all_to_all(mixed, ('xl', 'z1', 'z0'), 0, 0)]
    all_to_all x1, waiting for transfers between devices: 0.01 us -> 9.84 us  [local(): lax.all_to_all(part_a.reshape(16, 256, 128), ('y1', 'y0', 'xh', 'xl'), 0, 0)]
    all_to_all x1, waiting for transfers between devices: 1.5 us -> 8.03 us  [local(): sums_a = lax.all_to_all(sums_a, COL, 0, 0)]
    ppermute x3, waiting for transfers between devices: 10.3 us -> 15.7 us  [the longest x1 15.3 us: local(): early = lax.ppermute(send_b[0], ROW + COL, pairs_b[0])]
    ppermute x1, starting transfers between devices: 3.83 us -> 0.09 us  [local(): traded = lax.ppermute(mixed[:, 128:], 'k', SWAP)]
    all_to_all x0 -> x1, starting transfers between devices: none -> 3.56 us  [local(): mixed = lax.all_to_all(mixed, ('xl', 'z1', 'z0'), 0, 0)]
    all_to_all x1, blocking collectives: 25.3 us -> 27.7 us  [local(): last = lax.all_to_all(last, ('y1', 'y0', 'xh', 'xl'), 0, 0)]
  transfers between devices with their start and end apart: 29 -> 30, of which waited for: 13 -> 15; matrix products, arithmetic and copies ran while one was open for 1% -> 1% of each run, Pallas kernels for 9% -> 10%
where the time goes in v3:
time: 205 us; the launch traced here: 203 us
  waiting for transfers between devices  65.9 us (32%)
  starting transfers between devices  62 us (30%)
  blocking collectives  27.7 us (14%)
  Pallas kernels  27.3 us (13%)
  local copies, waits for them, and re-layouts  15.2 us (7%)
  other arithmetic  3.5 us (2%)
    all_to_all x1, blocking collectives, local(): last = lax.all_to_all(last, ('y1', 'y0', 'xh', 'xl'), 0, 0)  27.7 us
    ppermute x1, waiting for transfers between devices, local(): early = lax.ppermute(send_b[0], ROW + COL, pairs_b[0])  15.3 us
    unnamed x59, local copies, waits for them, and re-layouts  11.5 us
    pallas_call x2, Pallas kernels, gram_part(): call(functools.partial(gram_kernel, first), out, 0, 'gram_part', pl.ANY,...  11.4 us
    all_to_all x1, waiting for transfers between devices, local(): lax.all_to_all(part_a.reshape(16, 256, 128), ('y1', 'y0', 'xh', 'xl'), 0, 0)  9.84 us
    ppermute x5, starting transfers between devices, trade(): return [lax.ppermute(x, axis, SWAP) for x in blocks]  8.21 us
    all_to_all x1, waiting for transfers between devices, local(): sums_a = lax.all_to_all(sums_a, COL, 0, 0)  8.03 us
    all_to_all x1, starting transfers between devices, spread(): return lax.all_to_all(jnp.broadcast_to(x[None], (n,) + x.shape), axes, 0, 0)  7.77 us
  transfers between devices with their start and end apart: 30, of which 15 were waited for; matrix products, arithmetic and copies ran while one was open for 1% of the time, Pallas kernels for 10%

profile of v3, /device:TPU:9, one launch (start us, length us, event | category | flops | bytes accessed | tf_op | source)
XLA Modules:
  0.0 202.8 jit_solution(9771441317200047631)
XLA Ops:
  0.6 1.4 fusion.5
  2.4 2.5 %collective-permute-start.1 = (f32[2,1024]{1,0:T(2,128)S(1)}, f32[2,1024]{1,0:T(2,128)S(1)}, u32[]{:S(2)}, u32[]{:S(2)}) collective-permute-start(f32[2,1024]{1,0:T(2,128)S(1)} %pad_maximum_fusion.3), channel_id=1, source_target_pairs={{0,64},{32,96},{64,0},{96,32},{1,65},{33,97},{65,1},{97,33},{2,66}... | collective-permute-start | bytes 24584 | tf_op jit(solution)/shard_map/ppermute | solution.py:390
  4.9 1.6 collective-permute-start
  7.3 7.8 %all-to-all-start = ((f32[16,2,2048]{2,1,0:T(2,128)}), f32[16,2,2048]{2,1,0:T(2,128)S(1)}, u32[]{:S(2)}, u32[]{:S(2)}) async-start(f32[16,2,2048]{2,1,0:T(2,128)} %broadcast_in_dim.2), calls=%async_computation | async-start | bytes 524288 | tf_op jit(solution)/shard_map/all_to_all | solution.py:32
  15.1 2.6 %collective-permute-start.3 = (f32[2,1024]{1,0:T(2,128)S(1)}, f32[2,1024]{1,0:T(2,128)S(1)}, u32[]{:S(2)}, u32[]{:S(2)}) collective-permute-start(f32[2,1024]{1,0:T(2,128)S(1)} %add_add_fusion), channel_id=1, source_target_pairs={{0,16},{16,0},{1,17},{17,1},{2,18},{18,2},{3,19},{19,3},{4,20},{20... | collective-permute-start | bytes 24584 | tf_op jit(solution)/shard_map/ppermute | solution.py:391
  17.7 3.9 %collective-permute-done.3 = f32[2,1024]{1,0:T(2,128)S(1)} collective-permute-done((f32[2,1024]{1,0:T(2,128)S(1)}, f32[2,1024]{1,0:T(2,128)S(1)}, u32[]{:S(2)}, u32[]{:S(2)}) %collective-permute-start.3) | collective-permute-done | bytes 8224 | tf_op jit(solution)/shard_map/ppermute | solution.py:391
  22.9 1.1 constant_dynamic-slice_fusion.1
  25.1 1.5 collective-permute-start.7
  26.6 4.4 %collective-permute-done.4 = bf16[128,1024]{1,0:T(8,128)(2,1)S(1)} collective-permute-done((bf16[128,1024]{1,0:T(8,128)(2,1)S(1)}, bf16[128,1024]{1,0:T(8,128)(2,1)S(1)}, u32[]{:S(2)}, u32[]{:S(2)}) %collective-permute-start.4) | collective-permute-done | bytes 262176 | tf_op jit(solution)/shard_map/ppermute | solution.py:411
  31.1 2.5 %collective-permute-start.9 = (bf16[256,1024]{1,0:T(8,128)(2,1)S(1)}, bf16[256,1024]{1,0:T(8,128)(2,1)}, u32[]{:S(2)}, u32[]{:S(2)}) collective-permute-start(bf16[256,1024]{1,0:T(8,128)(2,1)S(1)} %multiply_convert_fusion.1.refs_0_.half), channel_id=1, source_target_pairs={{0,16},{16,0},{1,17},{17,1},{2,18},{18,2},{3,19},{19,3},{4,20},{20... | collective-permute-start | bytes 1572872 | tf_op jit(solution)/shard_map/ppermute | solution.py:99
  33.6 2.6 %collective-permute-start.6 = (bf16[256,1024]{1,0:T(8,128)(2,1)S(1)}, bf16[256,1024]{1,0:T(8,128)(2,1)}, u32[]{:S(2)}, u32[]{:S(2)}) collective-permute-start(bf16[256,1024]{1,0:T(8,128)(2,1)S(1)} %pad_maximum_fusion.refs_0_), channel_id=1, source_target_pairs={{0,6},{2,0},{4,2},{6,4},{1,7},{3,1},{5,3},{7,5},{8,14},{10,8},{12,... | collective-permute-start | bytes 1572872 | tf_op jit(solution)/shard_map/ppermute | solution.py:95
  36.2 1.6 collective-permute-done.8.refs_2_
  38.2 6.1 %collective-permute-done.9.refs_4_ = bf16[256,1024]{1,0:T(8,128)(2,1)} collective-permute-done((bf16[256,1024]{1,0:T(8,128)(2,1)S(1)}, bf16[256,1024]{1,0:T(8,128)(2,1)}, u32[]{:S(2)}, u32[]{:S(2)}) %collective-permute-start.9) | collective-permute-done | bytes 524320 | tf_op jit(solution)/shard_map/ppermute | solution.py:99
  44.3 2.0 collective-permute-done.6.refs_2_
  46.3 3.2 %collective-permute-done.5.refs_1_ = bf16[256,1024]{1,0:T(8,128)(2,1)} collective-permute-done((bf16[256,1024]{1,0:T(8,128)(2,1)S(1)}, bf16[256,1024]{1,0:T(8,128)(2,1)}, u32[]{:S(2)}, u32[]{:S(2)}) %collective-permute-start.5) | collective-permute-done | bytes 524320 | tf_op jit(solution)/shard_map/ppermute | solution.py:95
  49.6 1.1 broadcast_select_fusion
  51.0 1.5 collective-permute-start.15
  52.5 6.7 %collective-permute-done.10.refs_3_ = bf16[256,1024]{1,0:T(8,128)(2,1)S(1)} collective-permute-done((bf16[256,1024]{1,0:T(8,128)(2,1)S(1)}, bf16[256,1024]{1,0:T(8,128)(2,1)S(1)}, u32[]{:S(2)}, u32[]{:S(2)}) %collective-permute-start.10) | collective-permute-done | bytes 524320 | tf_op jit(solution)/shard_map/ppermute | solution.py:419
  59.2 4.3 %collective-permute-start.14 = (bf16[256,1024]{1,0:T(8,128)(2,1)S(1)}, bf16[256,1024]{1,0:T(8,128)(2,1)S(1)}, u32[]{:S(2)}, u32[]{:S(2)}) collective-permute-start(bf16[256,1024]{1,0:T(8,128)(2,1)S(1)} %collective-permute-done.10.refs_3_), channel_id=1, source_target_pairs={{0,1},{1,0},{2,3},{3,2},{4,5},{5,4},{6,7},{7,6},{8,9},{9,8},{10,11... | collective-permute-start | bytes 1572872 | tf_op jit(solution)/shard_map/ppermute | solution.py:99
  67.3 1.5 collective-permute-start.18
  69.6 1.0 copy-done.11
  70.6 1.0 copy-done.14
  71.7 5.4 %gram_part.2 = (bf16[8,2,256,128]{3,2,1,0:T(8,128)(2,1)S(1)}, bf16[2,128,1024]{2,1,0:T(8,128)(2,1)}) custom-call(s32[6]{0:T(128)S(1)} %pad_add_fusion.1.ids, bf16[256,1024]{1,0:T(8,128)(2,1)S(1)} %pad_maximum_fusion.refs_0_, bf16[256,1024]{1,0:T(8,128)(2,1)} %collective-permute-done.5.refs_1_, bf16[256,1024]{1,0:T(8,128)(2,1)} %collective-permute-done.6.refs_2_, ...), custom_call_target="tpu_custom_call" | custom-call | flops 1073741824 | bytes 4194304 | tf_op jit(solution)/shard_map/gram_part/pallas_call | solution.py:187
  77.1 1.0 copy-done.16
  78.1 1.0 collective-permute-done.17.refs_3_
  79.0 2.5 %collective-permute-done.18.refs_7_ = bf16[256,1024]{1,0:T(8,128)(2,1)} collective-permute-done((bf16[256,1024]{1,0:T(8,128)(2,1)}, bf16[256,1024]{1,0:T(8,128)(2,1)}, u32[]{:S(2)}, u32[]{:S(2)}) %collective-permute-start.18) | collective-permute-done | bytes 524320 | tf_op jit(solution)/shard_map/ppermute | solution.py:424
  81.5 7.0 %collective-permute-start.20 = (bf16[256,1024]{1,0:T(8,128)(2,1)}, bf16[256,1024]{1,0:T(8,128)(2,1)}, u32[]{:S(2)}, u32[]{:S(2)}) collective-permute-start(bf16[256,1024]{1,0:T(8,128)(2,1)} %bitcast.19), channel_id=1, source_target_pairs={{0,0},{13,1},{18,2},{31,3},{39,4},{42,5},{53,6},{56,7},{66,8},{79,... | collective-permute-start | bytes 1572872 | tf_op jit(solution)/shard_map/ppermute | solution.py:430
  89.3 4.4 %all-to-all-start.1 = ((bf16[16,256,128]{2,1,0:T(8,128)(2,1)}), bf16[16,256,128]{2,1,0:T(8,128)(2,1)}, u32[]{:S(2)}, u32[]{:S(2)}) async-start(bf16[16,256,128]{2,1,0:T(8,128)(2,1)} %bitcast.30), calls=%async_computation.1 | async-start | bytes 2097152 | tf_op jit(solution)/shard_map/all_to_all | solution.py:431
  93.8 6.0 %gram_part.3 = (bf16[8,128,256]{2,1,0:T(8,128)(2,1)S(1)}, bf16[8,128,256]{2,1,0:T(8,128)(2,1)}, bf16[64,1024]{1,0:T(8,128)(2,1)S(1)}, bf16[64,1024]{1,0:T(8,128)(2,1)S(1)}, bf16[128,1024]{1,0:T(8,128)(2,1)S(1)}) custom-call(s32[11]{0:T(128)S(1)} %pad_add_fusion.2.ids, bf16[256,1024]{1,0:T(8,128)(2,1)S(1)} %multiply_convert_fusion.1.refs_0_.half, ...), custom_call_target="tpu_custom_call" | custom-call | flops 1048576 | bytes 4096 | tf_op jit(solution)/shard_map/gram_part/pallas_call | solution.py:187
  101.3 1.2 partner.1
  102.5 9.8 %all-to-all-done.1.received = bf16[16,256,128]{2,1,0:T(8,128)(2,1)} async-done(((bf16[16,256,128]{2,1,0:T(8,128)(2,1)}), bf16[16,256,128]{2,1,0:T(8,128)(2,1)}, u32[]{:S(2)}, u32[]{:S(2)}) %all-to-all-start.1) | async-done | bytes 1048608 | tf_op jit(solution)/shard_map/all_to_all | solution.py:431
  112.3 1.6 blend.1
  113.9 1.0 copy-done.6
  114.9 3.6 %all-to-all-start.2 = ((bf16[8,256,256]{2,1,0:T(8,128)(2,1)}), bf16[8,256,256]{2,1,0:T(8,128)(2,1)S(1)}, u32[]{:S(2)}, u32[]{:S(2)}) async-start(bf16[8,256,256]{2,1,0:T(8,128)(2,1)} %copy-done.6), calls=%async_computation.2 | async-start | bytes 2097152 | tf_op jit(solution)/shard_map/all_to_all | solution.py:438
  118.4 3.8 %collective-permute-start.21 = (bf16[64,1024]{1,0:T(8,128)(2,1)}, bf16[64,1024]{1,0:T(8,128)(2,1)S(1)}, u32[]{:S(2)}, u32[]{:S(2)}) collective-permute-start(bf16[64,1024]{1,0:T(8,128)(2,1)} %copy-done.28), channel_id=1, source_target_pairs={{0,0},{97,1},{64,2},{33,3},{32,4},{65,5},{96,6},{1,7},{16,8},{113,... | collective-permute-start | bytes 393224 | tf_op jit(solution)/shard_map/ppermute | solution.py:437
  122.2 15.3 %collective-permute-done.21.early = bf16[64,1024]{1,0:T(8,128)(2,1)S(1)} collective-permute-done((bf16[64,1024]{1,0:T(8,128)(2,1)}, bf16[64,1024]{1,0:T(8,128)(2,1)S(1)}, u32[]{:S(2)}, u32[]{:S(2)}) %collective-permute-start.21) | collective-permute-done | bytes 131104 | tf_op jit(solution)/shard_map/ppermute | solution.py:437
  138.3 2.8 %collective-permute-start.23 = (bf16[64,1024]{1,0:T(8,128)(2,1)}, bf16[64,1024]{1,0:T(8,128)(2,1)S(1)}, u32[]{:S(2)}, u32[]{:S(2)}) collective-permute-start(bf16[64,1024]{1,0:T(8,128)(2,1)} %copy-done.27), channel_id=1, source_target_pairs={{0,0},{97,1},{64,2},{33,3},{32,4},{65,5},{96,6},{1,7},{16,8},{113,... | collective-permute-start | bytes 393224 | tf_op jit(solution)/shard_map/ppermute | solution.py:441
  141.2 3.3 %second_view.1 = (f32[256,1024]{1,0:T(8,128)S(1)}, bf16[16,160,256]{2,1,0:T(8,128)(2,1)S(1)}) custom-call(s32[11]{0:T(128)S(1)} %pad_add_fusion.2.ids, bf16[8,256,256]{2,1,0:T(8,128)(2,1)S(1)} %all-to-all-done.2.mixed, bf16[8,128,256]{2,1,0:T(8,128)(2,1)S(1)} %collective-permute-done.22.traded, f32[2,1024]{1,0:T(2,128)S(1)} %partner.1, ...), custom_call_target="tpu_custom_call" | custom-call | flops 1073741824 | bytes 4194304 | tf_op jit(solution)/shard_map/second_view/pallas_call | solution.py:269
  144.5 1.0 copy-done.17
  145.9 27.7 %all_to_all.25.last = bf16[16,160,256]{2,1,0:T(8,128)(2,1)S(1)} all-to-all(bf16[16,160,256]{2,1,0:T(8,128)(2,1)S(1)} %get-tuple-element.72), channel_id=1, replica_groups=mesh['y1'=2,'y0'=2,'xh'=2,'xl'=2,'z1'=2,'z0'=2,'k'=2] {'y1','y0','xh','xl'}, dimensions={0} | all-to-all | bytes 2621440 | tf_op jit(solution)/shard_map/all_to_all | solution.py:445
  173.6 4.0 %first_view.1 = (f32[128,1024]{1,0:T(8,128)S(1)}, bf16[128,1024]{1,0:T(8,128)(2,1)S(1)}, f32[16,5,1024]{2,1,0:T(8,128)}, f32[32,256]{1,0:T(8,128)S(1)}) custom-call(s32[6]{0:T(128)S(1)} %pad_add_fusion.1.ids, bf16[16,160,256]{2,1,0:T(8,128)(2,1)S(1)} %all_to_all.25.last, bf16[256,1024]{1,0:T(8,128)(2,1)S(1)} %copy-done.5, ...), custom_call_target="tpu_custom_call" | custom-call | flops 1048576 | bytes 4096 | tf_op jit(solution)/shard_map/first_view/pallas_call | solution.py:313
  178.8 5.2 %collective-permute-start.24 = (bf16[128,1024]{1,0:T(8,128)(2,1)S(1)}, bf16[128,1024]{1,0:T(8,128)(2,1)}, u32[]{:S(2)}, u32[]{:S(2)}) collective-permute-start(bf16[128,1024]{1,0:T(8,128)(2,1)S(1)} %get-tuple-element.80), channel_id=1, source_target_pairs={{1,0},{96,1},{65,2},{32,3},{33,4},{64,5},{97,6},{0,7},{17,8},{112,... | collective-permute-start | bytes 786440 | tf_op jit(solution)/shard_map/ppermute | solution.py:447
  184.0 3.5 %all-to-all-start.4 = ((f32[16,5,1024]{2,1,0:T(8,128)}), f32[16,5,1024]{2,1,0:T(8,128)S(1)}, u32[]{:S(2)}, u32[]{:S(2)}) async-start(f32[16,5,1024]{2,1,0:T(8,128)} %get-tuple-element.77), calls=%async_computation.4 | async-start | bytes 1048576 | tf_op jit(solution)/shard_map/all_to_all | solution.py:454
  187.5 1.2 copy-done.18
  188.8 2.4 %finish_second.1 = f32[256,1024]{1,0:T(8,128)} custom-call(s32[3]{0:T(128)S(1)} %pad_add_fusion.ids, f32[32,256]{1,0:T(8,128)S(1)} %get-tuple-element.87.terms, f32[2,1024]{1,0:T(2,128)S(1)} %pad_maximum_fusion.4.scales, f32[256,1024]{1,0:T(8,128)S(1)} %copy-done.1, f32[256,1024]{1,0:T(8,128)S(1)} %copy-done.18, ...), custom_call_target="tpu_custom_call" | custom-call | flops 1048576 | bytes 65536 | tf_op jit(solution)/shard_map/finish_second/pallas_call | solution.py:325
  191.2 1.2 arrange.1
  192.4 8.0 %all-to-all-done.4.sums = f32[16,5,1024]{2,1,0:T(8,128)S(1)} async-done(((f32[16,5,1024]{2,1,0:T(8,128)}), f32[16,5,1024]{2,1,0:T(8,128)S(1)}, u32[]{:S(2)}, u32[]{:S(2)}) %all-to-all-start.4) | async-done | bytes 327712 | tf_op jit(solution)/shard_map/all_to_all | solution.py:454
  200.4 2.2 %finish_first.1 = (f32[128,2048]{1,0:T(8,128)}, f32[1,1]{1,0:T(1,128)}) custom-call(s32[3]{0:T(128)S(1)} %pad_add_fusion.ids, f32[16,5,1024]{2,1,0:T(8,128)S(1)} %all-to-all-done.4.sums, f32[2,2048]{1,0:T(2,128)S(1)} %pad_maximum_fusion.2.scales, f32[128,2048]{1,0:T(8,128)S(1)} %copy-done, f32[128,2048]{1,0:T(8,128)S(1)} %get-tuple-element.83.up, ...), custom_call_target="tpu_custom_call" | custom-call | flops 1048576 | bytes 65536 | tf_op jit(solution)/shard_map/finish_first/pallas_call | solution.py:378
  (106 shorter events, 13.8 us)
Async XLA Ops:
  0.6 1.5 copy-start.1
  2.1 20.3 %copy-start = (f32[128,2048]{1,0:T(8,128)S(1)}, f32[128,2048]{1,0:T(8,128)}, u32[]{:S(2)}) copy-start(f32[128,2048]{1,0:T(8,128)} %view.2) | copy-start | bytes 3145732
  2.3 12.7 %collective-permute-start.2 = (f32[2,1024]{1,0:T(2,128)S(1)}, f32[2,1024]{1,0:T(2,128)S(1)}, u32[]{:S(2)}, u32[]{:S(2)}) collective-permute-start(f32[2,1024]{1,0:T(2,128)S(1)} %pad_maximum_fusion.3), channel_id=1, source_target_pairs={{0,96},{32,0},{64,32},{96,64},{1,97},{33,1},{65,33},{97,65},{2,98}... | collective-permute-start | bytes 24584 | tf_op jit(solution)/shard_map/ppermute | solution.py:390
  2.4 12.7 %collective-permute-start.1 = (f32[2,1024]{1,0:T(2,128)S(1)}, f32[2,1024]{1,0:T(2,128)S(1)}, u32[]{:S(2)}, u32[]{:S(2)}) collective-permute-start(f32[2,1024]{1,0:T(2,128)S(1)} %pad_maximum_fusion.3), channel_id=1, source_target_pairs={{0,64},{32,96},{64,0},{96,32},{1,65},{33,97},{65,1},{97,33},{2,66}... | collective-permute-start | bytes 24584 | tf_op jit(solution)/shard_map/ppermute | solution.py:390
  4.9 10.2 %collective-permute-start = (f32[2,1024]{1,0:T(2,128)S(1)}, f32[2,1024]{1,0:T(2,128)S(1)}, u32[]{:S(2)}, u32[]{:S(2)}) collective-permute-start(f32[2,1024]{1,0:T(2,128)S(1)} %pad_maximum_fusion.3), channel_id=1, source_target_pairs={{0,32},{32,64},{64,96},{96,0},{1,33},{33,65},{65,97},{97,1},{2,34}... | collective-permute-start | bytes 24584 | tf_op jit(solution)/shard_map/ppermute | solution.py:390
  7.3 14.9 %all-to-all-start = ((f32[16,2,2048]{2,1,0:T(2,128)}), f32[16,2,2048]{2,1,0:T(2,128)S(1)}, u32[]{:S(2)}, u32[]{:S(2)}) async-start(f32[16,2,2048]{2,1,0:T(2,128)} %broadcast_in_dim.2), calls=%async_computation | async-start | bytes 524288 | tf_op jit(solution)/shard_map/all_to_all | solution.py:32
  15.1 6.5 %collective-permute-start.3 = (f32[2,1024]{1,0:T(2,128)S(1)}, f32[2,1024]{1,0:T(2,128)S(1)}, u32[]{:S(2)}, u32[]{:S(2)}) collective-permute-start(f32[2,1024]{1,0:T(2,128)S(1)} %add_add_fusion), channel_id=1, source_target_pairs={{0,16},{16,0},{1,17},{17,1},{2,18},{18,2},{3,19},{19,3},{4,20},{20... | collective-permute-start | bytes 24584 | tf_op jit(solution)/shard_map/ppermute | solution.py:391
  24.0 6.9 %collective-permute-start.4 = (bf16[128,1024]{1,0:T(8,128)(2,1)S(1)}, bf16[128,1024]{1,0:T(8,128)(2,1)S(1)}, u32[]{:S(2)}, u32[]{:S(2)}) collective-permute-start(bf16[128,1024]{1,0:T(8,128)(2,1)S(1)} %bitcast.31), channel_id=1, source_target_pairs={{0,8},{8,0},{1,9},{9,1},{2,10},{10,2},{3,11},{11,3},{4,12},{12,4},... | collective-permute-start | bytes 786440 | tf_op jit(solution)/shard_map/ppermute | solution.py:411
  25.1 76.2 %copy-start.2 = (bf16[256,1024]{1,0:T(8,128)(2,1)}, bf16[256,1024]{1,0:T(8,128)(2,1)S(1)}, u32[]{:S(2)}) copy-start(bf16[256,1024]{1,0:T(8,128)(2,1)S(1)} %multiply_convert_fusion.1.refs_0_.half) | copy-start | bytes 1572868
  25.1 12.8 %collective-permute-start.8 = (bf16[256,1024]{1,0:T(8,128)(2,1)S(1)}, bf16[256,1024]{1,0:T(8,128)(2,1)}, u32[]{:S(2)}, u32[]{:S(2)}) collective-permute-start(bf16[256,1024]{1,0:T(8,128)(2,1)S(1)} %multiply_convert_fusion.1.refs_0_.half), channel_id=1, source_target_pairs={{0,96},{32,0},{64,32},{96,64},{1,97},{33,1},{65,33},{97,65},{2,98}... | collective-permute-start | bytes 1572872 | tf_op jit(solution)/shard_map/ppermute | solution.py:95
  25.1 13.1 %collective-permute-start.7 = (bf16[256,1024]{1,0:T(8,128)(2,1)S(1)}, bf16[256,1024]{1,0:T(8,128)(2,1)}, u32[]{:S(2)}, u32[]{:S(2)}) collective-permute-start(bf16[256,1024]{1,0:T(8,128)(2,1)S(1)} %multiply_convert_fusion.1.refs_0_.half), channel_id=1, source_target_pairs={{0,32},{32,64},{64,96},{96,0},{1,33},{33,65},{65,97},{97,1},{2,34}... | collective-permute-start | bytes 1572872 | tf_op jit(solution)/shard_map/ppermute | solution.py:95
  31.1 46.0 %copy-start.4 = (bf16[256,1024]{1,0:T(8,128)(2,1)}, bf16[256,1024]{1,0:T(8,128)(2,1)S(1)}, u32[]{:S(2)}) copy-start(bf16[256,1024]{1,0:T(8,128)(2,1)S(1)} %pad_maximum_fusion.refs_0_) | copy-start | bytes 1572868
  31.1 13.2 %collective-permute-start.9 = (bf16[256,1024]{1,0:T(8,128)(2,1)S(1)}, bf16[256,1024]{1,0:T(8,128)(2,1)}, u32[]{:S(2)}, u32[]{:S(2)}) collective-permute-start(bf16[256,1024]{1,0:T(8,128)(2,1)S(1)} %multiply_convert_fusion.1.refs_0_.half), channel_id=1, source_target_pairs={{0,16},{16,0},{1,17},{17,1},{2,18},{18,2},{3,19},{19,3},{4,20},{20... | collective-permute-start | bytes 1572872 | tf_op jit(solution)/shard_map/ppermute | solution.py:99
  33.6 12.7 %collective-permute-start.6 = (bf16[256,1024]{1,0:T(8,128)(2,1)S(1)}, bf16[256,1024]{1,0:T(8,128)(2,1)}, u32[]{:S(2)}, u32[]{:S(2)}) collective-permute-start(bf16[256,1024]{1,0:T(8,128)(2,1)S(1)} %pad_maximum_fusion.refs_0_), channel_id=1, source_target_pairs={{0,6},{2,0},{4,2},{6,4},{1,7},{3,1},{5,3},{7,5},{8,14},{10,8},{12,... | collective-permute-start | bytes 1572872 | tf_op jit(solution)/shard_map/ppermute | solution.py:95
  36.2 13.3 %collective-permute-start.5 = (bf16[256,1024]{1,0:T(8,128)(2,1)S(1)}, bf16[256,1024]{1,0:T(8,128)(2,1)}, u32[]{:S(2)}, u32[]{:S(2)}) collective-permute-start(bf16[256,1024]{1,0:T(8,128)(2,1)S(1)} %pad_maximum_fusion.refs_0_), channel_id=1, source_target_pairs={{0,2},{2,4},{4,6},{6,0},{1,3},{3,5},{5,7},{7,1},{8,10},{10,12},{12... | collective-permute-start | bytes 1572872 | tf_op jit(solution)/shard_map/ppermute | solution.py:95
  50.7 8.5 %collective-permute-start.10 = (bf16[256,1024]{1,0:T(8,128)(2,1)S(1)}, bf16[256,1024]{1,0:T(8,128)(2,1)S(1)}, u32[]{:S(2)}, u32[]{:S(2)}) collective-permute-start(bf16[256,1024]{1,0:T(8,128)(2,1)S(1)} %broadcast_select_fusion), channel_id=1, source_target_pairs={{0,2},{1,7},{2,4},{3,1},{4,6},{5,3},{6,0},{7,5},{8,10},{9,15},{10,... | collective-permute-start | bytes 1572872 | tf_op jit(solution)/shard_map/ppermute | solution.py:419
  51.0 13.8 %collective-permute-start.16 = (bf16[256,1024]{1,0:T(8,128)(2,1)}, bf16[256,1024]{1,0:T(8,128)(2,1)}, u32[]{:S(2)}, u32[]{:S(2)}) collective-permute-start(bf16[256,1024]{1,0:T(8,128)(2,1)} %collective-permute-done.9.refs_4_), channel_id=1, source_target_pairs={{0,96},{32,0},{64,32},{96,64},{1,97},{33,1},{65,33},{97,65},{2,98}... | collective-permute-start | bytes 1572872 | tf_op jit(solution)/shard_map/ppermute | solution.py:95
  51.0 14.7 %collective-permute-start.15 = (bf16[256,1024]{1,0:T(8,128)(2,1)}, bf16[256,1024]{1,0:T(8,128)(2,1)S(1)}, u32[]{:S(2)}, u32[]{:S(2)}) collective-permute-start(bf16[256,1024]{1,0:T(8,128)(2,1)} %collective-permute-done.9.refs_4_), channel_id=1, source_target_pairs={{0,32},{32,64},{64,96},{96,0},{1,33},{33,65},{65,97},{97,1},{2,34}... | collective-permute-start | bytes 1572872 | tf_op jit(solution)/shard_map/ppermute | solution.py:95
  59.2 7.3 %collective-permute-start.14 = (bf16[256,1024]{1,0:T(8,128)(2,1)S(1)}, bf16[256,1024]{1,0:T(8,128)(2,1)S(1)}, u32[]{:S(2)}, u32[]{:S(2)}) collective-permute-start(bf16[256,1024]{1,0:T(8,128)(2,1)S(1)} %collective-permute-done.10.refs_3_), channel_id=1, source_target_pairs={{0,1},{1,0},{2,3},{3,2},{4,5},{5,4},{6,7},{7,6},{8,9},{9,8},{10,11... | collective-permute-start | bytes 1572872 | tf_op jit(solution)/shard_map/ppermute | solution.py:99
  64.3 5.3 %collective-permute-start.11 = (bf16[256,1024]{1,0:T(8,128)(2,1)S(1)}, bf16[256,1024]{1,0:T(8,128)(2,1)}, u32[]{:S(2)}, u32[]{:S(2)}) collective-permute-start(bf16[256,1024]{1,0:T(8,128)(2,1)S(1)} %pad_maximum_fusion.refs_0_), channel_id=1, source_target_pairs={{0,1},{1,0},{2,3},{3,2},{4,5},{5,4},{6,7},{7,6},{8,9},{9,8},{10,11... | collective-permute-start | bytes 1572872 | tf_op jit(solution)/shard_map/ppermute | solution.py:99
  64.3 5.3 %collective-permute-start.12 = (bf16[256,1024]{1,0:T(8,128)(2,1)}, bf16[256,1024]{1,0:T(8,128)(2,1)}, u32[]{:S(2)}, u32[]{:S(2)}) collective-permute-start(bf16[256,1024]{1,0:T(8,128)(2,1)} %collective-permute-done.5.refs_1_), channel_id=1, source_target_pairs={{0,1},{1,0},{2,3},{3,2},{4,5},{5,4},{6,7},{7,6},{8,9},{9,8},{10,11... | collective-permute-start | bytes 1572872 | tf_op jit(solution)/shard_map/ppermute | solution.py:99
  64.8 4.8 %collective-permute-start.13 = (bf16[256,1024]{1,0:T(8,128)(2,1)}, bf16[256,1024]{1,0:T(8,128)(2,1)}, u32[]{:S(2)}, u32[]{:S(2)}) collective-permute-start(bf16[256,1024]{1,0:T(8,128)(2,1)} %collective-permute-done.6.refs_2_), channel_id=1, source_target_pairs={{0,1},{1,0},{2,3},{3,2},{4,5},{5,4},{6,7},{7,6},{8,9},{9,8},{10,11... | collective-permute-start | bytes 1572872 | tf_op jit(solution)/shard_map/ppermute | solution.py:99
  66.5 12.5 %collective-permute-start.17 = (bf16[256,1024]{1,0:T(8,128)(2,1)}, bf16[256,1024]{1,0:T(8,128)(2,1)}, u32[]{:S(2)}, u32[]{:S(2)}) collective-permute-start(bf16[256,1024]{1,0:T(8,128)(2,1)} %collective-permute-done.7.refs_1_), channel_id=1, source_target_pairs={{0,32},{32,64},{64,96},{96,0},{1,33},{33,65},{65,97},{97,1},{2,34}... | collective-permute-start | bytes 1572872 | tf_op jit(solution)/shard_map/ppermute | solution.py:422
  67.3 14.1 %collective-permute-start.18 = (bf16[256,1024]{1,0:T(8,128)(2,1)}, bf16[256,1024]{1,0:T(8,128)(2,1)}, u32[]{:S(2)}, u32[]{:S(2)}) collective-permute-start(bf16[256,1024]{1,0:T(8,128)(2,1)} %collective-permute-done.16.refs_6_), channel_id=1, source_target_pairs={{0,96},{32,0},{64,32},{96,64},{1,97},{33,1},{65,33},{97,65},{2,98}... | collective-permute-start | bytes 1572872 | tf_op jit(solution)/shard_map/ppermute | solution.py:424
  69.6 1.0 copy-start.11
  70.6 1.0 copy-start.14
  79.0 14.8 %copy-start.8 = (bf16[256,1024]{1,0:T(8,128)(2,1)S(1)}, bf16[256,1024]{1,0:T(8,128)(2,1)}, u32[]{:S(2)}) copy-start(bf16[256,1024]{1,0:T(8,128)(2,1)} %copy-done.7) | copy-start | bytes 1572868
  81.5 19.8 %collective-permute-start.20 = (bf16[256,1024]{1,0:T(8,128)(2,1)}, bf16[256,1024]{1,0:T(8,128)(2,1)}, u32[]{:S(2)}, u32[]{:S(2)}) collective-permute-start(bf16[256,1024]{1,0:T(8,128)(2,1)} %bitcast.19), channel_id=1, source_target_pairs={{0,0},{13,1},{18,2},{31,3},{39,4},{42,5},{53,6},{56,7},{66,8},{79,... | collective-permute-start | bytes 1572872 | tf_op jit(solution)/shard_map/ppermute | solution.py:430
  89.3 23.0 %all-to-all-start.1 = ((bf16[16,256,128]{2,1,0:T(8,128)(2,1)}), bf16[16,256,128]{2,1,0:T(8,128)(2,1)}, u32[]{:S(2)}, u32[]{:S(2)}) async-start(bf16[16,256,128]{2,1,0:T(8,128)(2,1)} %bitcast.30), calls=%async_computation.1 | async-start | bytes 2097152 | tf_op jit(solution)/shard_map/all_to_all | solution.py:431
  100.6 11.7 %copy-start.20 = (bf16[8,128,256]{2,1,0:T(8,128)(2,1)S(1)}, bf16[8,128,256]{2,1,0:T(8,128)(2,1)}, u32[]{:S(2)}) copy-start(bf16[8,128,256]{2,1,0:T(8,128)(2,1)} %copy-done.19) | copy-start | bytes 1572868
  100.6 11.7 %collective-permute-start.19 = (bf16[8,128,256]{2,1,0:T(8,128)(2,1)}, bf16[8,128,256]{2,1,0:T(8,128)(2,1)}, u32[]{:S(2)}, u32[]{:S(2)}) collective-permute-start(bf16[8,128,256]{2,1,0:T(8,128)(2,1)} %get-tuple-element.62), channel_id=1, source_target_pairs={{0,1},{1,0},{2,3},{3,2},{4,5},{5,4},{6,7},{7,6},{8,9},{9,8},{10,11... | collective-permute-start | bytes 1572872 | tf_op jit(solution)/shard_map/ppermute | solution.py:433
  114.9 23.3 %all-to-all-start.2 = ((bf16[8,256,256]{2,1,0:T(8,128)(2,1)}), bf16[8,256,256]{2,1,0:T(8,128)(2,1)S(1)}, u32[]{:S(2)}, u32[]{:S(2)}) async-start(bf16[8,256,256]{2,1,0:T(8,128)(2,1)} %copy-done.6), calls=%async_computation.2 | async-start | bytes 2097152 | tf_op jit(solution)/shard_map/all_to_all | solution.py:438
  118.4 19.1 %collective-permute-start.21 = (bf16[64,1024]{1,0:T(8,128)(2,1)}, bf16[64,1024]{1,0:T(8,128)(2,1)S(1)}, u32[]{:S(2)}, u32[]{:S(2)}) collective-permute-start(bf16[64,1024]{1,0:T(8,128)(2,1)} %copy-done.28), channel_id=1, source_target_pairs={{0,0},{97,1},{64,2},{33,3},{32,4},{65,5},{96,6},{1,7},{16,8},{113,... | collective-permute-start | bytes 393224 | tf_op jit(solution)/shard_map/ppermute | solution.py:437
  138.2 3.0 %copy-start.3 = (bf16[256,1024]{1,0:T(8,128)(2,1)S(1)}, bf16[256,1024]{1,0:T(8,128)(2,1)}, u32[]{:S(2)}) copy-start(bf16[256,1024]{1,0:T(8,128)(2,1)} %copy-done.2) | copy-start | bytes 1572868
  138.2 3.0 %copy-start.9 = (bf16[256,1024]{1,0:T(8,128)(2,1)S(1)}, bf16[256,1024]{1,0:T(8,128)(2,1)}, u32[]{:S(2)}) copy-start(bf16[256,1024]{1,0:T(8,128)(2,1)} %copy-done.7) | copy-start | bytes 1572868
  138.2 2.9 %collective-permute-start.22 = (bf16[8,128,256]{2,1,0:T(8,128)(2,1)S(1)}, bf16[8,128,256]{2,1,0:T(8,128)(2,1)S(1)}, u32[]{:S(2)}, u32[]{:S(2)}) collective-permute-start(bf16[8,128,256]{2,1,0:T(8,128)(2,1)S(1)} %slice.19), channel_id=1, source_target_pairs={{0,1},{1,0},{2,3},{3,2},{4,5},{5,4},{6,7},{7,6},{8,9},{9,8},{10,11... | collective-permute-start | bytes 1572872 | tf_op jit(solution)/shard_map/ppermute | solution.py:442
  138.3 7.6 %collective-permute-start.23 = (bf16[64,1024]{1,0:T(8,128)(2,1)}, bf16[64,1024]{1,0:T(8,128)(2,1)S(1)}, u32[]{:S(2)}, u32[]{:S(2)}) collective-permute-start(bf16[64,1024]{1,0:T(8,128)(2,1)} %copy-done.27), channel_id=1, source_target_pairs={{0,0},{97,1},{64,2},{33,3},{32,4},{65,5},{96,6},{1,7},{16,8},{113,... | collective-permute-start | bytes 393224 | tf_op jit(solution)/shard_map/ppermute | solution.py:441
  145.9 27.7 %copy-start.25 = (bf16[64,1024]{1,0:T(8,128)(2,1)}, bf16[64,1024]{1,0:T(8,128)(2,1)S(1)}, u32[]{:S(2)}) copy-start(bf16[64,1024]{1,0:T(8,128)(2,1)S(1)} %collective-permute-done.23.mid) | copy-start | bytes 393220
  145.9 27.7 %copy-start.5 = (bf16[256,1024]{1,0:T(8,128)(2,1)S(1)}, bf16[256,1024]{1,0:T(8,128)(2,1)}, u32[]{:S(2)}) copy-start(bf16[256,1024]{1,0:T(8,128)(2,1)} %copy-done.4) | copy-start | bytes 1572868
  145.9 27.7 %copy-start.12 = (bf16[256,1024]{1,0:T(8,128)(2,1)S(1)}, bf16[256,1024]{1,0:T(8,128)(2,1)}, u32[]{:S(2)}) copy-start(bf16[256,1024]{1,0:T(8,128)(2,1)} %copy-done.10) | copy-start | bytes 1572868
  145.9 27.7 %copy-start.15 = (bf16[256,1024]{1,0:T(8,128)(2,1)S(1)}, bf16[256,1024]{1,0:T(8,128)(2,1)}, u32[]{:S(2)}) copy-start(bf16[256,1024]{1,0:T(8,128)(2,1)} %copy-done.13) | copy-start | bytes 1572868
  178.4 12.8 %collective-permute-start.25 = (bf16[128,1024]{1,0:T(8,128)(2,1)S(1)}, bf16[128,1024]{1,0:T(8,128)(2,1)}, u32[]{:S(2)}, u32[]{:S(2)}) collective-permute-start(bf16[128,1024]{1,0:T(8,128)(2,1)S(1)} %get-tuple-element.82), channel_id=1, source_target_pairs={{0,8},{8,0},{1,9},{9,1},{2,10},{10,2},{3,11},{11,3},{4,12},{12,4},... | collective-permute-start | bytes 786440 | tf_op jit(solution)/shard_map/ppermute | solution.py:450
  178.8 12.4 %collective-permute-start.24 = (bf16[128,1024]{1,0:T(8,128)(2,1)S(1)}, bf16[128,1024]{1,0:T(8,128)(2,1)}, u32[]{:S(2)}, u32[]{:S(2)}) collective-permute-start(bf16[128,1024]{1,0:T(8,128)(2,1)S(1)} %get-tuple-element.80), channel_id=1, source_target_pairs={{1,0},{96,1},{65,2},{32,3},{33,4},{64,5},{97,6},{0,7},{17,8},{112,... | collective-permute-start | bytes 786440 | tf_op jit(solution)/shard_map/ppermute | solution.py:447
  184.0 16.4 %all-to-all-start.4 = ((f32[16,5,1024]{2,1,0:T(8,128)}), f32[16,5,1024]{2,1,0:T(8,128)S(1)}, u32[]{:S(2)}, u32[]{:S(2)}) async-start(f32[16,5,1024]{2,1,0:T(8,128)} %get-tuple-element.77), calls=%async_computation.4 | async-start | bytes 1048576 | tf_op jit(solution)/shard_map/all_to_all | solution.py:454
  187.5 1.2 copy-start.18
  188.8 2.4 %copy-start.22 = (f32[128,1024]{1,0:T(8,128)S(1)}, f32[128,1024]{1,0:T(8,128)}, u32[]{:S(2)}) copy-start(f32[128,1024]{1,0:T(8,128)} %copy-done.21) | copy-start | bytes 1572868
  188.8 2.4 %copy-start.24 = (bf16[64,1024]{1,0:T(8,128)(2,1)S(1)}, bf16[64,1024]{1,0:T(8,128)(2,1)}, u32[]{:S(2)}) copy-start(bf16[64,1024]{1,0:T(8,128)(2,1)} %copy-done.23) | copy-start | bytes 393220
  188.8 2.4 %copy-start.26 = (bf16[64,1024]{1,0:T(8,128)(2,1)S(1)}, bf16[64,1024]{1,0:T(8,128)(2,1)}, u32[]{:S(2)}) copy-start(bf16[64,1024]{1,0:T(8,128)(2,1)} %copy-done.25) | copy-start | bytes 393220
  (11 other events, 9.0 us)

commit v4 on v3

--- a/solution.py
+++ b/solution.py
@@ -155,11 +155,7 @@
 
                         @pl.when(wanted)
                         def _():
-                            if step == 0:
-                                sends[0][...] = held[flip, at : at + 64, :]
-                                sends[1][...] = held[flip, at + 64 : at + 128, :]
-                            else:
-                                sends[2][...] = held[flip, at : at + 128, :]
+                            sends[step][...] = held[flip, at : at + 128, :]
 
 
 def call(kernel, out_shape, extra, name, space=pltpu.VMEM, scratch=(), flops=2 * 256 * 2048 * 1024):
@@ -180,7 +176,7 @@
     if first:
         shapes = [(8, 2, 256, 128), (2, 128, 1024)]
     else:
-        shapes = [(8, 128, 256), (8, 128, 256), (64, 1024), (64, 1024), (128, 1024)]
+        shapes = [(8, 128, 256), (8, 128, 256), (128, 1024), (128, 1024)]
     out = [jax.ShapeDtypeStruct(shape, bf16) for shape in shapes]
     scratch = [pltpu.VMEM((2, 1024, 1024), bf16), pltpu.SemaphoreType.DMA((8,))]
     flops = 2 * 256 * 2048 * 1024 if first else 1 << 20
@@ -339,12 +335,80 @@
     out[1:2, :] = image_sum(other * half[...].astype(f32))
 
 
-def arrange_kernel(ids, early, mid, late, keep, traded, block, up):
+def arrange_kernel(which, ids, same, other, out):
+    for half in range(2):
+        picked = jnp.where(ids[which] == half, same[...].astype(out.dtype), other[...].astype(out.dtype))
+        out[:, 1024 * half : 1024 * (half + 1)] = picked
+
+
+def finish_second_kernel(ids, terms, scales, view, up, partner, grad):
+    for part in range(4):
+        columns = slice(256 * part, 256 * (part + 1))
+        rows = [terms[8 * part + i : 8 * part + i + 1] for i in range(8)]
+        diag, first, second = finish(rows[0], rows[4] + rows[5], rows[1], rows[6] + rows[7], BATCH)
+        mean, inv = scales[0:1, columns], scales[1:2, columns]
+        norm = (view[:, columns] - mean) * inv
+        grad[:, columns] = inv * (up[:, columns] + diag * partner[:, columns].astype(f32) - first - norm * second)
+
+
+def finish_kernel(ids, sums, scales, view, up, block, grad, loss):
+    row = ids[2]
+    loss[0, 0] = jnp.sum(sums[:, 2, :]) / FEAT
     for half in range(2):
         columns = slice(1024 * half, 1024 * (half + 1))
-        block[0:64, columns] = jnp.where(ids[1] == half, early[...], late[0:64])
-        block[64:128, columns] = jnp.where(ids[1] == half, mid[...], late[64:128])
-        up[:, columns] = jnp.where(ids[0] == half, keep[...], traded[...].astype(f32))
+        total = sums[8 * half]
+        for i in range(1, 8):
+            total = total + sums[8 * half + i]
+        partner = sums[2 * row + half]
+        diag, first, second = finish(total[0:1], total[1:2], partner[3:4], partner[4:5], BATCH)
+        mean, inv = scales[0:1, columns], scales[1:2, columns]
+        norm = (view[:, columns] - mean) * inv
+        grad[:, columns] = inv * (up[:, columns] + diag * block[:, columns].astype(f32) - first - norm * second)
+
+
+def finish_first(ids, *args):
+    vmem = pl.BlockSpec(memory_space=pltpu.VMEM)
+    smem = pl.BlockSpec(memory_space=pltpu.SMEM)
+    return pl.pallas_call(
+        finish_kernel,
+        out_shape=[jax.ShapeDtypeStruct((128, 2048), f32), jax.ShapeDtypeStruct((1, 1), f32)],
+        in_specs=[smem] + [vmem] * len(args),
+        out_specs=[vmem, smem],
+        compiler_params=pltpu.CompilerParams(vmem_limit_bytes=14 * 1024 * 1024),
+        cost_estimate=pl.CostEstimate(flops=1 << 20, bytes_accessed=1 << 16, transcendentals=0),
+        name="finish_first",
+    )(ids, *args)
+
+
+def row_sum(x):
+    x = x + lax.ppermute(x, "xh", SWAP)
+    return x + sum(lax.ppermute(x, ("y1", "y0"), [(i, (i + step) % 4) for i in range(4)]) for step in (1, 2, 3))
+
+
+def vmem_call(kernel, out_shape, args, name, flops):
+    vmem = pl.BlockSpec(memory_space=pltpu.VMEM)
+    smem = pl.BlockSpec(memory_space=pltpu.SMEM)
+    return pl.pallas_call(
+        kernel,
+        out_shape=out_shape,
+        in_specs=[smem] + [vmem] * (len(args) - 1),
+        out_specs=jax.tree.map(lambda _: vmem, out_shape),
+        compiler_params=pltpu.CompilerParams(vmem_limit_bytes=14 * 1024 * 1024),
+        cost_estimate=pl.CostEstimate(flops=flops, bytes_accessed=1 << 16, transcendentals=0),
+        name=name,
+    )(*args)
+
+
+def partner_kernel(ids, other, half, out):
+    other = other[...].astype(f32)
+    out[0:1, :] = image_sum(other)
+    out[1:2, :] = image_sum(other * half[...].astype(f32))
+
+
+def arrange_kernel(which, ids, same, other, out):
+    for half in range(2):
+        picked = jnp.where(ids[which] == half, same[...].astype(out.dtype), other[...].astype(out.dtype))
+        out[:, 1024 * half : 1024 * (half + 1)] = picked
 
 
 def finish_second_kernel(ids, terms, scales, view, up, partner, grad):
@@ -433,23 +497,23 @@
     mixed = blend(mine_b, lax.ppermute(give_b, "k", SWAP), piece_a)
     ids = jnp.stack([xl, core, lax.axis_index(ROW)])
     partner = vmem_call(partner_kernel, jax.ShapeDtypeStruct((2, 1024), f32), (ids, other_a, half_b), "partner", 1 << 34)
-    mixed, partner = tie(mixed, partner)
     early = lax.ppermute(send_b[0], ROW + COL, pairs_b[0])
+    mixed, partner, early = tie(mixed, partner, early)
     mixed = lax.all_to_all(mixed, ("xl", "z1", "z0"), 0, 0)
 
-    mixed, early, mid = tie(mixed, early, send_b[1])
-    mid = lax.ppermute(mid, ROW + COL, pairs_b[0])
     traded = lax.ppermute(mixed[:, 128:], "k", SWAP)
     up_b, last = second_view(ids_b, mixed, traded, partner, blocks_b)
-    last, mid = tie(last, mid)
     last = lax.all_to_all(last, ("y1", "y0", "xh", "xl"), 0, 0)
-    last, late = tie(last, send_b[2])
+    last, late = tie(last, send_b[1])
     late = lax.ppermute(late, ROW + COL, pairs_b[1])
 
     keep, give, sums_a, sums_b = first_view(ids_a, last, blocks_a)
     traded = lax.ppermute(give, "xl", SWAP)
-    out = [jax.ShapeDtypeStruct((128, 2048), bf16), jax.ShapeDtypeStruct((128, 2048), f32)]
-    block, up_own = vmem_call(arrange_kernel, out, (ids, early, mid, late, keep, traded), "arrange", 1 << 34)
+    block = jax.ShapeDtypeStruct((128, 2048), bf16)
+    block = vmem_call(functools.partial(arrange_kernel, 1), block, (ids, early, late), "arrange_block", 1 << 34)
+    keep, block = tie(keep, block)
+    up_own = jax.ShapeDtypeStruct((128, 2048), f32)
+    up_own = vmem_call(functools.partial(arrange_kernel, 0), up_own, (ids, keep, traded), "arrange_up", 1 << 33)
     sums_a, sums_b = tie(sums_a, sums_b)
     sums_a = lax.all_to_all(sums_a, COL, 0, 0)
 

time: 205 us -> 204 us (level)
  blocking collectives: 27.7 us -> 47.3 us
  waiting for transfers between devices: 65.9 us -> 49.4 us
  starting transfers between devices: 62 us -> 54.1 us
  local copies, waits for them, and re-layouts: 15.2 us -> 17.5 us
    all_to_all x0 -> x1, blocking collectives: none -> 23.7 us  [local(): mixed = lax.all_to_all(mixed, ('xl', 'z1', 'z0'), 0, 0)]
    ppermute x1, waiting for transfers between devices: 15.3 us -> 1.98 us  [local(): early = lax.ppermute(send_b[0], ROW + COL, pairs_b[0])]
    all_to_all x1, waiting for transfers between devices: 8.03 us -> 0.01 us  [local(): sums_a = lax.all_to_all(sums_a, COL, 0, 0)]
    ppermute x1, waiting for transfers between devices: 0.01 us -> 6.75 us  [local(): traded = lax.ppermute(give, 'xl', SWAP)]
    all_to_all x1, blocking collectives: 27.7 us -> 23.6 us  [local(): last = lax.all_to_all(last, ('y1', 'y0', 'xh', 'xl'), 0, 0)]
    all_to_all x1 -> x0, starting transfers between devices: 3.56 us -> none  [local(): mixed = lax.all_to_all(mixed, ('xl', 'z1', 'z0'), 0, 0)]
    all_to_all x1, waiting for transfers between devices: 9.84 us -> 6.39 us  [local(): lax.all_to_all(part_a.reshape(16, 256, 128), ('y1', 'y0', 'xh', 'xl'), 0, 0)]
    ppermute x1 -> x0, starting transfers between devices: 2.81 us -> none  [local(): mid = lax.ppermute(mid, ROW + COL, pairs_b[0])]
  transfers between devices with their start and end apart: 30 -> 28, of which waited for: 15 -> 15; matrix products, arithmetic and copies ran while one was open for 1% -> 1% of each run, Pallas kernels for 10% -> 11%
where the time goes in v4:
time: 204 us; the launch traced here: 200 us
  starting transfers between devices  54.1 us (27%)
  waiting for transfers between devices  49.4 us (24%)
  blocking collectives  47.3 us (23%)
  Pallas kernels  27.1 us (13%)
  local copies, waits for them, and re-layouts  17.5 us (9%)
  other arithmetic  3.5 us (2%)
    all_to_all x1, blocking collectives, local(): mixed = lax.all_to_all(mixed, ('xl', 'z1', 'z0'), 0, 0)  23.7 us
    all_to_all x1, blocking collectives, local(): last = lax.all_to_all(last, ('y1', 'y0', 'xh', 'xl'), 0, 0)  23.6 us
    unnamed x45, local copies, waits for them, and re-layouts  13.8 us
    pallas_call x2, Pallas kernels, gram_part(): call(functools.partial(gram_kernel, first), out, 0, 'gram_part', pl.ANY,...  11.6 us
    ppermute x5, starting transfers between devices, trade(): return [lax.ppermute(x, axis, SWAP) for x in blocks]  8.23 us
    all_to_all x1, starting transfers between devices, spread(): return lax.all_to_all(jnp.broadcast_to(x[None], (n,) + x.shape), axes, 0, 0)  7.77 us
    ppermute x6, waiting for transfers between devices, ring_near(): return [lax.ppermute(own, ring, AHEAD), lax.ppermute(own, ring, BACK)]  7.21 us
    ppermute x1, starting transfers between devices, local(): other_a = lax.ppermute(send_a.reshape(256, 1024), ROW + COL, pairs_a)  6.99 us
  transfers between devices with their start and end apart: 28, of which 15 were waited for; matrix products, arithmetic and copies ran while one was open for 1% of the time, Pallas kernels for 11%

profile of v4, /device:TPU:9, one launch (start us, length us, event | category | flops | bytes accessed | tf_op | source)
XLA Modules:
  0.0 200.1 jit_solution(12833905034498953373)
XLA Ops:
  0.6 1.4 fusion.5
  2.4 2.5 %collective-permute-start.1 = (f32[2,1024]{1,0:T(2,128)S(1)}, f32[2,1024]{1,0:T(2,128)S(1)}, u32[]{:S(2)}, u32[]{:S(2)}) collective-permute-start(f32[2,1024]{1,0:T(2,128)S(1)} %pad_maximum_fusion.3), channel_id=1, source_target_pairs={{0,64},{32,96},{64,0},{96,32},{1,65},{33,97},{65,1},{97,33},{2,66}... | collective-permute-start | bytes 24584 | tf_op jit(solution)/shard_map/ppermute | solution.py:454
  4.9 1.6 collective-permute-start
  7.3 7.8 %all-to-all-start = ((f32[16,2,2048]{2,1,0:T(2,128)}), f32[16,2,2048]{2,1,0:T(2,128)S(1)}, u32[]{:S(2)}, u32[]{:S(2)}) async-start(f32[16,2,2048]{2,1,0:T(2,128)} %broadcast_in_dim.2), calls=%async_computation | async-start | bytes 524288 | tf_op jit(solution)/shard_map/all_to_all | solution.py:32
  15.1 2.6 %collective-permute-start.3 = (f32[2,1024]{1,0:T(2,128)S(1)}, f32[2,1024]{1,0:T(2,128)S(1)}, u32[]{:S(2)}, u32[]{:S(2)}) collective-permute-start(f32[2,1024]{1,0:T(2,128)S(1)} %add_add_fusion), channel_id=1, source_target_pairs={{0,16},{16,0},{1,17},{17,1},{2,18},{18,2},{3,19},{19,3},{4,20},{20... | collective-permute-start | bytes 24584 | tf_op jit(solution)/shard_map/ppermute | solution.py:455
  17.7 3.9 %collective-permute-done.3 = f32[2,1024]{1,0:T(2,128)S(1)} collective-permute-done((f32[2,1024]{1,0:T(2,128)S(1)}, f32[2,1024]{1,0:T(2,128)S(1)}, u32[]{:S(2)}, u32[]{:S(2)}) %collective-permute-start.3) | collective-permute-done | bytes 8224 | tf_op jit(solution)/shard_map/ppermute | solution.py:455
  22.9 1.1 constant_dynamic-slice_fusion.1
  25.1 1.5 collective-permute-start.7
  26.6 4.4 %collective-permute-done.4 = bf16[128,1024]{1,0:T(8,128)(2,1)S(1)} collective-permute-done((bf16[128,1024]{1,0:T(8,128)(2,1)S(1)}, bf16[128,1024]{1,0:T(8,128)(2,1)S(1)}, u32[]{:S(2)}, u32[]{:S(2)}) %collective-permute-start.4) | collective-permute-done | bytes 262176 | tf_op jit(solution)/shard_map/ppermute | solution.py:475
  31.1 2.5 %collective-permute-start.9 = (bf16[256,1024]{1,0:T(8,128)(2,1)S(1)}, bf16[256,1024]{1,0:T(8,128)(2,1)}, u32[]{:S(2)}, u32[]{:S(2)}) collective-permute-start(bf16[256,1024]{1,0:T(8,128)(2,1)S(1)} %multiply_convert_fusion.1.refs_0_.half), channel_id=1, source_target_pairs={{0,16},{16,0},{1,17},{17,1},{2,18},{18,2},{3,19},{19,3},{4,20},{20... | collective-permute-start | bytes 1572872 | tf_op jit(solution)/shard_map/ppermute | solution.py:99
  33.6 2.6 %collective-permute-start.6 = (bf16[256,1024]{1,0:T(8,128)(2,1)S(1)}, bf16[256,1024]{1,0:T(8,128)(2,1)}, u32[]{:S(2)}, u32[]{:S(2)}) collective-permute-start(bf16[256,1024]{1,0:T(8,128)(2,1)S(1)} %pad_maximum_fusion.refs_0_), channel_id=1, source_target_pairs={{0,6},{2,0},{4,2},{6,4},{1,7},{3,1},{5,3},{7,5},{8,14},{10,8},{12,... | collective-permute-start | bytes 1572872 | tf_op jit(solution)/shard_map/ppermute | solution.py:95
  36.2 1.6 collective-permute-done.8.refs_2_
  38.2 6.1 %collective-permute-done.9.refs_4_ = bf16[256,1024]{1,0:T(8,128)(2,1)} collective-permute-done((bf16[256,1024]{1,0:T(8,128)(2,1)S(1)}, bf16[256,1024]{1,0:T(8,128)(2,1)}, u32[]{:S(2)}, u32[]{:S(2)}) %collective-permute-start.9) | collective-permute-done | bytes 524320 | tf_op jit(solution)/shard_map/ppermute | solution.py:99
  44.3 2.0 %collective-permute-done.6.refs_2_ = bf16[256,1024]{1,0:T(8,128)(2,1)} collective-permute-done((bf16[256,1024]{1,0:T(8,128)(2,1)S(1)}, bf16[256,1024]{1,0:T(8,128)(2,1)}, u32[]{:S(2)}, u32[]{:S(2)}) %collective-permute-start.6) | collective-permute-done | bytes 524320 | tf_op jit(solution)/shard_map/ppermute | solution.py:95
  46.3 3.2 %collective-permute-done.5.refs_1_ = bf16[256,1024]{1,0:T(8,128)(2,1)} collective-permute-done((bf16[256,1024]{1,0:T(8,128)(2,1)S(1)}, bf16[256,1024]{1,0:T(8,128)(2,1)}, u32[]{:S(2)}, u32[]{:S(2)}) %collective-permute-start.5) | collective-permute-done | bytes 524320 | tf_op jit(solution)/shard_map/ppermute | solution.py:95
  49.6 1.1 broadcast_select_fusion
  51.0 1.5 collective-permute-start.15
  52.5 6.7 %collective-permute-done.10.refs_3_ = bf16[256,1024]{1,0:T(8,128)(2,1)S(1)} collective-permute-done((bf16[256,1024]{1,0:T(8,128)(2,1)S(1)}, bf16[256,1024]{1,0:T(8,128)(2,1)S(1)}, u32[]{:S(2)}, u32[]{:S(2)}) %collective-permute-start.10) | collective-permute-done | bytes 524320 | tf_op jit(solution)/shard_map/ppermute | solution.py:483
  59.2 4.3 %collective-permute-start.14 = (bf16[256,1024]{1,0:T(8,128)(2,1)S(1)}, bf16[256,1024]{1,0:T(8,128)(2,1)S(1)}, u32[]{:S(2)}, u32[]{:S(2)}) collective-permute-start(bf16[256,1024]{1,0:T(8,128)(2,1)S(1)} %collective-permute-done.10.refs_3_), channel_id=1, source_target_pairs={{0,1},{1,0},{2,3},{3,2},{4,5},{5,4},{6,7},{7,6},{8,9},{9,8},{10,11... | collective-permute-start | bytes 1572872 | tf_op jit(solution)/shard_map/ppermute | solution.py:99
  67.3 1.5 collective-permute-start.18
  69.5 1.0 copy-done.6
  70.6 1.0 copy-done.9
  71.6 5.4 %gram_part.2 = (bf16[8,2,256,128]{3,2,1,0:T(8,128)(2,1)S(1)}, bf16[2,128,1024]{2,1,0:T(8,128)(2,1)}) custom-call(s32[6]{0:T(128)S(1)} %pad_add_fusion.1.ids, bf16[256,1024]{1,0:T(8,128)(2,1)S(1)} %pad_maximum_fusion.refs_0_, bf16[256,1024]{1,0:T(8,128)(2,1)} %collective-permute-done.5.refs_1_, bf16[256,1024]{1,0:T(8,128)(2,1)} %collective-permute-done.6.refs_2_, ...), custom_call_target="tpu_custom_call" | custom-call | flops 1073741824 | bytes 4194304 | tf_op jit(solution)/shard_map/gram_part/pallas_call | solution.py:183
  78.0 1.0 collective-permute-done.17.refs_3_
  79.0 2.4 %collective-permute-done.18.refs_7_ = bf16[256,1024]{1,0:T(8,128)(2,1)} collective-permute-done((bf16[256,1024]{1,0:T(8,128)(2,1)}, bf16[256,1024]{1,0:T(8,128)(2,1)}, u32[]{:S(2)}, u32[]{:S(2)}) %collective-permute-start.18) | collective-permute-done | bytes 524320 | tf_op jit(solution)/shard_map/ppermute | solution.py:488
  81.4 7.0 %collective-permute-start.20 = (bf16[256,1024]{1,0:T(8,128)(2,1)}, bf16[256,1024]{1,0:T(8,128)(2,1)}, u32[]{:S(2)}, u32[]{:S(2)}) collective-permute-start(bf16[256,1024]{1,0:T(8,128)(2,1)} %bitcast.19), channel_id=1, source_target_pairs={{0,0},{13,1},{18,2},{31,3},{39,4},{42,5},{53,6},{56,7},{66,8},{79,... | collective-permute-start | bytes 1572872 | tf_op jit(solution)/shard_map/ppermute | solution.py:494
  89.2 4.4 %all-to-all-start.1 = ((bf16[16,256,128]{2,1,0:T(8,128)(2,1)}), bf16[16,256,128]{2,1,0:T(8,128)(2,1)}, u32[]{:S(2)}, u32[]{:S(2)}) async-start(bf16[16,256,128]{2,1,0:T(8,128)(2,1)} %bitcast.30), calls=%async_computation.1 | async-start | bytes 2097152 | tf_op jit(solution)/shard_map/all_to_all | solution.py:495
  93.7 1.0 copy-done.3
  94.7 6.2 %gram_part.3 = (bf16[8,128,256]{2,1,0:T(8,128)(2,1)S(1)}, bf16[8,128,256]{2,1,0:T(8,128)(2,1)}, bf16[128,1024]{1,0:T(8,128)(2,1)}, bf16[128,1024]{1,0:T(8,128)(2,1)}) custom-call(s32[11]{0:T(128)S(1)} %pad_add_fusion.2.ids, bf16[256,1024]{1,0:T(8,128)(2,1)S(1)} %multiply_convert_fusion.1.refs_0_.half, bf16[256,1024]{1,0:T(8,128)(2,1)} %collective-permute-done.7.refs_1_, ...), custom_call_target="tpu_custom_call" | custom-call | flops 1048576 | bytes 4096 | tf_op jit(solution)/shard_map/gram_part/pallas_call | solution.py:183
  101.7 2.4 %collective-permute-start.21 = (bf16[128,1024]{1,0:T(8,128)(2,1)}, bf16[128,1024]{1,0:T(8,128)(2,1)S(1)}, u32[]{:S(2)}, u32[]{:S(2)}) collective-permute-start(bf16[128,1024]{1,0:T(8,128)(2,1)} %get-tuple-element.60), channel_id=1, source_target_pairs={{0,0},{97,1},{64,2},{33,3},{32,4},{65,5},{96,6},{1,7},{16,8},{113,... | collective-permute-start | bytes 786440 | tf_op jit(solution)/shard_map/ppermute | solution.py:500
  104.7 1.2 partner.1
  105.8 6.4 %all-to-all-done.1.received = bf16[16,256,128]{2,1,0:T(8,128)(2,1)} async-done(((bf16[16,256,128]{2,1,0:T(8,128)(2,1)}), bf16[16,256,128]{2,1,0:T(8,128)(2,1)}, u32[]{:S(2)}, u32[]{:S(2)}) %all-to-all-start.1) | async-done | bytes 1048608 | tf_op jit(solution)/shard_map/all_to_all | solution.py:495
  112.2 1.0 copy-done.16
  113.3 1.6 blend.1
  114.9 2.0 collective-permute-done.21.same
  116.9 23.7 %all_to_all.25.mixed = bf16[8,256,256]{2,1,0:T(8,128)(2,1)S(1)} all-to-all(bf16[8,256,256]{2,1,0:T(8,128)(2,1)S(1)} %blend.1), channel_id=1, replica_groups=mesh['y1'=2,'y0'=2,'xh'=2,'xl'=2,'z1'=2,'z0'=2,'k'=2] {'xl','z1','z0'}, dimensions={0} | all-to-all | bytes 2097152 | tf_op jit(solution)/shard_map/all_to_all | solution.py:502
  140.7 1.9 collective-permute-done.22.traded
  142.6 3.3 %second_view.1 = (f32[256,1024]{1,0:T(8,128)S(1)}, bf16[16,160,256]{2,1,0:T(8,128)(2,1)S(1)}) custom-call(s32[11]{0:T(128)S(1)} %pad_add_fusion.2.ids, bf16[8,256,256]{2,1,0:T(8,128)(2,1)S(1)} %all_to_all.25.mixed, bf16[8,128,256]{2,1,0:T(8,128)(2,1)S(1)} %collective-permute-done.22.traded, f32[2,1024]{1,0:T(2,128)S(1)} %partner.1, ...), custom_call_target="tpu_custom_call" | custom-call | flops 1073741824 | bytes 4194304 | tf_op jit(solution)/shard_map/second_view/pallas_call | solution.py:265
  146.0 23.6 %all_to_all.26.last = bf16[16,160,256]{2,1,0:T(8,128)(2,1)S(1)} all-to-all(bf16[16,160,256]{2,1,0:T(8,128)(2,1)S(1)} %get-tuple-element.63), channel_id=1, replica_groups=mesh['y1'=2,'y0'=2,'xh'=2,'xl'=2,'z1'=2,'z0'=2,'k'=2] {'y1','y0','xh','xl'}, dimensions={0} | all-to-all | bytes 2621440 | tf_op jit(solution)/shard_map/all_to_all | solution.py:506
  169.6 4.4 %collective-permute-start.23 = (bf16[128,1024]{1,0:T(8,128)(2,1)}, bf16[128,1024]{1,0:T(8,128)(2,1)}, u32[]{:S(2)}, u32[]{:S(2)}) collective-permute-start(bf16[128,1024]{1,0:T(8,128)(2,1)} %get-tuple-element.71), channel_id=1, source_target_pairs={{1,0},{96,1},{65,2},{32,3},{33,4},{64,5},{97,6},{0,7},{17,8},{112,... | collective-permute-start | bytes 786440 | tf_op jit(solution)/shard_map/ppermute | solution.py:508
  174.0 3.2 %first_view.1 = (f32[128,1024]{1,0:T(8,128)S(1)}, bf16[128,1024]{1,0:T(8,128)(2,1)S(1)}, f32[16,5,1024]{2,1,0:T(8,128)S(1)}, f32[32,256]{1,0:T(8,128)S(1)}) custom-call(s32[6]{0:T(128)S(1)} %pad_add_fusion.1.ids, bf16[16,160,256]{2,1,0:T(8,128)(2,1)S(1)} %all_to_all.26.last, bf16[256,1024]{1,0:T(8,128)(2,1)S(1)} %pad_maximum_fusion.refs_0_, ...), custom_call_target="tpu_custom_call" | custom-call | flops 1048576 | bytes 4096 | tf_op jit(solution)/shard_map/first_view/pallas_call | solution.py:309
  179.5 3.5 %all-to-all-start.4 = ((f32[16,5,1024]{2,1,0:T(8,128)}), f32[16,5,1024]{2,1,0:T(8,128)S(1)}, u32[]{:S(2)}, u32[]{:S(2)}) async-start(f32[16,5,1024]{2,1,0:T(8,128)} %copy-done.14), calls=%async_computation.4 | async-start | bytes 1048576 | tf_op jit(solution)/shard_map/all_to_all | solution.py:518
  183.8 1.2 copy-done.13
  185.0 2.3 %finish_second.1 = f32[256,1024]{1,0:T(8,128)} custom-call(s32[3]{0:T(128)S(1)} %pad_add_fusion.ids, f32[32,256]{1,0:T(8,128)S(1)} %get-tuple-element.77.terms, f32[2,1024]{1,0:T(2,128)S(1)} %pad_maximum_fusion.4.scales, f32[256,1024]{1,0:T(8,128)S(1)} %copy-done.1, f32[256,1024]{1,0:T(8,128)S(1)} %copy-done.13, ...), custom_call_target="tpu_custom_call" | custom-call | flops 1048576 | bytes 65536 | tf_op jit(solution)/shard_map/finish_second/pallas_call | solution.py:391
  187.4 1.1 arrange_block.1.block
  189.3 6.7 %collective-permute-done.24.other = bf16[128,1024]{1,0:T(8,128)(2,1)S(1)} collective-permute-done((bf16[128,1024]{1,0:T(8,128)(2,1)}, bf16[128,1024]{1,0:T(8,128)(2,1)S(1)}, u32[]{:S(2)}, u32[]{:S(2)}) %collective-permute-start.24) | collective-permute-done | bytes 262176 | tf_op jit(solution)/shard_map/ppermute | solution.py:511
  196.7 1.0 copy-done.18
  197.7 2.2 %finish_first.1 = (f32[128,2048]{1,0:T(8,128)}, f32[1,1]{1,0:T(1,128)}) custom-call(s32[3]{0:T(128)S(1)} %pad_add_fusion.ids, f32[16,5,1024]{2,1,0:T(8,128)S(1)} %all-to-all-done.4.sums, f32[2,2048]{1,0:T(2,128)S(1)} %pad_maximum_fusion.2.scales, f32[128,2048]{1,0:T(8,128)S(1)} %copy-done, f32[128,2048]{1,0:T(8,128)S(1)} %arrange_up.1.up, ...), custom_call_target="tpu_custom_call" | custom-call | flops 1048576 | bytes 65536 | tf_op jit(solution)/shard_map/finish_first/pallas_call | solution.py:442
  (90 shorter events, 16.8 us)
Async XLA Ops:
  0.6 1.5 copy-start.1
  2.1 20.3 %copy-start = (f32[128,2048]{1,0:T(8,128)S(1)}, f32[128,2048]{1,0:T(8,128)}, u32[]{:S(2)}) copy-start(f32[128,2048]{1,0:T(8,128)} %view.2) | copy-start | bytes 3145732
  2.3 12.7 %collective-permute-start.2 = (f32[2,1024]{1,0:T(2,128)S(1)}, f32[2,1024]{1,0:T(2,128)S(1)}, u32[]{:S(2)}, u32[]{:S(2)}) collective-permute-start(f32[2,1024]{1,0:T(2,128)S(1)} %pad_maximum_fusion.3), channel_id=1, source_target_pairs={{0,96},{32,0},{64,32},{96,64},{1,97},{33,1},{65,33},{97,65},{2,98}... | collective-permute-start | bytes 24584 | tf_op jit(solution)/shard_map/ppermute | solution.py:454
  2.4 12.7 %collective-permute-start.1 = (f32[2,1024]{1,0:T(2,128)S(1)}, f32[2,1024]{1,0:T(2,128)S(1)}, u32[]{:S(2)}, u32[]{:S(2)}) collective-permute-start(f32[2,1024]{1,0:T(2,128)S(1)} %pad_maximum_fusion.3), channel_id=1, source_target_pairs={{0,64},{32,96},{64,0},{96,32},{1,65},{33,97},{65,1},{97,33},{2,66}... | collective-permute-start | bytes 24584 | tf_op jit(solution)/shard_map/ppermute | solution.py:454
  4.9 10.2 %collective-permute-start = (f32[2,1024]{1,0:T(2,128)S(1)}, f32[2,1024]{1,0:T(2,128)S(1)}, u32[]{:S(2)}, u32[]{:S(2)}) collective-permute-start(f32[2,1024]{1,0:T(2,128)S(1)} %pad_maximum_fusion.3), channel_id=1, source_target_pairs={{0,32},{32,64},{64,96},{96,0},{1,33},{33,65},{65,97},{97,1},{2,34}... | collective-permute-start | bytes 24584 | tf_op jit(solution)/shard_map/ppermute | solution.py:454
  7.3 14.9 %all-to-all-start = ((f32[16,2,2048]{2,1,0:T(2,128)}), f32[16,2,2048]{2,1,0:T(2,128)S(1)}, u32[]{:S(2)}, u32[]{:S(2)}) async-start(f32[16,2,2048]{2,1,0:T(2,128)} %broadcast_in_dim.2), calls=%async_computation | async-start | bytes 524288 | tf_op jit(solution)/shard_map/all_to_all | solution.py:32
  15.1 6.5 %collective-permute-start.3 = (f32[2,1024]{1,0:T(2,128)S(1)}, f32[2,1024]{1,0:T(2,128)S(1)}, u32[]{:S(2)}, u32[]{:S(2)}) collective-permute-start(f32[2,1024]{1,0:T(2,128)S(1)} %add_add_fusion), channel_id=1, source_target_pairs={{0,16},{16,0},{1,17},{17,1},{2,18},{18,2},{3,19},{19,3},{4,20},{20... | collective-permute-start | bytes 24584 | tf_op jit(solution)/shard_map/ppermute | solution.py:455
  24.0 6.9 %collective-permute-start.4 = (bf16[128,1024]{1,0:T(8,128)(2,1)S(1)}, bf16[128,1024]{1,0:T(8,128)(2,1)S(1)}, u32[]{:S(2)}, u32[]{:S(2)}) collective-permute-start(bf16[128,1024]{1,0:T(8,128)(2,1)S(1)} %bitcast.31), channel_id=1, source_target_pairs={{0,8},{8,0},{1,9},{9,1},{2,10},{10,2},{3,11},{11,3},{4,12},{12,4},... | collective-permute-start | bytes 786440 | tf_op jit(solution)/shard_map/ppermute | solution.py:475
  25.1 12.8 %collective-permute-start.8 = (bf16[256,1024]{1,0:T(8,128)(2,1)S(1)}, bf16[256,1024]{1,0:T(8,128)(2,1)}, u32[]{:S(2)}, u32[]{:S(2)}) collective-permute-start(bf16[256,1024]{1,0:T(8,128)(2,1)S(1)} %multiply_convert_fusion.1.refs_0_.half), channel_id=1, source_target_pairs={{0,96},{32,0},{64,32},{96,64},{1,97},{33,1},{65,33},{97,65},{2,98}... | collective-permute-start | bytes 1572872 | tf_op jit(solution)/shard_map/ppermute | solution.py:95
  25.1 13.1 %collective-permute-start.7 = (bf16[256,1024]{1,0:T(8,128)(2,1)S(1)}, bf16[256,1024]{1,0:T(8,128)(2,1)}, u32[]{:S(2)}, u32[]{:S(2)}) collective-permute-start(bf16[256,1024]{1,0:T(8,128)(2,1)S(1)} %multiply_convert_fusion.1.refs_0_.half), channel_id=1, source_target_pairs={{0,32},{32,64},{64,96},{96,0},{1,33},{33,65},{65,97},{97,1},{2,34}... | collective-permute-start | bytes 1572872 | tf_op jit(solution)/shard_map/ppermute | solution.py:95
  31.1 13.2 %collective-permute-start.9 = (bf16[256,1024]{1,0:T(8,128)(2,1)S(1)}, bf16[256,1024]{1,0:T(8,128)(2,1)}, u32[]{:S(2)}, u32[]{:S(2)}) collective-permute-start(bf16[256,1024]{1,0:T(8,128)(2,1)S(1)} %multiply_convert_fusion.1.refs_0_.half), channel_id=1, source_target_pairs={{0,16},{16,0},{1,17},{17,1},{2,18},{18,2},{3,19},{19,3},{4,20},{20... | collective-permute-start | bytes 1572872 | tf_op jit(solution)/shard_map/ppermute | solution.py:99
  33.6 12.7 %collective-permute-start.6 = (bf16[256,1024]{1,0:T(8,128)(2,1)S(1)}, bf16[256,1024]{1,0:T(8,128)(2,1)}, u32[]{:S(2)}, u32[]{:S(2)}) collective-permute-start(bf16[256,1024]{1,0:T(8,128)(2,1)S(1)} %pad_maximum_fusion.refs_0_), channel_id=1, source_target_pairs={{0,6},{2,0},{4,2},{6,4},{1,7},{3,1},{5,3},{7,5},{8,14},{10,8},{12,... | collective-permute-start | bytes 1572872 | tf_op jit(solution)/shard_map/ppermute | solution.py:95
  36.2 13.3 %collective-permute-start.5 = (bf16[256,1024]{1,0:T(8,128)(2,1)S(1)}, bf16[256,1024]{1,0:T(8,128)(2,1)}, u32[]{:S(2)}, u32[]{:S(2)}) collective-permute-start(bf16[256,1024]{1,0:T(8,128)(2,1)S(1)} %pad_maximum_fusion.refs_0_), channel_id=1, source_target_pairs={{0,2},{2,4},{4,6},{6,0},{1,3},{3,5},{5,7},{7,1},{8,10},{10,12},{12... | collective-permute-start | bytes 1572872 | tf_op jit(solution)/shard_map/ppermute | solution.py:95
  50.7 8.5 %collective-permute-start.10 = (bf16[256,1024]{1,0:T(8,128)(2,1)S(1)}, bf16[256,1024]{1,0:T(8,128)(2,1)S(1)}, u32[]{:S(2)}, u32[]{:S(2)}) collective-permute-start(bf16[256,1024]{1,0:T(8,128)(2,1)S(1)} %broadcast_select_fusion), channel_id=1, source_target_pairs={{0,2},{1,7},{2,4},{3,1},{4,6},{5,3},{6,0},{7,5},{8,10},{9,15},{10,... | collective-permute-start | bytes 1572872 | tf_op jit(solution)/shard_map/ppermute | solution.py:483
  51.0 13.8 %collective-permute-start.16 = (bf16[256,1024]{1,0:T(8,128)(2,1)}, bf16[256,1024]{1,0:T(8,128)(2,1)}, u32[]{:S(2)}, u32[]{:S(2)}) collective-permute-start(bf16[256,1024]{1,0:T(8,128)(2,1)} %collective-permute-done.9.refs_4_), channel_id=1, source_target_pairs={{0,96},{32,0},{64,32},{96,64},{1,97},{33,1},{65,33},{97,65},{2,98}... | collective-permute-start | bytes 1572872 | tf_op jit(solution)/shard_map/ppermute | solution.py:95
  51.0 14.7 %collective-permute-start.15 = (bf16[256,1024]{1,0:T(8,128)(2,1)}, bf16[256,1024]{1,0:T(8,128)(2,1)S(1)}, u32[]{:S(2)}, u32[]{:S(2)}) collective-permute-start(bf16[256,1024]{1,0:T(8,128)(2,1)} %collective-permute-done.9.refs_4_), channel_id=1, source_target_pairs={{0,32},{32,64},{64,96},{96,0},{1,33},{33,65},{65,97},{97,1},{2,34}... | collective-permute-start | bytes 1572872 | tf_op jit(solution)/shard_map/ppermute | solution.py:95
  59.2 7.3 %collective-permute-start.14 = (bf16[256,1024]{1,0:T(8,128)(2,1)S(1)}, bf16[256,1024]{1,0:T(8,128)(2,1)S(1)}, u32[]{:S(2)}, u32[]{:S(2)}) collective-permute-start(bf16[256,1024]{1,0:T(8,128)(2,1)S(1)} %collective-permute-done.10.refs_3_), channel_id=1, source_target_pairs={{0,1},{1,0},{2,3},{3,2},{4,5},{5,4},{6,7},{7,6},{8,9},{9,8},{10,11... | collective-permute-start | bytes 1572872 | tf_op jit(solution)/shard_map/ppermute | solution.py:99
  63.5 0.8 copy-start.5
  64.3 5.2 %collective-permute-start.11 = (bf16[256,1024]{1,0:T(8,128)(2,1)S(1)}, bf16[256,1024]{1,0:T(8,128)(2,1)}, u32[]{:S(2)}, u32[]{:S(2)}) collective-permute-start(bf16[256,1024]{1,0:T(8,128)(2,1)S(1)} %pad_maximum_fusion.refs_0_), channel_id=1, source_target_pairs={{0,1},{1,0},{2,3},{3,2},{4,5},{5,4},{6,7},{7,6},{8,9},{9,8},{10,11... | collective-permute-start | bytes 1572872 | tf_op jit(solution)/shard_map/ppermute | solution.py:99
  64.3 5.2 %collective-permute-start.12 = (bf16[256,1024]{1,0:T(8,128)(2,1)}, bf16[256,1024]{1,0:T(8,128)(2,1)}, u32[]{:S(2)}, u32[]{:S(2)}) collective-permute-start(bf16[256,1024]{1,0:T(8,128)(2,1)} %collective-permute-done.5.refs_1_), channel_id=1, source_target_pairs={{0,1},{1,0},{2,3},{3,2},{4,5},{5,4},{6,7},{7,6},{8,9},{9,8},{10,11... | collective-permute-start | bytes 1572872 | tf_op jit(solution)/shard_map/ppermute | solution.py:99
  64.8 4.7 %collective-permute-start.13 = (bf16[256,1024]{1,0:T(8,128)(2,1)}, bf16[256,1024]{1,0:T(8,128)(2,1)}, u32[]{:S(2)}, u32[]{:S(2)}) collective-permute-start(bf16[256,1024]{1,0:T(8,128)(2,1)} %collective-permute-done.6.refs_2_), channel_id=1, source_target_pairs={{0,1},{1,0},{2,3},{3,2},{4,5},{5,4},{6,7},{7,6},{8,9},{9,8},{10,11... | collective-permute-start | bytes 1572872 | tf_op jit(solution)/shard_map/ppermute | solution.py:99
  65.7 0.8 copy-start.2
  66.5 12.5 %collective-permute-start.17 = (bf16[256,1024]{1,0:T(8,128)(2,1)}, bf16[256,1024]{1,0:T(8,128)(2,1)}, u32[]{:S(2)}, u32[]{:S(2)}) collective-permute-start(bf16[256,1024]{1,0:T(8,128)(2,1)} %collective-permute-done.7.refs_1_), channel_id=1, source_target_pairs={{0,32},{32,64},{64,96},{96,0},{1,33},{33,65},{65,97},{97,1},{2,34}... | collective-permute-start | bytes 1572872 | tf_op jit(solution)/shard_map/ppermute | solution.py:486
  67.3 14.1 %collective-permute-start.18 = (bf16[256,1024]{1,0:T(8,128)(2,1)}, bf16[256,1024]{1,0:T(8,128)(2,1)}, u32[]{:S(2)}, u32[]{:S(2)}) collective-permute-start(bf16[256,1024]{1,0:T(8,128)(2,1)} %collective-permute-done.16.refs_6_), channel_id=1, source_target_pairs={{0,96},{32,0},{64,32},{96,64},{1,97},{33,1},{65,33},{97,65},{2,98}... | collective-permute-start | bytes 1572872 | tf_op jit(solution)/shard_map/ppermute | solution.py:488
  69.5 1.0 copy-start.6
  70.6 1.0 copy-start.9
  77.0 1.0 copy-start.11
  81.4 23.3 %collective-permute-start.20 = (bf16[256,1024]{1,0:T(8,128)(2,1)}, bf16[256,1024]{1,0:T(8,128)(2,1)}, u32[]{:S(2)}, u32[]{:S(2)}) collective-permute-start(bf16[256,1024]{1,0:T(8,128)(2,1)} %bitcast.19), channel_id=1, source_target_pairs={{0,0},{13,1},{18,2},{31,3},{39,4},{42,5},{53,6},{56,7},{66,8},{79,... | collective-permute-start | bytes 1572872 | tf_op jit(solution)/shard_map/ppermute | solution.py:494
  89.2 23.0 %all-to-all-start.1 = ((bf16[16,256,128]{2,1,0:T(8,128)(2,1)}), bf16[16,256,128]{2,1,0:T(8,128)(2,1)}, u32[]{:S(2)}, u32[]{:S(2)}) async-start(bf16[16,256,128]{2,1,0:T(8,128)(2,1)} %bitcast.30), calls=%async_computation.1 | async-start | bytes 2097152 | tf_op jit(solution)/shard_map/all_to_all | solution.py:495
  93.7 1.0 copy-start.3
  100.9 0.8 copy-start.15
  101.7 15.1 %collective-permute-start.21 = (bf16[128,1024]{1,0:T(8,128)(2,1)}, bf16[128,1024]{1,0:T(8,128)(2,1)S(1)}, u32[]{:S(2)}, u32[]{:S(2)}) collective-permute-start(bf16[128,1024]{1,0:T(8,128)(2,1)} %get-tuple-element.60), channel_id=1, source_target_pairs={{0,0},{97,1},{64,2},{33,3},{32,4},{65,5},{96,6},{1,7},{16,8},{113,... | collective-permute-start | bytes 786440 | tf_op jit(solution)/shard_map/ppermute | solution.py:500
  104.2 8.0 %collective-permute-start.19 = (bf16[8,128,256]{2,1,0:T(8,128)(2,1)}, bf16[8,128,256]{2,1,0:T(8,128)(2,1)}, u32[]{:S(2)}, u32[]{:S(2)}) collective-permute-start(bf16[8,128,256]{2,1,0:T(8,128)(2,1)} %get-tuple-element.57), channel_id=1, source_target_pairs={{0,1},{1,0},{2,3},{3,2},{4,5},{5,4},{6,7},{7,6},{8,9},{9,8},{10,11... | collective-permute-start | bytes 1572872 | tf_op jit(solution)/shard_map/ppermute | solution.py:497
  112.2 1.0 copy-start.16
  114.9 27.7 %copy-start.4 = (bf16[256,1024]{1,0:T(8,128)(2,1)S(1)}, bf16[256,1024]{1,0:T(8,128)(2,1)}, u32[]{:S(2)}) copy-start(bf16[256,1024]{1,0:T(8,128)(2,1)} %copy-done.2) | copy-start | bytes 1572868
  140.6 2.0 collective-permute-start.22
  145.9 23.7 %copy-start.12 = (f32[256,1024]{1,0:T(8,128)}, f32[256,1024]{1,0:T(8,128)S(1)}, u32[]{:S(2)}) copy-start(f32[256,1024]{1,0:T(8,128)S(1)} %get-tuple-element.78.up) | copy-start | bytes 3145732
  145.9 28.1 %copy-start.7 = (bf16[256,1024]{1,0:T(8,128)(2,1)S(1)}, bf16[256,1024]{1,0:T(8,128)(2,1)}, u32[]{:S(2)}) copy-start(bf16[256,1024]{1,0:T(8,128)(2,1)} %copy-done.5) | copy-start | bytes 1572868
  145.9 28.1 %copy-start.10 = (bf16[256,1024]{1,0:T(8,128)(2,1)S(1)}, bf16[256,1024]{1,0:T(8,128)(2,1)}, u32[]{:S(2)}) copy-start(bf16[256,1024]{1,0:T(8,128)(2,1)} %copy-done.8) | copy-start | bytes 1572868
  169.6 17.8 %collective-permute-start.23 = (bf16[128,1024]{1,0:T(8,128)(2,1)}, bf16[128,1024]{1,0:T(8,128)(2,1)}, u32[]{:S(2)}, u32[]{:S(2)}) collective-permute-start(bf16[128,1024]{1,0:T(8,128)(2,1)} %get-tuple-element.71), channel_id=1, source_target_pairs={{1,0},{96,1},{65,2},{32,3},{33,4},{64,5},{97,6},{0,7},{17,8},{112,... | collective-permute-start | bytes 786440 | tf_op jit(solution)/shard_map/ppermute | solution.py:508
  177.2 0.8 copy-start.14
  178.0 0.8 copy-start.19
  179.5 17.1 %all-to-all-start.4 = ((f32[16,5,1024]{2,1,0:T(8,128)}), f32[16,5,1024]{2,1,0:T(8,128)S(1)}, u32[]{:S(2)}, u32[]{:S(2)}) async-start(f32[16,5,1024]{2,1,0:T(8,128)} %copy-done.14), calls=%async_computation.4 | async-start | bytes 1048576 | tf_op jit(solution)/shard_map/all_to_all | solution.py:518
  183.0 13.0 %collective-permute-start.24 = (bf16[128,1024]{1,0:T(8,128)(2,1)}, bf16[128,1024]{1,0:T(8,128)(2,1)S(1)}, u32[]{:S(2)}, u32[]{:S(2)}) collective-permute-start(bf16[128,1024]{1,0:T(8,128)(2,1)} %copy-done.21), channel_id=1, source_target_pairs={{0,8},{8,0},{1,9},{9,1},{2,10},{10,2},{3,11},{11,3},{4,12},{12,4},... | collective-permute-start | bytes 786440 | tf_op jit(solution)/shard_map/ppermute | solution.py:511
  183.8 1.2 copy-start.13
  187.4 8.6 %copy-start.20 = (f32[128,1024]{1,0:T(8,128)S(1)}, f32[128,1024]{1,0:T(8,128)}, u32[]{:S(2)}) copy-start(f32[128,1024]{1,0:T(8,128)} %copy-done.19) | copy-start | bytes 1572868
  188.5 0.8 copy-start.17
  196.7 1.0 copy-start.18
  (2 other events, 1.5 us)

commit v5 on v3

--- a/solution.py
+++ b/solution.py
@@ -155,11 +155,7 @@
 
                         @pl.when(wanted)
                         def _():
-                            if step == 0:
-                                sends[0][...] = held[flip, at : at + 64, :]
-                                sends[1][...] = held[flip, at + 64 : at + 128, :]
-                            else:
-                                sends[2][...] = held[flip, at : at + 128, :]
+                            sends[step][...] = held[flip, at : at + 128, :]
 
 
 def call(kernel, out_shape, extra, name, space=pltpu.VMEM, scratch=(), flops=2 * 256 * 2048 * 1024):
@@ -180,7 +176,7 @@
     if first:
         shapes = [(8, 2, 256, 128), (2, 128, 1024)]
     else:
-        shapes = [(8, 128, 256), (8, 128, 256), (64, 1024), (64, 1024), (128, 1024)]
+        shapes = [(8, 128, 256), (8, 128, 256), (128, 1024), (128, 1024)]
     out = [jax.ShapeDtypeStruct(shape, bf16) for shape in shapes]
     scratch = [pltpu.VMEM((2, 1024, 1024), bf16), pltpu.SemaphoreType.DMA((8,))]
     flops = 2 * 256 * 2048 * 1024 if first else 1 << 20
@@ -339,12 +335,10 @@
     out[1:2, :] = image_sum(other * half[...].astype(f32))
 
 
-def arrange_kernel(ids, early, mid, late, keep, traded, block, up):
+def arrange_kernel(which, ids, same, other, out):
     for half in range(2):
-        columns = slice(1024 * half, 1024 * (half + 1))
-        block[0:64, columns] = jnp.where(ids[1] == half, early[...], late[0:64])
-        block[64:128, columns] = jnp.where(ids[1] == half, mid[...], late[64:128])
-        up[:, columns] = jnp.where(ids[0] == half, keep[...], traded[...].astype(f32))
+        picked = jnp.where(ids[which] == half, same[...].astype(out.dtype), other[...].astype(out.dtype))
+        out[:, 1024 * half : 1024 * (half + 1)] = picked
 
 
 def finish_second_kernel(ids, terms, scales, view, up, partner, grad):
@@ -387,8 +381,8 @@
 
 
 def row_sum(x):
-    x = x + sum(lax.ppermute(x, ("y1", "y0"), [(i, (i + step) % 4) for i in range(4)]) for step in (1, 2, 3))
-    return x + lax.ppermute(x, "xh", SWAP)
+    x = x + lax.ppermute(x, "xh", SWAP)
+    return x + sum(lax.ppermute(x, ("y1", "y0"), [(i, (i + step) % 4) for i in range(4)]) for step in (1, 2, 3))
 
 
 def local(view_a, view_b):
@@ -433,23 +427,23 @@
     mixed = blend(mine_b, lax.ppermute(give_b, "k", SWAP), piece_a)
     ids = jnp.stack([xl, core, lax.axis_index(ROW)])
     partner = vmem_call(partner_kernel, jax.ShapeDtypeStruct((2, 1024), f32), (ids, other_a, half_b), "partner", 1 << 34)
-    mixed, partner = tie(mixed, partner)
     early = lax.ppermute(send_b[0], ROW + COL, pairs_b[0])
+    mixed, partner, early = tie(mixed, partner, early)
     mixed = lax.all_to_all(mixed, ("xl", "z1", "z0"), 0, 0)
 
-    mixed, early, mid = tie(mixed, early, send_b[1])
-    mid = lax.ppermute(mid, ROW + COL, pairs_b[0])
     traded = lax.ppermute(mixed[:, 128:], "k", SWAP)
     up_b, last = second_view(ids_b, mixed, traded, partner, blocks_b)
-    last, mid = tie(last, mid)
     last = lax.all_to_all(last, ("y1", "y0", "xh", "xl"), 0, 0)
-    last, late = tie(last, send_b[2])
+    last, late = tie(last, send_b[1])
     late = lax.ppermute(late, ROW + COL, pairs_b[1])
 
     keep, give, sums_a, sums_b = first_view(ids_a, last, blocks_a)
-    traded = lax.ppermute(give, "xl", SWAP)
-    out = [jax.ShapeDtypeStruct((128, 2048), bf16), jax.ShapeDtypeStruct((128, 2048), f32)]
-    block, up_own = vmem_call(arrange_kernel, out, (ids, early, mid, late, keep, traded), "arrange", 1 << 34)
+    traded = lax.ppermute(lax.ppermute(give, ("xl", "k"), [(i, 3 - i) for i in range(4)]), "k", SWAP)
+    block = jax.ShapeDtypeStruct((128, 2048), bf16)
+    block = vmem_call(functools.partial(arrange_kernel, 1), block, (ids, early, late), "arrange_block", 1 << 34)
+    keep, block = tie(keep, block)
+    up_own = jax.ShapeDtypeStruct((128, 2048), f32)
+    up_own = vmem_call(functools.partial(arrange_kernel, 0), up_own, (ids, keep, traded), "arrange_up", 1 << 33)
     sums_a, sums_b = tie(sums_a, sums_b)
     sums_a = lax.all_to_all(sums_a, COL, 0, 0)
 

time: 205 us -> 212 us (1.034)
  blocking collectives: 27.7 us -> 47.4 us
  waiting for transfers between devices: 65.9 us -> 53.7 us
  starting transfers between devices: 62 us -> 57.8 us
  local copies, waits for them, and re-layouts: 15.2 us -> 17.8 us
    all_to_all x0 -> x1, blocking collectives: none -> 25.3 us  [local(): mixed = lax.all_to_all(mixed, ('xl', 'z1', 'z0'), 0, 0)]
    ppermute x1, waiting for transfers between devices: 15.3 us -> 1.73 us  [local(): early = lax.ppermute(send_b[0], ROW + COL, pairs_b[0])]
    all_to_all x1, waiting for transfers between devices: 0.62 us -> 7.09 us  [spread(): return lax.all_to_all(jnp.broadcast_to(x[None], (n,) + x.shape), axes, 0, 0)]
    all_to_all x1, blocking collectives: 27.7 us -> 22.2 us  [local(): last = lax.all_to_all(last, ('y1', 'y0', 'xh', 'xl'), 0, 0)]
    all_to_all x1, waiting for transfers between devices: 8.03 us -> 3.05 us  [local(): sums_a = lax.all_to_all(sums_a, COL, 0, 0)]
    ppermute x1, waiting for transfers between devices: 0.01 us -> 4.9 us  [local(): late = lax.ppermute(late, ROW + COL, pairs_b[1])]
    all_to_all x1 -> x0, starting transfers between devices: 3.56 us -> none  [local(): mixed = lax.all_to_all(mixed, ('xl', 'z1', 'z0'), 0, 0)]
    all_to_all x1, waiting for transfers between devices: 9.84 us -> 6.29 us  [local(): lax.all_to_all(part_a.reshape(16, 256, 128), ('y1', 'y0', 'xh', 'xl'), 0, 0)]
  transfers between devices with their start and end apart: 30 -> 29, of which waited for: 15 -> 16; matrix products, arithmetic and copies ran while one was open for 1% -> 1% of each run, Pallas kernels for 10% -> 9%
where the time goes in v5:
time: 212 us; the launch traced here: 209 us
  starting transfers between devices  57.8 us (27%)
  waiting for transfers between devices  53.7 us (25%)
  blocking collectives  47.4 us (22%)
  Pallas kernels  27.7 us (13%)
  local copies, waits for them, and re-layouts  17.8 us (8%)
  other arithmetic  3.51 us (2%)
    all_to_all x1, blocking collectives, local(): mixed = lax.all_to_all(mixed, ('xl', 'z1', 'z0'), 0, 0)  25.3 us
    all_to_all x1, blocking collectives, local(): last = lax.all_to_all(last, ('y1', 'y0', 'xh', 'xl'), 0, 0)  22.2 us
    unnamed x43, local copies, waits for them, and re-layouts  14.1 us
    pallas_call x2, Pallas kernels, gram_part(): call(functools.partial(gram_kernel, first), out, 0, 'gram_part', pl.ANY,...  11.6 us
    all_to_all x1, starting transfers between devices, spread(): return lax.all_to_all(jnp.broadcast_to(x[None], (n,) + x.shape), axes, 0, 0)  8.92 us
    ppermute x5, starting transfers between devices, trade(): return [lax.ppermute(x, axis, SWAP) for x in blocks]  8.23 us
    ppermute x1, starting transfers between devices, local(): other_a = lax.ppermute(send_a.reshape(256, 1024), ROW + COL, pairs_a)  7.22 us
    all_to_all x1, waiting for transfers between devices, spread(): return lax.all_to_all(jnp.broadcast_to(x[None], (n,) + x.shape), axes, 0, 0)  7.09 us
  transfers between devices with their start and end apart: 29, of which 16 were waited for; matrix products, arithmetic and copies ran while one was open for 1% of the time, Pallas kernels for 9%

profile of v5, /device:TPU:9, one launch (start us, length us, event | category | flops | bytes accessed | tf_op | source)
XLA Modules:
  0.0 209.1 jit_solution(551488393901263126)
XLA Ops:
  0.6 1.4 fusion.6
  2.3 2.8 %collective-permute-start = (f32[2,1024]{1,0:T(2,128)S(1)}, f32[2,1024]{1,0:T(2,128)S(1)}, u32[]{:S(2)}, u32[]{:S(2)}) collective-permute-start(f32[2,1024]{1,0:T(2,128)S(1)} %pad_maximum_fusion.3), channel_id=1, source_target_pairs={{0,16},{16,0},{1,17},{17,1},{2,18},{18,2},{3,19},{19,3},{4,20},{20... | collective-permute-start | bytes 24584 | tf_op jit(solution)/shard_map/ppermute | solution.py:384
  5.1 1.3 collective-permute-done
  6.5 2.5 %collective-permute-start.2 = (f32[2,1024]{1,0:T(2,128)S(1)}, f32[2,1024]{1,0:T(2,128)S(1)}, u32[]{:S(2)}, u32[]{:S(2)}) collective-permute-start(f32[2,1024]{1,0:T(2,128)S(1)} %fusion.4), channel_id=1, source_target_pairs={{0,64},{32,96},{64,0},{96,32},{1,65},{33,97},{65,1},{97,33},{2,66}... | collective-permute-start | bytes 24584 | tf_op jit(solution)/shard_map/ppermute | solution.py:385
  9.0 1.6 collective-permute-start.1
  11.4 8.9 %all-to-all-start = ((f32[16,2,2048]{2,1,0:T(2,128)}), f32[16,2,2048]{2,1,0:T(2,128)S(1)}, u32[]{:S(2)}, u32[]{:S(2)}) async-start(f32[16,2,2048]{2,1,0:T(2,128)} %broadcast_in_dim.2), calls=%async_computation | async-start | bytes 524288 | tf_op jit(solution)/shard_map/all_to_all | solution.py:32
  20.4 7.1 %all-to-all-done = f32[16,2,2048]{2,1,0:T(2,128)S(1)} async-done(((f32[16,2,2048]{2,1,0:T(2,128)}), f32[16,2,2048]{2,1,0:T(2,128)S(1)}, u32[]{:S(2)}, u32[]{:S(2)}) %all-to-all-start) | async-done | bytes 262176 | tf_op jit(solution)/shard_map/all_to_all | solution.py:32
  28.1 1.1 constant_dynamic-slice_fusion.1
  30.4 1.5 collective-permute-start.7
  31.8 4.5 %collective-permute-done.4 = bf16[128,1024]{1,0:T(8,128)(2,1)S(1)} collective-permute-done((bf16[128,1024]{1,0:T(8,128)(2,1)S(1)}, bf16[128,1024]{1,0:T(8,128)(2,1)S(1)}, u32[]{:S(2)}, u32[]{:S(2)}) %collective-permute-start.4) | collective-permute-done | bytes 262176 | tf_op jit(solution)/shard_map/ppermute | solution.py:405
  36.4 2.5 %collective-permute-start.9 = (bf16[256,1024]{1,0:T(8,128)(2,1)S(1)}, bf16[256,1024]{1,0:T(8,128)(2,1)}, u32[]{:S(2)}, u32[]{:S(2)}) collective-permute-start(bf16[256,1024]{1,0:T(8,128)(2,1)S(1)} %multiply_convert_fusion.1.refs_0_.half), channel_id=1, source_target_pairs={{0,16},{16,0},{1,17},{17,1},{2,18},{18,2},{3,19},{19,3},{4,20},{20... | collective-permute-start | bytes 1572872 | tf_op jit(solution)/shard_map/ppermute | solution.py:99
  39.0 2.3 %collective-permute-start.6 = (bf16[256,1024]{1,0:T(8,128)(2,1)S(1)}, bf16[256,1024]{1,0:T(8,128)(2,1)}, u32[]{:S(2)}, u32[]{:S(2)}) collective-permute-start(bf16[256,1024]{1,0:T(8,128)(2,1)S(1)} %pad_maximum_fusion.refs_0_), channel_id=1, source_target_pairs={{0,6},{2,0},{4,2},{6,4},{1,7},{3,1},{5,3},{7,5},{8,14},{10,8},{12,... | collective-permute-start | bytes 1572872 | tf_op jit(solution)/shard_map/ppermute | solution.py:95
  41.3 1.8 collective-permute-done.8.refs_2_
  43.5 6.3 %collective-permute-done.9.refs_4_ = bf16[256,1024]{1,0:T(8,128)(2,1)} collective-permute-done((bf16[256,1024]{1,0:T(8,128)(2,1)S(1)}, bf16[256,1024]{1,0:T(8,128)(2,1)}, u32[]{:S(2)}, u32[]{:S(2)}) %collective-permute-start.9) | collective-permute-done | bytes 524320 | tf_op jit(solution)/shard_map/ppermute | solution.py:99
  49.8 1.6 collective-permute-done.6.refs_2_
  51.3 3.2 %collective-permute-done.5.refs_1_ = bf16[256,1024]{1,0:T(8,128)(2,1)} collective-permute-done((bf16[256,1024]{1,0:T(8,128)(2,1)S(1)}, bf16[256,1024]{1,0:T(8,128)(2,1)}, u32[]{:S(2)}, u32[]{:S(2)}) %collective-permute-start.5) | collective-permute-done | bytes 524320 | tf_op jit(solution)/shard_map/ppermute | solution.py:95
  54.6 1.1 broadcast_select_fusion
  56.0 1.5 collective-permute-start.15
  57.5 6.7 %collective-permute-done.10.refs_3_ = bf16[256,1024]{1,0:T(8,128)(2,1)S(1)} collective-permute-done((bf16[256,1024]{1,0:T(8,128)(2,1)S(1)}, bf16[256,1024]{1,0:T(8,128)(2,1)S(1)}, u32[]{:S(2)}, u32[]{:S(2)}) %collective-permute-start.10) | collective-permute-done | bytes 524320 | tf_op jit(solution)/shard_map/ppermute | solution.py:413
  64.2 4.4 %collective-permute-start.14 = (bf16[256,1024]{1,0:T(8,128)(2,1)S(1)}, bf16[256,1024]{1,0:T(8,128)(2,1)S(1)}, u32[]{:S(2)}, u32[]{:S(2)}) collective-permute-start(bf16[256,1024]{1,0:T(8,128)(2,1)S(1)} %collective-permute-done.10.refs_3_), channel_id=1, source_target_pairs={{0,1},{1,0},{2,3},{3,2},{4,5},{5,4},{6,7},{7,6},{8,9},{9,8},{10,11... | collective-permute-start | bytes 1572872 | tf_op jit(solution)/shard_map/ppermute | solution.py:99
  72.3 1.5 collective-permute-start.18
  76.6 5.4 %gram_part.2 = (bf16[8,2,256,128]{3,2,1,0:T(8,128)(2,1)S(1)}, bf16[2,128,1024]{2,1,0:T(8,128)(2,1)}) custom-call(s32[6]{0:T(128)S(1)} %pad_add_fusion.1.ids, bf16[256,1024]{1,0:T(8,128)(2,1)S(1)} %pad_maximum_fusion.refs_0_, bf16[256,1024]{1,0:T(8,128)(2,1)} %collective-permute-done.5.refs_1_, bf16[256,1024]{1,0:T(8,128)(2,1)} %collective-permute-done.6.refs_2_, ...), custom_call_target="tpu_custom_call" | custom-call | flops 1073741824 | bytes 4194304 | tf_op jit(solution)/shard_map/gram_part/pallas_call | solution.py:183
  83.0 1.0 collective-permute-done.17.refs_3_
  84.0 2.4 %collective-permute-done.18.refs_7_ = bf16[256,1024]{1,0:T(8,128)(2,1)} collective-permute-done((bf16[256,1024]{1,0:T(8,128)(2,1)}, bf16[256,1024]{1,0:T(8,128)(2,1)}, u32[]{:S(2)}, u32[]{:S(2)}) %collective-permute-start.18) | collective-permute-done | bytes 524320 | tf_op jit(solution)/shard_map/ppermute | solution.py:418
  86.4 7.2 %collective-permute-start.20 = (bf16[256,1024]{1,0:T(8,128)(2,1)}, bf16[256,1024]{1,0:T(8,128)(2,1)}, u32[]{:S(2)}, u32[]{:S(2)}) collective-permute-start(bf16[256,1024]{1,0:T(8,128)(2,1)} %bitcast.19), channel_id=1, source_target_pairs={{0,0},{13,1},{18,2},{31,3},{39,4},{42,5},{53,6},{56,7},{66,8},{79,... | collective-permute-start | bytes 1572872 | tf_op jit(solution)/shard_map/ppermute | solution.py:424
  94.5 4.4 %all-to-all-start.1 = ((bf16[16,256,128]{2,1,0:T(8,128)(2,1)}), bf16[16,256,128]{2,1,0:T(8,128)(2,1)}, u32[]{:S(2)}, u32[]{:S(2)}) async-start(bf16[16,256,128]{2,1,0:T(8,128)(2,1)} %bitcast.30), calls=%async_computation.1 | async-start | bytes 2097152 | tf_op jit(solution)/shard_map/all_to_all | solution.py:425
  100.0 6.2 %gram_part.3 = (bf16[8,128,256]{2,1,0:T(8,128)(2,1)S(1)}, bf16[8,128,256]{2,1,0:T(8,128)(2,1)}, bf16[128,1024]{1,0:T(8,128)(2,1)}, bf16[128,1024]{1,0:T(8,128)(2,1)}) custom-call(s32[11]{0:T(128)S(1)} %pad_add_fusion.2.ids, bf16[256,1024]{1,0:T(8,128)(2,1)S(1)} %multiply_convert_fusion.1.refs_0_.half, bf16[256,1024]{1,0:T(8,128)(2,1)} %collective-permute-done.7.refs_1_, ...), custom_call_target="tpu_custom_call" | custom-call | flops 1048576 | bytes 4096 | tf_op jit(solution)/shard_map/gram_part/pallas_call | solution.py:183
  107.0 2.2 %collective-permute-start.21 = (bf16[128,1024]{1,0:T(8,128)(2,1)}, bf16[128,1024]{1,0:T(8,128)(2,1)S(1)}, u32[]{:S(2)}, u32[]{:S(2)}) collective-permute-start(bf16[128,1024]{1,0:T(8,128)(2,1)} %get-tuple-element.60), channel_id=1, source_target_pairs={{0,0},{97,1},{64,2},{33,3},{32,4},{65,5},{96,6},{1,7},{16,8},{113,... | collective-permute-start | bytes 786440 | tf_op jit(solution)/shard_map/ppermute | solution.py:430
  109.9 1.2 partner.1
  111.1 6.3 %all-to-all-done.1.received = bf16[16,256,128]{2,1,0:T(8,128)(2,1)} async-done(((bf16[16,256,128]{2,1,0:T(8,128)(2,1)}), bf16[16,256,128]{2,1,0:T(8,128)(2,1)}, u32[]{:S(2)}, u32[]{:S(2)}) %all-to-all-start.1) | async-done | bytes 1048608 | tf_op jit(solution)/shard_map/all_to_all | solution.py:425
  117.4 1.0 copy-done.16
  118.4 1.6 blend.1
  120.0 1.7 collective-permute-done.21.same
  121.7 25.3 %all_to_all.25.mixed = bf16[8,256,256]{2,1,0:T(8,128)(2,1)S(1)} all-to-all(bf16[8,256,256]{2,1,0:T(8,128)(2,1)S(1)} %blend.1), channel_id=1, replica_groups=mesh['y1'=2,'y0'=2,'xh'=2,'xl'=2,'z1'=2,'z0'=2,'k'=2] {'xl','z1','z0'}, dimensions={0} | all-to-all | bytes 2097152 | tf_op jit(solution)/shard_map/all_to_all | solution.py:432
  147.0 2.3 %collective-permute-start.22 = (bf16[8,128,256]{2,1,0:T(8,128)(2,1)S(1)}, bf16[8,128,256]{2,1,0:T(8,128)(2,1)S(1)}, u32[]{:S(2)}, u32[]{:S(2)}) collective-permute-start(bf16[8,128,256]{2,1,0:T(8,128)(2,1)S(1)} %slice.24), channel_id=1, source_target_pairs={{0,1},{1,0},{2,3},{3,2},{4,5},{5,4},{6,7},{7,6},{8,9},{9,8},{10,11... | collective-permute-start | bytes 1572872 | tf_op jit(solution)/shard_map/ppermute | solution.py:434
  149.3 1.5 collective-permute-done.22.traded
  150.8 3.3 %second_view.1 = (f32[256,1024]{1,0:T(8,128)S(1)}, bf16[16,160,256]{2,1,0:T(8,128)(2,1)S(1)}) custom-call(s32[11]{0:T(128)S(1)} %pad_add_fusion.2.ids, bf16[8,256,256]{2,1,0:T(8,128)(2,1)S(1)} %all_to_all.25.mixed, bf16[8,128,256]{2,1,0:T(8,128)(2,1)S(1)} %collective-permute-done.22.traded, f32[2,1024]{1,0:T(2,128)S(1)} %partner.1, ...), custom_call_target="tpu_custom_call" | custom-call | flops 1073741824 | bytes 4194304 | tf_op jit(solution)/shard_map/second_view/pallas_call | solution.py:265
  155.2 22.2 %all_to_all.26.last = bf16[16,160,256]{2,1,0:T(8,128)(2,1)S(1)} all-to-all(bf16[16,160,256]{2,1,0:T(8,128)(2,1)S(1)} %get-tuple-element.63), channel_id=1, replica_groups=mesh['y1'=2,'y0'=2,'xh'=2,'xl'=2,'z1'=2,'z0'=2,'k'=2] {'y1','y0','xh','xl'}, dimensions={0} | all-to-all | bytes 2621440 | tf_op jit(solution)/shard_map/all_to_all | solution.py:436
  177.3 3.9 %first_view.1 = (f32[128,1024]{1,0:T(8,128)S(1)}, bf16[128,1024]{1,0:T(8,128)(2,1)}, f32[16,5,1024]{2,1,0:T(8,128)S(1)}, f32[32,256]{1,0:T(8,128)S(1)}) custom-call(s32[6]{0:T(128)S(1)} %pad_add_fusion.1.ids, bf16[16,160,256]{2,1,0:T(8,128)(2,1)S(1)} %all_to_all.26.last, bf16[256,1024]{1,0:T(8,128)(2,1)S(1)} %pad_maximum_fusion.refs_0_, ...), custom_call_target="tpu_custom_call" | custom-call | flops 1048576 | bytes 4096 | tf_op jit(solution)/shard_map/first_view/pallas_call | solution.py:309
  182.8 2.1 %collective-permute-start.24 = (bf16[128,1024]{1,0:T(8,128)(2,1)}, bf16[128,1024]{1,0:T(8,128)(2,1)}, u32[]{:S(2)}, u32[]{:S(2)}) collective-permute-start(bf16[128,1024]{1,0:T(8,128)(2,1)} %get-tuple-element.73), channel_id=1, source_target_pairs={{0,9},{1,8},{8,1},{9,0},{2,11},{3,10},{10,3},{11,2},{4,13},{5,12},... | collective-permute-start | bytes 786440 | tf_op jit(solution)/shard_map/ppermute | solution.py:441
  184.9 2.3 %collective-permute-start.23 = (bf16[128,1024]{1,0:T(8,128)(2,1)}, bf16[128,1024]{1,0:T(8,128)(2,1)}, u32[]{:S(2)}, u32[]{:S(2)}) collective-permute-start(bf16[128,1024]{1,0:T(8,128)(2,1)} %get-tuple-element.71), channel_id=1, source_target_pairs={{1,0},{96,1},{65,2},{32,3},{33,4},{64,5},{97,6},{0,7},{17,8},{112,... | collective-permute-start | bytes 786440 | tf_op jit(solution)/shard_map/ppermute | solution.py:438
  187.2 4.3 %all-to-all-start.4 = ((f32[16,5,1024]{2,1,0:T(8,128)}), f32[16,5,1024]{2,1,0:T(8,128)S(1)}, u32[]{:S(2)}, u32[]{:S(2)}) async-start(f32[16,5,1024]{2,1,0:T(8,128)} %copy-done.14), calls=%async_computation.4 | async-start | bytes 1048576 | tf_op jit(solution)/shard_map/all_to_all | solution.py:448
  191.6 1.2 copy-done.13
  192.8 2.3 %finish_second.1 = f32[256,1024]{1,0:T(8,128)} custom-call(s32[3]{0:T(128)S(1)} %pad_add_fusion.ids, f32[32,256]{1,0:T(8,128)S(1)} %get-tuple-element.77.terms, f32[2,1024]{1,0:T(2,128)S(1)} %pad_maximum_fusion.4.scales, f32[256,1024]{1,0:T(8,128)S(1)} %copy-done.1, f32[256,1024]{1,0:T(8,128)S(1)} %copy-done.13, ...), custom_call_target="tpu_custom_call" | custom-call | flops 1048576 | bytes 65536 | tf_op jit(solution)/shard_map/finish_second/pallas_call | solution.py:321
  195.2 4.9 %collective-permute-done.23.other = bf16[128,1024]{1,0:T(8,128)(2,1)} collective-permute-done((bf16[128,1024]{1,0:T(8,128)(2,1)}, bf16[128,1024]{1,0:T(8,128)(2,1)}, u32[]{:S(2)}, u32[]{:S(2)}) %collective-permute-start.23) | collective-permute-done | bytes 262176 | tf_op jit(solution)/shard_map/ppermute | solution.py:438
  202.6 3.1 %all-to-all-done.4.sums = f32[16,5,1024]{2,1,0:T(8,128)S(1)} async-done(((f32[16,5,1024]{2,1,0:T(8,128)}), f32[16,5,1024]{2,1,0:T(8,128)S(1)}, u32[]{:S(2)}, u32[]{:S(2)}) %all-to-all-start.4) | async-done | bytes 327712 | tf_op jit(solution)/shard_map/all_to_all | solution.py:448
  205.7 1.0 copy-done.18
  206.7 2.2 %finish_first.1 = (f32[128,2048]{1,0:T(8,128)}, f32[1,1]{1,0:T(1,128)}) custom-call(s32[3]{0:T(128)S(1)} %pad_add_fusion.ids, f32[16,5,1024]{2,1,0:T(8,128)S(1)} %all-to-all-done.4.sums, f32[2,2048]{1,0:T(2,128)S(1)} %pad_maximum_fusion.2.scales, f32[128,2048]{1,0:T(8,128)S(1)} %copy-done, f32[128,2048]{1,0:T(8,128)S(1)} %arrange_up.1.up, ...), custom_call_target="tpu_custom_call" | custom-call | flops 1048576 | bytes 65536 | tf_op jit(solution)/shard_map/finish_first/pallas_call | solution.py:372
  (90 shorter events, 19.9 us)
Async XLA Ops:
  0.6 1.5 copy-start.1
  2.1 25.5 %copy-start = (f32[128,2048]{1,0:T(8,128)S(1)}, f32[128,2048]{1,0:T(8,128)}, u32[]{:S(2)}) copy-start(f32[128,2048]{1,0:T(8,128)} %view.2) | copy-start | bytes 3145732
  2.3 4.1 %collective-permute-start = (f32[2,1024]{1,0:T(2,128)S(1)}, f32[2,1024]{1,0:T(2,128)S(1)}, u32[]{:S(2)}, u32[]{:S(2)}) collective-permute-start(f32[2,1024]{1,0:T(2,128)S(1)} %pad_maximum_fusion.3), channel_id=1, source_target_pairs={{0,16},{16,0},{1,17},{17,1},{2,18},{18,2},{3,19},{19,3},{4,20},{20... | collective-permute-start | bytes 24584 | tf_op jit(solution)/shard_map/ppermute | solution.py:384
  6.4 13.9 %collective-permute-start.3 = (f32[2,1024]{1,0:T(2,128)S(1)}, f32[2,1024]{1,0:T(2,128)S(1)}, u32[]{:S(2)}, u32[]{:S(2)}) collective-permute-start(f32[2,1024]{1,0:T(2,128)S(1)} %fusion.4), channel_id=1, source_target_pairs={{0,96},{32,0},{64,32},{96,64},{1,97},{33,1},{65,33},{97,65},{2,98}... | collective-permute-start | bytes 24584 | tf_op jit(solution)/shard_map/ppermute | solution.py:385
  6.5 13.8 %collective-permute-start.2 = (f32[2,1024]{1,0:T(2,128)S(1)}, f32[2,1024]{1,0:T(2,128)S(1)}, u32[]{:S(2)}, u32[]{:S(2)}) collective-permute-start(f32[2,1024]{1,0:T(2,128)S(1)} %fusion.4), channel_id=1, source_target_pairs={{0,64},{32,96},{64,0},{96,32},{1,65},{33,97},{65,1},{97,33},{2,66}... | collective-permute-start | bytes 24584 | tf_op jit(solution)/shard_map/ppermute | solution.py:385
  9.0 11.3 %collective-permute-start.1 = (f32[2,1024]{1,0:T(2,128)S(1)}, f32[2,1024]{1,0:T(2,128)S(1)}, u32[]{:S(2)}, u32[]{:S(2)}) collective-permute-start(f32[2,1024]{1,0:T(2,128)S(1)} %fusion.4), channel_id=1, source_target_pairs={{0,32},{32,64},{64,96},{96,0},{1,33},{33,65},{65,97},{97,1},{2,34}... | collective-permute-start | bytes 24584 | tf_op jit(solution)/shard_map/ppermute | solution.py:385
  11.4 16.1 %all-to-all-start = ((f32[16,2,2048]{2,1,0:T(2,128)}), f32[16,2,2048]{2,1,0:T(2,128)S(1)}, u32[]{:S(2)}, u32[]{:S(2)}) async-start(f32[16,2,2048]{2,1,0:T(2,128)} %broadcast_in_dim.2), calls=%async_computation | async-start | bytes 524288 | tf_op jit(solution)/shard_map/all_to_all | solution.py:32
  29.3 7.0 %collective-permute-start.4 = (bf16[128,1024]{1,0:T(8,128)(2,1)S(1)}, bf16[128,1024]{1,0:T(8,128)(2,1)S(1)}, u32[]{:S(2)}, u32[]{:S(2)}) collective-permute-start(bf16[128,1024]{1,0:T(8,128)(2,1)S(1)} %bitcast.31), channel_id=1, source_target_pairs={{0,8},{8,0},{1,9},{9,1},{2,10},{10,2},{3,11},{11,3},{4,12},{12,4},... | collective-permute-start | bytes 786440 | tf_op jit(solution)/shard_map/ppermute | solution.py:405
  30.3 12.8 %collective-permute-start.8 = (bf16[256,1024]{1,0:T(8,128)(2,1)S(1)}, bf16[256,1024]{1,0:T(8,128)(2,1)}, u32[]{:S(2)}, u32[]{:S(2)}) collective-permute-start(bf16[256,1024]{1,0:T(8,128)(2,1)S(1)} %multiply_convert_fusion.1.refs_0_.half), channel_id=1, source_target_pairs={{0,96},{32,0},{64,32},{96,64},{1,97},{33,1},{65,33},{97,65},{2,98}... | collective-permute-start | bytes 1572872 | tf_op jit(solution)/shard_map/ppermute | solution.py:95
  30.4 13.1 %collective-permute-start.7 = (bf16[256,1024]{1,0:T(8,128)(2,1)S(1)}, bf16[256,1024]{1,0:T(8,128)(2,1)}, u32[]{:S(2)}, u32[]{:S(2)}) collective-permute-start(bf16[256,1024]{1,0:T(8,128)(2,1)S(1)} %multiply_convert_fusion.1.refs_0_.half), channel_id=1, source_target_pairs={{0,32},{32,64},{64,96},{96,0},{1,33},{33,65},{65,97},{97,1},{2,34}... | collective-permute-start | bytes 1572872 | tf_op jit(solution)/shard_map/ppermute | solution.py:95
  36.4 13.3 %collective-permute-start.9 = (bf16[256,1024]{1,0:T(8,128)(2,1)S(1)}, bf16[256,1024]{1,0:T(8,128)(2,1)}, u32[]{:S(2)}, u32[]{:S(2)}) collective-permute-start(bf16[256,1024]{1,0:T(8,128)(2,1)S(1)} %multiply_convert_fusion.1.refs_0_.half), channel_id=1, source_target_pairs={{0,16},{16,0},{1,17},{17,1},{2,18},{18,2},{3,19},{19,3},{4,20},{20... | collective-permute-start | bytes 1572872 | tf_op jit(solution)/shard_map/ppermute | solution.py:99
  39.0 12.4 %collective-permute-start.6 = (bf16[256,1024]{1,0:T(8,128)(2,1)S(1)}, bf16[256,1024]{1,0:T(8,128)(2,1)}, u32[]{:S(2)}, u32[]{:S(2)}) collective-permute-start(bf16[256,1024]{1,0:T(8,128)(2,1)S(1)} %pad_maximum_fusion.refs_0_), channel_id=1, source_target_pairs={{0,6},{2,0},{4,2},{6,4},{1,7},{3,1},{5,3},{7,5},{8,14},{10,8},{12,... | collective-permute-start | bytes 1572872 | tf_op jit(solution)/shard_map/ppermute | solution.py:95
  41.3 13.3 %collective-permute-start.5 = (bf16[256,1024]{1,0:T(8,128)(2,1)S(1)}, bf16[256,1024]{1,0:T(8,128)(2,1)}, u32[]{:S(2)}, u32[]{:S(2)}) collective-permute-start(bf16[256,1024]{1,0:T(8,128)(2,1)S(1)} %pad_maximum_fusion.refs_0_), channel_id=1, source_target_pairs={{0,2},{2,4},{4,6},{6,0},{1,3},{3,5},{5,7},{7,1},{8,10},{10,12},{12... | collective-permute-start | bytes 1572872 | tf_op jit(solution)/shard_map/ppermute | solution.py:95
  55.7 8.5 %collective-permute-start.10 = (bf16[256,1024]{1,0:T(8,128)(2,1)S(1)}, bf16[256,1024]{1,0:T(8,128)(2,1)S(1)}, u32[]{:S(2)}, u32[]{:S(2)}) collective-permute-start(bf16[256,1024]{1,0:T(8,128)(2,1)S(1)} %broadcast_select_fusion), channel_id=1, source_target_pairs={{0,2},{1,7},{2,4},{3,1},{4,6},{5,3},{6,0},{7,5},{8,10},{9,15},{10,... | collective-permute-start | bytes 1572872 | tf_op jit(solution)/shard_map/ppermute | solution.py:413
  56.0 13.8 %collective-permute-start.16 = (bf16[256,1024]{1,0:T(8,128)(2,1)}, bf16[256,1024]{1,0:T(8,128)(2,1)}, u32[]{:S(2)}, u32[]{:S(2)}) collective-permute-start(bf16[256,1024]{1,0:T(8,128)(2,1)} %collective-permute-done.9.refs_4_), channel_id=1, source_target_pairs={{0,96},{32,0},{64,32},{96,64},{1,97},{33,1},{65,33},{97,65},{2,98}... | collective-permute-start | bytes 1572872 | tf_op jit(solution)/shard_map/ppermute | solution.py:95
  56.0 14.7 %collective-permute-start.15 = (bf16[256,1024]{1,0:T(8,128)(2,1)}, bf16[256,1024]{1,0:T(8,128)(2,1)S(1)}, u32[]{:S(2)}, u32[]{:S(2)}) collective-permute-start(bf16[256,1024]{1,0:T(8,128)(2,1)} %collective-permute-done.9.refs_4_), channel_id=1, source_target_pairs={{0,32},{32,64},{64,96},{96,0},{1,33},{33,65},{65,97},{97,1},{2,34}... | collective-permute-start | bytes 1572872 | tf_op jit(solution)/shard_map/ppermute | solution.py:95
  64.2 7.3 %collective-permute-start.14 = (bf16[256,1024]{1,0:T(8,128)(2,1)S(1)}, bf16[256,1024]{1,0:T(8,128)(2,1)S(1)}, u32[]{:S(2)}, u32[]{:S(2)}) collective-permute-start(bf16[256,1024]{1,0:T(8,128)(2,1)S(1)} %collective-permute-done.10.refs_3_), channel_id=1, source_target_pairs={{0,1},{1,0},{2,3},{3,2},{4,5},{5,4},{6,7},{7,6},{8,9},{9,8},{10,11... | collective-permute-start | bytes 1572872 | tf_op jit(solution)/shard_map/ppermute | solution.py:99
  68.5 0.8 copy-start.5
  69.4 5.2 %collective-permute-start.11 = (bf16[256,1024]{1,0:T(8,128)(2,1)S(1)}, bf16[256,1024]{1,0:T(8,128)(2,1)}, u32[]{:S(2)}, u32[]{:S(2)}) collective-permute-start(bf16[256,1024]{1,0:T(8,128)(2,1)S(1)} %pad_maximum_fusion.refs_0_), channel_id=1, source_target_pairs={{0,1},{1,0},{2,3},{3,2},{4,5},{5,4},{6,7},{7,6},{8,9},{9,8},{10,11... | collective-permute-start | bytes 1572872 | tf_op jit(solution)/shard_map/ppermute | solution.py:99
  69.4 5.2 %collective-permute-start.12 = (bf16[256,1024]{1,0:T(8,128)(2,1)}, bf16[256,1024]{1,0:T(8,128)(2,1)}, u32[]{:S(2)}, u32[]{:S(2)}) collective-permute-start(bf16[256,1024]{1,0:T(8,128)(2,1)} %collective-permute-done.5.refs_1_), channel_id=1, source_target_pairs={{0,1},{1,0},{2,3},{3,2},{4,5},{5,4},{6,7},{7,6},{8,9},{9,8},{10,11... | collective-permute-start | bytes 1572872 | tf_op jit(solution)/shard_map/ppermute | solution.py:99
  69.9 4.7 %collective-permute-start.13 = (bf16[256,1024]{1,0:T(8,128)(2,1)}, bf16[256,1024]{1,0:T(8,128)(2,1)}, u32[]{:S(2)}, u32[]{:S(2)}) collective-permute-start(bf16[256,1024]{1,0:T(8,128)(2,1)} %collective-permute-done.6.refs_2_), channel_id=1, source_target_pairs={{0,1},{1,0},{2,3},{3,2},{4,5},{5,4},{6,7},{7,6},{8,9},{9,8},{10,11... | collective-permute-start | bytes 1572872 | tf_op jit(solution)/shard_map/ppermute | solution.py:99
  70.7 0.8 copy-start.2
  71.5 12.5 %collective-permute-start.17 = (bf16[256,1024]{1,0:T(8,128)(2,1)}, bf16[256,1024]{1,0:T(8,128)(2,1)}, u32[]{:S(2)}, u32[]{:S(2)}) collective-permute-start(bf16[256,1024]{1,0:T(8,128)(2,1)} %collective-permute-done.7.refs_1_), channel_id=1, source_target_pairs={{0,32},{32,64},{64,96},{96,0},{1,33},{33,65},{65,97},{97,1},{2,34}... | collective-permute-start | bytes 1572872 | tf_op jit(solution)/shard_map/ppermute | solution.py:416
  72.3 14.1 %collective-permute-start.18 = (bf16[256,1024]{1,0:T(8,128)(2,1)}, bf16[256,1024]{1,0:T(8,128)(2,1)}, u32[]{:S(2)}, u32[]{:S(2)}) collective-permute-start(bf16[256,1024]{1,0:T(8,128)(2,1)} %collective-permute-done.16.refs_6_), channel_id=1, source_target_pairs={{0,96},{32,0},{64,32},{96,64},{1,97},{33,1},{65,33},{97,65},{2,98}... | collective-permute-start | bytes 1572872 | tf_op jit(solution)/shard_map/ppermute | solution.py:418
  74.5 1.0 copy-start.6
  75.6 1.0 copy-start.9
  82.0 1.0 copy-start.11
  86.4 23.5 %collective-permute-start.20 = (bf16[256,1024]{1,0:T(8,128)(2,1)}, bf16[256,1024]{1,0:T(8,128)(2,1)}, u32[]{:S(2)}, u32[]{:S(2)}) collective-permute-start(bf16[256,1024]{1,0:T(8,128)(2,1)} %bitcast.19), channel_id=1, source_target_pairs={{0,0},{13,1},{18,2},{31,3},{39,4},{42,5},{53,6},{56,7},{66,8},{79,... | collective-permute-start | bytes 1572872 | tf_op jit(solution)/shard_map/ppermute | solution.py:424
  94.5 22.9 %all-to-all-start.1 = ((bf16[16,256,128]{2,1,0:T(8,128)(2,1)}), bf16[16,256,128]{2,1,0:T(8,128)(2,1)}, u32[]{:S(2)}, u32[]{:S(2)}) async-start(bf16[16,256,128]{2,1,0:T(8,128)(2,1)} %bitcast.30), calls=%async_computation.1 | async-start | bytes 2097152 | tf_op jit(solution)/shard_map/all_to_all | solution.py:425
  98.9 1.0 copy-start.3
  106.2 0.8 copy-start.15
  107.0 14.8 %collective-permute-start.21 = (bf16[128,1024]{1,0:T(8,128)(2,1)}, bf16[128,1024]{1,0:T(8,128)(2,1)S(1)}, u32[]{:S(2)}, u32[]{:S(2)}) collective-permute-start(bf16[128,1024]{1,0:T(8,128)(2,1)} %get-tuple-element.60), channel_id=1, source_target_pairs={{0,0},{97,1},{64,2},{33,3},{32,4},{65,5},{96,6},{1,7},{16,8},{113,... | collective-permute-start | bytes 786440 | tf_op jit(solution)/shard_map/ppermute | solution.py:430
  109.2 8.1 %collective-permute-start.19 = (bf16[8,128,256]{2,1,0:T(8,128)(2,1)}, bf16[8,128,256]{2,1,0:T(8,128)(2,1)}, u32[]{:S(2)}, u32[]{:S(2)}) collective-permute-start(bf16[8,128,256]{2,1,0:T(8,128)(2,1)} %get-tuple-element.57), channel_id=1, source_target_pairs={{0,1},{1,0},{2,3},{3,2},{4,5},{5,4},{6,7},{7,6},{8,9},{9,8},{10,11... | collective-permute-start | bytes 1572872 | tf_op jit(solution)/shard_map/ppermute | solution.py:427
  117.4 1.0 copy-start.16
  120.0 30.8 %copy-start.4 = (bf16[256,1024]{1,0:T(8,128)(2,1)S(1)}, bf16[256,1024]{1,0:T(8,128)(2,1)}, u32[]{:S(2)}) copy-start(bf16[256,1024]{1,0:T(8,128)(2,1)} %copy-done.2) | copy-start | bytes 1572868
  147.0 3.8 %collective-permute-start.22 = (bf16[8,128,256]{2,1,0:T(8,128)(2,1)S(1)}, bf16[8,128,256]{2,1,0:T(8,128)(2,1)S(1)}, u32[]{:S(2)}, u32[]{:S(2)}) collective-permute-start(bf16[8,128,256]{2,1,0:T(8,128)(2,1)S(1)} %slice.24), channel_id=1, source_target_pairs={{0,1},{1,0},{2,3},{3,2},{4,5},{5,4},{6,7},{7,6},{8,9},{9,8},{10,11... | collective-permute-start | bytes 1572872 | tf_op jit(solution)/shard_map/ppermute | solution.py:434
  154.2 1.0 copy-start.12
  155.1 22.2 %copy-start.7 = (bf16[256,1024]{1,0:T(8,128)(2,1)S(1)}, bf16[256,1024]{1,0:T(8,128)(2,1)}, u32[]{:S(2)}) copy-start(bf16[256,1024]{1,0:T(8,128)(2,1)} %copy-done.5) | copy-start | bytes 1572868
  155.1 22.2 %copy-start.10 = (bf16[256,1024]{1,0:T(8,128)(2,1)S(1)}, bf16[256,1024]{1,0:T(8,128)(2,1)}, u32[]{:S(2)}) copy-start(bf16[256,1024]{1,0:T(8,128)(2,1)} %copy-done.8) | copy-start | bytes 1572868
  182.0 0.8 copy-start.19
  182.8 12.3 %collective-permute-start.24 = (bf16[128,1024]{1,0:T(8,128)(2,1)}, bf16[128,1024]{1,0:T(8,128)(2,1)}, u32[]{:S(2)}, u32[]{:S(2)}) collective-permute-start(bf16[128,1024]{1,0:T(8,128)(2,1)} %get-tuple-element.73), channel_id=1, source_target_pairs={{0,9},{1,8},{8,1},{9,0},{2,11},{3,10},{10,3},{11,2},{4,13},{5,12},... | collective-permute-start | bytes 786440 | tf_op jit(solution)/shard_map/ppermute | solution.py:441
  184.9 15.2 %collective-permute-start.23 = (bf16[128,1024]{1,0:T(8,128)(2,1)}, bf16[128,1024]{1,0:T(8,128)(2,1)}, u32[]{:S(2)}, u32[]{:S(2)}) collective-permute-start(bf16[128,1024]{1,0:T(8,128)(2,1)} %get-tuple-element.71), channel_id=1, source_target_pairs={{1,0},{96,1},{65,2},{32,3},{33,4},{64,5},{97,6},{0,7},{17,8},{112,... | collective-permute-start | bytes 786440 | tf_op jit(solution)/shard_map/ppermute | solution.py:438
  187.2 18.4 %all-to-all-start.4 = ((f32[16,5,1024]{2,1,0:T(8,128)}), f32[16,5,1024]{2,1,0:T(8,128)S(1)}, u32[]{:S(2)}, u32[]{:S(2)}) async-start(f32[16,5,1024]{2,1,0:T(8,128)} %copy-done.14), calls=%async_computation.4 | async-start | bytes 1048576 | tf_op jit(solution)/shard_map/all_to_all | solution.py:448
  191.6 1.2 copy-start.13
  195.1 6.8 %copy-start.20 = (f32[128,1024]{1,0:T(8,128)S(1)}, f32[128,1024]{1,0:T(8,128)}, u32[]{:S(2)}) copy-start(f32[128,1024]{1,0:T(8,128)} %copy-done.19) | copy-start | bytes 1572868
  195.1 6.8 %collective-permute-start.25 = (bf16[128,1024]{1,0:T(8,128)(2,1)}, bf16[128,1024]{1,0:T(8,128)(2,1)S(1)}, u32[]{:S(2)}, u32[]{:S(2)}) collective-permute-start(bf16[128,1024]{1,0:T(8,128)(2,1)} %collective-permute-done.24), channel_id=1, source_target_pairs={{0,1},{1,0},{2,3},{3,2},{4,5},{5,4},{6,7},{7,6},{8,9},{9,8},{10,11... | collective-permute-start | bytes 786440 | tf_op jit(solution)/shard_map/ppermute | solution.py:441
  201.1 0.8 copy-start.17
  205.7 1.0 copy-start.18
  (2 other events, 1.6 us)

commit v6 on v5

--- a/solution.py
+++ b/solution.py
@@ -335,10 +335,11 @@
     out[1:2, :] = image_sum(other * half[...].astype(f32))
 
 
-def arrange_kernel(which, ids, same, other, out):
+def arrange_kernel(ids, same, other, keep, traded, block, up):
     for half in range(2):
-        picked = jnp.where(ids[which] == half, same[...].astype(out.dtype), other[...].astype(out.dtype))
-        out[:, 1024 * half : 1024 * (half + 1)] = picked
+        columns = slice(1024 * half, 1024 * (half + 1))
+        block[:, columns] = jnp.where(ids[1] == half, same[...], other[...])
+        up[:, columns] = jnp.where(ids[0] == half, keep[...], traded[...].astype(f32))
 
 
 def finish_second_kernel(ids, terms, scales, view, up, partner, grad):
@@ -381,8 +382,8 @@
 
 
 def row_sum(x):
-    x = x + lax.ppermute(x, "xh", SWAP)
-    return x + sum(lax.ppermute(x, ("y1", "y0"), [(i, (i + step) % 4) for i in range(4)]) for step in (1, 2, 3))
+    x = x + sum(lax.ppermute(x, ("y1", "y0"), [(i, (i + step) % 4) for i in range(4)]) for step in (1, 2, 3))
+    return x + lax.ppermute(x, "xh", SWAP)
 
 
 def local(view_a, view_b):
@@ -438,12 +439,9 @@
     late = lax.ppermute(late, ROW + COL, pairs_b[1])
 
     keep, give, sums_a, sums_b = first_view(ids_a, last, blocks_a)
-    traded = lax.ppermute(lax.ppermute(give, ("xl", "k"), [(i, 3 - i) for i in range(4)]), "k", SWAP)
-    block = jax.ShapeDtypeStruct((128, 2048), bf16)
-    block = vmem_call(functools.partial(arrange_kernel, 1), block, (ids, early, late), "arrange_block", 1 << 34)
-    keep, block = tie(keep, block)
-    up_own = jax.ShapeDtypeStruct((128, 2048), f32)
-    up_own = vmem_call(functools.partial(arrange_kernel, 0), up_own, (ids, keep, traded), "arrange_up", 1 << 33)
+    traded = lax.ppermute(give, "xl", SWAP)
+    out = [jax.ShapeDtypeStruct((128, 2048), bf16), jax.ShapeDtypeStruct((128, 2048), f32)]
+    block, up_own = vmem_call(arrange_kernel, out, (ids, early, late, keep, traded), "arrange", 1 << 34)
     sums_a, sums_b = tie(sums_a, sums_b)
     sums_a = lax.all_to_all(sums_a, COL, 0, 0)
 

time: 212 us -> 205 us (0.967)
  starting transfers between devices: 57.8 us -> 53.9 us
  waiting for transfers between devices: 53.7 us -> 50.1 us
    all_to_all x1, waiting for transfers between devices: 7.09 us -> 0.62 us  [spread(): return lax.all_to_all(jnp.broadcast_to(x[None], (n,) + x.shape), axes, 0, 0)]
    ppermute x1, waiting for transfers between devices: 4.9 us -> 1.09 us  [local(): late = lax.ppermute(late, ROW + COL, pairs_b[1])]
    all_to_all x1, waiting for transfers between devices: 3.05 us -> 6.39 us  [local(): sums_a = lax.all_to_all(sums_a, COL, 0, 0)]
    ppermute x3 -> x2, waiting for transfers between devices: 1.27 us -> 3.91 us  [the longest x1 3.91 us: row_sum(): return x + lax.ppermute(x, 'xh', SWAP)]
    ppermute x1, starting transfers between devices: 2.29 us -> 4.65 us  [local(): late = lax.ppermute(late, ROW + COL, pairs_b[1])]
    ppermute x1, starting transfers between devices: 2.27 us -> 0.09 us  [local(): traded = lax.ppermute(mixed[:, 128:], 'k', SWAP)]
    ppermute x3 -> x2, starting transfers between devices: 5.05 us -> 2.89 us  [the longest x1 2.55 us: row_sum(): return x + lax.ppermute(x, 'xh', SWAP)]
    pallas_call x4 -> x3, Pallas kernels: 5.14 us -> 4.76 us  [vmem_call(): pl.pallas_call(kernel, out_shape=out_shape, in_specs=[smem] + [vmem] * (l...]
  transfers between devices with their start and end apart: 29 -> 28, of which waited for: 16 -> 16; matrix products, arithmetic and copies ran while one was open for 1% -> 1% of each run, Pallas kernels for 9% -> 9%
where the time goes in v6:
time: 205 us; the launch traced here: 201 us
  starting transfers between devices  53.9 us (26%)
  waiting for transfers between devices  50.1 us (24%)
  blocking collectives  47.3 us (23%)
  Pallas kernels  27.3 us (13%)
  local copies, waits for them, and re-layouts  17.8 us (9%)
  other arithmetic  3.5 us (2%)
    all_to_all x1, blocking collectives, local(): mixed = lax.all_to_all(mixed, ('xl', 'z1', 'z0'), 0, 0)  23.7 us
    all_to_all x1, blocking collectives, local(): last = lax.all_to_all(last, ('y1', 'y0', 'xh', 'xl'), 0, 0)  23.6 us
    unnamed x43, local copies, waits for them, and re-layouts  14.1 us
    pallas_call x2, Pallas kernels, gram_part(): call(functools.partial(gram_kernel, first), out, 0, 'gram_part', pl.ANY,...  11.6 us
    ppermute x5, starting transfers between devices, trade(): return [lax.ppermute(x, axis, SWAP) for x in blocks]  8.23 us
    all_to_all x1, starting transfers between devices, spread(): return lax.all_to_all(jnp.broadcast_to(x[None], (n,) + x.shape), axes, 0, 0)  7.77 us
    ppermute x6, waiting for transfers between devices, ring_near(): return [lax.ppermute(own, ring, AHEAD), lax.ppermute(own, ring, BACK)]  7.21 us
    ppermute x1, starting transfers between devices, local(): other_a = lax.ppermute(send_a.reshape(256, 1024), ROW + COL, pairs_a)  6.99 us
  transfers between devices with their start and end apart: 28, of which 16 were waited for; matrix products, arithmetic and copies ran while one was open for 1% of the time, Pallas kernels for 9%

profile of v6, /device:TPU:9, one launch (start us, length us, event | category | flops | bytes accessed | tf_op | source)
XLA Modules:
  0.0 201.0 jit_solution(5544817165974127972)
XLA Ops:
  0.6 1.4 fusion.5
  2.4 2.5 %collective-permute-start.1 = (f32[2,1024]{1,0:T(2,128)S(1)}, f32[2,1024]{1,0:T(2,128)S(1)}, u32[]{:S(2)}, u32[]{:S(2)}) collective-permute-start(f32[2,1024]{1,0:T(2,128)S(1)} %pad_maximum_fusion.3), channel_id=1, source_target_pairs={{0,64},{32,96},{64,0},{96,32},{1,65},{33,97},{65,1},{97,33},{2,66}... | collective-permute-start | bytes 24584 | tf_op jit(solution)/shard_map/ppermute | solution.py:385
  4.9 1.6 collective-permute-start
  7.3 7.8 %all-to-all-start = ((f32[16,2,2048]{2,1,0:T(2,128)}), f32[16,2,2048]{2,1,0:T(2,128)S(1)}, u32[]{:S(2)}, u32[]{:S(2)}) async-start(f32[16,2,2048]{2,1,0:T(2,128)} %broadcast_in_dim.2), calls=%async_computation | async-start | bytes 524288 | tf_op jit(solution)/shard_map/all_to_all | solution.py:32
  15.1 2.6 %collective-permute-start.3 = (f32[2,1024]{1,0:T(2,128)S(1)}, f32[2,1024]{1,0:T(2,128)S(1)}, u32[]{:S(2)}, u32[]{:S(2)}) collective-permute-start(f32[2,1024]{1,0:T(2,128)S(1)} %add_add_fusion), channel_id=1, source_target_pairs={{0,16},{16,0},{1,17},{17,1},{2,18},{18,2},{3,19},{19,3},{4,20},{20... | collective-permute-start | bytes 24584 | tf_op jit(solution)/shard_map/ppermute | solution.py:386
  17.7 3.9 %collective-permute-done.3 = f32[2,1024]{1,0:T(2,128)S(1)} collective-permute-done((f32[2,1024]{1,0:T(2,128)S(1)}, f32[2,1024]{1,0:T(2,128)S(1)}, u32[]{:S(2)}, u32[]{:S(2)}) %collective-permute-start.3) | collective-permute-done | bytes 8224 | tf_op jit(solution)/shard_map/ppermute | solution.py:386
  22.9 1.1 constant_dynamic-slice_fusion.1
  25.1 1.5 collective-permute-start.7
  26.6 4.4 %collective-permute-done.4 = bf16[128,1024]{1,0:T(8,128)(2,1)S(1)} collective-permute-done((bf16[128,1024]{1,0:T(8,128)(2,1)S(1)}, bf16[128,1024]{1,0:T(8,128)(2,1)S(1)}, u32[]{:S(2)}, u32[]{:S(2)}) %collective-permute-start.4) | collective-permute-done | bytes 262176 | tf_op jit(solution)/shard_map/ppermute | solution.py:406
  31.1 2.5 %collective-permute-start.9 = (bf16[256,1024]{1,0:T(8,128)(2,1)S(1)}, bf16[256,1024]{1,0:T(8,128)(2,1)}, u32[]{:S(2)}, u32[]{:S(2)}) collective-permute-start(bf16[256,1024]{1,0:T(8,128)(2,1)S(1)} %multiply_convert_fusion.1.refs_0_.half), channel_id=1, source_target_pairs={{0,16},{16,0},{1,17},{17,1},{2,18},{18,2},{3,19},{19,3},{4,20},{20... | collective-permute-start | bytes 1572872 | tf_op jit(solution)/shard_map/ppermute | solution.py:99
  33.6 2.6 %collective-permute-start.6 = (bf16[256,1024]{1,0:T(8,128)(2,1)S(1)}, bf16[256,1024]{1,0:T(8,128)(2,1)}, u32[]{:S(2)}, u32[]{:S(2)}) collective-permute-start(bf16[256,1024]{1,0:T(8,128)(2,1)S(1)} %pad_maximum_fusion.refs_0_), channel_id=1, source_target_pairs={{0,6},{2,0},{4,2},{6,4},{1,7},{3,1},{5,3},{7,5},{8,14},{10,8},{12,... | collective-permute-start | bytes 1572872 | tf_op jit(solution)/shard_map/ppermute | solution.py:95
  36.2 1.6 collective-permute-done.8.refs_2_
  38.2 6.1 %collective-permute-done.9.refs_4_ = bf16[256,1024]{1,0:T(8,128)(2,1)} collective-permute-done((bf16[256,1024]{1,0:T(8,128)(2,1)S(1)}, bf16[256,1024]{1,0:T(8,128)(2,1)}, u32[]{:S(2)}, u32[]{:S(2)}) %collective-permute-start.9) | collective-permute-done | bytes 524320 | tf_op jit(solution)/shard_map/ppermute | solution.py:99
  44.3 2.0 collective-permute-done.6.refs_2_
  46.3 3.2 %collective-permute-done.5.refs_1_ = bf16[256,1024]{1,0:T(8,128)(2,1)} collective-permute-done((bf16[256,1024]{1,0:T(8,128)(2,1)S(1)}, bf16[256,1024]{1,0:T(8,128)(2,1)}, u32[]{:S(2)}, u32[]{:S(2)}) %collective-permute-start.5) | collective-permute-done | bytes 524320 | tf_op jit(solution)/shard_map/ppermute | solution.py:95
  49.6 1.1 broadcast_select_fusion
  51.0 1.5 collective-permute-start.15
  52.5 6.7 %collective-permute-done.10.refs_3_ = bf16[256,1024]{1,0:T(8,128)(2,1)S(1)} collective-permute-done((bf16[256,1024]{1,0:T(8,128)(2,1)S(1)}, bf16[256,1024]{1,0:T(8,128)(2,1)S(1)}, u32[]{:S(2)}, u32[]{:S(2)}) %collective-permute-start.10) | collective-permute-done | bytes 524320 | tf_op jit(solution)/shard_map/ppermute | solution.py:414
  59.2 4.3 %collective-permute-start.14 = (bf16[256,1024]{1,0:T(8,128)(2,1)S(1)}, bf16[256,1024]{1,0:T(8,128)(2,1)S(1)}, u32[]{:S(2)}, u32[]{:S(2)}) collective-permute-start(bf16[256,1024]{1,0:T(8,128)(2,1)S(1)} %collective-permute-done.10.refs_3_), channel_id=1, source_target_pairs={{0,1},{1,0},{2,3},{3,2},{4,5},{5,4},{6,7},{7,6},{8,9},{9,8},{10,11... | collective-permute-start | bytes 1572872 | tf_op jit(solution)/shard_map/ppermute | solution.py:99
  67.3 1.5 collective-permute-start.18
  70.6 1.0 copy-done.9
  71.6 5.4 %gram_part.2 = (bf16[8,2,256,128]{3,2,1,0:T(8,128)(2,1)S(1)}, bf16[2,128,1024]{2,1,0:T(8,128)(2,1)}) custom-call(s32[6]{0:T(128)S(1)} %pad_add_fusion.1.ids, bf16[256,1024]{1,0:T(8,128)(2,1)S(1)} %pad_maximum_fusion.refs_0_, bf16[256,1024]{1,0:T(8,128)(2,1)} %collective-permute-done.5.refs_1_, bf16[256,1024]{1,0:T(8,128)(2,1)} %collective-permute-done.6.refs_2_, ...), custom_call_target="tpu_custom_call" | custom-call | flops 1073741824 | bytes 4194304 | tf_op jit(solution)/shard_map/gram_part/pallas_call | solution.py:183
  78.0 1.0 collective-permute-done.17.refs_3_
  79.0 2.4 %collective-permute-done.18.refs_7_ = bf16[256,1024]{1,0:T(8,128)(2,1)} collective-permute-done((bf16[256,1024]{1,0:T(8,128)(2,1)}, bf16[256,1024]{1,0:T(8,128)(2,1)}, u32[]{:S(2)}, u32[]{:S(2)}) %collective-permute-start.18) | collective-permute-done | bytes 524320 | tf_op jit(solution)/shard_map/ppermute | solution.py:419
  81.4 7.0 %collective-permute-start.20 = (bf16[256,1024]{1,0:T(8,128)(2,1)}, bf16[256,1024]{1,0:T(8,128)(2,1)}, u32[]{:S(2)}, u32[]{:S(2)}) collective-permute-start(bf16[256,1024]{1,0:T(8,128)(2,1)} %bitcast.19), channel_id=1, source_target_pairs={{0,0},{13,1},{18,2},{31,3},{39,4},{42,5},{53,6},{56,7},{66,8},{79,... | collective-permute-start | bytes 1572872 | tf_op jit(solution)/shard_map/ppermute | solution.py:425
  89.2 4.4 %all-to-all-start.1 = ((bf16[16,256,128]{2,1,0:T(8,128)(2,1)}), bf16[16,256,128]{2,1,0:T(8,128)(2,1)}, u32[]{:S(2)}, u32[]{:S(2)}) async-start(bf16[16,256,128]{2,1,0:T(8,128)(2,1)} %bitcast.30), calls=%async_computation.1 | async-start | bytes 2097152 | tf_op jit(solution)/shard_map/all_to_all | solution.py:426
  93.7 1.0 copy-done.3
  94.7 6.2 %gram_part.3 = (bf16[8,128,256]{2,1,0:T(8,128)(2,1)S(1)}, bf16[8,128,256]{2,1,0:T(8,128)(2,1)}, bf16[128,1024]{1,0:T(8,128)(2,1)}, bf16[128,1024]{1,0:T(8,128)(2,1)}) custom-call(s32[11]{0:T(128)S(1)} %pad_add_fusion.2.ids, bf16[256,1024]{1,0:T(8,128)(2,1)S(1)} %multiply_convert_fusion.1.refs_0_.half, bf16[256,1024]{1,0:T(8,128)(2,1)} %collective-permute-done.7.refs_1_, ...), custom_call_target="tpu_custom_call" | custom-call | flops 1048576 | bytes 4096 | tf_op jit(solution)/shard_map/gram_part/pallas_call | solution.py:183
  101.7 2.4 %collective-permute-start.21 = (bf16[128,1024]{1,0:T(8,128)(2,1)}, bf16[128,1024]{1,0:T(8,128)(2,1)S(1)}, u32[]{:S(2)}, u32[]{:S(2)}) collective-permute-start(bf16[128,1024]{1,0:T(8,128)(2,1)} %get-tuple-element.60), channel_id=1, source_target_pairs={{0,0},{97,1},{64,2},{33,3},{32,4},{65,5},{96,6},{1,7},{16,8},{113,... | collective-permute-start | bytes 786440 | tf_op jit(solution)/shard_map/ppermute | solution.py:431
  104.7 1.2 partner.1
  105.8 6.4 %all-to-all-done.1.received = bf16[16,256,128]{2,1,0:T(8,128)(2,1)} async-done(((bf16[16,256,128]{2,1,0:T(8,128)(2,1)}), bf16[16,256,128]{2,1,0:T(8,128)(2,1)}, u32[]{:S(2)}, u32[]{:S(2)}) %all-to-all-start.1) | async-done | bytes 1048608 | tf_op jit(solution)/shard_map/all_to_all | solution.py:426
  112.2 1.0 copy-done.16
  113.3 1.6 blend.1
  114.9 2.0 collective-permute-done.21.same
  116.9 23.7 %all_to_all.25.mixed = bf16[8,256,256]{2,1,0:T(8,128)(2,1)S(1)} all-to-all(bf16[8,256,256]{2,1,0:T(8,128)(2,1)S(1)} %blend.1), channel_id=1, replica_groups=mesh['y1'=2,'y0'=2,'xh'=2,'xl'=2,'z1'=2,'z0'=2,'k'=2] {'xl','z1','z0'}, dimensions={0} | all-to-all | bytes 2097152 | tf_op jit(solution)/shard_map/all_to_all | solution.py:433
  140.7 1.9 collective-permute-done.22.traded
  142.6 3.3 %second_view.1 = (f32[256,1024]{1,0:T(8,128)S(1)}, bf16[16,160,256]{2,1,0:T(8,128)(2,1)S(1)}) custom-call(s32[11]{0:T(128)S(1)} %pad_add_fusion.2.ids, bf16[8,256,256]{2,1,0:T(8,128)(2,1)S(1)} %all_to_all.25.mixed, bf16[8,128,256]{2,1,0:T(8,128)(2,1)S(1)} %collective-permute-done.22.traded, f32[2,1024]{1,0:T(2,128)S(1)} %partner.1, ...), custom_call_target="tpu_custom_call" | custom-call | flops 1073741824 | bytes 4194304 | tf_op jit(solution)/shard_map/second_view/pallas_call | solution.py:265
  146.9 23.6 %all_to_all.26.last = bf16[16,160,256]{2,1,0:T(8,128)(2,1)S(1)} all-to-all(bf16[16,160,256]{2,1,0:T(8,128)(2,1)S(1)} %get-tuple-element.63), channel_id=1, replica_groups=mesh['y1'=2,'y0'=2,'xh'=2,'xl'=2,'z1'=2,'z0'=2,'k'=2] {'y1','y0','xh','xl'}, dimensions={0} | all-to-all | bytes 2621440 | tf_op jit(solution)/shard_map/all_to_all | solution.py:437
  170.5 3.9 %first_view.1 = (f32[128,1024]{1,0:T(8,128)S(1)}, bf16[128,1024]{1,0:T(8,128)(2,1)}, f32[16,5,1024]{2,1,0:T(8,128)S(1)}, f32[32,256]{1,0:T(8,128)S(1)}) custom-call(s32[6]{0:T(128)S(1)} %pad_add_fusion.1.ids, bf16[16,160,256]{2,1,0:T(8,128)(2,1)S(1)} %all_to_all.26.last, bf16[256,1024]{1,0:T(8,128)(2,1)S(1)} %pad_maximum_fusion.refs_0_, ...), custom_call_target="tpu_custom_call" | custom-call | flops 1048576 | bytes 4096 | tf_op jit(solution)/shard_map/first_view/pallas_call | solution.py:309
  176.3 4.6 %collective-permute-start.23 = (bf16[128,1024]{1,0:T(8,128)(2,1)}, bf16[128,1024]{1,0:T(8,128)(2,1)}, u32[]{:S(2)}, u32[]{:S(2)}) collective-permute-start(bf16[128,1024]{1,0:T(8,128)(2,1)} %get-tuple-element.70), channel_id=1, source_target_pairs={{1,0},{96,1},{65,2},{32,3},{33,4},{64,5},{97,6},{0,7},{17,8},{112,... | collective-permute-start | bytes 786440 | tf_op jit(solution)/shard_map/ppermute | solution.py:439
  181.0 3.5 %all-to-all-start.4 = ((f32[16,5,1024]{2,1,0:T(8,128)}), f32[16,5,1024]{2,1,0:T(8,128)S(1)}, u32[]{:S(2)}, u32[]{:S(2)}) async-start(f32[16,5,1024]{2,1,0:T(8,128)} %copy-done.14), calls=%async_computation.4 | async-start | bytes 1048576 | tf_op jit(solution)/shard_map/all_to_all | solution.py:446
  184.5 1.2 copy-done.13
  185.7 2.4 %finish_second.1 = f32[256,1024]{1,0:T(8,128)} custom-call(s32[3]{0:T(128)S(1)} %pad_add_fusion.ids, f32[32,256]{1,0:T(8,128)S(1)} %get-tuple-element.77.terms, f32[2,1024]{1,0:T(2,128)S(1)} %pad_maximum_fusion.4.scales, f32[256,1024]{1,0:T(8,128)S(1)} %copy-done.1, f32[256,1024]{1,0:T(8,128)S(1)} %copy-done.13, ...), custom_call_target="tpu_custom_call" | custom-call | flops 1048576 | bytes 65536 | tf_op jit(solution)/shard_map/finish_second/pallas_call | solution.py:321
  188.1 1.1 collective-permute-done.23.other
  189.2 1.2 arrange.1
  191.2 6.4 %all-to-all-done.4.sums = f32[16,5,1024]{2,1,0:T(8,128)S(1)} async-done(((f32[16,5,1024]{2,1,0:T(8,128)}), f32[16,5,1024]{2,1,0:T(8,128)S(1)}, u32[]{:S(2)}, u32[]{:S(2)}) %all-to-all-start.4) | async-done | bytes 327712 | tf_op jit(solution)/shard_map/all_to_all | solution.py:446
  197.6 1.0 copy-done.18
  198.6 2.2 %finish_first.1 = (f32[128,2048]{1,0:T(8,128)}, f32[1,1]{1,0:T(1,128)}) custom-call(s32[3]{0:T(128)S(1)} %pad_add_fusion.ids, f32[16,5,1024]{2,1,0:T(8,128)S(1)} %all-to-all-done.4.sums, f32[2,2048]{1,0:T(2,128)S(1)} %pad_maximum_fusion.2.scales, f32[128,2048]{1,0:T(8,128)S(1)} %copy-done, f32[128,2048]{1,0:T(8,128)S(1)} %get-tuple-element.73.up, ...), custom_call_target="tpu_custom_call" | custom-call | flops 1048576 | bytes 65536 | tf_op jit(solution)/shard_map/finish_first/pallas_call | solution.py:373
  (87 shorter events, 17.0 us)
Async XLA Ops:
  0.6 1.5 copy-start.1
  2.1 20.3 %copy-start = (f32[128,2048]{1,0:T(8,128)S(1)}, f32[128,2048]{1,0:T(8,128)}, u32[]{:S(2)}) copy-start(f32[128,2048]{1,0:T(8,128)} %view.2) | copy-start | bytes 3145732
  2.3 12.7 %collective-permute-start.2 = (f32[2,1024]{1,0:T(2,128)S(1)}, f32[2,1024]{1,0:T(2,128)S(1)}, u32[]{:S(2)}, u32[]{:S(2)}) collective-permute-start(f32[2,1024]{1,0:T(2,128)S(1)} %pad_maximum_fusion.3), channel_id=1, source_target_pairs={{0,96},{32,0},{64,32},{96,64},{1,97},{33,1},{65,33},{97,65},{2,98}... | collective-permute-start | bytes 24584 | tf_op jit(solution)/shard_map/ppermute | solution.py:385
  2.4 12.7 %collective-permute-start.1 = (f32[2,1024]{1,0:T(2,128)S(1)}, f32[2,1024]{1,0:T(2,128)S(1)}, u32[]{:S(2)}, u32[]{:S(2)}) collective-permute-start(f32[2,1024]{1,0:T(2,128)S(1)} %pad_maximum_fusion.3), channel_id=1, source_target_pairs={{0,64},{32,96},{64,0},{96,32},{1,65},{33,97},{65,1},{97,33},{2,66}... | collective-permute-start | bytes 24584 | tf_op jit(solution)/shard_map/ppermute | solution.py:385
  4.9 10.2 %collective-permute-start = (f32[2,1024]{1,0:T(2,128)S(1)}, f32[2,1024]{1,0:T(2,128)S(1)}, u32[]{:S(2)}, u32[]{:S(2)}) collective-permute-start(f32[2,1024]{1,0:T(2,128)S(1)} %pad_maximum_fusion.3), channel_id=1, source_target_pairs={{0,32},{32,64},{64,96},{96,0},{1,33},{33,65},{65,97},{97,1},{2,34}... | collective-permute-start | bytes 24584 | tf_op jit(solution)/shard_map/ppermute | solution.py:385
  7.3 14.9 %all-to-all-start = ((f32[16,2,2048]{2,1,0:T(2,128)}), f32[16,2,2048]{2,1,0:T(2,128)S(1)}, u32[]{:S(2)}, u32[]{:S(2)}) async-start(f32[16,2,2048]{2,1,0:T(2,128)} %broadcast_in_dim.2), calls=%async_computation | async-start | bytes 524288 | tf_op jit(solution)/shard_map/all_to_all | solution.py:32
  15.1 6.5 %collective-permute-start.3 = (f32[2,1024]{1,0:T(2,128)S(1)}, f32[2,1024]{1,0:T(2,128)S(1)}, u32[]{:S(2)}, u32[]{:S(2)}) collective-permute-start(f32[2,1024]{1,0:T(2,128)S(1)} %add_add_fusion), channel_id=1, source_target_pairs={{0,16},{16,0},{1,17},{17,1},{2,18},{18,2},{3,19},{19,3},{4,20},{20... | collective-permute-start | bytes 24584 | tf_op jit(solution)/shard_map/ppermute | solution.py:386
  24.0 6.9 %collective-permute-start.4 = (bf16[128,1024]{1,0:T(8,128)(2,1)S(1)}, bf16[128,1024]{1,0:T(8,128)(2,1)S(1)}, u32[]{:S(2)}, u32[]{:S(2)}) collective-permute-start(bf16[128,1024]{1,0:T(8,128)(2,1)S(1)} %bitcast.31), channel_id=1, source_target_pairs={{0,8},{8,0},{1,9},{9,1},{2,10},{10,2},{3,11},{11,3},{4,12},{12,4},... | collective-permute-start | bytes 786440 | tf_op jit(solution)/shard_map/ppermute | solution.py:406
  25.1 12.8 %collective-permute-start.8 = (bf16[256,1024]{1,0:T(8,128)(2,1)S(1)}, bf16[256,1024]{1,0:T(8,128)(2,1)}, u32[]{:S(2)}, u32[]{:S(2)}) collective-permute-start(bf16[256,1024]{1,0:T(8,128)(2,1)S(1)} %multiply_convert_fusion.1.refs_0_.half), channel_id=1, source_target_pairs={{0,96},{32,0},{64,32},{96,64},{1,97},{33,1},{65,33},{97,65},{2,98}... | collective-permute-start | bytes 1572872 | tf_op jit(solution)/shard_map/ppermute | solution.py:95
  25.1 13.1 %collective-permute-start.7 = (bf16[256,1024]{1,0:T(8,128)(2,1)S(1)}, bf16[256,1024]{1,0:T(8,128)(2,1)}, u32[]{:S(2)}, u32[]{:S(2)}) collective-permute-start(bf16[256,1024]{1,0:T(8,128)(2,1)S(1)} %multiply_convert_fusion.1.refs_0_.half), channel_id=1, source_target_pairs={{0,32},{32,64},{64,96},{96,0},{1,33},{33,65},{65,97},{97,1},{2,34}... | collective-permute-start | bytes 1572872 | tf_op jit(solution)/shard_map/ppermute | solution.py:95
  31.1 13.2 %collective-permute-start.9 = (bf16[256,1024]{1,0:T(8,128)(2,1)S(1)}, bf16[256,1024]{1,0:T(8,128)(2,1)}, u32[]{:S(2)}, u32[]{:S(2)}) collective-permute-start(bf16[256,1024]{1,0:T(8,128)(2,1)S(1)} %multiply_convert_fusion.1.refs_0_.half), channel_id=1, source_target_pairs={{0,16},{16,0},{1,17},{17,1},{2,18},{18,2},{3,19},{19,3},{4,20},{20... | collective-permute-start | bytes 1572872 | tf_op jit(solution)/shard_map/ppermute | solution.py:99
  33.6 12.7 %collective-permute-start.6 = (bf16[256,1024]{1,0:T(8,128)(2,1)S(1)}, bf16[256,1024]{1,0:T(8,128)(2,1)}, u32[]{:S(2)}, u32[]{:S(2)}) collective-permute-start(bf16[256,1024]{1,0:T(8,128)(2,1)S(1)} %pad_maximum_fusion.refs_0_), channel_id=1, source_target_pairs={{0,6},{2,0},{4,2},{6,4},{1,7},{3,1},{5,3},{7,5},{8,14},{10,8},{12,... | collective-permute-start | bytes 1572872 | tf_op jit(solution)/shard_map/ppermute | solution.py:95
  36.2 13.3 %collective-permute-start.5 = (bf16[256,1024]{1,0:T(8,128)(2,1)S(1)}, bf16[256,1024]{1,0:T(8,128)(2,1)}, u32[]{:S(2)}, u32[]{:S(2)}) collective-permute-start(bf16[256,1024]{1,0:T(8,128)(2,1)S(1)} %pad_maximum_fusion.refs_0_), channel_id=1, source_target_pairs={{0,2},{2,4},{4,6},{6,0},{1,3},{3,5},{5,7},{7,1},{8,10},{10,12},{12... | collective-permute-start | bytes 1572872 | tf_op jit(solution)/shard_map/ppermute | solution.py:95
  50.7 8.5 %collective-permute-start.10 = (bf16[256,1024]{1,0:T(8,128)(2,1)S(1)}, bf16[256,1024]{1,0:T(8,128)(2,1)S(1)}, u32[]{:S(2)}, u32[]{:S(2)}) collective-permute-start(bf16[256,1024]{1,0:T(8,128)(2,1)S(1)} %broadcast_select_fusion), channel_id=1, source_target_pairs={{0,2},{1,7},{2,4},{3,1},{4,6},{5,3},{6,0},{7,5},{8,10},{9,15},{10,... | collective-permute-start | bytes 1572872 | tf_op jit(solution)/shard_map/ppermute | solution.py:414
  51.0 13.8 %collective-permute-start.16 = (bf16[256,1024]{1,0:T(8,128)(2,1)}, bf16[256,1024]{1,0:T(8,128)(2,1)}, u32[]{:S(2)}, u32[]{:S(2)}) collective-permute-start(bf16[256,1024]{1,0:T(8,128)(2,1)} %collective-permute-done.9.refs_4_), channel_id=1, source_target_pairs={{0,96},{32,0},{64,32},{96,64},{1,97},{33,1},{65,33},{97,65},{2,98}... | collective-permute-start | bytes 1572872 | tf_op jit(solution)/shard_map/ppermute | solution.py:95
  51.0 14.7 %collective-permute-start.15 = (bf16[256,1024]{1,0:T(8,128)(2,1)}, bf16[256,1024]{1,0:T(8,128)(2,1)S(1)}, u32[]{:S(2)}, u32[]{:S(2)}) collective-permute-start(bf16[256,1024]{1,0:T(8,128)(2,1)} %collective-permute-done.9.refs_4_), channel_id=1, source_target_pairs={{0,32},{32,64},{64,96},{96,0},{1,33},{33,65},{65,97},{97,1},{2,34}... | collective-permute-start | bytes 1572872 | tf_op jit(solution)/shard_map/ppermute | solution.py:95
  59.2 7.3 %collective-permute-start.14 = (bf16[256,1024]{1,0:T(8,128)(2,1)S(1)}, bf16[256,1024]{1,0:T(8,128)(2,1)S(1)}, u32[]{:S(2)}, u32[]{:S(2)}) collective-permute-start(bf16[256,1024]{1,0:T(8,128)(2,1)S(1)} %collective-permute-done.10.refs_3_), channel_id=1, source_target_pairs={{0,1},{1,0},{2,3},{3,2},{4,5},{5,4},{6,7},{7,6},{8,9},{9,8},{10,11... | collective-permute-start | bytes 1572872 | tf_op jit(solution)/shard_map/ppermute | solution.py:99
  63.5 0.8 copy-start.5
  64.3 5.2 %collective-permute-start.11 = (bf16[256,1024]{1,0:T(8,128)(2,1)S(1)}, bf16[256,1024]{1,0:T(8,128)(2,1)}, u32[]{:S(2)}, u32[]{:S(2)}) collective-permute-start(bf16[256,1024]{1,0:T(8,128)(2,1)S(1)} %pad_maximum_fusion.refs_0_), channel_id=1, source_target_pairs={{0,1},{1,0},{2,3},{3,2},{4,5},{5,4},{6,7},{7,6},{8,9},{9,8},{10,11... | collective-permute-start | bytes 1572872 | tf_op jit(solution)/shard_map/ppermute | solution.py:99
  64.3 5.2 %collective-permute-start.12 = (bf16[256,1024]{1,0:T(8,128)(2,1)}, bf16[256,1024]{1,0:T(8,128)(2,1)}, u32[]{:S(2)}, u32[]{:S(2)}) collective-permute-start(bf16[256,1024]{1,0:T(8,128)(2,1)} %collective-permute-done.5.refs_1_), channel_id=1, source_target_pairs={{0,1},{1,0},{2,3},{3,2},{4,5},{5,4},{6,7},{7,6},{8,9},{9,8},{10,11... | collective-permute-start | bytes 1572872 | tf_op jit(solution)/shard_map/ppermute | solution.py:99
  64.8 4.7 %collective-permute-start.13 = (bf16[256,1024]{1,0:T(8,128)(2,1)}, bf16[256,1024]{1,0:T(8,128)(2,1)}, u32[]{:S(2)}, u32[]{:S(2)}) collective-permute-start(bf16[256,1024]{1,0:T(8,128)(2,1)} %collective-permute-done.6.refs_2_), channel_id=1, source_target_pairs={{0,1},{1,0},{2,3},{3,2},{4,5},{5,4},{6,7},{7,6},{8,9},{9,8},{10,11... | collective-permute-start | bytes 1572872 | tf_op jit(solution)/shard_map/ppermute | solution.py:99
  65.7 0.8 copy-start.2
  66.5 12.5 %collective-permute-start.17 = (bf16[256,1024]{1,0:T(8,128)(2,1)}, bf16[256,1024]{1,0:T(8,128)(2,1)}, u32[]{:S(2)}, u32[]{:S(2)}) collective-permute-start(bf16[256,1024]{1,0:T(8,128)(2,1)} %collective-permute-done.7.refs_1_), channel_id=1, source_target_pairs={{0,32},{32,64},{64,96},{96,0},{1,33},{33,65},{65,97},{97,1},{2,34}... | collective-permute-start | bytes 1572872 | tf_op jit(solution)/shard_map/ppermute | solution.py:417
  66.5 0.8 copy-start.8
  67.3 14.1 %collective-permute-start.18 = (bf16[256,1024]{1,0:T(8,128)(2,1)}, bf16[256,1024]{1,0:T(8,128)(2,1)}, u32[]{:S(2)}, u32[]{:S(2)}) collective-permute-start(bf16[256,1024]{1,0:T(8,128)(2,1)} %collective-permute-done.16.refs_6_), channel_id=1, source_target_pairs={{0,96},{32,0},{64,32},{96,64},{1,97},{33,1},{65,33},{97,65},{2,98}... | collective-permute-start | bytes 1572872 | tf_op jit(solution)/shard_map/ppermute | solution.py:419
  69.5 1.0 copy-start.6
  70.6 1.0 copy-start.9
  77.0 1.0 copy-start.11
  81.4 23.3 %collective-permute-start.20 = (bf16[256,1024]{1,0:T(8,128)(2,1)}, bf16[256,1024]{1,0:T(8,128)(2,1)}, u32[]{:S(2)}, u32[]{:S(2)}) collective-permute-start(bf16[256,1024]{1,0:T(8,128)(2,1)} %bitcast.19), channel_id=1, source_target_pairs={{0,0},{13,1},{18,2},{31,3},{39,4},{42,5},{53,6},{56,7},{66,8},{79,... | collective-permute-start | bytes 1572872 | tf_op jit(solution)/shard_map/ppermute | solution.py:425
  89.2 23.0 %all-to-all-start.1 = ((bf16[16,256,128]{2,1,0:T(8,128)(2,1)}), bf16[16,256,128]{2,1,0:T(8,128)(2,1)}, u32[]{:S(2)}, u32[]{:S(2)}) async-start(bf16[16,256,128]{2,1,0:T(8,128)(2,1)} %bitcast.30), calls=%async_computation.1 | async-start | bytes 2097152 | tf_op jit(solution)/shard_map/all_to_all | solution.py:426
  93.7 1.0 copy-start.3
  100.9 0.8 copy-start.15
  101.7 15.1 %collective-permute-start.21 = (bf16[128,1024]{1,0:T(8,128)(2,1)}, bf16[128,1024]{1,0:T(8,128)(2,1)S(1)}, u32[]{:S(2)}, u32[]{:S(2)}) collective-permute-start(bf16[128,1024]{1,0:T(8,128)(2,1)} %get-tuple-element.60), channel_id=1, source_target_pairs={{0,0},{97,1},{64,2},{33,3},{32,4},{65,5},{96,6},{1,7},{16,8},{113,... | collective-permute-start | bytes 786440 | tf_op jit(solution)/shard_map/ppermute | solution.py:431
  104.2 8.0 %collective-permute-start.19 = (bf16[8,128,256]{2,1,0:T(8,128)(2,1)}, bf16[8,128,256]{2,1,0:T(8,128)(2,1)}, u32[]{:S(2)}, u32[]{:S(2)}) collective-permute-start(bf16[8,128,256]{2,1,0:T(8,128)(2,1)} %get-tuple-element.57), channel_id=1, source_target_pairs={{0,1},{1,0},{2,3},{3,2},{4,5},{5,4},{6,7},{7,6},{8,9},{9,8},{10,11... | collective-permute-start | bytes 1572872 | tf_op jit(solution)/shard_map/ppermute | solution.py:428
  112.2 1.0 copy-start.16
  114.9 27.7 %copy-start.4 = (bf16[256,1024]{1,0:T(8,128)(2,1)S(1)}, bf16[256,1024]{1,0:T(8,128)(2,1)}, u32[]{:S(2)}) copy-start(bf16[256,1024]{1,0:T(8,128)(2,1)} %copy-done.2) | copy-start | bytes 1572868
  140.6 2.0 collective-permute-start.22
  145.9 1.0 copy-start.12
  146.9 23.6 %copy-start.7 = (bf16[256,1024]{1,0:T(8,128)(2,1)S(1)}, bf16[256,1024]{1,0:T(8,128)(2,1)}, u32[]{:S(2)}) copy-start(bf16[256,1024]{1,0:T(8,128)(2,1)} %copy-done.5) | copy-start | bytes 1572868
  146.9 23.6 %copy-start.10 = (bf16[256,1024]{1,0:T(8,128)(2,1)S(1)}, bf16[256,1024]{1,0:T(8,128)(2,1)}, u32[]{:S(2)}) copy-start(bf16[256,1024]{1,0:T(8,128)(2,1)} %copy-done.8) | copy-start | bytes 1572868
  175.1 0.8 copy-start.19
  175.9 12.1 %collective-permute-start.24 = (bf16[128,1024]{1,0:T(8,128)(2,1)}, bf16[128,1024]{1,0:T(8,128)(2,1)}, u32[]{:S(2)}, u32[]{:S(2)}) collective-permute-start(bf16[128,1024]{1,0:T(8,128)(2,1)} %get-tuple-element.72), channel_id=1, source_target_pairs={{0,8},{8,0},{1,9},{9,1},{2,10},{10,2},{3,11},{11,3},{4,12},{12,4},... | collective-permute-start | bytes 786440 | tf_op jit(solution)/shard_map/ppermute | solution.py:442
  176.3 12.9 %collective-permute-start.23 = (bf16[128,1024]{1,0:T(8,128)(2,1)}, bf16[128,1024]{1,0:T(8,128)(2,1)}, u32[]{:S(2)}, u32[]{:S(2)}) collective-permute-start(bf16[128,1024]{1,0:T(8,128)(2,1)} %get-tuple-element.70), channel_id=1, source_target_pairs={{1,0},{96,1},{65,2},{32,3},{33,4},{64,5},{97,6},{0,7},{17,8},{112,... | collective-permute-start | bytes 786440 | tf_op jit(solution)/shard_map/ppermute | solution.py:439
  181.0 16.6 %all-to-all-start.4 = ((f32[16,5,1024]{2,1,0:T(8,128)}), f32[16,5,1024]{2,1,0:T(8,128)S(1)}, u32[]{:S(2)}, u32[]{:S(2)}) async-start(f32[16,5,1024]{2,1,0:T(8,128)} %copy-done.14), calls=%async_computation.4 | async-start | bytes 1048576 | tf_op jit(solution)/shard_map/all_to_all | solution.py:446
  184.5 1.2 copy-start.13
  185.7 3.5 %copy-start.20 = (f32[128,1024]{1,0:T(8,128)S(1)}, f32[128,1024]{1,0:T(8,128)}, u32[]{:S(2)}) copy-start(f32[128,1024]{1,0:T(8,128)} %copy-done.19) | copy-start | bytes 1572868
  190.4 0.8 copy-start.17
  197.6 1.0 copy-start.18
  (1 other events, 0.8 us)

commit v7 on v5

--- a/solution.py
+++ b/solution.py
@@ -292,18 +292,19 @@
         miss = 1.0 - corr
         loss = loss + miss * miss - off_weight * corr * corr
     sums.append(jnp.concatenate([loss, jnp.zeros((1, 768), f32)], axis=1))
-    sums.append(jnp.concatenate([terms[8 * j + 2 : 8 * j + 3] for j in range(4)], axis=1))
-    sums.append(jnp.concatenate(products, axis=1))
-    for i in range(16):
-        for j in range(5):
-            out[i, j : j + 1, :] = sums[j]
+    pair = [jnp.concatenate([terms[8 * j + 2 : 8 * j + 3] for j in range(4)], axis=1), jnp.concatenate(products, axis=1)]
+    for half in range(2):
+        sums += [jnp.where(ids[1] == half, x, 0.0) for x in pair]
+    sums.append(jnp.zeros((1, 1024), f32))
+    for j in range(8):
+        out[j : j + 1, :] = sums[j]
 
 
 def first_view(ids, last, blocks):
     out = [
         jax.ShapeDtypeStruct((128, 1024), f32),
         jax.ShapeDtypeStruct((128, 1024), bf16),
-        jax.ShapeDtypeStruct((16, 5, 1024), f32),
+        jax.ShapeDtypeStruct((8, 1024), f32),
         jax.ShapeDtypeStruct((32, 256), f32),
     ]
     return call(first_kernel, out, 1, "first_view", flops=1 << 20)(ids, last, *blocks)
@@ -354,13 +355,12 @@
 def finish_kernel(ids, sums, scales, view, up, block, grad, loss):
     row = ids[2]
     loss[0, 0] = jnp.sum(sums[:, 2, :]) / FEAT
+    partner = sums[row]
     for half in range(2):
         columns = slice(1024 * half, 1024 * (half + 1))
-        total = sums[8 * half]
-        for i in range(1, 8):
-            total = total + sums[8 * half + i]
-        partner = sums[2 * row + half]
-        diag, first, second = finish(total[0:1], total[1:2], partner[3:4], partner[4:5], BATCH)
+        total = sums[4 * half] + sums[4 * half + 1] + sums[4 * half + 2] + sums[4 * half + 3]
+        rows = [partner[3 + 2 * half : 4 + 2 * half], partner[4 + 2 * half : 5 + 2 * half]]
+        diag, first, second = finish(total[0:1], total[1:2], *rows, BATCH)
         mean, inv = scales[0:1, columns], scales[1:2, columns]
         norm = (view[:, columns] - mean) * inv
         grad[:, columns] = inv * (up[:, columns] + diag * block[:, columns].astype(f32) - first - norm * second)
@@ -381,8 +381,8 @@
 
 
 def row_sum(x):
-    x = x + lax.ppermute(x, "xh", SWAP)
-    return x + sum(lax.ppermute(x, ("y1", "y0"), [(i, (i + step) % 4) for i in range(4)]) for step in (1, 2, 3))
+    x = x + sum(lax.ppermute(x, ("y1", "y0"), [(i, (i + step) % 4) for i in range(4)]) for step in (1, 2, 3))
+    return x + lax.ppermute(x, "xh", SWAP)
 
 
 def local(view_a, view_b):
@@ -438,14 +438,14 @@
     late = lax.ppermute(late, ROW + COL, pairs_b[1])
 
     keep, give, sums_a, sums_b = first_view(ids_a, last, blocks_a)
-    traded = lax.ppermute(lax.ppermute(give, ("xl", "k"), [(i, 3 - i) for i in range(4)]), "k", SWAP)
+    traded = lax.ppermute(give, "xl", SWAP)
     block = jax.ShapeDtypeStruct((128, 2048), bf16)
     block = vmem_call(functools.partial(arrange_kernel, 1), block, (ids, early, late), "arrange_block", 1 << 34)
     keep, block = tie(keep, block)
     up_own = jax.ShapeDtypeStruct((128, 2048), f32)
     up_own = vmem_call(functools.partial(arrange_kernel, 0), up_own, (ids, keep, traded), "arrange_up", 1 << 33)
     sums_a, sums_b = tie(sums_a, sums_b)
-    sums_a = lax.all_to_all(sums_a, COL, 0, 0)
+    sums_a = spread(sums_a + lax.ppermute(sums_a, "k", SWAP), ("xl", "z1", "z0"), 8)
 
     args = (ids, sums_b, jnp.stack([mean_b, inv_b]), view_b, up_b, other_a)
     grad_b = vmem_call(finish_second_kernel, jax.ShapeDtypeStruct((256, 1024), f32), args, "finish_second", 1 << 20)

time: 212 us -> 198 us (0.934)
  waiting for transfers between devices: 53.7 us -> 46.2 us
  starting transfers between devices: 57.8 us -> 53.5 us
  local copies, waits for them, and re-layouts: 17.8 us -> 14.7 us
    ppermute x1, waiting for transfers between devices: 4.9 us -> 0.01 us  [local(): late = lax.ppermute(late, ROW + COL, pairs_b[1])]
    all_to_all x1 -> x0, starting transfers between devices: 4.32 us -> none  [local(): sums_a = lax.all_to_all(sums_a, COL, 0, 0)]
    unnamed x43 -> x37, local copies, waits for them, and re-layouts: 14.1 us -> 10.3 us
    all_to_all x1 -> x0, waiting for transfers between devices: 3.05 us -> none  [local(): sums_a = lax.all_to_all(sums_a, COL, 0, 0)]
    all_to_all x1 -> x2, waiting for transfers between devices: 7.09 us -> 4.21 us  [spread(): return lax.all_to_all(jnp.broadcast_to(x[None], (n,) + x.shape), axes, 0, 0)]
    ppermute x3, waiting for transfers between devices: 1.27 us -> 3.92 us  [the longest x1 3.91 us: row_sum(): return x + lax.ppermute(x, 'xh', SWAP)]
    all_to_all x1 -> x2, starting transfers between devices: 8.92 us -> 11.4 us  [spread(): return lax.all_to_all(jnp.broadcast_to(x[None], (n,) + x.shape), axes, 0, 0)]
    ppermute x3, starting transfers between devices: 5.05 us -> 2.64 us  [the longest x1 2.55 us: row_sum(): return x + lax.ppermute(x, 'xh', SWAP)]
  transfers between devices with their start and end apart: 29 -> 29, of which waited for: 16 -> 15; matrix products, arithmetic and copies ran while one was open for 1% -> 2% of each run, Pallas kernels for 9% -> 11%
where the time goes in v7:
time: 198 us; the launch traced here: 194 us
  starting transfers between devices  53.5 us (27%)
  blocking collectives  47.3 us (24%)
  waiting for transfers between devices  46.2 us (23%)
  Pallas kernels  27.8 us (14%)
  local copies, waits for them, and re-layouts  14.7 us (7%)
  other arithmetic  3.5 us (2%)
    all_to_all x1, blocking collectives, local(): mixed = lax.all_to_all(mixed, ('xl', 'z1', 'z0'), 0, 0)  23.7 us
    all_to_all x1, blocking collectives, local(): last = lax.all_to_all(last, ('y1', 'y0', 'xh', 'xl'), 0, 0)  23.6 us
    pallas_call x2, Pallas kernels, gram_part(): call(functools.partial(gram_kernel, first), out, 0, 'gram_part', pl.ANY,...  11.6 us
    all_to_all x2, starting transfers between devices, spread(): return lax.all_to_all(jnp.broadcast_to(x[None], (n,) + x.shape), axes, 0, 0)  11.4 us
    unnamed x37, local copies, waits for them, and re-layouts  10.3 us
    ppermute x5, starting transfers between devices, trade(): return [lax.ppermute(x, axis, SWAP) for x in blocks]  8.22 us
    ppermute x6, waiting for transfers between devices, ring_near(): return [lax.ppermute(own, ring, AHEAD), lax.ppermute(own, ring, BACK)]  7.21 us
    ppermute x1, starting transfers between devices, local(): other_a = lax.ppermute(send_a.reshape(256, 1024), ROW + COL, pairs_a)  6.99 us
  transfers between devices with their start and end apart: 29, of which 15 were waited for; matrix products, arithmetic and copies ran while one was open for 2% of the time, Pallas kernels for 11%

profile of v7, /device:TPU:9, one launch (start us, length us, event | category | flops | bytes accessed | tf_op | source)
XLA Modules:
  0.0 194.2 jit_solution(81913774285661876)
XLA Ops:
  0.6 1.4 fusion.5
  2.4 2.5 %collective-permute-start.1 = (f32[2,1024]{1,0:T(2,128)S(1)}, f32[2,1024]{1,0:T(2,128)S(1)}, u32[]{:S(2)}, u32[]{:S(2)}) collective-permute-start(f32[2,1024]{1,0:T(2,128)S(1)} %pad_maximum_fusion.3), channel_id=1, source_target_pairs={{0,64},{32,96},{64,0},{96,32},{1,65},{33,97},{65,1},{97,33},{2,66}... | collective-permute-start | bytes 24584 | tf_op jit(solution)/shard_map/ppermute | solution.py:384
  4.9 1.6 collective-permute-start
  7.3 7.8 %all-to-all-start = ((f32[16,2,2048]{2,1,0:T(2,128)}), f32[16,2,2048]{2,1,0:T(2,128)S(1)}, u32[]{:S(2)}, u32[]{:S(2)}) async-start(f32[16,2,2048]{2,1,0:T(2,128)} %broadcast_in_dim.4), calls=%async_computation | async-start | bytes 524288 | tf_op jit(solution)/shard_map/all_to_all | solution.py:32
  15.1 2.6 %collective-permute-start.3 = (f32[2,1024]{1,0:T(2,128)S(1)}, f32[2,1024]{1,0:T(2,128)S(1)}, u32[]{:S(2)}, u32[]{:S(2)}) collective-permute-start(f32[2,1024]{1,0:T(2,128)S(1)} %add_add_fusion), channel_id=1, source_target_pairs={{0,16},{16,0},{1,17},{17,1},{2,18},{18,2},{3,19},{19,3},{4,20},{20... | collective-permute-start | bytes 24584 | tf_op jit(solution)/shard_map/ppermute | solution.py:385
  17.7 3.9 %collective-permute-done.3 = f32[2,1024]{1,0:T(2,128)S(1)} collective-permute-done((f32[2,1024]{1,0:T(2,128)S(1)}, f32[2,1024]{1,0:T(2,128)S(1)}, u32[]{:S(2)}, u32[]{:S(2)}) %collective-permute-start.3) | collective-permute-done | bytes 8224 | tf_op jit(solution)/shard_map/ppermute | solution.py:385
  22.9 1.1 constant_dynamic-slice_fusion.1
  25.1 1.5 collective-permute-start.7
  26.6 4.4 %collective-permute-done.4 = bf16[128,1024]{1,0:T(8,128)(2,1)S(1)} collective-permute-done((bf16[128,1024]{1,0:T(8,128)(2,1)S(1)}, bf16[128,1024]{1,0:T(8,128)(2,1)S(1)}, u32[]{:S(2)}, u32[]{:S(2)}) %collective-permute-start.4) | collective-permute-done | bytes 262176 | tf_op jit(solution)/shard_map/ppermute | solution.py:405
  31.1 2.5 %collective-permute-start.9 = (bf16[256,1024]{1,0:T(8,128)(2,1)S(1)}, bf16[256,1024]{1,0:T(8,128)(2,1)}, u32[]{:S(2)}, u32[]{:S(2)}) collective-permute-start(bf16[256,1024]{1,0:T(8,128)(2,1)S(1)} %multiply_convert_fusion.1.refs_0_.half), channel_id=1, source_target_pairs={{0,16},{16,0},{1,17},{17,1},{2,18},{18,2},{3,19},{19,3},{4,20},{20... | collective-permute-start | bytes 1572872 | tf_op jit(solution)/shard_map/ppermute | solution.py:99
  33.6 2.6 %collective-permute-start.6 = (bf16[256,1024]{1,0:T(8,128)(2,1)S(1)}, bf16[256,1024]{1,0:T(8,128)(2,1)}, u32[]{:S(2)}, u32[]{:S(2)}) collective-permute-start(bf16[256,1024]{1,0:T(8,128)(2,1)S(1)} %pad_maximum_fusion.refs_0_), channel_id=1, source_target_pairs={{0,6},{2,0},{4,2},{6,4},{1,7},{3,1},{5,3},{7,5},{8,14},{10,8},{12,... | collective-permute-start | bytes 1572872 | tf_op jit(solution)/shard_map/ppermute | solution.py:95
  36.2 1.6 collective-permute-done.8.refs_2_
  38.2 6.1 %collective-permute-done.9.refs_4_ = bf16[256,1024]{1,0:T(8,128)(2,1)} collective-permute-done((bf16[256,1024]{1,0:T(8,128)(2,1)S(1)}, bf16[256,1024]{1,0:T(8,128)(2,1)}, u32[]{:S(2)}, u32[]{:S(2)}) %collective-permute-start.9) | collective-permute-done | bytes 524320 | tf_op jit(solution)/shard_map/ppermute | solution.py:99
  44.3 2.0 %collective-permute-done.6.refs_2_ = bf16[256,1024]{1,0:T(8,128)(2,1)} collective-permute-done((bf16[256,1024]{1,0:T(8,128)(2,1)S(1)}, bf16[256,1024]{1,0:T(8,128)(2,1)}, u32[]{:S(2)}, u32[]{:S(2)}) %collective-permute-start.6) | collective-permute-done | bytes 524320 | tf_op jit(solution)/shard_map/ppermute | solution.py:95
  46.3 3.2 %collective-permute-done.5.refs_1_ = bf16[256,1024]{1,0:T(8,128)(2,1)} collective-permute-done((bf16[256,1024]{1,0:T(8,128)(2,1)S(1)}, bf16[256,1024]{1,0:T(8,128)(2,1)}, u32[]{:S(2)}, u32[]{:S(2)}) %collective-permute-start.5) | collective-permute-done | bytes 524320 | tf_op jit(solution)/shard_map/ppermute | solution.py:95
  49.6 1.1 broadcast_select_fusion
  51.0 1.5 collective-permute-start.15
  52.5 6.7 %collective-permute-done.10.refs_3_ = bf16[256,1024]{1,0:T(8,128)(2,1)S(1)} collective-permute-done((bf16[256,1024]{1,0:T(8,128)(2,1)S(1)}, bf16[256,1024]{1,0:T(8,128)(2,1)S(1)}, u32[]{:S(2)}, u32[]{:S(2)}) %collective-permute-start.10) | collective-permute-done | bytes 524320 | tf_op jit(solution)/shard_map/ppermute | solution.py:413
  59.2 4.3 %collective-permute-start.14 = (bf16[256,1024]{1,0:T(8,128)(2,1)S(1)}, bf16[256,1024]{1,0:T(8,128)(2,1)S(1)}, u32[]{:S(2)}, u32[]{:S(2)}) collective-permute-start(bf16[256,1024]{1,0:T(8,128)(2,1)S(1)} %collective-permute-done.10.refs_3_), channel_id=1, source_target_pairs={{0,1},{1,0},{2,3},{3,2},{4,5},{5,4},{6,7},{7,6},{8,9},{9,8},{10,11... | collective-permute-start | bytes 1572872 | tf_op jit(solution)/shard_map/ppermute | solution.py:99
  67.3 1.5 collective-permute-start.18
  69.5 1.0 copy-done.6
  70.6 1.0 copy-done.9
  71.6 5.4 %gram_part.2 = (bf16[8,2,256,128]{3,2,1,0:T(8,128)(2,1)S(1)}, bf16[2,128,1024]{2,1,0:T(8,128)(2,1)}) custom-call(s32[6]{0:T(128)S(1)} %pad_add_fusion.1.ids, bf16[256,1024]{1,0:T(8,128)(2,1)S(1)} %pad_maximum_fusion.refs_0_, bf16[256,1024]{1,0:T(8,128)(2,1)} %collective-permute-done.5.refs_1_, bf16[256,1024]{1,0:T(8,128)(2,1)} %collective-permute-done.6.refs_2_, ...), custom_call_target="tpu_custom_call" | custom-call | flops 1073741824 | bytes 4194304 | tf_op jit(solution)/shard_map/gram_part/pallas_call | solution.py:183
  77.0 1.0 copy-done.11
  78.0 1.0 collective-permute-done.17.refs_3_
  79.0 2.4 %collective-permute-done.18.refs_7_ = bf16[256,1024]{1,0:T(8,128)(2,1)} collective-permute-done((bf16[256,1024]{1,0:T(8,128)(2,1)}, bf16[256,1024]{1,0:T(8,128)(2,1)}, u32[]{:S(2)}, u32[]{:S(2)}) %collective-permute-start.18) | collective-permute-done | bytes 524320 | tf_op jit(solution)/shard_map/ppermute | solution.py:418
  81.4 7.0 %collective-permute-start.20 = (bf16[256,1024]{1,0:T(8,128)(2,1)}, bf16[256,1024]{1,0:T(8,128)(2,1)}, u32[]{:S(2)}, u32[]{:S(2)}) collective-permute-start(bf16[256,1024]{1,0:T(8,128)(2,1)} %bitcast.19), channel_id=1, source_target_pairs={{0,0},{13,1},{18,2},{31,3},{39,4},{42,5},{53,6},{56,7},{66,8},{79,... | collective-permute-start | bytes 1572872 | tf_op jit(solution)/shard_map/ppermute | solution.py:424
  89.3 4.4 %all-to-all-start.1 = ((bf16[16,256,128]{2,1,0:T(8,128)(2,1)}), bf16[16,256,128]{2,1,0:T(8,128)(2,1)}, u32[]{:S(2)}, u32[]{:S(2)}) async-start(bf16[16,256,128]{2,1,0:T(8,128)(2,1)} %bitcast.30), calls=%async_computation.1 | async-start | bytes 2097152 | tf_op jit(solution)/shard_map/all_to_all | solution.py:425
  93.7 1.0 copy-done.3
  94.7 6.2 %gram_part.3 = (bf16[8,128,256]{2,1,0:T(8,128)(2,1)S(1)}, bf16[8,128,256]{2,1,0:T(8,128)(2,1)}, bf16[128,1024]{1,0:T(8,128)(2,1)}, bf16[128,1024]{1,0:T(8,128)(2,1)}) custom-call(s32[11]{0:T(128)S(1)} %pad_add_fusion.2.ids, bf16[256,1024]{1,0:T(8,128)(2,1)S(1)} %multiply_convert_fusion.1.refs_0_.half, bf16[256,1024]{1,0:T(8,128)(2,1)} %collective-permute-done.7.refs_1_, ...), custom_call_target="tpu_custom_call" | custom-call | flops 1048576 | bytes 4096 | tf_op jit(solution)/shard_map/gram_part/pallas_call | solution.py:183
  101.7 2.4 %collective-permute-start.21 = (bf16[128,1024]{1,0:T(8,128)(2,1)}, bf16[128,1024]{1,0:T(8,128)(2,1)S(1)}, u32[]{:S(2)}, u32[]{:S(2)}) collective-permute-start(bf16[128,1024]{1,0:T(8,128)(2,1)} %get-tuple-element.60), channel_id=1, source_target_pairs={{0,0},{97,1},{64,2},{33,3},{32,4},{65,5},{96,6},{1,7},{16,8},{113,... | collective-permute-start | bytes 786440 | tf_op jit(solution)/shard_map/ppermute | solution.py:430
  104.7 1.2 partner.1
  105.8 6.4 %all-to-all-done.1.received = bf16[16,256,128]{2,1,0:T(8,128)(2,1)} async-done(((bf16[16,256,128]{2,1,0:T(8,128)(2,1)}), bf16[16,256,128]{2,1,0:T(8,128)(2,1)}, u32[]{:S(2)}, u32[]{:S(2)}) %all-to-all-start.1) | async-done | bytes 1048608 | tf_op jit(solution)/shard_map/all_to_all | solution.py:425
  112.3 1.0 copy-done.15
  113.3 1.6 blend.1
  114.9 2.0 %collective-permute-done.21.same = bf16[128,1024]{1,0:T(8,128)(2,1)S(1)} collective-permute-done((bf16[128,1024]{1,0:T(8,128)(2,1)}, bf16[128,1024]{1,0:T(8,128)(2,1)S(1)}, u32[]{:S(2)}, u32[]{:S(2)}) %collective-permute-start.21) | collective-permute-done | bytes 262176 | tf_op jit(solution)/shard_map/ppermute | solution.py:430
  116.9 23.7 %all_to_all.25.mixed = bf16[8,256,256]{2,1,0:T(8,128)(2,1)S(1)} all-to-all(bf16[8,256,256]{2,1,0:T(8,128)(2,1)S(1)} %blend.1), channel_id=1, replica_groups=mesh['y1'=2,'y0'=2,'xh'=2,'xl'=2,'z1'=2,'z0'=2,'k'=2] {'xl','z1','z0'}, dimensions={0} | all-to-all | bytes 2097152 | tf_op jit(solution)/shard_map/all_to_all | solution.py:432
  140.7 1.9 collective-permute-done.22.traded
  142.6 3.3 %second_view.1 = (f32[256,1024]{1,0:T(8,128)S(1)}, bf16[16,160,256]{2,1,0:T(8,128)(2,1)S(1)}) custom-call(s32[11]{0:T(128)S(1)} %pad_add_fusion.2.ids, bf16[8,256,256]{2,1,0:T(8,128)(2,1)S(1)} %all_to_all.25.mixed, bf16[8,128,256]{2,1,0:T(8,128)(2,1)S(1)} %collective-permute-done.22.traded, f32[2,1024]{1,0:T(2,128)S(1)} %partner.1, ...), custom_call_target="tpu_custom_call" | custom-call | flops 1073741824 | bytes 4194304 | tf_op jit(solution)/shard_map/second_view/pallas_call | solution.py:265
  146.0 23.6 %all_to_all.26.last = bf16[16,160,256]{2,1,0:T(8,128)(2,1)S(1)} all-to-all(bf16[16,160,256]{2,1,0:T(8,128)(2,1)S(1)} %get-tuple-element.63), channel_id=1, replica_groups=mesh['y1'=2,'y0'=2,'xh'=2,'xl'=2,'z1'=2,'z0'=2,'k'=2] {'y1','y0','xh','xl'}, dimensions={0} | all-to-all | bytes 2621440 | tf_op jit(solution)/shard_map/all_to_all | solution.py:436
  169.5 4.4 %collective-permute-start.24 = (bf16[128,1024]{1,0:T(8,128)(2,1)}, bf16[128,1024]{1,0:T(8,128)(2,1)}, u32[]{:S(2)}, u32[]{:S(2)}) collective-permute-start(bf16[128,1024]{1,0:T(8,128)(2,1)} %get-tuple-element.71), channel_id=1, source_target_pairs={{1,0},{96,1},{65,2},{32,3},{33,4},{64,5},{97,6},{0,7},{17,8},{112,... | collective-permute-start | bytes 786440 | tf_op jit(solution)/shard_map/ppermute | solution.py:438
  174.0 3.8 %first_view.1 = (f32[128,1024]{1,0:T(8,128)S(1)}, bf16[128,1024]{1,0:T(8,128)(2,1)}, f32[8,1024]{1,0:T(8,128)S(1)}, f32[32,256]{1,0:T(8,128)S(1)}) custom-call(s32[6]{0:T(128)S(1)} %pad_add_fusion.1.ids, bf16[16,160,256]{2,1,0:T(8,128)(2,1)S(1)} %all_to_all.26.last, bf16[256,1024]{1,0:T(8,128)(2,1)S(1)} %pad_maximum_fusion.refs_0_, ...), custom_call_target="tpu_custom_call" | custom-call | flops 1048576 | bytes 4096 | tf_op jit(solution)/shard_map/first_view/pallas_call | solution.py:310
  177.9 2.4 %finish_second.1 = f32[256,1024]{1,0:T(8,128)} custom-call(s32[3]{0:T(128)S(1)} %pad_add_fusion.ids, f32[32,256]{1,0:T(8,128)S(1)} %get-tuple-element.77.terms, f32[2,1024]{1,0:T(2,128)S(1)} %pad_maximum_fusion.4.scales, f32[256,1024]{1,0:T(8,128)S(1)} %copy-done.1, f32[256,1024]{1,0:T(8,128)S(1)} %get-tuple-element.78.up, ...), custom_call_target="tpu_custom_call" | custom-call | flops 1048576 | bytes 65536 | tf_op jit(solution)/shard_map/finish_second/pallas_call | solution.py:322
  181.1 3.6 %all-to-all-start.4 = ((f32[8,8,1024]{2,1,0:T(8,128)}), f32[8,8,1024]{2,1,0:T(8,128)S(1)}, u32[]{:S(2)}, u32[]{:S(2)}) async-start(f32[8,8,1024]{2,1,0:T(8,128)} %broadcast_in_dim.5), calls=%async_computation.4 | async-start | bytes 524288 | tf_op jit(solution)/shard_map/all_to_all | solution.py:32
  184.7 1.1 arrange_block.1.block
  187.3 3.6 %all-to-all-done.4.sums = f32[8,8,1024]{2,1,0:T(8,128)S(1)} async-done(((f32[8,8,1024]{2,1,0:T(8,128)}), f32[8,8,1024]{2,1,0:T(8,128)S(1)}, u32[]{:S(2)}, u32[]{:S(2)}) %all-to-all-start.4) | async-done | bytes 262176 | tf_op jit(solution)/shard_map/all_to_all | solution.py:32
  190.8 1.0 copy-done.13
  191.9 2.2 %finish_first.1 = (f32[128,2048]{1,0:T(8,128)}, f32[1,1]{1,0:T(1,128)}) custom-call(s32[3]{0:T(128)S(1)} %pad_add_fusion.ids, f32[8,8,1024]{2,1,0:T(8,128)S(1)} %all-to-all-done.4.sums, f32[2,2048]{1,0:T(2,128)S(1)} %pad_maximum_fusion.2.scales, f32[128,2048]{1,0:T(8,128)S(1)} %copy-done, f32[128,2048]{1,0:T(8,128)S(1)} %arrange_up.1.up, ...), custom_call_target="tpu_custom_call" | custom-call | flops 1048576 | bytes 65536 | tf_op jit(solution)/shard_map/finish_first/pallas_call | solution.py:372
  (86 shorter events, 13.6 us)
Async XLA Ops:
  0.6 1.5 copy-start.1
  2.1 20.3 %copy-start = (f32[128,2048]{1,0:T(8,128)S(1)}, f32[128,2048]{1,0:T(8,128)}, u32[]{:S(2)}) copy-start(f32[128,2048]{1,0:T(8,128)} %view.2) | copy-start | bytes 3145732
  2.3 12.7 %collective-permute-start.2 = (f32[2,1024]{1,0:T(2,128)S(1)}, f32[2,1024]{1,0:T(2,128)S(1)}, u32[]{:S(2)}, u32[]{:S(2)}) collective-permute-start(f32[2,1024]{1,0:T(2,128)S(1)} %pad_maximum_fusion.3), channel_id=1, source_target_pairs={{0,96},{32,0},{64,32},{96,64},{1,97},{33,1},{65,33},{97,65},{2,98}... | collective-permute-start | bytes 24584 | tf_op jit(solution)/shard_map/ppermute | solution.py:384
  2.4 12.7 %collective-permute-start.1 = (f32[2,1024]{1,0:T(2,128)S(1)}, f32[2,1024]{1,0:T(2,128)S(1)}, u32[]{:S(2)}, u32[]{:S(2)}) collective-permute-start(f32[2,1024]{1,0:T(2,128)S(1)} %pad_maximum_fusion.3), channel_id=1, source_target_pairs={{0,64},{32,96},{64,0},{96,32},{1,65},{33,97},{65,1},{97,33},{2,66}... | collective-permute-start | bytes 24584 | tf_op jit(solution)/shard_map/ppermute | solution.py:384
  4.9 10.2 %collective-permute-start = (f32[2,1024]{1,0:T(2,128)S(1)}, f32[2,1024]{1,0:T(2,128)S(1)}, u32[]{:S(2)}, u32[]{:S(2)}) collective-permute-start(f32[2,1024]{1,0:T(2,128)S(1)} %pad_maximum_fusion.3), channel_id=1, source_target_pairs={{0,32},{32,64},{64,96},{96,0},{1,33},{33,65},{65,97},{97,1},{2,34}... | collective-permute-start | bytes 24584 | tf_op jit(solution)/shard_map/ppermute | solution.py:384
  7.3 14.9 %all-to-all-start = ((f32[16,2,2048]{2,1,0:T(2,128)}), f32[16,2,2048]{2,1,0:T(2,128)S(1)}, u32[]{:S(2)}, u32[]{:S(2)}) async-start(f32[16,2,2048]{2,1,0:T(2,128)} %broadcast_in_dim.4), calls=%async_computation | async-start | bytes 524288 | tf_op jit(solution)/shard_map/all_to_all | solution.py:32
  15.1 6.5 %collective-permute-start.3 = (f32[2,1024]{1,0:T(2,128)S(1)}, f32[2,1024]{1,0:T(2,128)S(1)}, u32[]{:S(2)}, u32[]{:S(2)}) collective-permute-start(f32[2,1024]{1,0:T(2,128)S(1)} %add_add_fusion), channel_id=1, source_target_pairs={{0,16},{16,0},{1,17},{17,1},{2,18},{18,2},{3,19},{19,3},{4,20},{20... | collective-permute-start | bytes 24584 | tf_op jit(solution)/shard_map/ppermute | solution.py:385
  24.0 6.9 %collective-permute-start.4 = (bf16[128,1024]{1,0:T(8,128)(2,1)S(1)}, bf16[128,1024]{1,0:T(8,128)(2,1)S(1)}, u32[]{:S(2)}, u32[]{:S(2)}) collective-permute-start(bf16[128,1024]{1,0:T(8,128)(2,1)S(1)} %bitcast.31), channel_id=1, source_target_pairs={{0,8},{8,0},{1,9},{9,1},{2,10},{10,2},{3,11},{11,3},{4,12},{12,4},... | collective-permute-start | bytes 786440 | tf_op jit(solution)/shard_map/ppermute | solution.py:405
  25.1 12.8 %collective-permute-start.8 = (bf16[256,1024]{1,0:T(8,128)(2,1)S(1)}, bf16[256,1024]{1,0:T(8,128)(2,1)}, u32[]{:S(2)}, u32[]{:S(2)}) collective-permute-start(bf16[256,1024]{1,0:T(8,128)(2,1)S(1)} %multiply_convert_fusion.1.refs_0_.half), channel_id=1, source_target_pairs={{0,96},{32,0},{64,32},{96,64},{1,97},{33,1},{65,33},{97,65},{2,98}... | collective-permute-start | bytes 1572872 | tf_op jit(solution)/shard_map/ppermute | solution.py:95
  25.1 13.1 %collective-permute-start.7 = (bf16[256,1024]{1,0:T(8,128)(2,1)S(1)}, bf16[256,1024]{1,0:T(8,128)(2,1)}, u32[]{:S(2)}, u32[]{:S(2)}) collective-permute-start(bf16[256,1024]{1,0:T(8,128)(2,1)S(1)} %multiply_convert_fusion.1.refs_0_.half), channel_id=1, source_target_pairs={{0,32},{32,64},{64,96},{96,0},{1,33},{33,65},{65,97},{97,1},{2,34}... | collective-permute-start | bytes 1572872 | tf_op jit(solution)/shard_map/ppermute | solution.py:95
  31.1 13.2 %collective-permute-start.9 = (bf16[256,1024]{1,0:T(8,128)(2,1)S(1)}, bf16[256,1024]{1,0:T(8,128)(2,1)}, u32[]{:S(2)}, u32[]{:S(2)}) collective-permute-start(bf16[256,1024]{1,0:T(8,128)(2,1)S(1)} %multiply_convert_fusion.1.refs_0_.half), channel_id=1, source_target_pairs={{0,16},{16,0},{1,17},{17,1},{2,18},{18,2},{3,19},{19,3},{4,20},{20... | collective-permute-start | bytes 1572872 | tf_op jit(solution)/shard_map/ppermute | solution.py:99
  33.6 12.7 %collective-permute-start.6 = (bf16[256,1024]{1,0:T(8,128)(2,1)S(1)}, bf16[256,1024]{1,0:T(8,128)(2,1)}, u32[]{:S(2)}, u32[]{:S(2)}) collective-permute-start(bf16[256,1024]{1,0:T(8,128)(2,1)S(1)} %pad_maximum_fusion.refs_0_), channel_id=1, source_target_pairs={{0,6},{2,0},{4,2},{6,4},{1,7},{3,1},{5,3},{7,5},{8,14},{10,8},{12,... | collective-permute-start | bytes 1572872 | tf_op jit(solution)/shard_map/ppermute | solution.py:95
  36.2 13.3 %collective-permute-start.5 = (bf16[256,1024]{1,0:T(8,128)(2,1)S(1)}, bf16[256,1024]{1,0:T(8,128)(2,1)}, u32[]{:S(2)}, u32[]{:S(2)}) collective-permute-start(bf16[256,1024]{1,0:T(8,128)(2,1)S(1)} %pad_maximum_fusion.refs_0_), channel_id=1, source_target_pairs={{0,2},{2,4},{4,6},{6,0},{1,3},{3,5},{5,7},{7,1},{8,10},{10,12},{12... | collective-permute-start | bytes 1572872 | tf_op jit(solution)/shard_map/ppermute | solution.py:95
  50.7 8.5 %collective-permute-start.10 = (bf16[256,1024]{1,0:T(8,128)(2,1)S(1)}, bf16[256,1024]{1,0:T(8,128)(2,1)S(1)}, u32[]{:S(2)}, u32[]{:S(2)}) collective-permute-start(bf16[256,1024]{1,0:T(8,128)(2,1)S(1)} %broadcast_select_fusion), channel_id=1, source_target_pairs={{0,2},{1,7},{2,4},{3,1},{4,6},{5,3},{6,0},{7,5},{8,10},{9,15},{10,... | collective-permute-start | bytes 1572872 | tf_op jit(solution)/shard_map/ppermute | solution.py:413
  51.0 13.8 %collective-permute-start.16 = (bf16[256,1024]{1,0:T(8,128)(2,1)}, bf16[256,1024]{1,0:T(8,128)(2,1)}, u32[]{:S(2)}, u32[]{:S(2)}) collective-permute-start(bf16[256,1024]{1,0:T(8,128)(2,1)} %collective-permute-done.9.refs_4_), channel_id=1, source_target_pairs={{0,96},{32,0},{64,32},{96,64},{1,97},{33,1},{65,33},{97,65},{2,98}... | collective-permute-start | bytes 1572872 | tf_op jit(solution)/shard_map/ppermute | solution.py:95
  51.0 14.7 %collective-permute-start.15 = (bf16[256,1024]{1,0:T(8,128)(2,1)}, bf16[256,1024]{1,0:T(8,128)(2,1)S(1)}, u32[]{:S(2)}, u32[]{:S(2)}) collective-permute-start(bf16[256,1024]{1,0:T(8,128)(2,1)} %collective-permute-done.9.refs_4_), channel_id=1, source_target_pairs={{0,32},{32,64},{64,96},{96,0},{1,33},{33,65},{65,97},{97,1},{2,34}... | collective-permute-start | bytes 1572872 | tf_op jit(solution)/shard_map/ppermute | solution.py:95
  59.2 7.3 %collective-permute-start.14 = (bf16[256,1024]{1,0:T(8,128)(2,1)S(1)}, bf16[256,1024]{1,0:T(8,128)(2,1)S(1)}, u32[]{:S(2)}, u32[]{:S(2)}) collective-permute-start(bf16[256,1024]{1,0:T(8,128)(2,1)S(1)} %collective-permute-done.10.refs_3_), channel_id=1, source_target_pairs={{0,1},{1,0},{2,3},{3,2},{4,5},{5,4},{6,7},{7,6},{8,9},{9,8},{10,11... | collective-permute-start | bytes 1572872 | tf_op jit(solution)/shard_map/ppermute | solution.py:99
  63.5 0.8 copy-start.5
  64.3 5.3 %collective-permute-start.11 = (bf16[256,1024]{1,0:T(8,128)(2,1)S(1)}, bf16[256,1024]{1,0:T(8,128)(2,1)}, u32[]{:S(2)}, u32[]{:S(2)}) collective-permute-start(bf16[256,1024]{1,0:T(8,128)(2,1)S(1)} %pad_maximum_fusion.refs_0_), channel_id=1, source_target_pairs={{0,1},{1,0},{2,3},{3,2},{4,5},{5,4},{6,7},{7,6},{8,9},{9,8},{10,11... | collective-permute-start | bytes 1572872 | tf_op jit(solution)/shard_map/ppermute | solution.py:99
  64.3 5.3 %collective-permute-start.12 = (bf16[256,1024]{1,0:T(8,128)(2,1)}, bf16[256,1024]{1,0:T(8,128)(2,1)}, u32[]{:S(2)}, u32[]{:S(2)}) collective-permute-start(bf16[256,1024]{1,0:T(8,128)(2,1)} %collective-permute-done.5.refs_1_), channel_id=1, source_target_pairs={{0,1},{1,0},{2,3},{3,2},{4,5},{5,4},{6,7},{7,6},{8,9},{9,8},{10,11... | collective-permute-start | bytes 1572872 | tf_op jit(solution)/shard_map/ppermute | solution.py:99
  64.8 4.7 %collective-permute-start.13 = (bf16[256,1024]{1,0:T(8,128)(2,1)}, bf16[256,1024]{1,0:T(8,128)(2,1)}, u32[]{:S(2)}, u32[]{:S(2)}) collective-permute-start(bf16[256,1024]{1,0:T(8,128)(2,1)} %collective-permute-done.6.refs_2_), channel_id=1, source_target_pairs={{0,1},{1,0},{2,3},{3,2},{4,5},{5,4},{6,7},{7,6},{8,9},{9,8},{10,11... | collective-permute-start | bytes 1572872 | tf_op jit(solution)/shard_map/ppermute | solution.py:99
  65.7 0.8 copy-start.2
  66.5 12.5 %collective-permute-start.17 = (bf16[256,1024]{1,0:T(8,128)(2,1)}, bf16[256,1024]{1,0:T(8,128)(2,1)}, u32[]{:S(2)}, u32[]{:S(2)}) collective-permute-start(bf16[256,1024]{1,0:T(8,128)(2,1)} %collective-permute-done.7.refs_1_), channel_id=1, source_target_pairs={{0,32},{32,64},{64,96},{96,0},{1,33},{33,65},{65,97},{97,1},{2,34}... | collective-permute-start | bytes 1572872 | tf_op jit(solution)/shard_map/ppermute | solution.py:416
  66.5 0.8 copy-start.8
  67.3 14.1 %collective-permute-start.18 = (bf16[256,1024]{1,0:T(8,128)(2,1)}, bf16[256,1024]{1,0:T(8,128)(2,1)}, u32[]{:S(2)}, u32[]{:S(2)}) collective-permute-start(bf16[256,1024]{1,0:T(8,128)(2,1)} %collective-permute-done.16.refs_6_), channel_id=1, source_target_pairs={{0,96},{32,0},{64,32},{96,64},{1,97},{33,1},{65,33},{97,65},{2,98}... | collective-permute-start | bytes 1572872 | tf_op jit(solution)/shard_map/ppermute | solution.py:418
  69.5 1.0 copy-start.6
  70.6 1.0 copy-start.9
  77.0 1.0 copy-start.11
  81.4 23.3 %collective-permute-start.20 = (bf16[256,1024]{1,0:T(8,128)(2,1)}, bf16[256,1024]{1,0:T(8,128)(2,1)}, u32[]{:S(2)}, u32[]{:S(2)}) collective-permute-start(bf16[256,1024]{1,0:T(8,128)(2,1)} %bitcast.19), channel_id=1, source_target_pairs={{0,0},{13,1},{18,2},{31,3},{39,4},{42,5},{53,6},{56,7},{66,8},{79,... | collective-permute-start | bytes 1572872 | tf_op jit(solution)/shard_map/ppermute | solution.py:424
  89.3 23.0 %all-to-all-start.1 = ((bf16[16,256,128]{2,1,0:T(8,128)(2,1)}), bf16[16,256,128]{2,1,0:T(8,128)(2,1)}, u32[]{:S(2)}, u32[]{:S(2)}) async-start(bf16[16,256,128]{2,1,0:T(8,128)(2,1)} %bitcast.30), calls=%async_computation.1 | async-start | bytes 2097152 | tf_op jit(solution)/shard_map/all_to_all | solution.py:425
  93.7 1.0 copy-start.3
  100.9 0.8 copy-start.14
  101.7 15.1 %collective-permute-start.21 = (bf16[128,1024]{1,0:T(8,128)(2,1)}, bf16[128,1024]{1,0:T(8,128)(2,1)S(1)}, u32[]{:S(2)}, u32[]{:S(2)}) collective-permute-start(bf16[128,1024]{1,0:T(8,128)(2,1)} %get-tuple-element.60), channel_id=1, source_target_pairs={{0,0},{97,1},{64,2},{33,3},{32,4},{65,5},{96,6},{1,7},{16,8},{113,... | collective-permute-start | bytes 786440 | tf_op jit(solution)/shard_map/ppermute | solution.py:430
  104.2 8.1 %collective-permute-start.19 = (bf16[8,128,256]{2,1,0:T(8,128)(2,1)}, bf16[8,128,256]{2,1,0:T(8,128)(2,1)}, u32[]{:S(2)}, u32[]{:S(2)}) collective-permute-start(bf16[8,128,256]{2,1,0:T(8,128)(2,1)} %get-tuple-element.57), channel_id=1, source_target_pairs={{0,1},{1,0},{2,3},{3,2},{4,5},{5,4},{6,7},{7,6},{8,9},{9,8},{10,11... | collective-permute-start | bytes 1572872 | tf_op jit(solution)/shard_map/ppermute | solution.py:427
  112.3 1.0 copy-start.15
  114.9 27.7 %copy-start.4 = (bf16[256,1024]{1,0:T(8,128)(2,1)S(1)}, bf16[256,1024]{1,0:T(8,128)(2,1)}, u32[]{:S(2)}) copy-start(bf16[256,1024]{1,0:T(8,128)(2,1)} %copy-done.2) | copy-start | bytes 1572868
  140.6 2.0 %collective-permute-start.22 = (bf16[8,128,256]{2,1,0:T(8,128)(2,1)S(1)}, bf16[8,128,256]{2,1,0:T(8,128)(2,1)S(1)}, u32[]{:S(2)}, u32[]{:S(2)}) collective-permute-start(bf16[8,128,256]{2,1,0:T(8,128)(2,1)S(1)} %slice.24), channel_id=1, source_target_pairs={{0,1},{1,0},{2,3},{3,2},{4,5},{5,4},{6,7},{7,6},{8,9},{9,8},{10,11... | collective-permute-start | bytes 1572872 | tf_op jit(solution)/shard_map/ppermute | solution.py:434
  145.9 28.0 %copy-start.7 = (bf16[256,1024]{1,0:T(8,128)(2,1)S(1)}, bf16[256,1024]{1,0:T(8,128)(2,1)}, u32[]{:S(2)}) copy-start(bf16[256,1024]{1,0:T(8,128)(2,1)} %copy-done.5) | copy-start | bytes 1572868
  145.9 28.0 %copy-start.10 = (bf16[256,1024]{1,0:T(8,128)(2,1)S(1)}, bf16[256,1024]{1,0:T(8,128)(2,1)}, u32[]{:S(2)}) copy-start(bf16[256,1024]{1,0:T(8,128)(2,1)} %copy-done.8) | copy-start | bytes 1572868
  169.5 15.2 %collective-permute-start.24 = (bf16[128,1024]{1,0:T(8,128)(2,1)}, bf16[128,1024]{1,0:T(8,128)(2,1)}, u32[]{:S(2)}, u32[]{:S(2)}) collective-permute-start(bf16[128,1024]{1,0:T(8,128)(2,1)} %get-tuple-element.71), channel_id=1, source_target_pairs={{1,0},{96,1},{65,2},{32,3},{33,4},{64,5},{97,6},{0,7},{17,8},{112,... | collective-permute-start | bytes 786440 | tf_op jit(solution)/shard_map/ppermute | solution.py:438
  177.8 2.5 %copy-start.16 = (f32[128,1024]{1,0:T(8,128)}, f32[128,1024]{1,0:T(8,128)S(1)}, u32[]{:S(2)}) copy-start(f32[128,1024]{1,0:T(8,128)S(1)} %get-tuple-element.72.same) | copy-start | bytes 1572868
  177.8 2.5 %collective-permute-start.23 = (f32[8,1024]{1,0:T(8,128)S(1)}, f32[8,1024]{1,0:T(8,128)S(1)}, u32[]{:S(2)}, u32[]{:S(2)}) collective-permute-start(f32[8,1024]{1,0:T(8,128)S(1)} %get-tuple-element.68), channel_id=1, source_target_pairs={{0,1},{1,0},{2,3},{3,2},{4,5},{5,4},{6,7},{7,6},{8,9},{9,8},{10,11... | collective-permute-start | bytes 98312 | tf_op jit(solution)/shard_map/ppermute | solution.py:448
  177.9 8.8 %collective-permute-start.25 = (bf16[128,1024]{1,0:T(8,128)(2,1)}, bf16[128,1024]{1,0:T(8,128)(2,1)S(1)}, u32[]{:S(2)}, u32[]{:S(2)}) collective-permute-start(bf16[128,1024]{1,0:T(8,128)(2,1)} %get-tuple-element.73), channel_id=1, source_target_pairs={{0,8},{8,0},{1,9},{9,1},{2,10},{10,2},{3,11},{11,3},{4,12},{12,4},... | collective-permute-start | bytes 786440 | tf_op jit(solution)/shard_map/ppermute | solution.py:441
  181.1 9.7 %all-to-all-start.4 = ((f32[8,8,1024]{2,1,0:T(8,128)}), f32[8,8,1024]{2,1,0:T(8,128)S(1)}, u32[]{:S(2)}, u32[]{:S(2)}) async-start(f32[8,8,1024]{2,1,0:T(8,128)} %broadcast_in_dim.5), calls=%async_computation.4 | async-start | bytes 524288 | tf_op jit(solution)/shard_map/all_to_all | solution.py:32
  184.7 1.9 copy-start.17
  185.8 0.8 copy-start.12
  190.8 1.0 copy-start.13

commit v8 on v7

--- a/solution.py
+++ b/solution.py
@@ -404,18 +404,18 @@
     parts_a = jnp.transpose(half_a.reshape(128, 2, 1024), (1, 0, 2))
     own_a = both(xl, pick(parts_a, xl), lax.ppermute(pick(parts_a, 1 - xl), "xl", SWAP), 0)
     near_b = ring_near(half_b, ys)
-    own_a, late_half_b = tie(own_a, half_b)
+    other_own_b = trade([half_b], "xh")
+    other_near_b = ring_near(other_own_b[0], ys)
     near_a = ring_near(own_a, zs)
     other_own_a = trade([own_a], "k")
-    other_own_b = trade([late_half_b], "xh")
-    *near_a, near_b[0], near_b[1], other_own_b[0] = tie(*near_a, *near_b, *other_own_b)
+    near_a[0], near_a[1], *near_b = tie(*near_a, *near_b, *other_near_b)
+    near_b, other_near_b = near_b[:2], near_b[2:]
     far_pairs = [(2 * i + k, 2 * ((i + (3 if k else 1)) % 4) + k) for i in range(4) for k in range(2)]
     far_a = lax.ppermute(jnp.where(core == 0, near_a[0], near_a[1]), zs + ("k",), far_pairs)
     other_near_a = trade(near_a, "k")
-    other_near_b = ring_near(other_own_b[0], ys)
     far_b = lax.ppermute(near_b[0], ys, AHEAD)
-    other_far_a, *other_near_b = tie(*trade([far_a], "k"), *other_near_b)
     other_far_b = lax.ppermute(other_near_b[1], ys, BACK)
+    other_far_a, far_b, other_far_b = tie(*trade([far_a], "k"), far_b, other_far_b)
     blocks_a = [own_a, *near_a, far_a, *other_own_a, *other_near_a, other_far_a]
 
     part_a, send_a = gram_part(True, ids_a, blocks_a)
@@ -444,8 +444,8 @@
     keep, block = tie(keep, block)
     up_own = jax.ShapeDtypeStruct((128, 2048), f32)
     up_own = vmem_call(functools.partial(arrange_kernel, 0), up_own, (ids, keep, traded), "arrange_up", 1 << 33)
-    sums_a, sums_b = tie(sums_a, sums_b)
-    sums_a = spread(sums_a + lax.ppermute(sums_a, "k", SWAP), ("xl", "z1", "z0"), 8)
+    sums_a, sums_b = tie(sums_a + lax.ppermute(sums_a, "k", SWAP), sums_b)
+    sums_a = spread(sums_a, ("xl", "z1", "z0"), 8)
 
     args = (ids, sums_b, jnp.stack([mean_b, inv_b]), view_b, up_b, other_a)
     grad_b = vmem_call(finish_second_kernel, jax.ShapeDtypeStruct((256, 1024), f32), args, "finish_second", 1 << 20)

time: 198 us -> 205 us (1.035)
  starting transfers between devices: 53.5 us -> 61.2 us
    ppermute x5, waiting for transfers between devices: 6.13 us -> 13.1 us  [trade(): return [lax.ppermute(x, axis, SWAP) for x in blocks]]
    all_to_all x1, blocking collectives: 23.7 us -> 17.3 us  [local(): mixed = lax.all_to_all(mixed, ('xl', 'z1', 'z0'), 0, 0)]
    ppermute x1, starting transfers between devices: 0.09 us -> 6.33 us  [local(): traded = lax.ppermute(mixed[:, 128:], 'k', SWAP)]
    all_to_all x1, blocking collectives: 23.6 us -> 28.6 us  [local(): last = lax.all_to_all(last, ('y1', 'y0', 'xh', 'xl'), 0, 0)]
    ppermute x6, waiting for transfers between devices: 7.21 us -> 11.2 us  [ring_near(): return [lax.ppermute(own, ring, AHEAD), lax.ppermute(own, ring, BACK)]]
    all_to_all x2, waiting for transfers between devices: 4.21 us -> 0.74 us  [spread(): return lax.all_to_all(jnp.broadcast_to(x[None], (n,) + x.shape), axes, 0, 0)]
    ppermute x1, starting transfers between devices: 6.99 us -> 3.74 us  [local(): other_a = lax.ppermute(send_a.reshape(256, 1024), ROW + COL, pairs_a)]
    all_to_all x1, waiting for transfers between devices: 6.4 us -> 3.25 us  [local(): lax.all_to_all(part_a.reshape(16, 256, 128), ('y1', 'y0', 'xh', 'xl'), 0, 0)]
  transfers between devices with their start and end apart: 29 -> 29, of which waited for: 15 -> 14; matrix products, arithmetic and copies ran while one was open for 2% -> 2% of each run, Pallas kernels for 11% -> 8%
where the time goes in v8:
time: 205 us; the launch traced here: 202 us
  starting transfers between devices  61.2 us (30%)
  waiting for transfers between devices  47.2 us (23%)
  blocking collectives  45.9 us (22%)
  Pallas kernels  27.8 us (14%)
  local copies, waits for them, and re-layouts  14.8 us (7%)
  other arithmetic  3.5 us (2%)
    all_to_all x1, blocking collectives, local(): last = lax.all_to_all(last, ('y1', 'y0', 'xh', 'xl'), 0, 0)  28.6 us
    all_to_all x1, blocking collectives, local(): mixed = lax.all_to_all(mixed, ('xl', 'z1', 'z0'), 0, 0)  17.3 us
    ppermute x5, waiting for transfers between devices, trade(): return [lax.ppermute(x, axis, SWAP) for x in blocks]  13.1 us
    pallas_call x2, Pallas kernels, gram_part(): call(functools.partial(gram_kernel, first), out, 0, 'gram_part', pl.ANY,...  11.4 us
    ppermute x6, waiting for transfers between devices, ring_near(): return [lax.ppermute(own, ring, AHEAD), lax.ppermute(own, ring, BACK)]  11.2 us
    all_to_all x2, starting transfers between devices, spread(): return lax.all_to_all(jnp.broadcast_to(x[None], (n,) + x.shape), axes, 0, 0)  11.2 us
    unnamed x33, local copies, waits for them, and re-layouts  10.4 us
    ppermute x5, starting transfers between devices, trade(): return [lax.ppermute(x, axis, SWAP) for x in blocks]  10.1 us
  transfers between devices with their start and end apart: 29, of which 14 were waited for; matrix products, arithmetic and copies ran while one was open for 2% of the time, Pallas kernels for 8%

profile of v8, /device:TPU:9, one launch (start us, length us, event | category | flops | bytes accessed | tf_op | source)
XLA Modules:
  0.0 201.5 jit_solution(14076523334264008542)
XLA Ops:
  0.6 1.4 fusion.5
  2.4 2.5 %collective-permute-start.1 = (f32[2,1024]{1,0:T(2,128)S(1)}, f32[2,1024]{1,0:T(2,128)S(1)}, u32[]{:S(2)}, u32[]{:S(2)}) collective-permute-start(f32[2,1024]{1,0:T(2,128)S(1)} %pad_maximum_fusion.3), channel_id=1, source_target_pairs={{0,64},{32,96},{64,0},{96,32},{1,65},{33,97},{65,1},{97,33},{2,66}... | collective-permute-start | bytes 24584 | tf_op jit(solution)/shard_map/ppermute | solution.py:384
  4.9 1.6 collective-permute-start
  7.3 7.8 %all-to-all-start = ((f32[16,2,2048]{2,1,0:T(2,128)}), f32[16,2,2048]{2,1,0:T(2,128)S(1)}, u32[]{:S(2)}, u32[]{:S(2)}) async-start(f32[16,2,2048]{2,1,0:T(2,128)} %broadcast_in_dim.4), calls=%async_computation | async-start | bytes 524288 | tf_op jit(solution)/shard_map/all_to_all | solution.py:32
  15.1 2.6 %collective-permute-start.3 = (f32[2,1024]{1,0:T(2,128)S(1)}, f32[2,1024]{1,0:T(2,128)S(1)}, u32[]{:S(2)}, u32[]{:S(2)}) collective-permute-start(f32[2,1024]{1,0:T(2,128)S(1)} %add_add_fusion), channel_id=1, source_target_pairs={{0,16},{16,0},{1,17},{17,1},{2,18},{18,2},{3,19},{19,3},{4,20},{20... | collective-permute-start | bytes 24584 | tf_op jit(solution)/shard_map/ppermute | solution.py:385
  17.7 3.9 %collective-permute-done.3 = f32[2,1024]{1,0:T(2,128)S(1)} collective-permute-done((f32[2,1024]{1,0:T(2,128)S(1)}, f32[2,1024]{1,0:T(2,128)S(1)}, u32[]{:S(2)}, u32[]{:S(2)}) %collective-permute-start.3) | collective-permute-done | bytes 8224 | tf_op jit(solution)/shard_map/ppermute | solution.py:385
  22.9 1.1 constant_dynamic-slice_fusion.1
  25.7 2.5 %collective-permute-start.9 = (bf16[256,1024]{1,0:T(8,128)(2,1)S(1)}, bf16[256,1024]{1,0:T(8,128)(2,1)}, u32[]{:S(2)}, u32[]{:S(2)}) collective-permute-start(bf16[256,1024]{1,0:T(8,128)(2,1)S(1)} %multiply_convert_fusion.1.refs_0_.half), channel_id=1, source_target_pairs={{0,16},{16,0},{1,17},{17,1},{2,18},{18,2},{3,19},{19,3},{4,20},{20... | collective-permute-start | bytes 1572872 | tf_op jit(solution)/shard_map/ppermute | solution.py:99
  28.2 1.5 collective-permute-start.7
  29.7 2.0 collective-permute-done.4
  31.8 1.5 collective-permute-start.6
  33.4 12.0 %collective-permute-done.9.refs_4_ = bf16[256,1024]{1,0:T(8,128)(2,1)} collective-permute-done((bf16[256,1024]{1,0:T(8,128)(2,1)S(1)}, bf16[256,1024]{1,0:T(8,128)(2,1)}, u32[]{:S(2)}, u32[]{:S(2)}) %collective-permute-start.9) | collective-permute-done | bytes 524320 | tf_op jit(solution)/shard_map/ppermute | solution.py:99
  45.4 1.5 collective-permute-start.10
  46.9 10.8 %collective-permute-done.11.refs_6_ = bf16[256,1024]{1,0:T(8,128)(2,1)} collective-permute-done((bf16[256,1024]{1,0:T(8,128)(2,1)}, bf16[256,1024]{1,0:T(8,128)(2,1)}, u32[]{:S(2)}, u32[]{:S(2)}) %collective-permute-start.11) | collective-permute-done | bytes 524320 | tf_op jit(solution)/shard_map/ppermute | solution.py:95
  58.1 1.1 broadcast_select_fusion
  60.6 1.6 collective-permute-start.18
  62.2 5.5 %collective-permute-done.12.refs_3_ = bf16[256,1024]{1,0:T(8,128)(2,1)} collective-permute-done((bf16[256,1024]{1,0:T(8,128)(2,1)S(1)}, bf16[256,1024]{1,0:T(8,128)(2,1)}, u32[]{:S(2)}, u32[]{:S(2)}) %collective-permute-start.12) | collective-permute-done | bytes 524320 | tf_op jit(solution)/shard_map/ppermute | solution.py:414
  67.7 4.4 %collective-permute-start.16 = (bf16[256,1024]{1,0:T(8,128)(2,1)}, bf16[256,1024]{1,0:T(8,128)(2,1)}, u32[]{:S(2)}, u32[]{:S(2)}) collective-permute-start(bf16[256,1024]{1,0:T(8,128)(2,1)} %collective-permute-done.12.refs_3_), channel_id=1, source_target_pairs={{0,1},{1,0},{2,3},{3,2},{4,5},{5,4},{6,7},{7,6},{8,9},{9,8},{10,11... | collective-permute-start | bytes 1572872 | tf_op jit(solution)/shard_map/ppermute | solution.py:99
  73.4 2.7 %collective-permute-start.15 = (bf16[256,1024]{1,0:T(8,128)(2,1)}, bf16[256,1024]{1,0:T(8,128)(2,1)}, u32[]{:S(2)}, u32[]{:S(2)}) collective-permute-start(bf16[256,1024]{1,0:T(8,128)(2,1)} %collective-permute-done.6.refs_2_), channel_id=1, source_target_pairs={{0,1},{1,0},{2,3},{3,2},{4,5},{5,4},{6,7},{7,6},{8,9},{9,8},{10,11... | collective-permute-start | bytes 1572872 | tf_op jit(solution)/shard_map/ppermute | solution.py:99
  76.9 1.1 collective-permute-done.15.refs_6_
  78.0 5.6 %gram_part.2 = (bf16[8,2,256,128]{3,2,1,0:T(8,128)(2,1)S(1)}, bf16[2,128,1024]{2,1,0:T(8,128)(2,1)}) custom-call(s32[6]{0:T(128)S(1)} %pad_add_fusion.1.ids, bf16[256,1024]{1,0:T(8,128)(2,1)S(1)} %pad_maximum_fusion.refs_0_, bf16[256,1024]{1,0:T(8,128)(2,1)} %collective-permute-done.5.refs_1_, bf16[256,1024]{1,0:T(8,128)(2,1)} %collective-permute-done.6.refs_2_, ...), custom_call_target="tpu_custom_call" | custom-call | flops 1073741824 | bytes 4194304 | tf_op jit(solution)/shard_map/gram_part/pallas_call | solution.py:183
  83.5 1.0 copy-done.5
  84.5 3.7 %collective-permute-start.20 = (bf16[256,1024]{1,0:T(8,128)(2,1)}, bf16[256,1024]{1,0:T(8,128)(2,1)}, u32[]{:S(2)}, u32[]{:S(2)}) collective-permute-start(bf16[256,1024]{1,0:T(8,128)(2,1)} %bitcast.19), channel_id=1, source_target_pairs={{0,0},{13,1},{18,2},{31,3},{39,4},{42,5},{53,6},{56,7},{66,8},{79,... | collective-permute-start | bytes 1572872 | tf_op jit(solution)/shard_map/ppermute | solution.py:424
  89.1 6.2 %all-to-all-start.1 = ((bf16[16,256,128]{2,1,0:T(8,128)(2,1)}), bf16[16,256,128]{2,1,0:T(8,128)(2,1)}, u32[]{:S(2)}, u32[]{:S(2)}) async-start(bf16[16,256,128]{2,1,0:T(8,128)(2,1)} %bitcast.30), calls=%async_computation.1 | async-start | bytes 2097152 | tf_op jit(solution)/shard_map/all_to_all | solution.py:425
  95.3 1.0 copy-done.3
  96.4 5.8 %gram_part.3 = (bf16[8,128,256]{2,1,0:T(8,128)(2,1)S(1)}, bf16[8,128,256]{2,1,0:T(8,128)(2,1)S(1)}, bf16[128,1024]{1,0:T(8,128)(2,1)}, bf16[128,1024]{1,0:T(8,128)(2,1)}) custom-call(s32[11]{0:T(128)S(1)} %pad_add_fusion.2.ids, bf16[256,1024]{1,0:T(8,128)(2,1)S(1)} %multiply_convert_fusion.1.refs_0_.half, bf16[256,1024]{1,0:T(8,128)(2,1)} %collective-permute-done.7.refs_1_, ...), custom_call_target="tpu_custom_call" | custom-call | flops 1048576 | bytes 4096 | tf_op jit(solution)/shard_map/gram_part/pallas_call | solution.py:183
  102.2 2.7 %collective-permute-start.21 = (bf16[128,1024]{1,0:T(8,128)(2,1)}, bf16[128,1024]{1,0:T(8,128)(2,1)S(1)}, u32[]{:S(2)}, u32[]{:S(2)}) collective-permute-start(bf16[128,1024]{1,0:T(8,128)(2,1)} %get-tuple-element.58), channel_id=1, source_target_pairs={{0,0},{97,1},{64,2},{33,3},{32,4},{65,5},{96,6},{1,7},{16,8},{113,... | collective-permute-start | bytes 786440 | tf_op jit(solution)/shard_map/ppermute | solution.py:430
  105.0 2.1 %collective-permute-start.19 = (bf16[8,128,256]{2,1,0:T(8,128)(2,1)S(1)}, bf16[8,128,256]{2,1,0:T(8,128)(2,1)S(1)}, u32[]{:S(2)}, u32[]{:S(2)}) collective-permute-start(bf16[8,128,256]{2,1,0:T(8,128)(2,1)S(1)} %get-tuple-element.55), channel_id=1, source_target_pairs={{0,1},{1,0},{2,3},{3,2},{4,5},{5,4},{6,7},{7,6},{8,9},{9,8},{10,11... | collective-permute-start | bytes 1572872 | tf_op jit(solution)/shard_map/ppermute | solution.py:427
  107.1 1.2 partner.1
  109.4 3.3 %all-to-all-done.1.received = bf16[16,256,128]{2,1,0:T(8,128)(2,1)} async-done(((bf16[16,256,128]{2,1,0:T(8,128)(2,1)}), bf16[16,256,128]{2,1,0:T(8,128)(2,1)}, u32[]{:S(2)}, u32[]{:S(2)}) %all-to-all-start.1) | async-done | bytes 1048608 | tf_op jit(solution)/shard_map/all_to_all | solution.py:425
  112.7 1.0 copy-done.11
  113.7 1.0 copy-done.13
  114.8 1.6 blend.1
  116.4 4.4 %collective-permute-done.21.same = bf16[128,1024]{1,0:T(8,128)(2,1)S(1)} collective-permute-done((bf16[128,1024]{1,0:T(8,128)(2,1)}, bf16[128,1024]{1,0:T(8,128)(2,1)S(1)}, u32[]{:S(2)}, u32[]{:S(2)}) %collective-permute-start.21) | collective-permute-done | bytes 262176 | tf_op jit(solution)/shard_map/ppermute | solution.py:430
  120.8 17.3 %all_to_all.25.mixed = bf16[8,256,256]{2,1,0:T(8,128)(2,1)S(1)} all-to-all(bf16[8,256,256]{2,1,0:T(8,128)(2,1)S(1)} %blend.1), channel_id=1, replica_groups=mesh['y1'=2,'y0'=2,'xh'=2,'xl'=2,'z1'=2,'z0'=2,'k'=2] {'xl','z1','z0'}, dimensions={0} | all-to-all | bytes 2097152 | tf_op jit(solution)/shard_map/all_to_all | solution.py:432
  138.1 6.3 %collective-permute-start.22 = (bf16[8,128,256]{2,1,0:T(8,128)(2,1)S(1)}, bf16[8,128,256]{2,1,0:T(8,128)(2,1)S(1)}, u32[]{:S(2)}, u32[]{:S(2)}) collective-permute-start(bf16[8,128,256]{2,1,0:T(8,128)(2,1)S(1)} %slice.24), channel_id=1, source_target_pairs={{0,1},{1,0},{2,3},{3,2},{4,5},{5,4},{6,7},{7,6},{8,9},{9,8},{10,11... | collective-permute-start | bytes 1572872 | tf_op jit(solution)/shard_map/ppermute | solution.py:434
  144.5 1.5 collective-permute-done.22.traded
  146.0 3.3 %second_view.1 = (f32[256,1024]{1,0:T(8,128)S(1)}, bf16[16,160,256]{2,1,0:T(8,128)(2,1)S(1)}) custom-call(s32[11]{0:T(128)S(1)} %pad_add_fusion.2.ids, bf16[8,256,256]{2,1,0:T(8,128)(2,1)S(1)} %all_to_all.25.mixed, bf16[8,128,256]{2,1,0:T(8,128)(2,1)S(1)} %collective-permute-done.22.traded, f32[2,1024]{1,0:T(2,128)S(1)} %partner.1, ...), custom_call_target="tpu_custom_call" | custom-call | flops 1073741824 | bytes 4194304 | tf_op jit(solution)/shard_map/second_view/pallas_call | solution.py:265
  149.4 28.6 %all_to_all.26.last = bf16[16,160,256]{2,1,0:T(8,128)(2,1)S(1)} all-to-all(bf16[16,160,256]{2,1,0:T(8,128)(2,1)S(1)} %get-tuple-element.61), channel_id=1, replica_groups=mesh['y1'=2,'y0'=2,'xh'=2,'xl'=2,'z1'=2,'z0'=2,'k'=2] {'y1','y0','xh','xl'}, dimensions={0} | all-to-all | bytes 2621440 | tf_op jit(solution)/shard_map/all_to_all | solution.py:436
  178.0 3.7 %collective-permute-start.24 = (bf16[128,1024]{1,0:T(8,128)(2,1)}, bf16[128,1024]{1,0:T(8,128)(2,1)}, u32[]{:S(2)}, u32[]{:S(2)}) collective-permute-start(bf16[128,1024]{1,0:T(8,128)(2,1)} %get-tuple-element.69), channel_id=1, source_target_pairs={{1,0},{96,1},{65,2},{32,3},{33,4},{64,5},{97,6},{0,7},{17,8},{112,... | collective-permute-start | bytes 786440 | tf_op jit(solution)/shard_map/ppermute | solution.py:438
  181.6 4.1 %first_view.1 = (f32[128,1024]{1,0:T(8,128)S(1)}, bf16[128,1024]{1,0:T(8,128)(2,1)}, f32[8,1024]{1,0:T(8,128)S(1)}, f32[32,256]{1,0:T(8,128)S(1)}) custom-call(s32[6]{0:T(128)S(1)} %pad_add_fusion.1.ids, bf16[16,160,256]{2,1,0:T(8,128)(2,1)S(1)} %all_to_all.26.last, bf16[256,1024]{1,0:T(8,128)(2,1)S(1)} %pad_maximum_fusion.refs_0_, ...), custom_call_target="tpu_custom_call" | custom-call | flops 1048576 | bytes 4096 | tf_op jit(solution)/shard_map/first_view/pallas_call | solution.py:310
  186.7 1.1 collective-permute-done.23
  188.5 3.4 %all-to-all-start.4 = ((f32[8,8,1024]{2,1,0:T(8,128)}), f32[8,8,1024]{2,1,0:T(8,128)S(1)}, u32[]{:S(2)}, u32[]{:S(2)}) async-start(f32[8,8,1024]{2,1,0:T(8,128)} %broadcast_in_dim.5), calls=%async_computation.4 | async-start | bytes 524288 | tf_op jit(solution)/shard_map/all_to_all | solution.py:32
  192.0 1.2 copy-done.7
  193.2 2.3 %finish_second.1 = f32[256,1024]{1,0:T(8,128)} custom-call(s32[3]{0:T(128)S(1)} %pad_add_fusion.ids, f32[32,256]{1,0:T(8,128)S(1)} %get-tuple-element.75.terms, f32[2,1024]{1,0:T(2,128)S(1)} %pad_maximum_fusion.4.scales, f32[256,1024]{1,0:T(8,128)S(1)} %copy-done.1, f32[256,1024]{1,0:T(8,128)S(1)} %copy-done.7, ...), custom_call_target="tpu_custom_call" | custom-call | flops 1048576 | bytes 65536 | tf_op jit(solution)/shard_map/finish_second/pallas_call | solution.py:322
  195.5 1.1 arrange_block.1.block
  198.2 1.0 copy-done.9
  199.2 2.2 %finish_first.1 = (f32[128,2048]{1,0:T(8,128)}, f32[1,1]{1,0:T(1,128)}) custom-call(s32[3]{0:T(128)S(1)} %pad_add_fusion.ids, f32[8,8,1024]{2,1,0:T(8,128)S(1)} %all-to-all-done.4.sums, f32[2,2048]{1,0:T(2,128)S(1)} %pad_maximum_fusion.2.scales, f32[128,2048]{1,0:T(8,128)S(1)} %copy-done, f32[128,2048]{1,0:T(8,128)S(1)} %arrange_up.1.up, ...), custom_call_target="tpu_custom_call" | custom-call | flops 1048576 | bytes 65536 | tf_op jit(solution)/shard_map/finish_first/pallas_call | solution.py:372
  (82 shorter events, 13.5 us)
Async XLA Ops:
  0.6 1.5 copy-start.1
  2.1 20.3 %copy-start = (f32[128,2048]{1,0:T(8,128)S(1)}, f32[128,2048]{1,0:T(8,128)}, u32[]{:S(2)}) copy-start(f32[128,2048]{1,0:T(8,128)} %view.2) | copy-start | bytes 3145732
  2.3 12.7 %collective-permute-start.2 = (f32[2,1024]{1,0:T(2,128)S(1)}, f32[2,1024]{1,0:T(2,128)S(1)}, u32[]{:S(2)}, u32[]{:S(2)}) collective-permute-start(f32[2,1024]{1,0:T(2,128)S(1)} %pad_maximum_fusion.3), channel_id=1, source_target_pairs={{0,96},{32,0},{64,32},{96,64},{1,97},{33,1},{65,33},{97,65},{2,98}... | collective-permute-start | bytes 24584 | tf_op jit(solution)/shard_map/ppermute | solution.py:384
  2.4 12.7 %collective-permute-start.1 = (f32[2,1024]{1,0:T(2,128)S(1)}, f32[2,1024]{1,0:T(2,128)S(1)}, u32[]{:S(2)}, u32[]{:S(2)}) collective-permute-start(f32[2,1024]{1,0:T(2,128)S(1)} %pad_maximum_fusion.3), channel_id=1, source_target_pairs={{0,64},{32,96},{64,0},{96,32},{1,65},{33,97},{65,1},{97,33},{2,66}... | collective-permute-start | bytes 24584 | tf_op jit(solution)/shard_map/ppermute | solution.py:384
  4.9 10.2 %collective-permute-start = (f32[2,1024]{1,0:T(2,128)S(1)}, f32[2,1024]{1,0:T(2,128)S(1)}, u32[]{:S(2)}, u32[]{:S(2)}) collective-permute-start(f32[2,1024]{1,0:T(2,128)S(1)} %pad_maximum_fusion.3), channel_id=1, source_target_pairs={{0,32},{32,64},{64,96},{96,0},{1,33},{33,65},{65,97},{97,1},{2,34}... | collective-permute-start | bytes 24584 | tf_op jit(solution)/shard_map/ppermute | solution.py:384
  7.3 14.9 %all-to-all-start = ((f32[16,2,2048]{2,1,0:T(2,128)}), f32[16,2,2048]{2,1,0:T(2,128)S(1)}, u32[]{:S(2)}, u32[]{:S(2)}) async-start(f32[16,2,2048]{2,1,0:T(2,128)} %broadcast_in_dim.4), calls=%async_computation | async-start | bytes 524288 | tf_op jit(solution)/shard_map/all_to_all | solution.py:32
  15.1 6.5 %collective-permute-start.3 = (f32[2,1024]{1,0:T(2,128)S(1)}, f32[2,1024]{1,0:T(2,128)S(1)}, u32[]{:S(2)}, u32[]{:S(2)}) collective-permute-start(f32[2,1024]{1,0:T(2,128)S(1)} %add_add_fusion), channel_id=1, source_target_pairs={{0,16},{16,0},{1,17},{17,1},{2,18},{18,2},{3,19},{19,3},{4,20},{20... | collective-permute-start | bytes 24584 | tf_op jit(solution)/shard_map/ppermute | solution.py:385
  24.7 6.9 %collective-permute-start.4 = (bf16[128,1024]{1,0:T(8,128)(2,1)}, bf16[128,1024]{1,0:T(8,128)(2,1)S(1)}, u32[]{:S(2)}, u32[]{:S(2)}) collective-permute-start(bf16[128,1024]{1,0:T(8,128)(2,1)} %bitcast.29), channel_id=1, source_target_pairs={{0,8},{8,0},{1,9},{9,1},{2,10},{10,2},{3,11},{11,3},{4,12},{12,4},... | collective-permute-start | bytes 786440 | tf_op jit(solution)/shard_map/ppermute | solution.py:405
  25.7 19.7 %collective-permute-start.9 = (bf16[256,1024]{1,0:T(8,128)(2,1)S(1)}, bf16[256,1024]{1,0:T(8,128)(2,1)}, u32[]{:S(2)}, u32[]{:S(2)}) collective-permute-start(bf16[256,1024]{1,0:T(8,128)(2,1)S(1)} %multiply_convert_fusion.1.refs_0_.half), channel_id=1, source_target_pairs={{0,16},{16,0},{1,17},{17,1},{2,18},{18,2},{3,19},{19,3},{4,20},{20... | collective-permute-start | bytes 1572872 | tf_op jit(solution)/shard_map/ppermute | solution.py:99
  28.2 17.2 %collective-permute-start.8 = (bf16[256,1024]{1,0:T(8,128)(2,1)S(1)}, bf16[256,1024]{1,0:T(8,128)(2,1)}, u32[]{:S(2)}, u32[]{:S(2)}) collective-permute-start(bf16[256,1024]{1,0:T(8,128)(2,1)S(1)} %multiply_convert_fusion.1.refs_0_.half), channel_id=1, source_target_pairs={{0,96},{32,0},{64,32},{96,64},{1,97},{33,1},{65,33},{97,65},{2,98}... | collective-permute-start | bytes 1572872 | tf_op jit(solution)/shard_map/ppermute | solution.py:95
  28.2 18.6 %collective-permute-start.7 = (bf16[256,1024]{1,0:T(8,128)(2,1)S(1)}, bf16[256,1024]{1,0:T(8,128)(2,1)}, u32[]{:S(2)}, u32[]{:S(2)}) collective-permute-start(bf16[256,1024]{1,0:T(8,128)(2,1)S(1)} %multiply_convert_fusion.1.refs_0_.half), channel_id=1, source_target_pairs={{0,32},{32,64},{64,96},{96,0},{1,33},{33,65},{65,97},{97,1},{2,34}... | collective-permute-start | bytes 1572872 | tf_op jit(solution)/shard_map/ppermute | solution.py:95
  31.8 15.0 %collective-permute-start.6 = (bf16[256,1024]{1,0:T(8,128)(2,1)S(1)}, bf16[256,1024]{1,0:T(8,128)(2,1)}, u32[]{:S(2)}, u32[]{:S(2)}) collective-permute-start(bf16[256,1024]{1,0:T(8,128)(2,1)S(1)} %pad_maximum_fusion.refs_0_), channel_id=1, source_target_pairs={{0,6},{2,0},{4,2},{6,4},{1,7},{3,1},{5,3},{7,5},{8,14},{10,8},{12,... | collective-permute-start | bytes 1572872 | tf_op jit(solution)/shard_map/ppermute | solution.py:95
  33.4 13.5 %collective-permute-start.5 = (bf16[256,1024]{1,0:T(8,128)(2,1)S(1)}, bf16[256,1024]{1,0:T(8,128)(2,1)}, u32[]{:S(2)}, u32[]{:S(2)}) collective-permute-start(bf16[256,1024]{1,0:T(8,128)(2,1)S(1)} %pad_maximum_fusion.refs_0_), channel_id=1, source_target_pairs={{0,2},{2,4},{4,6},{6,0},{1,3},{3,5},{5,7},{7,1},{8,10},{10,12},{12... | collective-permute-start | bytes 1572872 | tf_op jit(solution)/shard_map/ppermute | solution.py:95
  45.4 12.3 %collective-permute-start.11 = (bf16[256,1024]{1,0:T(8,128)(2,1)}, bf16[256,1024]{1,0:T(8,128)(2,1)}, u32[]{:S(2)}, u32[]{:S(2)}) collective-permute-start(bf16[256,1024]{1,0:T(8,128)(2,1)} %collective-permute-done.9.refs_4_), channel_id=1, source_target_pairs={{0,96},{32,0},{64,32},{96,64},{1,97},{33,1},{65,33},{97,65},{2,98}... | collective-permute-start | bytes 1572872 | tf_op jit(solution)/shard_map/ppermute | solution.py:95
  45.4 12.7 %collective-permute-start.10 = (bf16[256,1024]{1,0:T(8,128)(2,1)}, bf16[256,1024]{1,0:T(8,128)(2,1)}, u32[]{:S(2)}, u32[]{:S(2)}) collective-permute-start(bf16[256,1024]{1,0:T(8,128)(2,1)} %collective-permute-done.9.refs_4_), channel_id=1, source_target_pairs={{0,32},{32,64},{64,96},{96,0},{1,33},{33,65},{65,97},{97,1},{2,34}... | collective-permute-start | bytes 1572872 | tf_op jit(solution)/shard_map/ppermute | solution.py:95
  59.2 8.5 %collective-permute-start.12 = (bf16[256,1024]{1,0:T(8,128)(2,1)S(1)}, bf16[256,1024]{1,0:T(8,128)(2,1)}, u32[]{:S(2)}, u32[]{:S(2)}) collective-permute-start(bf16[256,1024]{1,0:T(8,128)(2,1)S(1)} %broadcast_select_fusion), channel_id=1, source_target_pairs={{0,2},{1,7},{2,4},{3,1},{4,6},{5,3},{6,0},{7,5},{8,10},{9,15},{10,... | collective-permute-start | bytes 1572872 | tf_op jit(solution)/shard_map/ppermute | solution.py:414
  59.9 12.8 %collective-permute-start.17 = (bf16[256,1024]{1,0:T(8,128)(2,1)}, bf16[256,1024]{1,0:T(8,128)(2,1)S(1)}, u32[]{:S(2)}, u32[]{:S(2)}) collective-permute-start(bf16[256,1024]{1,0:T(8,128)(2,1)} %collective-permute-done.7.refs_1_), channel_id=1, source_target_pairs={{0,32},{32,64},{64,96},{96,0},{1,33},{33,65},{65,97},{97,1},{2,34}... | collective-permute-start | bytes 1572872 | tf_op jit(solution)/shard_map/ppermute | solution.py:416
  60.6 16.2 %collective-permute-start.18 = (bf16[256,1024]{1,0:T(8,128)(2,1)}, bf16[256,1024]{1,0:T(8,128)(2,1)}, u32[]{:S(2)}, u32[]{:S(2)}) collective-permute-start(bf16[256,1024]{1,0:T(8,128)(2,1)} %collective-permute-done.11.refs_6_), channel_id=1, source_target_pairs={{0,96},{32,0},{64,32},{96,64},{1,97},{33,1},{65,33},{97,65},{2,98}... | collective-permute-start | bytes 1572872 | tf_op jit(solution)/shard_map/ppermute | solution.py:417
  67.7 9.2 %collective-permute-start.16 = (bf16[256,1024]{1,0:T(8,128)(2,1)}, bf16[256,1024]{1,0:T(8,128)(2,1)}, u32[]{:S(2)}, u32[]{:S(2)}) collective-permute-start(bf16[256,1024]{1,0:T(8,128)(2,1)} %collective-permute-done.12.refs_3_), channel_id=1, source_target_pairs={{0,1},{1,0},{2,3},{3,2},{4,5},{5,4},{6,7},{7,6},{8,9},{9,8},{10,11... | collective-permute-start | bytes 1572872 | tf_op jit(solution)/shard_map/ppermute | solution.py:99
  72.1 4.8 %collective-permute-start.13 = (bf16[256,1024]{1,0:T(8,128)(2,1)S(1)}, bf16[256,1024]{1,0:T(8,128)(2,1)}, u32[]{:S(2)}, u32[]{:S(2)}) collective-permute-start(bf16[256,1024]{1,0:T(8,128)(2,1)S(1)} %pad_maximum_fusion.refs_0_), channel_id=1, source_target_pairs={{0,1},{1,0},{2,3},{3,2},{4,5},{5,4},{6,7},{7,6},{8,9},{9,8},{10,11... | collective-permute-start | bytes 1572872 | tf_op jit(solution)/shard_map/ppermute | solution.py:99
  72.1 4.8 %collective-permute-start.14 = (bf16[256,1024]{1,0:T(8,128)(2,1)}, bf16[256,1024]{1,0:T(8,128)(2,1)}, u32[]{:S(2)}, u32[]{:S(2)}) collective-permute-start(bf16[256,1024]{1,0:T(8,128)(2,1)} %collective-permute-done.5.refs_1_), channel_id=1, source_target_pairs={{0,1},{1,0},{2,3},{3,2},{4,5},{5,4},{6,7},{7,6},{8,9},{9,8},{10,11... | collective-permute-start | bytes 1572872 | tf_op jit(solution)/shard_map/ppermute | solution.py:99
  72.6 0.8 copy-start.2
  73.4 4.6 %collective-permute-start.15 = (bf16[256,1024]{1,0:T(8,128)(2,1)}, bf16[256,1024]{1,0:T(8,128)(2,1)}, u32[]{:S(2)}, u32[]{:S(2)}) collective-permute-start(bf16[256,1024]{1,0:T(8,128)(2,1)} %collective-permute-done.6.refs_2_), channel_id=1, source_target_pairs={{0,1},{1,0},{2,3},{3,2},{4,5},{5,4},{6,7},{7,6},{8,9},{9,8},{10,11... | collective-permute-start | bytes 1572872 | tf_op jit(solution)/shard_map/ppermute | solution.py:99
  83.5 1.0 copy-start.5
  84.5 22.5 %collective-permute-start.20 = (bf16[256,1024]{1,0:T(8,128)(2,1)}, bf16[256,1024]{1,0:T(8,128)(2,1)}, u32[]{:S(2)}, u32[]{:S(2)}) collective-permute-start(bf16[256,1024]{1,0:T(8,128)(2,1)} %bitcast.19), channel_id=1, source_target_pairs={{0,0},{13,1},{18,2},{31,3},{39,4},{42,5},{53,6},{56,7},{66,8},{79,... | collective-permute-start | bytes 1572872 | tf_op jit(solution)/shard_map/ppermute | solution.py:424
  89.1 23.6 %all-to-all-start.1 = ((bf16[16,256,128]{2,1,0:T(8,128)(2,1)}), bf16[16,256,128]{2,1,0:T(8,128)(2,1)}, u32[]{:S(2)}, u32[]{:S(2)}) async-start(bf16[16,256,128]{2,1,0:T(8,128)(2,1)} %bitcast.30), calls=%async_computation.1 | async-start | bytes 2097152 | tf_op jit(solution)/shard_map/all_to_all | solution.py:425
  95.3 1.0 copy-start.3
  102.2 6.0 %copy-start.10 = (bf16[8,128,256]{2,1,0:T(8,128)(2,1)}, bf16[8,128,256]{2,1,0:T(8,128)(2,1)S(1)}, u32[]{:S(2)}) copy-start(bf16[8,128,256]{2,1,0:T(8,128)(2,1)S(1)} %get-tuple-element.54.mine) | copy-start | bytes 1572868
  102.2 18.5 %collective-permute-start.21 = (bf16[128,1024]{1,0:T(8,128)(2,1)}, bf16[128,1024]{1,0:T(8,128)(2,1)S(1)}, u32[]{:S(2)}, u32[]{:S(2)}) collective-permute-start(bf16[128,1024]{1,0:T(8,128)(2,1)} %get-tuple-element.58), channel_id=1, source_target_pairs={{0,0},{97,1},{64,2},{33,3},{32,4},{65,5},{96,6},{1,7},{16,8},{113,... | collective-permute-start | bytes 786440 | tf_op jit(solution)/shard_map/ppermute | solution.py:430
  105.0 3.6 %collective-permute-start.19 = (bf16[8,128,256]{2,1,0:T(8,128)(2,1)S(1)}, bf16[8,128,256]{2,1,0:T(8,128)(2,1)S(1)}, u32[]{:S(2)}, u32[]{:S(2)}) collective-permute-start(bf16[8,128,256]{2,1,0:T(8,128)(2,1)S(1)} %get-tuple-element.55), channel_id=1, source_target_pairs={{0,1},{1,0},{2,3},{3,2},{4,5},{5,4},{6,7},{7,6},{8,9},{9,8},{10,11... | collective-permute-start | bytes 1572872 | tf_op jit(solution)/shard_map/ppermute | solution.py:427
  108.6 0.8 copy-start.12
  112.7 1.0 copy-start.11
  113.7 1.0 copy-start.13
  116.4 29.7 %copy-start.4 = (bf16[256,1024]{1,0:T(8,128)(2,1)S(1)}, bf16[256,1024]{1,0:T(8,128)(2,1)}, u32[]{:S(2)}) copy-start(bf16[256,1024]{1,0:T(8,128)(2,1)} %copy-done.2) | copy-start | bytes 1572868
  138.1 7.9 %collective-permute-start.22 = (bf16[8,128,256]{2,1,0:T(8,128)(2,1)S(1)}, bf16[8,128,256]{2,1,0:T(8,128)(2,1)S(1)}, u32[]{:S(2)}, u32[]{:S(2)}) collective-permute-start(bf16[8,128,256]{2,1,0:T(8,128)(2,1)S(1)} %slice.24), channel_id=1, source_target_pairs={{0,1},{1,0},{2,3},{3,2},{4,5},{5,4},{6,7},{7,6},{8,9},{9,8},{10,11... | collective-permute-start | bytes 1572872 | tf_op jit(solution)/shard_map/ppermute | solution.py:434
  149.4 28.6 %copy-start.6 = (f32[256,1024]{1,0:T(8,128)}, f32[256,1024]{1,0:T(8,128)S(1)}, u32[]{:S(2)}) copy-start(f32[256,1024]{1,0:T(8,128)S(1)} %get-tuple-element.76.up) | copy-start | bytes 3145732
  178.0 17.6 %collective-permute-start.24 = (bf16[128,1024]{1,0:T(8,128)(2,1)}, bf16[128,1024]{1,0:T(8,128)(2,1)}, u32[]{:S(2)}, u32[]{:S(2)}) collective-permute-start(bf16[128,1024]{1,0:T(8,128)(2,1)} %get-tuple-element.69), channel_id=1, source_target_pairs={{1,0},{96,1},{65,2},{32,3},{33,4},{64,5},{97,6},{0,7},{17,8},{112,... | collective-permute-start | bytes 786440 | tf_op jit(solution)/shard_map/ppermute | solution.py:438
  185.8 0.8 copy-start.14
  186.6 1.2 collective-permute-start.23
  186.6 10.8 %collective-permute-start.25 = (bf16[128,1024]{1,0:T(8,128)(2,1)}, bf16[128,1024]{1,0:T(8,128)(2,1)S(1)}, u32[]{:S(2)}, u32[]{:S(2)}) collective-permute-start(bf16[128,1024]{1,0:T(8,128)(2,1)} %get-tuple-element.71), channel_id=1, source_target_pairs={{0,8},{8,0},{1,9},{9,1},{2,10},{10,2},{3,11},{11,3},{4,12},{12,4},... | collective-permute-start | bytes 786440 | tf_op jit(solution)/shard_map/ppermute | solution.py:441
  188.5 9.6 %all-to-all-start.4 = ((f32[8,8,1024]{2,1,0:T(8,128)}), f32[8,8,1024]{2,1,0:T(8,128)S(1)}, u32[]{:S(2)}, u32[]{:S(2)}) async-start(f32[8,8,1024]{2,1,0:T(8,128)} %broadcast_in_dim.5), calls=%async_computation.4 | async-start | bytes 524288 | tf_op jit(solution)/shard_map/all_to_all | solution.py:32
  191.9 1.2 copy-start.7
  195.5 1.9 copy-start.15
  196.6 0.8 copy-start.8
  198.2 1.0 copy-start.9

commit v9 on v7

--- a/solution.py
+++ b/solution.py
@@ -336,10 +336,9 @@
     out[1:2, :] = image_sum(other * half[...].astype(f32))
 
 
-def arrange_kernel(which, ids, same, other, out):
+def arrange_kernel(ids, same, other, block):
     for half in range(2):
-        picked = jnp.where(ids[which] == half, same[...].astype(out.dtype), other[...].astype(out.dtype))
-        out[:, 1024 * half : 1024 * (half + 1)] = picked
+        block[:, 1024 * half : 1024 * (half + 1)] = jnp.where(ids[1] == half, same[...], other[...])
 
 
 def finish_second_kernel(ids, terms, scales, view, up, partner, grad):
@@ -352,7 +351,7 @@
         grad[:, columns] = inv * (up[:, columns] + diag * partner[:, columns].astype(f32) - first - norm * second)
 
 
-def finish_kernel(ids, sums, scales, view, up, block, grad, loss):
+def finish_kernel(ids, sums, scales, view, keep, traded, block, grad, loss):
     row = ids[2]
     loss[0, 0] = jnp.sum(sums[:, 2, :]) / FEAT
     partner = sums[row]
@@ -363,7 +362,8 @@
         diag, first, second = finish(total[0:1], total[1:2], *rows, BATCH)
         mean, inv = scales[0:1, columns], scales[1:2, columns]
         norm = (view[:, columns] - mean) * inv
-        grad[:, columns] = inv * (up[:, columns] + diag * block[:, columns].astype(f32) - first - norm * second)
+        up = jnp.where(ids[0] == half, keep[...], traded[...].astype(f32))
+        grad[:, columns] = inv * (up + diag * block[:, columns].astype(f32) - first - norm * second)
 
 
 def finish_first(ids, *args):
@@ -440,16 +440,13 @@
     keep, give, sums_a, sums_b = first_view(ids_a, last, blocks_a)
     traded = lax.ppermute(give, "xl", SWAP)
     block = jax.ShapeDtypeStruct((128, 2048), bf16)
-    block = vmem_call(functools.partial(arrange_kernel, 1), block, (ids, early, late), "arrange_block", 1 << 34)
-    keep, block = tie(keep, block)
-    up_own = jax.ShapeDtypeStruct((128, 2048), f32)
-    up_own = vmem_call(functools.partial(arrange_kernel, 0), up_own, (ids, keep, traded), "arrange_up", 1 << 33)
+    block = vmem_call(arrange_kernel, block, (ids, early, late), "arrange_block", 1 << 34)
     sums_a, sums_b = tie(sums_a, sums_b)
     sums_a = spread(sums_a + lax.ppermute(sums_a, "k", SWAP), ("xl", "z1", "z0"), 8)
 
     args = (ids, sums_b, jnp.stack([mean_b, inv_b]), view_b, up_b, other_a)
     grad_b = vmem_call(finish_second_kernel, jax.ShapeDtypeStruct((256, 1024), f32), args, "finish_second", 1 << 20)
-    grad_a, loss_value = finish_first(ids, sums_a, jnp.stack([mean_a, inv_a]), view_a, up_own, block)
+    grad_a, loss_value = finish_first(ids, sums_a, jnp.stack([mean_a, inv_a]), view_a, keep, traded, block)
     return (loss_value[0, 0], grad_a, grad_b)
 
 

time: 198 us -> 199 us (level)
    pallas_call x4 -> x3, Pallas kernels: 5.27 us -> 4.59 us  [vmem_call(): pl.pallas_call(kernel, out_shape=out_shape, in_specs=[smem] + [vmem] * (l...]
where the time goes in v9:
time: 199 us; the launch traced here: 195 us
  starting transfers between devices  53.5 us (27%)
  blocking collectives  47.3 us (24%)
  waiting for transfers between devices  46.9 us (24%)
  Pallas kernels  27.2 us (14%)
  local copies, waits for them, and re-layouts  15.8 us (8%)
  other arithmetic  3.5 us (2%)
    all_to_all x1, blocking collectives, local(): mixed = lax.all_to_all(mixed, ('xl', 'z1', 'z0'), 0, 0)  23.7 us
    all_to_all x1, blocking collectives, local(): last = lax.all_to_all(last, ('y1', 'y0', 'xh', 'xl'), 0, 0)  23.6 us
    pallas_call x2, Pallas kernels, gram_part(): call(functools.partial(gram_kernel, first), out, 0, 'gram_part', pl.ANY,...  11.6 us
    all_to_all x2, starting transfers between devices, spread(): return lax.all_to_all(jnp.broadcast_to(x[None], (n,) + x.shape), axes, 0, 0)  11.4 us
    unnamed x37, local copies, waits for them, and re-layouts  11.3 us
    ppermute x5, starting transfers between devices, trade(): return [lax.ppermute(x, axis, SWAP) for x in blocks]  8.22 us
    ppermute x6, waiting for transfers between devices, ring_near(): return [lax.ppermute(own, ring, AHEAD), lax.ppermute(own, ring, BACK)]  7.21 us
    ppermute x1, starting transfers between devices, local(): other_a = lax.ppermute(send_a.reshape(256, 1024), ROW + COL, pairs_a)  6.99 us
  transfers between devices with their start and end apart: 29, of which 15 were waited for; matrix products, arithmetic and copies ran while one was open for 2% of the time, Pallas kernels for 11%

profile of v9, /device:TPU:9, one launch (start us, length us, event | category | flops | bytes accessed | tf_op | source)
XLA Modules:
  0.0 195.4 jit_solution(3923025047234650161)
XLA Ops:
  0.6 1.4 fusion.5
  2.4 2.5 %collective-permute-start.1 = (f32[2,1024]{1,0:T(2,128)S(1)}, f32[2,1024]{1,0:T(2,128)S(1)}, u32[]{:S(2)}, u32[]{:S(2)}) collective-permute-start(f32[2,1024]{1,0:T(2,128)S(1)} %pad_maximum_fusion.3), channel_id=1, source_target_pairs={{0,64},{32,96},{64,0},{96,32},{1,65},{33,97},{65,1},{97,33},{2,66}... | collective-permute-start | bytes 24584 | tf_op jit(solution)/shard_map/ppermute | solution.py:384
  4.9 1.6 collective-permute-start
  7.3 7.8 %all-to-all-start = ((f32[16,2,2048]{2,1,0:T(2,128)}), f32[16,2,2048]{2,1,0:T(2,128)S(1)}, u32[]{:S(2)}, u32[]{:S(2)}) async-start(f32[16,2,2048]{2,1,0:T(2,128)} %broadcast_in_dim.4), calls=%async_computation | async-start | bytes 524288 | tf_op jit(solution)/shard_map/all_to_all | solution.py:32
  15.1 2.6 %collective-permute-start.3 = (f32[2,1024]{1,0:T(2,128)S(1)}, f32[2,1024]{1,0:T(2,128)S(1)}, u32[]{:S(2)}, u32[]{:S(2)}) collective-permute-start(f32[2,1024]{1,0:T(2,128)S(1)} %add_add_fusion), channel_id=1, source_target_pairs={{0,16},{16,0},{1,17},{17,1},{2,18},{18,2},{3,19},{19,3},{4,20},{20... | collective-permute-start | bytes 24584 | tf_op jit(solution)/shard_map/ppermute | solution.py:385
  17.7 3.9 %collective-permute-done.3 = f32[2,1024]{1,0:T(2,128)S(1)} collective-permute-done((f32[2,1024]{1,0:T(2,128)S(1)}, f32[2,1024]{1,0:T(2,128)S(1)}, u32[]{:S(2)}, u32[]{:S(2)}) %collective-permute-start.3) | collective-permute-done | bytes 8224 | tf_op jit(solution)/shard_map/ppermute | solution.py:385
  22.9 1.1 constant_dynamic-slice_fusion.1
  25.1 1.5 collective-permute-start.7
  26.6 4.4 %collective-permute-done.4 = bf16[128,1024]{1,0:T(8,128)(2,1)S(1)} collective-permute-done((bf16[128,1024]{1,0:T(8,128)(2,1)S(1)}, bf16[128,1024]{1,0:T(8,128)(2,1)S(1)}, u32[]{:S(2)}, u32[]{:S(2)}) %collective-permute-start.4) | collective-permute-done | bytes 262176 | tf_op jit(solution)/shard_map/ppermute | solution.py:405
  31.1 2.5 %collective-permute-start.9 = (bf16[256,1024]{1,0:T(8,128)(2,1)S(1)}, bf16[256,1024]{1,0:T(8,128)(2,1)}, u32[]{:S(2)}, u32[]{:S(2)}) collective-permute-start(bf16[256,1024]{1,0:T(8,128)(2,1)S(1)} %multiply_convert_fusion.1.refs_0_.half), channel_id=1, source_target_pairs={{0,16},{16,0},{1,17},{17,1},{2,18},{18,2},{3,19},{19,3},{4,20},{20... | collective-permute-start | bytes 1572872 | tf_op jit(solution)/shard_map/ppermute | solution.py:99
  33.6 2.6 %collective-permute-start.6 = (bf16[256,1024]{1,0:T(8,128)(2,1)S(1)}, bf16[256,1024]{1,0:T(8,128)(2,1)}, u32[]{:S(2)}, u32[]{:S(2)}) collective-permute-start(bf16[256,1024]{1,0:T(8,128)(2,1)S(1)} %pad_maximum_fusion.refs_0_), channel_id=1, source_target_pairs={{0,6},{2,0},{4,2},{6,4},{1,7},{3,1},{5,3},{7,5},{8,14},{10,8},{12,... | collective-permute-start | bytes 1572872 | tf_op jit(solution)/shard_map/ppermute | solution.py:95
  36.2 1.6 collective-permute-done.8.refs_2_
  38.2 6.1 %collective-permute-done.9.refs_4_ = bf16[256,1024]{1,0:T(8,128)(2,1)} collective-permute-done((bf16[256,1024]{1,0:T(8,128)(2,1)S(1)}, bf16[256,1024]{1,0:T(8,128)(2,1)}, u32[]{:S(2)}, u32[]{:S(2)}) %collective-permute-start.9) | collective-permute-done | bytes 524320 | tf_op jit(solution)/shard_map/ppermute | solution.py:99
  44.3 2.0 %collective-permute-done.6.refs_2_ = bf16[256,1024]{1,0:T(8,128)(2,1)} collective-permute-done((bf16[256,1024]{1,0:T(8,128)(2,1)S(1)}, bf16[256,1024]{1,0:T(8,128)(2,1)}, u32[]{:S(2)}, u32[]{:S(2)}) %collective-permute-start.6) | collective-permute-done | bytes 524320 | tf_op jit(solution)/shard_map/ppermute | solution.py:95
  46.3 3.2 %collective-permute-done.5.refs_1_ = bf16[256,1024]{1,0:T(8,128)(2,1)} collective-permute-done((bf16[256,1024]{1,0:T(8,128)(2,1)S(1)}, bf16[256,1024]{1,0:T(8,128)(2,1)}, u32[]{:S(2)}, u32[]{:S(2)}) %collective-permute-start.5) | collective-permute-done | bytes 524320 | tf_op jit(solution)/shard_map/ppermute | solution.py:95
  49.6 1.1 broadcast_select_fusion
  51.0 1.5 collective-permute-start.15
  52.5 6.7 %collective-permute-done.10.refs_3_ = bf16[256,1024]{1,0:T(8,128)(2,1)S(1)} collective-permute-done((bf16[256,1024]{1,0:T(8,128)(2,1)S(1)}, bf16[256,1024]{1,0:T(8,128)(2,1)S(1)}, u32[]{:S(2)}, u32[]{:S(2)}) %collective-permute-start.10) | collective-permute-done | bytes 524320 | tf_op jit(solution)/shard_map/ppermute | solution.py:413
  59.2 4.3 %collective-permute-start.14 = (bf16[256,1024]{1,0:T(8,128)(2,1)S(1)}, bf16[256,1024]{1,0:T(8,128)(2,1)S(1)}, u32[]{:S(2)}, u32[]{:S(2)}) collective-permute-start(bf16[256,1024]{1,0:T(8,128)(2,1)S(1)} %collective-permute-done.10.refs_3_), channel_id=1, source_target_pairs={{0,1},{1,0},{2,3},{3,2},{4,5},{5,4},{6,7},{7,6},{8,9},{9,8},{10,11... | collective-permute-start | bytes 1572872 | tf_op jit(solution)/shard_map/ppermute | solution.py:99
  67.3 1.5 collective-permute-start.18
  69.5 1.0 copy-done.6
  70.6 1.0 copy-done.9
  71.6 5.4 %gram_part.2 = (bf16[8,2,256,128]{3,2,1,0:T(8,128)(2,1)S(1)}, bf16[2,128,1024]{2,1,0:T(8,128)(2,1)}) custom-call(s32[6]{0:T(128)S(1)} %pad_add_fusion.1.ids, bf16[256,1024]{1,0:T(8,128)(2,1)S(1)} %pad_maximum_fusion.refs_0_, bf16[256,1024]{1,0:T(8,128)(2,1)} %collective-permute-done.5.refs_1_, bf16[256,1024]{1,0:T(8,128)(2,1)} %collective-permute-done.6.refs_2_, ...), custom_call_target="tpu_custom_call" | custom-call | flops 1073741824 | bytes 4194304 | tf_op jit(solution)/shard_map/gram_part/pallas_call | solution.py:183
  78.0 1.0 collective-permute-done.17.refs_3_
  79.0 2.4 %collective-permute-done.18.refs_7_ = bf16[256,1024]{1,0:T(8,128)(2,1)} collective-permute-done((bf16[256,1024]{1,0:T(8,128)(2,1)}, bf16[256,1024]{1,0:T(8,128)(2,1)}, u32[]{:S(2)}, u32[]{:S(2)}) %collective-permute-start.18) | collective-permute-done | bytes 524320 | tf_op jit(solution)/shard_map/ppermute | solution.py:418
  81.4 7.0 %collective-permute-start.20 = (bf16[256,1024]{1,0:T(8,128)(2,1)}, bf16[256,1024]{1,0:T(8,128)(2,1)}, u32[]{:S(2)}, u32[]{:S(2)}) collective-permute-start(bf16[256,1024]{1,0:T(8,128)(2,1)} %bitcast.19), channel_id=1, source_target_pairs={{0,0},{13,1},{18,2},{31,3},{39,4},{42,5},{53,6},{56,7},{66,8},{79,... | collective-permute-start | bytes 1572872 | tf_op jit(solution)/shard_map/ppermute | solution.py:424
  89.3 4.4 %all-to-all-start.1 = ((bf16[16,256,128]{2,1,0:T(8,128)(2,1)}), bf16[16,256,128]{2,1,0:T(8,128)(2,1)}, u32[]{:S(2)}, u32[]{:S(2)}) async-start(bf16[16,256,128]{2,1,0:T(8,128)(2,1)} %bitcast.30), calls=%async_computation.1 | async-start | bytes 2097152 | tf_op jit(solution)/shard_map/all_to_all | solution.py:425
  93.7 1.0 copy-done.3
  94.7 6.2 %gram_part.3 = (bf16[8,128,256]{2,1,0:T(8,128)(2,1)S(1)}, bf16[8,128,256]{2,1,0:T(8,128)(2,1)}, bf16[128,1024]{1,0:T(8,128)(2,1)}, bf16[128,1024]{1,0:T(8,128)(2,1)}) custom-call(s32[11]{0:T(128)S(1)} %pad_add_fusion.2.ids, bf16[256,1024]{1,0:T(8,128)(2,1)S(1)} %multiply_convert_fusion.1.refs_0_.half, bf16[256,1024]{1,0:T(8,128)(2,1)} %collective-permute-done.7.refs_1_, ...), custom_call_target="tpu_custom_call" | custom-call | flops 1048576 | bytes 4096 | tf_op jit(solution)/shard_map/gram_part/pallas_call | solution.py:183
  101.7 2.4 %collective-permute-start.21 = (bf16[128,1024]{1,0:T(8,128)(2,1)}, bf16[128,1024]{1,0:T(8,128)(2,1)S(1)}, u32[]{:S(2)}, u32[]{:S(2)}) collective-permute-start(bf16[128,1024]{1,0:T(8,128)(2,1)} %get-tuple-element.58), channel_id=1, source_target_pairs={{0,0},{97,1},{64,2},{33,3},{32,4},{65,5},{96,6},{1,7},{16,8},{113,... | collective-permute-start | bytes 786440 | tf_op jit(solution)/shard_map/ppermute | solution.py:430
  104.7 1.2 partner.1
  105.8 6.4 %all-to-all-done.1.received = bf16[16,256,128]{2,1,0:T(8,128)(2,1)} async-done(((bf16[16,256,128]{2,1,0:T(8,128)(2,1)}), bf16[16,256,128]{2,1,0:T(8,128)(2,1)}, u32[]{:S(2)}, u32[]{:S(2)}) %all-to-all-start.1) | async-done | bytes 1048608 | tf_op jit(solution)/shard_map/all_to_all | solution.py:425
  112.3 1.0 copy-done.15
  113.3 1.6 blend.1
  114.9 2.0 %collective-permute-done.21.same = bf16[128,1024]{1,0:T(8,128)(2,1)S(1)} collective-permute-done((bf16[128,1024]{1,0:T(8,128)(2,1)}, bf16[128,1024]{1,0:T(8,128)(2,1)S(1)}, u32[]{:S(2)}, u32[]{:S(2)}) %collective-permute-start.21) | collective-permute-done | bytes 262176 | tf_op jit(solution)/shard_map/ppermute | solution.py:430
  116.9 23.7 %all_to_all.25.mixed = bf16[8,256,256]{2,1,0:T(8,128)(2,1)S(1)} all-to-all(bf16[8,256,256]{2,1,0:T(8,128)(2,1)S(1)} %blend.1), channel_id=1, replica_groups=mesh['y1'=2,'y0'=2,'xh'=2,'xl'=2,'z1'=2,'z0'=2,'k'=2] {'xl','z1','z0'}, dimensions={0} | all-to-all | bytes 2097152 | tf_op jit(solution)/shard_map/all_to_all | solution.py:432
  140.7 1.9 collective-permute-done.22.traded
  142.6 3.3 %second_view.1 = (f32[256,1024]{1,0:T(8,128)S(1)}, bf16[16,160,256]{2,1,0:T(8,128)(2,1)S(1)}) custom-call(s32[11]{0:T(128)S(1)} %pad_add_fusion.2.ids, bf16[8,256,256]{2,1,0:T(8,128)(2,1)S(1)} %all_to_all.25.mixed, bf16[8,128,256]{2,1,0:T(8,128)(2,1)S(1)} %collective-permute-done.22.traded, f32[2,1024]{1,0:T(2,128)S(1)} %partner.1, ...), custom_call_target="tpu_custom_call" | custom-call | flops 1073741824 | bytes 4194304 | tf_op jit(solution)/shard_map/second_view/pallas_call | solution.py:265
  146.0 23.6 %all_to_all.26.last = bf16[16,160,256]{2,1,0:T(8,128)(2,1)S(1)} all-to-all(bf16[16,160,256]{2,1,0:T(8,128)(2,1)S(1)} %get-tuple-element.61), channel_id=1, replica_groups=mesh['y1'=2,'y0'=2,'xh'=2,'xl'=2,'z1'=2,'z0'=2,'k'=2] {'y1','y0','xh','xl'}, dimensions={0} | all-to-all | bytes 2621440 | tf_op jit(solution)/shard_map/all_to_all | solution.py:436
  169.5 4.4 %collective-permute-start.25 = (bf16[128,1024]{1,0:T(8,128)(2,1)}, bf16[128,1024]{1,0:T(8,128)(2,1)}, u32[]{:S(2)}, u32[]{:S(2)}) collective-permute-start(bf16[128,1024]{1,0:T(8,128)(2,1)} %get-tuple-element.70), channel_id=1, source_target_pairs={{1,0},{96,1},{65,2},{32,3},{33,4},{64,5},{97,6},{0,7},{17,8},{112,... | collective-permute-start | bytes 786440 | tf_op jit(solution)/shard_map/ppermute | solution.py:438
  174.0 3.8 %first_view.1 = (f32[128,1024]{1,0:T(8,128)S(1)}, bf16[128,1024]{1,0:T(8,128)(2,1)}, f32[8,1024]{1,0:T(8,128)S(1)}, f32[32,256]{1,0:T(8,128)S(1)}) custom-call(s32[6]{0:T(128)S(1)} %pad_add_fusion.1.ids, bf16[16,160,256]{2,1,0:T(8,128)(2,1)S(1)} %all_to_all.26.last, bf16[256,1024]{1,0:T(8,128)(2,1)S(1)} %pad_maximum_fusion.refs_0_, ...), custom_call_target="tpu_custom_call" | custom-call | flops 1048576 | bytes 4096 | tf_op jit(solution)/shard_map/first_view/pallas_call | solution.py:310
  177.9 2.4 %finish_second.1 = f32[256,1024]{1,0:T(8,128)} custom-call(s32[3]{0:T(128)S(1)} %pad_add_fusion.ids, f32[32,256]{1,0:T(8,128)S(1)} %get-tuple-element.73.terms, f32[2,1024]{1,0:T(2,128)S(1)} %pad_maximum_fusion.4.scales, f32[256,1024]{1,0:T(8,128)S(1)} %copy-done.1, f32[256,1024]{1,0:T(8,128)S(1)} %get-tuple-element.74.up, ...), custom_call_target="tpu_custom_call" | custom-call | flops 1048576 | bytes 65536 | tf_op jit(solution)/shard_map/finish_second/pallas_call | solution.py:322
  181.1 3.6 %all-to-all-start.4 = ((f32[8,8,1024]{2,1,0:T(8,128)}), f32[8,8,1024]{2,1,0:T(8,128)S(1)}, u32[]{:S(2)}, u32[]{:S(2)}) async-start(f32[8,8,1024]{2,1,0:T(8,128)} %broadcast_in_dim.5), calls=%async_computation.4 | async-start | bytes 524288 | tf_op jit(solution)/shard_map/all_to_all | solution.py:32
  184.7 1.0 arrange_block.1.block
  186.5 4.3 %all-to-all-done.4.sums = f32[8,8,1024]{2,1,0:T(8,128)S(1)} async-done(((f32[8,8,1024]{2,1,0:T(8,128)}), f32[8,8,1024]{2,1,0:T(8,128)S(1)}, u32[]{:S(2)}, u32[]{:S(2)}) %all-to-all-start.4) | async-done | bytes 262176 | tf_op jit(solution)/shard_map/all_to_all | solution.py:32
  190.8 1.0 copy-done.13
  191.9 1.0 copy-done.17
  192.9 2.3 %finish_first.1 = (f32[128,2048]{1,0:T(8,128)}, f32[1,1]{1,0:T(1,128)}) custom-call(s32[3]{0:T(128)S(1)} %pad_add_fusion.ids, f32[8,8,1024]{2,1,0:T(8,128)S(1)} %all-to-all-done.4.sums, f32[2,2048]{1,0:T(2,128)S(1)} %pad_maximum_fusion.2.scales, f32[128,2048]{1,0:T(8,128)S(1)} %copy-done, f32[128,1024]{1,0:T(8,128)S(1)} %copy-done.13, ...), custom_call_target="tpu_custom_call" | custom-call | flops 1048576 | bytes 65536 | tf_op jit(solution)/shard_map/finish_first/pallas_call | solution.py:372
  (85 shorter events, 13.9 us)
Async XLA Ops:
  0.6 1.5 copy-start.1
  2.1 20.3 %copy-start = (f32[128,2048]{1,0:T(8,128)S(1)}, f32[128,2048]{1,0:T(8,128)}, u32[]{:S(2)}) copy-start(f32[128,2048]{1,0:T(8,128)} %view.2) | copy-start | bytes 3145732
  2.3 12.7 %collective-permute-start.2 = (f32[2,1024]{1,0:T(2,128)S(1)}, f32[2,1024]{1,0:T(2,128)S(1)}, u32[]{:S(2)}, u32[]{:S(2)}) collective-permute-start(f32[2,1024]{1,0:T(2,128)S(1)} %pad_maximum_fusion.3), channel_id=1, source_target_pairs={{0,96},{32,0},{64,32},{96,64},{1,97},{33,1},{65,33},{97,65},{2,98}... | collective-permute-start | bytes 24584 | tf_op jit(solution)/shard_map/ppermute | solution.py:384
  2.4 12.7 %collective-permute-start.1 = (f32[2,1024]{1,0:T(2,128)S(1)}, f32[2,1024]{1,0:T(2,128)S(1)}, u32[]{:S(2)}, u32[]{:S(2)}) collective-permute-start(f32[2,1024]{1,0:T(2,128)S(1)} %pad_maximum_fusion.3), channel_id=1, source_target_pairs={{0,64},{32,96},{64,0},{96,32},{1,65},{33,97},{65,1},{97,33},{2,66}... | collective-permute-start | bytes 24584 | tf_op jit(solution)/shard_map/ppermute | solution.py:384
  4.9 10.2 %collective-permute-start = (f32[2,1024]{1,0:T(2,128)S(1)}, f32[2,1024]{1,0:T(2,128)S(1)}, u32[]{:S(2)}, u32[]{:S(2)}) collective-permute-start(f32[2,1024]{1,0:T(2,128)S(1)} %pad_maximum_fusion.3), channel_id=1, source_target_pairs={{0,32},{32,64},{64,96},{96,0},{1,33},{33,65},{65,97},{97,1},{2,34}... | collective-permute-start | bytes 24584 | tf_op jit(solution)/shard_map/ppermute | solution.py:384
  7.3 14.9 %all-to-all-start = ((f32[16,2,2048]{2,1,0:T(2,128)}), f32[16,2,2048]{2,1,0:T(2,128)S(1)}, u32[]{:S(2)}, u32[]{:S(2)}) async-start(f32[16,2,2048]{2,1,0:T(2,128)} %broadcast_in_dim.4), calls=%async_computation | async-start | bytes 524288 | tf_op jit(solution)/shard_map/all_to_all | solution.py:32
  15.1 6.5 %collective-permute-start.3 = (f32[2,1024]{1,0:T(2,128)S(1)}, f32[2,1024]{1,0:T(2,128)S(1)}, u32[]{:S(2)}, u32[]{:S(2)}) collective-permute-start(f32[2,1024]{1,0:T(2,128)S(1)} %add_add_fusion), channel_id=1, source_target_pairs={{0,16},{16,0},{1,17},{17,1},{2,18},{18,2},{3,19},{19,3},{4,20},{20... | collective-permute-start | bytes 24584 | tf_op jit(solution)/shard_map/ppermute | solution.py:385
  24.0 6.9 %collective-permute-start.4 = (bf16[128,1024]{1,0:T(8,128)(2,1)S(1)}, bf16[128,1024]{1,0:T(8,128)(2,1)S(1)}, u32[]{:S(2)}, u32[]{:S(2)}) collective-permute-start(bf16[128,1024]{1,0:T(8,128)(2,1)S(1)} %bitcast.31), channel_id=1, source_target_pairs={{0,8},{8,0},{1,9},{9,1},{2,10},{10,2},{3,11},{11,3},{4,12},{12,4},... | collective-permute-start | bytes 786440 | tf_op jit(solution)/shard_map/ppermute | solution.py:405
  25.1 12.8 %collective-permute-start.8 = (bf16[256,1024]{1,0:T(8,128)(2,1)S(1)}, bf16[256,1024]{1,0:T(8,128)(2,1)}, u32[]{:S(2)}, u32[]{:S(2)}) collective-permute-start(bf16[256,1024]{1,0:T(8,128)(2,1)S(1)} %multiply_convert_fusion.1.refs_0_.half), channel_id=1, source_target_pairs={{0,96},{32,0},{64,32},{96,64},{1,97},{33,1},{65,33},{97,65},{2,98}... | collective-permute-start | bytes 1572872 | tf_op jit(solution)/shard_map/ppermute | solution.py:95
  25.1 13.1 %collective-permute-start.7 = (bf16[256,1024]{1,0:T(8,128)(2,1)S(1)}, bf16[256,1024]{1,0:T(8,128)(2,1)}, u32[]{:S(2)}, u32[]{:S(2)}) collective-permute-start(bf16[256,1024]{1,0:T(8,128)(2,1)S(1)} %multiply_convert_fusion.1.refs_0_.half), channel_id=1, source_target_pairs={{0,32},{32,64},{64,96},{96,0},{1,33},{33,65},{65,97},{97,1},{2,34}... | collective-permute-start | bytes 1572872 | tf_op jit(solution)/shard_map/ppermute | solution.py:95
  31.1 13.2 %collective-permute-start.9 = (bf16[256,1024]{1,0:T(8,128)(2,1)S(1)}, bf16[256,1024]{1,0:T(8,128)(2,1)}, u32[]{:S(2)}, u32[]{:S(2)}) collective-permute-start(bf16[256,1024]{1,0:T(8,128)(2,1)S(1)} %multiply_convert_fusion.1.refs_0_.half), channel_id=1, source_target_pairs={{0,16},{16,0},{1,17},{17,1},{2,18},{18,2},{3,19},{19,3},{4,20},{20... | collective-permute-start | bytes 1572872 | tf_op jit(solution)/shard_map/ppermute | solution.py:99
  33.6 12.7 %collective-permute-start.6 = (bf16[256,1024]{1,0:T(8,128)(2,1)S(1)}, bf16[256,1024]{1,0:T(8,128)(2,1)}, u32[]{:S(2)}, u32[]{:S(2)}) collective-permute-start(bf16[256,1024]{1,0:T(8,128)(2,1)S(1)} %pad_maximum_fusion.refs_0_), channel_id=1, source_target_pairs={{0,6},{2,0},{4,2},{6,4},{1,7},{3,1},{5,3},{7,5},{8,14},{10,8},{12,... | collective-permute-start | bytes 1572872 | tf_op jit(solution)/shard_map/ppermute | solution.py:95
  36.2 13.3 %collective-permute-start.5 = (bf16[256,1024]{1,0:T(8,128)(2,1)S(1)}, bf16[256,1024]{1,0:T(8,128)(2,1)}, u32[]{:S(2)}, u32[]{:S(2)}) collective-permute-start(bf16[256,1024]{1,0:T(8,128)(2,1)S(1)} %pad_maximum_fusion.refs_0_), channel_id=1, source_target_pairs={{0,2},{2,4},{4,6},{6,0},{1,3},{3,5},{5,7},{7,1},{8,10},{10,12},{12... | collective-permute-start | bytes 1572872 | tf_op jit(solution)/shard_map/ppermute | solution.py:95
  50.7 8.5 %collective-permute-start.10 = (bf16[256,1024]{1,0:T(8,128)(2,1)S(1)}, bf16[256,1024]{1,0:T(8,128)(2,1)S(1)}, u32[]{:S(2)}, u32[]{:S(2)}) collective-permute-start(bf16[256,1024]{1,0:T(8,128)(2,1)S(1)} %broadcast_select_fusion), channel_id=1, source_target_pairs={{0,2},{1,7},{2,4},{3,1},{4,6},{5,3},{6,0},{7,5},{8,10},{9,15},{10,... | collective-permute-start | bytes 1572872 | tf_op jit(solution)/shard_map/ppermute | solution.py:413
  51.0 13.8 %collective-permute-start.16 = (bf16[256,1024]{1,0:T(8,128)(2,1)}, bf16[256,1024]{1,0:T(8,128)(2,1)}, u32[]{:S(2)}, u32[]{:S(2)}) collective-permute-start(bf16[256,1024]{1,0:T(8,128)(2,1)} %collective-permute-done.9.refs_4_), channel_id=1, source_target_pairs={{0,96},{32,0},{64,32},{96,64},{1,97},{33,1},{65,33},{97,65},{2,98}... | collective-permute-start | bytes 1572872 | tf_op jit(solution)/shard_map/ppermute | solution.py:95
  51.0 14.7 %collective-permute-start.15 = (bf16[256,1024]{1,0:T(8,128)(2,1)}, bf16[256,1024]{1,0:T(8,128)(2,1)S(1)}, u32[]{:S(2)}, u32[]{:S(2)}) collective-permute-start(bf16[256,1024]{1,0:T(8,128)(2,1)} %collective-permute-done.9.refs_4_), channel_id=1, source_target_pairs={{0,32},{32,64},{64,96},{96,0},{1,33},{33,65},{65,97},{97,1},{2,34}... | collective-permute-start | bytes 1572872 | tf_op jit(solution)/shard_map/ppermute | solution.py:95
  59.2 7.3 %collective-permute-start.14 = (bf16[256,1024]{1,0:T(8,128)(2,1)S(1)}, bf16[256,1024]{1,0:T(8,128)(2,1)S(1)}, u32[]{:S(2)}, u32[]{:S(2)}) collective-permute-start(bf16[256,1024]{1,0:T(8,128)(2,1)S(1)} %collective-permute-done.10.refs_3_), channel_id=1, source_target_pairs={{0,1},{1,0},{2,3},{3,2},{4,5},{5,4},{6,7},{7,6},{8,9},{9,8},{10,11... | collective-permute-start | bytes 1572872 | tf_op jit(solution)/shard_map/ppermute | solution.py:99
  63.5 0.8 copy-start.5
  64.3 5.3 %collective-permute-start.11 = (bf16[256,1024]{1,0:T(8,128)(2,1)S(1)}, bf16[256,1024]{1,0:T(8,128)(2,1)}, u32[]{:S(2)}, u32[]{:S(2)}) collective-permute-start(bf16[256,1024]{1,0:T(8,128)(2,1)S(1)} %pad_maximum_fusion.refs_0_), channel_id=1, source_target_pairs={{0,1},{1,0},{2,3},{3,2},{4,5},{5,4},{6,7},{7,6},{8,9},{9,8},{10,11... | collective-permute-start | bytes 1572872 | tf_op jit(solution)/shard_map/ppermute | solution.py:99
  64.3 5.3 %collective-permute-start.12 = (bf16[256,1024]{1,0:T(8,128)(2,1)}, bf16[256,1024]{1,0:T(8,128)(2,1)}, u32[]{:S(2)}, u32[]{:S(2)}) collective-permute-start(bf16[256,1024]{1,0:T(8,128)(2,1)} %collective-permute-done.5.refs_1_), channel_id=1, source_target_pairs={{0,1},{1,0},{2,3},{3,2},{4,5},{5,4},{6,7},{7,6},{8,9},{9,8},{10,11... | collective-permute-start | bytes 1572872 | tf_op jit(solution)/shard_map/ppermute | solution.py:99
  64.8 4.7 %collective-permute-start.13 = (bf16[256,1024]{1,0:T(8,128)(2,1)}, bf16[256,1024]{1,0:T(8,128)(2,1)}, u32[]{:S(2)}, u32[]{:S(2)}) collective-permute-start(bf16[256,1024]{1,0:T(8,128)(2,1)} %collective-permute-done.6.refs_2_), channel_id=1, source_target_pairs={{0,1},{1,0},{2,3},{3,2},{4,5},{5,4},{6,7},{7,6},{8,9},{9,8},{10,11... | collective-permute-start | bytes 1572872 | tf_op jit(solution)/shard_map/ppermute | solution.py:99
  65.7 0.8 copy-start.2
  66.5 12.5 %collective-permute-start.17 = (bf16[256,1024]{1,0:T(8,128)(2,1)}, bf16[256,1024]{1,0:T(8,128)(2,1)}, u32[]{:S(2)}, u32[]{:S(2)}) collective-permute-start(bf16[256,1024]{1,0:T(8,128)(2,1)} %collective-permute-done.7.refs_1_), channel_id=1, source_target_pairs={{0,32},{32,64},{64,96},{96,0},{1,33},{33,65},{65,97},{97,1},{2,34}... | collective-permute-start | bytes 1572872 | tf_op jit(solution)/shard_map/ppermute | solution.py:416
  66.5 0.8 copy-start.8
  67.3 14.1 %collective-permute-start.18 = (bf16[256,1024]{1,0:T(8,128)(2,1)}, bf16[256,1024]{1,0:T(8,128)(2,1)}, u32[]{:S(2)}, u32[]{:S(2)}) collective-permute-start(bf16[256,1024]{1,0:T(8,128)(2,1)} %collective-permute-done.16.refs_6_), channel_id=1, source_target_pairs={{0,96},{32,0},{64,32},{96,64},{1,97},{33,1},{65,33},{97,65},{2,98}... | collective-permute-start | bytes 1572872 | tf_op jit(solution)/shard_map/ppermute | solution.py:418
  69.5 1.0 copy-start.6
  70.6 1.0 copy-start.9
  77.0 1.0 copy-start.11
  81.4 23.3 %collective-permute-start.20 = (bf16[256,1024]{1,0:T(8,128)(2,1)}, bf16[256,1024]{1,0:T(8,128)(2,1)}, u32[]{:S(2)}, u32[]{:S(2)}) collective-permute-start(bf16[256,1024]{1,0:T(8,128)(2,1)} %bitcast.19), channel_id=1, source_target_pairs={{0,0},{13,1},{18,2},{31,3},{39,4},{42,5},{53,6},{56,7},{66,8},{79,... | collective-permute-start | bytes 1572872 | tf_op jit(solution)/shard_map/ppermute | solution.py:424
  89.3 23.0 %all-to-all-start.1 = ((bf16[16,256,128]{2,1,0:T(8,128)(2,1)}), bf16[16,256,128]{2,1,0:T(8,128)(2,1)}, u32[]{:S(2)}, u32[]{:S(2)}) async-start(bf16[16,256,128]{2,1,0:T(8,128)(2,1)} %bitcast.30), calls=%async_computation.1 | async-start | bytes 2097152 | tf_op jit(solution)/shard_map/all_to_all | solution.py:425
  93.7 1.0 copy-start.3
  100.9 0.8 copy-start.14
  101.7 15.1 %collective-permute-start.21 = (bf16[128,1024]{1,0:T(8,128)(2,1)}, bf16[128,1024]{1,0:T(8,128)(2,1)S(1)}, u32[]{:S(2)}, u32[]{:S(2)}) collective-permute-start(bf16[128,1024]{1,0:T(8,128)(2,1)} %get-tuple-element.58), channel_id=1, source_target_pairs={{0,0},{97,1},{64,2},{33,3},{32,4},{65,5},{96,6},{1,7},{16,8},{113,... | collective-permute-start | bytes 786440 | tf_op jit(solution)/shard_map/ppermute | solution.py:430
  104.2 8.1 %collective-permute-start.19 = (bf16[8,128,256]{2,1,0:T(8,128)(2,1)}, bf16[8,128,256]{2,1,0:T(8,128)(2,1)}, u32[]{:S(2)}, u32[]{:S(2)}) collective-permute-start(bf16[8,128,256]{2,1,0:T(8,128)(2,1)} %get-tuple-element.55), channel_id=1, source_target_pairs={{0,1},{1,0},{2,3},{3,2},{4,5},{5,4},{6,7},{7,6},{8,9},{9,8},{10,11... | collective-permute-start | bytes 1572872 | tf_op jit(solution)/shard_map/ppermute | solution.py:427
  112.3 1.0 copy-start.15
  114.9 27.7 %copy-start.4 = (bf16[256,1024]{1,0:T(8,128)(2,1)S(1)}, bf16[256,1024]{1,0:T(8,128)(2,1)}, u32[]{:S(2)}) copy-start(bf16[256,1024]{1,0:T(8,128)(2,1)} %copy-done.2) | copy-start | bytes 1572868
  140.6 2.0 %collective-permute-start.22 = (bf16[8,128,256]{2,1,0:T(8,128)(2,1)S(1)}, bf16[8,128,256]{2,1,0:T(8,128)(2,1)S(1)}, u32[]{:S(2)}, u32[]{:S(2)}) collective-permute-start(bf16[8,128,256]{2,1,0:T(8,128)(2,1)S(1)} %slice.24), channel_id=1, source_target_pairs={{0,1},{1,0},{2,3},{3,2},{4,5},{5,4},{6,7},{7,6},{8,9},{9,8},{10,11... | collective-permute-start | bytes 1572872 | tf_op jit(solution)/shard_map/ppermute | solution.py:434
  145.9 28.0 %copy-start.7 = (bf16[256,1024]{1,0:T(8,128)(2,1)S(1)}, bf16[256,1024]{1,0:T(8,128)(2,1)}, u32[]{:S(2)}) copy-start(bf16[256,1024]{1,0:T(8,128)(2,1)} %copy-done.5) | copy-start | bytes 1572868
  145.9 28.0 %copy-start.10 = (bf16[256,1024]{1,0:T(8,128)(2,1)S(1)}, bf16[256,1024]{1,0:T(8,128)(2,1)}, u32[]{:S(2)}) copy-start(bf16[256,1024]{1,0:T(8,128)(2,1)} %copy-done.8) | copy-start | bytes 1572868
  169.5 15.2 %collective-permute-start.25 = (bf16[128,1024]{1,0:T(8,128)(2,1)}, bf16[128,1024]{1,0:T(8,128)(2,1)}, u32[]{:S(2)}, u32[]{:S(2)}) collective-permute-start(bf16[128,1024]{1,0:T(8,128)(2,1)} %get-tuple-element.70), channel_id=1, source_target_pairs={{1,0},{96,1},{65,2},{32,3},{33,4},{64,5},{97,6},{0,7},{17,8},{112,... | collective-permute-start | bytes 786440 | tf_op jit(solution)/shard_map/ppermute | solution.py:438
  177.8 2.5 %copy-start.12 = (f32[128,1024]{1,0:T(8,128)}, f32[128,1024]{1,0:T(8,128)S(1)}, u32[]{:S(2)}) copy-start(f32[128,1024]{1,0:T(8,128)S(1)} %get-tuple-element.67.keep) | copy-start | bytes 1572868
  177.8 2.5 %collective-permute-start.23 = (f32[8,1024]{1,0:T(8,128)S(1)}, f32[8,1024]{1,0:T(8,128)S(1)}, u32[]{:S(2)}, u32[]{:S(2)}) collective-permute-start(f32[8,1024]{1,0:T(8,128)S(1)} %get-tuple-element.66), channel_id=1, source_target_pairs={{0,1},{1,0},{2,3},{3,2},{4,5},{5,4},{6,7},{7,6},{8,9},{9,8},{10,11... | collective-permute-start | bytes 98312 | tf_op jit(solution)/shard_map/ppermute | solution.py:445
  177.9 13.0 %collective-permute-start.24 = (bf16[128,1024]{1,0:T(8,128)(2,1)}, bf16[128,1024]{1,0:T(8,128)(2,1)S(1)}, u32[]{:S(2)}, u32[]{:S(2)}) collective-permute-start(bf16[128,1024]{1,0:T(8,128)(2,1)} %get-tuple-element.68), channel_id=1, source_target_pairs={{0,8},{8,0},{1,9},{9,1},{2,10},{10,2},{3,11},{11,3},{4,12},{12,4},... | collective-permute-start | bytes 786440 | tf_op jit(solution)/shard_map/ppermute | solution.py:441
  181.1 9.7 %all-to-all-start.4 = ((f32[8,8,1024]{2,1,0:T(8,128)}), f32[8,8,1024]{2,1,0:T(8,128)S(1)}, u32[]{:S(2)}, u32[]{:S(2)}) async-start(f32[8,8,1024]{2,1,0:T(8,128)} %broadcast_in_dim.5), calls=%async_computation.4 | async-start | bytes 524288 | tf_op jit(solution)/shard_map/all_to_all | solution.py:32
  185.7 0.8 copy-start.16
  190.8 1.0 copy-start.13
  191.9 1.0 copy-start.17

commit v10 on v7

--- a/solution.py
+++ b/solution.py
@@ -444,8 +444,8 @@
     keep, block = tie(keep, block)
     up_own = jax.ShapeDtypeStruct((128, 2048), f32)
     up_own = vmem_call(functools.partial(arrange_kernel, 0), up_own, (ids, keep, traded), "arrange_up", 1 << 33)
-    sums_a, sums_b = tie(sums_a, sums_b)
-    sums_a = spread(sums_a + lax.ppermute(sums_a, "k", SWAP), ("xl", "z1", "z0"), 8)
+    sums_a, sums_b = tie(sums_a + lax.ppermute(sums_a, "k", SWAP), sums_b)
+    sums_a = spread(sums_a, ("xl", "z1", "z0"), 8)
 
     args = (ids, sums_b, jnp.stack([mean_b, inv_b]), view_b, up_b, other_a)
     grad_b = vmem_call(finish_second_kernel, jax.ShapeDtypeStruct((256, 1024), f32), args, "finish_second", 1 << 20)

time: 198 us -> 197 us (level)
  waiting for transfers between devices: 46.2 us -> 43.9 us
  local copies, waits for them, and re-layouts: 14.7 us -> 16.7 us
    all_to_all x2, waiting for transfers between devices: 4.21 us -> 0.63 us  [spread(): return lax.all_to_all(jnp.broadcast_to(x[None], (n,) + x.shape), axes, 0, 0)]
    unnamed x37 -> x41, local copies, waits for them, and re-layouts: 10.3 us -> 12.3 us
where the time goes in v10:
time: 197 us; the launch traced here: 194 us
  starting transfers between devices  53.3 us (27%)
  blocking collectives  47.1 us (24%)
  waiting for transfers between devices  43.9 us (22%)
  Pallas kernels  27.7 us (14%)
  local copies, waits for them, and re-layouts  16.7 us (8%)
  other arithmetic  3.5 us (2%)
    all_to_all x1, blocking collectives, local(): last = lax.all_to_all(last, ('y1', 'y0', 'xh', 'xl'), 0, 0)  23.6 us
    all_to_all x1, blocking collectives, local(): mixed = lax.all_to_all(mixed, ('xl', 'z1', 'z0'), 0, 0)  23.5 us
    unnamed x41, local copies, waits for them, and re-layouts  12.3 us
    pallas_call x2, Pallas kernels, gram_part(): call(functools.partial(gram_kernel, first), out, 0, 'gram_part', pl.ANY,...  11.6 us
    all_to_all x2, starting transfers between devices, spread(): return lax.all_to_all(jnp.broadcast_to(x[None], (n,) + x.shape), axes, 0, 0)  11.2 us
    ppermute x5, starting transfers between devices, trade(): return [lax.ppermute(x, axis, SWAP) for x in blocks]  8.22 us
    ppermute x6, waiting for transfers between devices, ring_near(): return [lax.ppermute(own, ring, AHEAD), lax.ppermute(own, ring, BACK)]  7.21 us
    ppermute x1, starting transfers between devices, local(): other_a = lax.ppermute(send_a.reshape(256, 1024), ROW + COL, pairs_a)  6.99 us
  transfers between devices with their start and end apart: 29, of which 15 were waited for; matrix products, arithmetic and copies ran while one was open for 2% of the time, Pallas kernels for 11%

profile of v10, /device:TPU:9, one launch (start us, length us, event | category | flops | bytes accessed | tf_op | source)
XLA Modules:
  0.0 193.5 jit_solution(15157629296097056281)
XLA Ops:
  0.6 1.4 fusion.5
  2.4 2.5 %collective-permute-start.1 = (f32[2,1024]{1,0:T(2,128)S(1)}, f32[2,1024]{1,0:T(2,128)S(1)}, u32[]{:S(2)}, u32[]{:S(2)}) collective-permute-start(f32[2,1024]{1,0:T(2,128)S(1)} %pad_maximum_fusion.3), channel_id=1, source_target_pairs={{0,64},{32,96},{64,0},{96,32},{1,65},{33,97},{65,1},{97,33},{2,66}... | collective-permute-start | bytes 24584 | tf_op jit(solution)/shard_map/ppermute | solution.py:384
  4.9 1.6 collective-permute-start
  7.3 7.8 %all-to-all-start = ((f32[16,2,2048]{2,1,0:T(2,128)}), f32[16,2,2048]{2,1,0:T(2,128)S(1)}, u32[]{:S(2)}, u32[]{:S(2)}) async-start(f32[16,2,2048]{2,1,0:T(2,128)} %broadcast_in_dim.4), calls=%async_computation | async-start | bytes 524288 | tf_op jit(solution)/shard_map/all_to_all | solution.py:32
  15.1 2.6 %collective-permute-start.3 = (f32[2,1024]{1,0:T(2,128)S(1)}, f32[2,1024]{1,0:T(2,128)S(1)}, u32[]{:S(2)}, u32[]{:S(2)}) collective-permute-start(f32[2,1024]{1,0:T(2,128)S(1)} %add_add_fusion), channel_id=1, source_target_pairs={{0,16},{16,0},{1,17},{17,1},{2,18},{18,2},{3,19},{19,3},{4,20},{20... | collective-permute-start | bytes 24584 | tf_op jit(solution)/shard_map/ppermute | solution.py:385
  17.7 3.9 %collective-permute-done.3 = f32[2,1024]{1,0:T(2,128)S(1)} collective-permute-done((f32[2,1024]{1,0:T(2,128)S(1)}, f32[2,1024]{1,0:T(2,128)S(1)}, u32[]{:S(2)}, u32[]{:S(2)}) %collective-permute-start.3) | collective-permute-done | bytes 8224 | tf_op jit(solution)/shard_map/ppermute | solution.py:385
  22.9 1.1 constant_dynamic-slice_fusion.1
  25.1 1.5 collective-permute-start.7
  26.6 4.4 %collective-permute-done.4 = bf16[128,1024]{1,0:T(8,128)(2,1)S(1)} collective-permute-done((bf16[128,1024]{1,0:T(8,128)(2,1)S(1)}, bf16[128,1024]{1,0:T(8,128)(2,1)S(1)}, u32[]{:S(2)}, u32[]{:S(2)}) %collective-permute-start.4) | collective-permute-done | bytes 262176 | tf_op jit(solution)/shard_map/ppermute | solution.py:405
  31.1 2.5 %collective-permute-start.9 = (bf16[256,1024]{1,0:T(8,128)(2,1)S(1)}, bf16[256,1024]{1,0:T(8,128)(2,1)}, u32[]{:S(2)}, u32[]{:S(2)}) collective-permute-start(bf16[256,1024]{1,0:T(8,128)(2,1)S(1)} %multiply_convert_fusion.1.refs_0_.half), channel_id=1, source_target_pairs={{0,16},{16,0},{1,17},{17,1},{2,18},{18,2},{3,19},{19,3},{4,20},{20... | collective-permute-start | bytes 1572872 | tf_op jit(solution)/shard_map/ppermute | solution.py:99
  33.6 2.6 %collective-permute-start.6 = (bf16[256,1024]{1,0:T(8,128)(2,1)S(1)}, bf16[256,1024]{1,0:T(8,128)(2,1)}, u32[]{:S(2)}, u32[]{:S(2)}) collective-permute-start(bf16[256,1024]{1,0:T(8,128)(2,1)S(1)} %pad_maximum_fusion.refs_0_), channel_id=1, source_target_pairs={{0,6},{2,0},{4,2},{6,4},{1,7},{3,1},{5,3},{7,5},{8,14},{10,8},{12,... | collective-permute-start | bytes 1572872 | tf_op jit(solution)/shard_map/ppermute | solution.py:95
  36.2 1.6 collective-permute-done.8.refs_2_
  38.2 6.1 %collective-permute-done.9.refs_4_ = bf16[256,1024]{1,0:T(8,128)(2,1)} collective-permute-done((bf16[256,1024]{1,0:T(8,128)(2,1)S(1)}, bf16[256,1024]{1,0:T(8,128)(2,1)}, u32[]{:S(2)}, u32[]{:S(2)}) %collective-permute-start.9) | collective-permute-done | bytes 524320 | tf_op jit(solution)/shard_map/ppermute | solution.py:99
  44.3 2.0 %collective-permute-done.6.refs_2_ = bf16[256,1024]{1,0:T(8,128)(2,1)} collective-permute-done((bf16[256,1024]{1,0:T(8,128)(2,1)S(1)}, bf16[256,1024]{1,0:T(8,128)(2,1)}, u32[]{:S(2)}, u32[]{:S(2)}) %collective-permute-start.6) | collective-permute-done | bytes 524320 | tf_op jit(solution)/shard_map/ppermute | solution.py:95
  46.3 3.2 %collective-permute-done.5.refs_1_ = bf16[256,1024]{1,0:T(8,128)(2,1)} collective-permute-done((bf16[256,1024]{1,0:T(8,128)(2,1)S(1)}, bf16[256,1024]{1,0:T(8,128)(2,1)}, u32[]{:S(2)}, u32[]{:S(2)}) %collective-permute-start.5) | collective-permute-done | bytes 524320 | tf_op jit(solution)/shard_map/ppermute | solution.py:95
  49.6 1.1 broadcast_select_fusion
  51.0 1.5 collective-permute-start.15
  52.5 6.7 %collective-permute-done.10.refs_3_ = bf16[256,1024]{1,0:T(8,128)(2,1)S(1)} collective-permute-done((bf16[256,1024]{1,0:T(8,128)(2,1)S(1)}, bf16[256,1024]{1,0:T(8,128)(2,1)S(1)}, u32[]{:S(2)}, u32[]{:S(2)}) %collective-permute-start.10) | collective-permute-done | bytes 524320 | tf_op jit(solution)/shard_map/ppermute | solution.py:413
  59.2 4.3 %collective-permute-start.14 = (bf16[256,1024]{1,0:T(8,128)(2,1)S(1)}, bf16[256,1024]{1,0:T(8,128)(2,1)S(1)}, u32[]{:S(2)}, u32[]{:S(2)}) collective-permute-start(bf16[256,1024]{1,0:T(8,128)(2,1)S(1)} %collective-permute-done.10.refs_3_), channel_id=1, source_target_pairs={{0,1},{1,0},{2,3},{3,2},{4,5},{5,4},{6,7},{7,6},{8,9},{9,8},{10,11... | collective-permute-start | bytes 1572872 | tf_op jit(solution)/shard_map/ppermute | solution.py:99
  67.3 1.5 collective-permute-start.18
  69.5 1.0 copy-done.6
  70.6 1.0 copy-done.9
  71.6 5.4 %gram_part.2 = (bf16[8,2,256,128]{3,2,1,0:T(8,128)(2,1)S(1)}, bf16[2,128,1024]{2,1,0:T(8,128)(2,1)}) custom-call(s32[6]{0:T(128)S(1)} %pad_add_fusion.1.ids, bf16[256,1024]{1,0:T(8,128)(2,1)S(1)} %pad_maximum_fusion.refs_0_, bf16[256,1024]{1,0:T(8,128)(2,1)} %collective-permute-done.5.refs_1_, bf16[256,1024]{1,0:T(8,128)(2,1)} %collective-permute-done.6.refs_2_, ...), custom_call_target="tpu_custom_call" | custom-call | flops 1073741824 | bytes 4194304 | tf_op jit(solution)/shard_map/gram_part/pallas_call | solution.py:183
  78.0 1.0 collective-permute-done.17.refs_3_
  79.0 2.4 %collective-permute-done.18.refs_7_ = bf16[256,1024]{1,0:T(8,128)(2,1)} collective-permute-done((bf16[256,1024]{1,0:T(8,128)(2,1)}, bf16[256,1024]{1,0:T(8,128)(2,1)}, u32[]{:S(2)}, u32[]{:S(2)}) %collective-permute-start.18) | collective-permute-done | bytes 524320 | tf_op jit(solution)/shard_map/ppermute | solution.py:418
  81.4 7.0 %collective-permute-start.20 = (bf16[256,1024]{1,0:T(8,128)(2,1)}, bf16[256,1024]{1,0:T(8,128)(2,1)}, u32[]{:S(2)}, u32[]{:S(2)}) collective-permute-start(bf16[256,1024]{1,0:T(8,128)(2,1)} %bitcast.19), channel_id=1, source_target_pairs={{0,0},{13,1},{18,2},{31,3},{39,4},{42,5},{53,6},{56,7},{66,8},{79,... | collective-permute-start | bytes 1572872 | tf_op jit(solution)/shard_map/ppermute | solution.py:424
  89.3 4.4 %all-to-all-start.1 = ((bf16[16,256,128]{2,1,0:T(8,128)(2,1)}), bf16[16,256,128]{2,1,0:T(8,128)(2,1)}, u32[]{:S(2)}, u32[]{:S(2)}) async-start(bf16[16,256,128]{2,1,0:T(8,128)(2,1)} %bitcast.30), calls=%async_computation.1 | async-start | bytes 2097152 | tf_op jit(solution)/shard_map/all_to_all | solution.py:425
  93.7 1.0 copy-done.3
  94.7 6.2 %gram_part.3 = (bf16[8,128,256]{2,1,0:T(8,128)(2,1)S(1)}, bf16[8,128,256]{2,1,0:T(8,128)(2,1)}, bf16[128,1024]{1,0:T(8,128)(2,1)}, bf16[128,1024]{1,0:T(8,128)(2,1)}) custom-call(s32[11]{0:T(128)S(1)} %pad_add_fusion.2.ids, bf16[256,1024]{1,0:T(8,128)(2,1)S(1)} %multiply_convert_fusion.1.refs_0_.half, bf16[256,1024]{1,0:T(8,128)(2,1)} %collective-permute-done.7.refs_1_, ...), custom_call_target="tpu_custom_call" | custom-call | flops 1048576 | bytes 4096 | tf_op jit(solution)/shard_map/gram_part/pallas_call | solution.py:183
  101.7 2.5 %collective-permute-start.21 = (bf16[128,1024]{1,0:T(8,128)(2,1)}, bf16[128,1024]{1,0:T(8,128)(2,1)S(1)}, u32[]{:S(2)}, u32[]{:S(2)}) collective-permute-start(bf16[128,1024]{1,0:T(8,128)(2,1)} %get-tuple-element.60), channel_id=1, source_target_pairs={{0,0},{97,1},{64,2},{33,3},{32,4},{65,5},{96,6},{1,7},{16,8},{113,... | collective-permute-start | bytes 786440 | tf_op jit(solution)/shard_map/ppermute | solution.py:430
  104.7 1.2 partner.1
  105.9 6.4 %all-to-all-done.1.received = bf16[16,256,128]{2,1,0:T(8,128)(2,1)} async-done(((bf16[16,256,128]{2,1,0:T(8,128)(2,1)}), bf16[16,256,128]{2,1,0:T(8,128)(2,1)}, u32[]{:S(2)}, u32[]{:S(2)}) %all-to-all-start.1) | async-done | bytes 1048608 | tf_op jit(solution)/shard_map/all_to_all | solution.py:425
  112.2 1.0 copy-done.17
  113.3 1.6 blend.1
  114.9 2.2 %collective-permute-done.21.same = bf16[128,1024]{1,0:T(8,128)(2,1)S(1)} collective-permute-done((bf16[128,1024]{1,0:T(8,128)(2,1)}, bf16[128,1024]{1,0:T(8,128)(2,1)S(1)}, u32[]{:S(2)}, u32[]{:S(2)}) %collective-permute-start.21) | collective-permute-done | bytes 262176 | tf_op jit(solution)/shard_map/ppermute | solution.py:430
  117.1 23.5 %all_to_all.25.mixed = bf16[8,256,256]{2,1,0:T(8,128)(2,1)S(1)} all-to-all(bf16[8,256,256]{2,1,0:T(8,128)(2,1)S(1)} %blend.1), channel_id=1, replica_groups=mesh['y1'=2,'y0'=2,'xh'=2,'xl'=2,'z1'=2,'z0'=2,'k'=2] {'xl','z1','z0'}, dimensions={0} | all-to-all | bytes 2097152 | tf_op jit(solution)/shard_map/all_to_all | solution.py:432
  140.7 1.9 collective-permute-done.22.traded
  142.6 3.3 %second_view.1 = (f32[256,1024]{1,0:T(8,128)S(1)}, bf16[16,160,256]{2,1,0:T(8,128)(2,1)S(1)}) custom-call(s32[11]{0:T(128)S(1)} %pad_add_fusion.2.ids, bf16[8,256,256]{2,1,0:T(8,128)(2,1)S(1)} %all_to_all.25.mixed, bf16[8,128,256]{2,1,0:T(8,128)(2,1)S(1)} %collective-permute-done.22.traded, f32[2,1024]{1,0:T(2,128)S(1)} %partner.1, ...), custom_call_target="tpu_custom_call" | custom-call | flops 1073741824 | bytes 4194304 | tf_op jit(solution)/shard_map/second_view/pallas_call | solution.py:265
  146.0 23.6 %all_to_all.26.last = bf16[16,160,256]{2,1,0:T(8,128)(2,1)S(1)} all-to-all(bf16[16,160,256]{2,1,0:T(8,128)(2,1)S(1)} %get-tuple-element.63), channel_id=1, replica_groups=mesh['y1'=2,'y0'=2,'xh'=2,'xl'=2,'z1'=2,'z0'=2,'k'=2] {'y1','y0','xh','xl'}, dimensions={0} | all-to-all | bytes 2621440 | tf_op jit(solution)/shard_map/all_to_all | solution.py:436
  169.6 4.4 %collective-permute-start.24 = (bf16[128,1024]{1,0:T(8,128)(2,1)}, bf16[128,1024]{1,0:T(8,128)(2,1)}, u32[]{:S(2)}, u32[]{:S(2)}) collective-permute-start(bf16[128,1024]{1,0:T(8,128)(2,1)} %get-tuple-element.71), channel_id=1, source_target_pairs={{1,0},{96,1},{65,2},{32,3},{33,4},{64,5},{97,6},{0,7},{17,8},{112,... | collective-permute-start | bytes 786440 | tf_op jit(solution)/shard_map/ppermute | solution.py:438
  174.0 3.8 %first_view.1 = (f32[128,1024]{1,0:T(8,128)S(1)}, bf16[128,1024]{1,0:T(8,128)(2,1)}, f32[8,1024]{1,0:T(8,128)S(1)}, f32[32,256]{1,0:T(8,128)S(1)}) custom-call(s32[6]{0:T(128)S(1)} %pad_add_fusion.1.ids, bf16[16,160,256]{2,1,0:T(8,128)(2,1)S(1)} %all_to_all.26.last, bf16[256,1024]{1,0:T(8,128)(2,1)S(1)} %pad_maximum_fusion.refs_0_, ...), custom_call_target="tpu_custom_call" | custom-call | flops 1048576 | bytes 4096 | tf_op jit(solution)/shard_map/first_view/pallas_call | solution.py:310
  178.8 1.1 collective-permute-done.23
  180.6 3.4 %all-to-all-start.4 = ((f32[8,8,1024]{2,1,0:T(8,128)}), f32[8,8,1024]{2,1,0:T(8,128)S(1)}, u32[]{:S(2)}, u32[]{:S(2)}) async-start(f32[8,8,1024]{2,1,0:T(8,128)} %broadcast_in_dim.5), calls=%async_computation.4 | async-start | bytes 524288 | tf_op jit(solution)/shard_map/all_to_all | solution.py:32
  184.0 1.2 copy-done.13
  185.2 2.3 %finish_second.1 = f32[256,1024]{1,0:T(8,128)} custom-call(s32[3]{0:T(128)S(1)} %pad_add_fusion.ids, f32[32,256]{1,0:T(8,128)S(1)} %get-tuple-element.77.terms, f32[2,1024]{1,0:T(2,128)S(1)} %pad_maximum_fusion.4.scales, f32[256,1024]{1,0:T(8,128)S(1)} %copy-done.1, f32[256,1024]{1,0:T(8,128)S(1)} %copy-done.13, ...), custom_call_target="tpu_custom_call" | custom-call | flops 1048576 | bytes 65536 | tf_op jit(solution)/shard_map/finish_second/pallas_call | solution.py:322
  187.6 1.1 arrange_block.1.block
  190.1 1.0 copy-done.15
  191.2 2.2 %finish_first.1 = (f32[128,2048]{1,0:T(8,128)}, f32[1,1]{1,0:T(1,128)}) custom-call(s32[3]{0:T(128)S(1)} %pad_add_fusion.ids, f32[8,8,1024]{2,1,0:T(8,128)S(1)} %all-to-all-done.4.sums, f32[2,2048]{1,0:T(2,128)S(1)} %pad_maximum_fusion.2.scales, f32[128,2048]{1,0:T(8,128)S(1)} %copy-done, f32[128,2048]{1,0:T(8,128)S(1)} %arrange_up.1.up, ...), custom_call_target="tpu_custom_call" | custom-call | flops 1048576 | bytes 65536 | tf_op jit(solution)/shard_map/finish_first/pallas_call | solution.py:372
  (90 shorter events, 15.3 us)
Async XLA Ops:
  0.6 1.5 copy-start.1
  2.1 20.3 %copy-start = (f32[128,2048]{1,0:T(8,128)S(1)}, f32[128,2048]{1,0:T(8,128)}, u32[]{:S(2)}) copy-start(f32[128,2048]{1,0:T(8,128)} %view.2) | copy-start | bytes 3145732
  2.3 12.7 %collective-permute-start.2 = (f32[2,1024]{1,0:T(2,128)S(1)}, f32[2,1024]{1,0:T(2,128)S(1)}, u32[]{:S(2)}, u32[]{:S(2)}) collective-permute-start(f32[2,1024]{1,0:T(2,128)S(1)} %pad_maximum_fusion.3), channel_id=1, source_target_pairs={{0,96},{32,0},{64,32},{96,64},{1,97},{33,1},{65,33},{97,65},{2,98}... | collective-permute-start | bytes 24584 | tf_op jit(solution)/shard_map/ppermute | solution.py:384
  2.4 12.7 %collective-permute-start.1 = (f32[2,1024]{1,0:T(2,128)S(1)}, f32[2,1024]{1,0:T(2,128)S(1)}, u32[]{:S(2)}, u32[]{:S(2)}) collective-permute-start(f32[2,1024]{1,0:T(2,128)S(1)} %pad_maximum_fusion.3), channel_id=1, source_target_pairs={{0,64},{32,96},{64,0},{96,32},{1,65},{33,97},{65,1},{97,33},{2,66}... | collective-permute-start | bytes 24584 | tf_op jit(solution)/shard_map/ppermute | solution.py:384
  4.9 10.2 %collective-permute-start = (f32[2,1024]{1,0:T(2,128)S(1)}, f32[2,1024]{1,0:T(2,128)S(1)}, u32[]{:S(2)}, u32[]{:S(2)}) collective-permute-start(f32[2,1024]{1,0:T(2,128)S(1)} %pad_maximum_fusion.3), channel_id=1, source_target_pairs={{0,32},{32,64},{64,96},{96,0},{1,33},{33,65},{65,97},{97,1},{2,34}... | collective-permute-start | bytes 24584 | tf_op jit(solution)/shard_map/ppermute | solution.py:384
  7.3 14.9 %all-to-all-start = ((f32[16,2,2048]{2,1,0:T(2,128)}), f32[16,2,2048]{2,1,0:T(2,128)S(1)}, u32[]{:S(2)}, u32[]{:S(2)}) async-start(f32[16,2,2048]{2,1,0:T(2,128)} %broadcast_in_dim.4), calls=%async_computation | async-start | bytes 524288 | tf_op jit(solution)/shard_map/all_to_all | solution.py:32
  15.1 6.5 %collective-permute-start.3 = (f32[2,1024]{1,0:T(2,128)S(1)}, f32[2,1024]{1,0:T(2,128)S(1)}, u32[]{:S(2)}, u32[]{:S(2)}) collective-permute-start(f32[2,1024]{1,0:T(2,128)S(1)} %add_add_fusion), channel_id=1, source_target_pairs={{0,16},{16,0},{1,17},{17,1},{2,18},{18,2},{3,19},{19,3},{4,20},{20... | collective-permute-start | bytes 24584 | tf_op jit(solution)/shard_map/ppermute | solution.py:385
  24.0 6.9 %collective-permute-start.4 = (bf16[128,1024]{1,0:T(8,128)(2,1)S(1)}, bf16[128,1024]{1,0:T(8,128)(2,1)S(1)}, u32[]{:S(2)}, u32[]{:S(2)}) collective-permute-start(bf16[128,1024]{1,0:T(8,128)(2,1)S(1)} %bitcast.31), channel_id=1, source_target_pairs={{0,8},{8,0},{1,9},{9,1},{2,10},{10,2},{3,11},{11,3},{4,12},{12,4},... | collective-permute-start | bytes 786440 | tf_op jit(solution)/shard_map/ppermute | solution.py:405
  25.1 12.8 %collective-permute-start.8 = (bf16[256,1024]{1,0:T(8,128)(2,1)S(1)}, bf16[256,1024]{1,0:T(8,128)(2,1)}, u32[]{:S(2)}, u32[]{:S(2)}) collective-permute-start(bf16[256,1024]{1,0:T(8,128)(2,1)S(1)} %multiply_convert_fusion.1.refs_0_.half), channel_id=1, source_target_pairs={{0,96},{32,0},{64,32},{96,64},{1,97},{33,1},{65,33},{97,65},{2,98}... | collective-permute-start | bytes 1572872 | tf_op jit(solution)/shard_map/ppermute | solution.py:95
  25.1 13.1 %collective-permute-start.7 = (bf16[256,1024]{1,0:T(8,128)(2,1)S(1)}, bf16[256,1024]{1,0:T(8,128)(2,1)}, u32[]{:S(2)}, u32[]{:S(2)}) collective-permute-start(bf16[256,1024]{1,0:T(8,128)(2,1)S(1)} %multiply_convert_fusion.1.refs_0_.half), channel_id=1, source_target_pairs={{0,32},{32,64},{64,96},{96,0},{1,33},{33,65},{65,97},{97,1},{2,34}... | collective-permute-start | bytes 1572872 | tf_op jit(solution)/shard_map/ppermute | solution.py:95
  31.1 13.2 %collective-permute-start.9 = (bf16[256,1024]{1,0:T(8,128)(2,1)S(1)}, bf16[256,1024]{1,0:T(8,128)(2,1)}, u32[]{:S(2)}, u32[]{:S(2)}) collective-permute-start(bf16[256,1024]{1,0:T(8,128)(2,1)S(1)} %multiply_convert_fusion.1.refs_0_.half), channel_id=1, source_target_pairs={{0,16},{16,0},{1,17},{17,1},{2,18},{18,2},{3,19},{19,3},{4,20},{20... | collective-permute-start | bytes 1572872 | tf_op jit(solution)/shard_map/ppermute | solution.py:99
  33.6 12.7 %collective-permute-start.6 = (bf16[256,1024]{1,0:T(8,128)(2,1)S(1)}, bf16[256,1024]{1,0:T(8,128)(2,1)}, u32[]{:S(2)}, u32[]{:S(2)}) collective-permute-start(bf16[256,1024]{1,0:T(8,128)(2,1)S(1)} %pad_maximum_fusion.refs_0_), channel_id=1, source_target_pairs={{0,6},{2,0},{4,2},{6,4},{1,7},{3,1},{5,3},{7,5},{8,14},{10,8},{12,... | collective-permute-start | bytes 1572872 | tf_op jit(solution)/shard_map/ppermute | solution.py:95
  36.2 13.3 %collective-permute-start.5 = (bf16[256,1024]{1,0:T(8,128)(2,1)S(1)}, bf16[256,1024]{1,0:T(8,128)(2,1)}, u32[]{:S(2)}, u32[]{:S(2)}) collective-permute-start(bf16[256,1024]{1,0:T(8,128)(2,1)S(1)} %pad_maximum_fusion.refs_0_), channel_id=1, source_target_pairs={{0,2},{2,4},{4,6},{6,0},{1,3},{3,5},{5,7},{7,1},{8,10},{10,12},{12... | collective-permute-start | bytes 1572872 | tf_op jit(solution)/shard_map/ppermute | solution.py:95
  50.7 8.5 %collective-permute-start.10 = (bf16[256,1024]{1,0:T(8,128)(2,1)S(1)}, bf16[256,1024]{1,0:T(8,128)(2,1)S(1)}, u32[]{:S(2)}, u32[]{:S(2)}) collective-permute-start(bf16[256,1024]{1,0:T(8,128)(2,1)S(1)} %broadcast_select_fusion), channel_id=1, source_target_pairs={{0,2},{1,7},{2,4},{3,1},{4,6},{5,3},{6,0},{7,5},{8,10},{9,15},{10,... | collective-permute-start | bytes 1572872 | tf_op jit(solution)/shard_map/ppermute | solution.py:413
  51.0 13.8 %collective-permute-start.16 = (bf16[256,1024]{1,0:T(8,128)(2,1)}, bf16[256,1024]{1,0:T(8,128)(2,1)}, u32[]{:S(2)}, u32[]{:S(2)}) collective-permute-start(bf16[256,1024]{1,0:T(8,128)(2,1)} %collective-permute-done.9.refs_4_), channel_id=1, source_target_pairs={{0,96},{32,0},{64,32},{96,64},{1,97},{33,1},{65,33},{97,65},{2,98}... | collective-permute-start | bytes 1572872 | tf_op jit(solution)/shard_map/ppermute | solution.py:95
  51.0 14.7 %collective-permute-start.15 = (bf16[256,1024]{1,0:T(8,128)(2,1)}, bf16[256,1024]{1,0:T(8,128)(2,1)S(1)}, u32[]{:S(2)}, u32[]{:S(2)}) collective-permute-start(bf16[256,1024]{1,0:T(8,128)(2,1)} %collective-permute-done.9.refs_4_), channel_id=1, source_target_pairs={{0,32},{32,64},{64,96},{96,0},{1,33},{33,65},{65,97},{97,1},{2,34}... | collective-permute-start | bytes 1572872 | tf_op jit(solution)/shard_map/ppermute | solution.py:95
  59.2 7.3 %collective-permute-start.14 = (bf16[256,1024]{1,0:T(8,128)(2,1)S(1)}, bf16[256,1024]{1,0:T(8,128)(2,1)S(1)}, u32[]{:S(2)}, u32[]{:S(2)}) collective-permute-start(bf16[256,1024]{1,0:T(8,128)(2,1)S(1)} %collective-permute-done.10.refs_3_), channel_id=1, source_target_pairs={{0,1},{1,0},{2,3},{3,2},{4,5},{5,4},{6,7},{7,6},{8,9},{9,8},{10,11... | collective-permute-start | bytes 1572872 | tf_op jit(solution)/shard_map/ppermute | solution.py:99
  63.5 0.8 copy-start.5
  64.3 5.3 %collective-permute-start.11 = (bf16[256,1024]{1,0:T(8,128)(2,1)S(1)}, bf16[256,1024]{1,0:T(8,128)(2,1)}, u32[]{:S(2)}, u32[]{:S(2)}) collective-permute-start(bf16[256,1024]{1,0:T(8,128)(2,1)S(1)} %pad_maximum_fusion.refs_0_), channel_id=1, source_target_pairs={{0,1},{1,0},{2,3},{3,2},{4,5},{5,4},{6,7},{7,6},{8,9},{9,8},{10,11... | collective-permute-start | bytes 1572872 | tf_op jit(solution)/shard_map/ppermute | solution.py:99
  64.3 5.3 %collective-permute-start.12 = (bf16[256,1024]{1,0:T(8,128)(2,1)}, bf16[256,1024]{1,0:T(8,128)(2,1)}, u32[]{:S(2)}, u32[]{:S(2)}) collective-permute-start(bf16[256,1024]{1,0:T(8,128)(2,1)} %collective-permute-done.5.refs_1_), channel_id=1, source_target_pairs={{0,1},{1,0},{2,3},{3,2},{4,5},{5,4},{6,7},{7,6},{8,9},{9,8},{10,11... | collective-permute-start | bytes 1572872 | tf_op jit(solution)/shard_map/ppermute | solution.py:99
  64.8 4.8 %collective-permute-start.13 = (bf16[256,1024]{1,0:T(8,128)(2,1)}, bf16[256,1024]{1,0:T(8,128)(2,1)}, u32[]{:S(2)}, u32[]{:S(2)}) collective-permute-start(bf16[256,1024]{1,0:T(8,128)(2,1)} %collective-permute-done.6.refs_2_), channel_id=1, source_target_pairs={{0,1},{1,0},{2,3},{3,2},{4,5},{5,4},{6,7},{7,6},{8,9},{9,8},{10,11... | collective-permute-start | bytes 1572872 | tf_op jit(solution)/shard_map/ppermute | solution.py:99
  65.7 0.8 copy-start.2
  66.5 12.5 %collective-permute-start.17 = (bf16[256,1024]{1,0:T(8,128)(2,1)}, bf16[256,1024]{1,0:T(8,128)(2,1)}, u32[]{:S(2)}, u32[]{:S(2)}) collective-permute-start(bf16[256,1024]{1,0:T(8,128)(2,1)} %collective-permute-done.7.refs_1_), channel_id=1, source_target_pairs={{0,32},{32,64},{64,96},{96,0},{1,33},{33,65},{65,97},{97,1},{2,34}... | collective-permute-start | bytes 1572872 | tf_op jit(solution)/shard_map/ppermute | solution.py:416
  66.5 0.8 copy-start.8
  67.3 14.1 %collective-permute-start.18 = (bf16[256,1024]{1,0:T(8,128)(2,1)}, bf16[256,1024]{1,0:T(8,128)(2,1)}, u32[]{:S(2)}, u32[]{:S(2)}) collective-permute-start(bf16[256,1024]{1,0:T(8,128)(2,1)} %collective-permute-done.16.refs_6_), channel_id=1, source_target_pairs={{0,96},{32,0},{64,32},{96,64},{1,97},{33,1},{65,33},{97,65},{2,98}... | collective-permute-start | bytes 1572872 | tf_op jit(solution)/shard_map/ppermute | solution.py:418
  69.5 1.0 copy-start.6
  70.6 1.0 copy-start.9
  77.0 1.0 copy-start.11
  81.4 23.3 %collective-permute-start.20 = (bf16[256,1024]{1,0:T(8,128)(2,1)}, bf16[256,1024]{1,0:T(8,128)(2,1)}, u32[]{:S(2)}, u32[]{:S(2)}) collective-permute-start(bf16[256,1024]{1,0:T(8,128)(2,1)} %bitcast.19), channel_id=1, source_target_pairs={{0,0},{13,1},{18,2},{31,3},{39,4},{42,5},{53,6},{56,7},{66,8},{79,... | collective-permute-start | bytes 1572872 | tf_op jit(solution)/shard_map/ppermute | solution.py:424
  89.3 23.0 %all-to-all-start.1 = ((bf16[16,256,128]{2,1,0:T(8,128)(2,1)}), bf16[16,256,128]{2,1,0:T(8,128)(2,1)}, u32[]{:S(2)}, u32[]{:S(2)}) async-start(bf16[16,256,128]{2,1,0:T(8,128)(2,1)} %bitcast.30), calls=%async_computation.1 | async-start | bytes 2097152 | tf_op jit(solution)/shard_map/all_to_all | solution.py:425
  93.7 1.0 copy-start.3
  101.0 0.8 copy-start.16
  101.7 15.3 %collective-permute-start.21 = (bf16[128,1024]{1,0:T(8,128)(2,1)}, bf16[128,1024]{1,0:T(8,128)(2,1)S(1)}, u32[]{:S(2)}, u32[]{:S(2)}) collective-permute-start(bf16[128,1024]{1,0:T(8,128)(2,1)} %get-tuple-element.60), channel_id=1, source_target_pairs={{0,0},{97,1},{64,2},{33,3},{32,4},{65,5},{96,6},{1,7},{16,8},{113,... | collective-permute-start | bytes 786440 | tf_op jit(solution)/shard_map/ppermute | solution.py:430
  104.2 8.0 %collective-permute-start.19 = (bf16[8,128,256]{2,1,0:T(8,128)(2,1)}, bf16[8,128,256]{2,1,0:T(8,128)(2,1)}, u32[]{:S(2)}, u32[]{:S(2)}) collective-permute-start(bf16[8,128,256]{2,1,0:T(8,128)(2,1)} %get-tuple-element.57), channel_id=1, source_target_pairs={{0,1},{1,0},{2,3},{3,2},{4,5},{5,4},{6,7},{7,6},{8,9},{9,8},{10,11... | collective-permute-start | bytes 1572872 | tf_op jit(solution)/shard_map/ppermute | solution.py:427
  112.2 1.0 copy-start.17
  114.9 27.7 %copy-start.4 = (bf16[256,1024]{1,0:T(8,128)(2,1)S(1)}, bf16[256,1024]{1,0:T(8,128)(2,1)}, u32[]{:S(2)}) copy-start(bf16[256,1024]{1,0:T(8,128)(2,1)} %copy-done.2) | copy-start | bytes 1572868
  140.6 2.0 %collective-permute-start.22 = (bf16[8,128,256]{2,1,0:T(8,128)(2,1)S(1)}, bf16[8,128,256]{2,1,0:T(8,128)(2,1)S(1)}, u32[]{:S(2)}, u32[]{:S(2)}) collective-permute-start(bf16[8,128,256]{2,1,0:T(8,128)(2,1)S(1)} %slice.24), channel_id=1, source_target_pairs={{0,1},{1,0},{2,3},{3,2},{4,5},{5,4},{6,7},{7,6},{8,9},{9,8},{10,11... | collective-permute-start | bytes 1572872 | tf_op jit(solution)/shard_map/ppermute | solution.py:434
  145.9 23.6 %copy-start.12 = (f32[256,1024]{1,0:T(8,128)}, f32[256,1024]{1,0:T(8,128)S(1)}, u32[]{:S(2)}) copy-start(f32[256,1024]{1,0:T(8,128)S(1)} %get-tuple-element.78.up) | copy-start | bytes 3145732
  146.0 28.1 %copy-start.7 = (bf16[256,1024]{1,0:T(8,128)(2,1)S(1)}, bf16[256,1024]{1,0:T(8,128)(2,1)}, u32[]{:S(2)}) copy-start(bf16[256,1024]{1,0:T(8,128)(2,1)} %copy-done.5) | copy-start | bytes 1572868
  146.0 28.1 %copy-start.10 = (bf16[256,1024]{1,0:T(8,128)(2,1)S(1)}, bf16[256,1024]{1,0:T(8,128)(2,1)}, u32[]{:S(2)}) copy-start(bf16[256,1024]{1,0:T(8,128)(2,1)} %copy-done.8) | copy-start | bytes 1572868
  169.6 18.0 %collective-permute-start.24 = (bf16[128,1024]{1,0:T(8,128)(2,1)}, bf16[128,1024]{1,0:T(8,128)(2,1)}, u32[]{:S(2)}, u32[]{:S(2)}) collective-permute-start(bf16[128,1024]{1,0:T(8,128)(2,1)} %get-tuple-element.71), channel_id=1, source_target_pairs={{1,0},{96,1},{65,2},{32,3},{33,4},{64,5},{97,6},{0,7},{17,8},{112,... | collective-permute-start | bytes 786440 | tf_op jit(solution)/shard_map/ppermute | solution.py:438
  178.7 1.2 collective-permute-start.23
  178.7 10.8 %collective-permute-start.25 = (bf16[128,1024]{1,0:T(8,128)(2,1)}, bf16[128,1024]{1,0:T(8,128)(2,1)S(1)}, u32[]{:S(2)}, u32[]{:S(2)}) collective-permute-start(bf16[128,1024]{1,0:T(8,128)(2,1)} %get-tuple-element.73), channel_id=1, source_target_pairs={{0,8},{8,0},{1,9},{9,1},{2,10},{10,2},{3,11},{11,3},{4,12},{12,4},... | collective-permute-start | bytes 786440 | tf_op jit(solution)/shard_map/ppermute | solution.py:441
  180.6 9.5 %all-to-all-start.4 = ((f32[8,8,1024]{2,1,0:T(8,128)}), f32[8,8,1024]{2,1,0:T(8,128)S(1)}, u32[]{:S(2)}, u32[]{:S(2)}) async-start(f32[8,8,1024]{2,1,0:T(8,128)} %broadcast_in_dim.5), calls=%async_computation.4 | async-start | bytes 524288 | tf_op jit(solution)/shard_map/all_to_all | solution.py:32
  184.0 1.2 copy-start.13
  187.6 1.9 copy-start.19
  188.7 0.8 copy-start.14
  190.1 1.0 copy-start.15
  (1 other events, 0.8 us)
